TPU v7x, 128 devices: a whole 4x4x4 slice. The times are simulated.
128 devices in a mesh: ctx: 16 (over z, y), smp: 8 (over x, core).
Axes of the slice: x: 4, y: 4, z: 4, core: 2. Of those that a mesh axis runs over, the one named last changes fastest.
Arguments:
- layer_input: bfloat16 [8192, 4096], P('ctx'), may hold values from -6 to 6
- proj_weight: bfloat16 [4096, 8192], P(None, 'smp'), may hold values from -0.09375 to 0.09375
- step_size: float32 [8192, 128], P('ctx', 'smp'), may hold values from 0.01 to 0.16
- decay_log: float32 [128], P('smp'), as said below
- skip_gain: float32 [128], P('smp'), may hold values from 0.5 to 1.5
- write_vec: bfloat16 [8192, 8, 128], P('ctx', 'smp'), may hold values from -0.52734375 to 0.52734375
- read_vec: bfloat16 [8192, 8, 128], P('ctx', 'smp'), may hold values from -0.52734375 to 0.52734375
- out_grad: bfloat16 [8192, 8192], P('ctx', 'smp'), may hold values from -6 to 6
- start_state: float32 [16, 128, 64, 128], P('ctx', 'smp'), may hold values from -1 to 1
- fork_grad: float32 [32, 128, 64, 128], P('ctx', 'smp'), may hold values from -4.2426405 to 4.2426405
Outputs:
- input_grad: bfloat16 [8192, 4096], P(('ctx', 'smp'))
- weight_grad: bfloat16 [4096, 8192], P('ctx', 'smp')
- write_grad: float32 [8192, 8, 128], P('ctx', 'smp')
- read_grad: float32 [8192, 8, 128], P('ctx', 'smp')
Inputs may be any that keep to these rules, and one draw needn't show every extreme that they name: Minus exp(decay_log) is each head's decay coefficient.
All inputs are finite; a program needn't handle non-finite values.
Results may differ from a plain program's by a relative error of at most 0.022.
Values may be sent and summed in bfloat16 or wider, within the bound.
No kernel may reach another device: no remote copies, remote signals or barrier semaphores. Data moves between devices by JAX's collectives and lax.ppermute only.
A program may use at most 128 MiB of HBM per device.

v0:
```python
import jax
import jax.numpy as jnp
from jax import lax
from jax.sharding import PartitionSpec as P


def passed_along(block, axis, distance):
    devices = range(lax.axis_size(axis))
    route = [(i - distance, i) for i in devices if i - distance in devices]
    return lax.ppermute(block, axis, route)


def split_product(form, narrow, wide):
    high_part = wide.astype(jnp.bfloat16)
    low_part = (wide - high_part.astype(jnp.float32)).astype(jnp.bfloat16)
    first_term = jnp.einsum(form, narrow, high_part, preferred_element_type=jnp.float32)
    return first_term + jnp.einsum(form, narrow, low_part, preferred_element_type=jnp.float32)


def body(
    layer_input,
    proj_weight,
    step_size,
    decay_log,
    skip_gain,
    write_vec,
    read_vec,
    out_grad,
    start_state,
    fork_grad,
):
    length = layer_input.shape[0]
    head_count = step_size.shape[1]
    groups = write_vec.shape[1]
    per_group = head_count // groups
    head_width = out_grad.shape[1] // head_count
    state_size = write_vec.shape[2]
    projected = jnp.dot(layer_input, proj_weight, preferred_element_type=jnp.float32).astype(
        jnp.bfloat16
    )
    inputs = projected.reshape(length, groups, per_group, head_width)
    grad_heads = out_grad.reshape(length, groups, per_group, head_width)
    cumulative = jnp.cumsum(step_size * -jnp.exp(decay_log), axis=0)
    decays = jnp.exp(cumulative[length - 1])
    starts = jnp.exp(cumulative).reshape(length, groups, per_group)
    weighted = starts[..., None] * read_vec.astype(jnp.float32)[:, :, None, :]
    local_sum = split_product("tghp,tghn->ghpn", grad_heads, weighted).reshape(
        head_count, head_width, state_size
    )
    fork_sum = lax.psum(jnp.sum(fork_grad, axis=0).astype(jnp.bfloat16), "ctx").astype(jnp.float32)
    position = lax.axis_index("ctx")
    final_index = lax.axis_size("ctx") - 1

    def relay_step(turn_index, carried_in):
        incoming = passed_along(
            (local_sum + decays[:, None, None] * carried_in).astype(jnp.bfloat16), "ctx", -1
        ).astype(jnp.float32)
        return jnp.where(position == final_index, fork_sum, incoming)

    carried = lax.fori_loop(0, lax.axis_size("ctx") - 1, relay_step, fork_sum)
    carried = carried.reshape(groups, per_group, head_width, state_size)
    start_block = start_state[0].reshape(groups, per_group, head_width, state_size)
    scores = jnp.einsum("jgn,tgn->gjt", read_vec, write_vec, preferred_element_type=jnp.float32)
    cum_heads = cumulative.T.reshape(groups, per_group, length)
    offsets = cum_heads[:, :, :, None] - cum_heads[:, :, None, :]
    causal = jnp.arange(length)[:, None] >= jnp.arange(length)[None, :]
    kernel = jnp.where(causal, jnp.exp(jnp.minimum(offsets, 0.0)), 0.0)
    step_cols = step_size.T.reshape(groups, per_group, length)[:, :, None, :]
    mixing = (scores[:, None] * kernel * step_cols).astype(jnp.bfloat16)
    within = jnp.einsum("ghjt,jghp->tghp", mixing, grad_heads, preferred_element_type=jnp.float32)
    intersections = jnp.einsum(
        "jghp,tghp->ghjt", grad_heads, inputs, preferred_element_type=jnp.float32
    )
    coupling = jnp.sum(step_cols * kernel * intersections, axis=1).astype(jnp.bfloat16)
    end_weights = (step_size * jnp.exp(cumulative[length - 1][None, :] - cumulative)).reshape(
        length, groups, per_group
    )
    to_inputs = split_product("tgn,ghpn->tghp", write_vec, carried)
    input_state = split_product("tghp,ghpn->tghn", inputs, carried)
    from_start = split_product("tghp,ghpn->tghn", grad_heads, start_block)
    skip_term = skip_gain.reshape(groups, per_group)[None, :, :, None] * grad_heads.astype(
        jnp.float32
    )
    x_wide = within + end_weights[..., None] * to_inputs + skip_term
    x_grad = x_wide.reshape(length, head_count * head_width).astype(jnp.bfloat16)
    write_grad = jnp.einsum(
        "gjt,jgn->tgn", coupling, read_vec, preferred_element_type=jnp.float32
    ) + jnp.sum(end_weights[..., None] * input_state, axis=2)
    read_grad = jnp.einsum(
        "gjt,tgn->jgn", coupling, write_vec, preferred_element_type=jnp.float32
    ) + jnp.sum(starts[..., None] * from_start, axis=2)
    input_grad = lax.psum_scatter(
        lax.dot_general(
            x_grad, proj_weight, (((1,), (1,)), ((), ())), preferred_element_type=jnp.float32
        ).astype(jnp.bfloat16),
        "smp",
        scatter_dimension=0,
        tiled=True,
    )
    scale_factor = (length * lax.axis_size("ctx")) ** (-0.5)
    summed = lax.psum_scatter(
        lax.dot_general(
            layer_input, x_grad, (((0,), (0,)), ((), ())), preferred_element_type=jnp.float32
        ).astype(jnp.bfloat16),
        "ctx",
        scatter_dimension=0,
        tiled=True,
    ).astype(jnp.float32)
    weight_grad = (summed * scale_factor).astype(jnp.bfloat16)
    return (input_grad, weight_grad, write_grad, read_grad)


def solution(mesh):
    placed = (
        P("ctx", None),
        P(None, "smp"),
        P("ctx", "smp"),
        P("smp"),
        P("smp"),
        P("ctx", "smp", None),
        P("ctx", "smp", None),
        P("ctx", "smp"),
        P("ctx", "smp", None, None),
        P("ctx", "smp", None, None),
    )
    return jax.shard_map(
        body,
        mesh=mesh,
        in_specs=placed,
        out_specs=(
            P(("ctx", "smp"), None),
            P("ctx", "smp"),
            P("ctx", "smp", None),
            P("ctx", "smp", None),
        ),
        check_vma=False,
    )
```

profile of v0, /device:TPU:1, one launch (start us, length us, event | category | flops | bytes accessed | tf_op | source)
XLA Modules:
  0.0 409.5 jit_solution(4191976552574270695)
XLA Ops:
  7.2 2.1 reduce_sum.40
  9.4 0.7 exponential_negate_fusion
  10.0 0.8 copy_bitcast_fusion.1
  10.9 1.1 reduce-window.6
  12.5 0.9 exponential_multiply_fusion
  13.3 1.6 copy.41
  14.9 0.9 bitcast_convert_fusion
  15.9 1.4 fusion.6
  17.3 1.4 fusion.19
  18.7 0.8 iota_compare_fusion
  19.5 1.7 copy.43
  21.1 1.3 fusion.35
  22.4 75.8 %all-reduce.2.cloned.1.call-done = bf16[16,64,128]{2,1,0:T(8,128)(2,1)} async-done(((bf16[16,64,128]{2,1,0:T(8,128)(2,1)}), bf16[16,64,128]{2,1,0:T(8,128)(2,1)}) %all-reduce.2.cloned.1.call-update) | async-done | bytes 262160 | tf_op jit(solution)/shard_map/psum | solution.py:50
  98.2 1.0 convert_element_type.119
  99.2 141.8 %while.12 = (s32[]{:T(128)}, f32[16,64,128]{2,1,0:T(8,128)S(1)}, pred[]{:T(512)}, f32[16]{0:T(128)S(1)}, f32[16,64,128]{2,1,0:T(8,128)S(1)}, /*index=5*/f32[16,64,128]{2,1,0:T(8,128)S(1)}, s32[]{:T(128)}) while((s32[]{:T(128)}, f32[16,64,128]{2,1,0:T(8,128)S(1)}, pred[]{:T(512)}, f32[16]{0:T(128)S(1)}, f32[16,64,128]{2,1,0:T(8,128)S(1)}, ...), condition=%wide.region_5.6_spmd, body=%wide.region_4.5_spmd.sunk | while | flops 655362 | bytes 3670198 | solution.py:60
  99.4 1.3 collective-permute-start
  100.7 6.4 %collective-permute-done = bf16[16,64,128]{2,1,0:T(8,128)(2,1)S(1)} collective-permute-done((bf16[16,64,128]{2,1,0:T(8,128)(2,1)S(1)}, bf16[16,64,128]{2,1,0:T(8,128)(2,1)S(1)}, u32[]{:S(2)}, u32[]{:S(2)}) %collective-permute-start) | collective-permute-done | bytes 262176 | tf_op jit(solution)/shard_map/while/body/eval_jaxpr/ppermute | solution.py:10
  107.3 1.3 collective-permute-start
  108.6 5.8 %collective-permute-done = bf16[16,64,128]{2,1,0:T(8,128)(2,1)S(1)} collective-permute-done((bf16[16,64,128]{2,1,0:T(8,128)(2,1)S(1)}, bf16[16,64,128]{2,1,0:T(8,128)(2,1)S(1)}, u32[]{:S(2)}, u32[]{:S(2)}) %collective-permute-start) | collective-permute-done | bytes 262176 | tf_op jit(solution)/shard_map/while/body/eval_jaxpr/ppermute | solution.py:10
  114.6 1.3 collective-permute-start
  115.9 5.8 %collective-permute-done = bf16[16,64,128]{2,1,0:T(8,128)(2,1)S(1)} collective-permute-done((bf16[16,64,128]{2,1,0:T(8,128)(2,1)S(1)}, bf16[16,64,128]{2,1,0:T(8,128)(2,1)S(1)}, u32[]{:S(2)}, u32[]{:S(2)}) %collective-permute-start) | collective-permute-done | bytes 262176 | tf_op jit(solution)/shard_map/while/body/eval_jaxpr/ppermute | solution.py:10
  121.9 1.3 collective-permute-start
  123.2 5.8 %collective-permute-done = bf16[16,64,128]{2,1,0:T(8,128)(2,1)S(1)} collective-permute-done((bf16[16,64,128]{2,1,0:T(8,128)(2,1)S(1)}, bf16[16,64,128]{2,1,0:T(8,128)(2,1)S(1)}, u32[]{:S(2)}, u32[]{:S(2)}) %collective-permute-start) | collective-permute-done | bytes 262176 | tf_op jit(solution)/shard_map/while/body/eval_jaxpr/ppermute | solution.py:10
  129.3 1.3 collective-permute-start
  130.6 7.4 %collective-permute-done = bf16[16,64,128]{2,1,0:T(8,128)(2,1)S(1)} collective-permute-done((bf16[16,64,128]{2,1,0:T(8,128)(2,1)S(1)}, bf16[16,64,128]{2,1,0:T(8,128)(2,1)S(1)}, u32[]{:S(2)}, u32[]{:S(2)}) %collective-permute-start) | collective-permute-done | bytes 262176 | tf_op jit(solution)/shard_map/while/body/eval_jaxpr/ppermute | solution.py:10
  138.2 1.3 collective-permute-start
  139.5 8.1 %collective-permute-done = bf16[16,64,128]{2,1,0:T(8,128)(2,1)S(1)} collective-permute-done((bf16[16,64,128]{2,1,0:T(8,128)(2,1)S(1)}, bf16[16,64,128]{2,1,0:T(8,128)(2,1)S(1)}, u32[]{:S(2)}, u32[]{:S(2)}) %collective-permute-start) | collective-permute-done | bytes 262176 | tf_op jit(solution)/shard_map/while/body/eval_jaxpr/ppermute | solution.py:10
  147.8 1.3 collective-permute-start
  149.1 9.4 %collective-permute-done = bf16[16,64,128]{2,1,0:T(8,128)(2,1)S(1)} collective-permute-done((bf16[16,64,128]{2,1,0:T(8,128)(2,1)S(1)}, bf16[16,64,128]{2,1,0:T(8,128)(2,1)S(1)}, u32[]{:S(2)}, u32[]{:S(2)}) %collective-permute-start) | collective-permute-done | bytes 262176 | tf_op jit(solution)/shard_map/while/body/eval_jaxpr/ppermute | solution.py:10
  158.7 1.3 collective-permute-start
  160.0 10.8 %collective-permute-done = bf16[16,64,128]{2,1,0:T(8,128)(2,1)S(1)} collective-permute-done((bf16[16,64,128]{2,1,0:T(8,128)(2,1)S(1)}, bf16[16,64,128]{2,1,0:T(8,128)(2,1)S(1)}, u32[]{:S(2)}, u32[]{:S(2)}) %collective-permute-start) | collective-permute-done | bytes 262176 | tf_op jit(solution)/shard_map/while/body/eval_jaxpr/ppermute | solution.py:10
  171.1 1.3 collective-permute-start
  172.4 11.5 %collective-permute-done = bf16[16,64,128]{2,1,0:T(8,128)(2,1)S(1)} collective-permute-done((bf16[16,64,128]{2,1,0:T(8,128)(2,1)S(1)}, bf16[16,64,128]{2,1,0:T(8,128)(2,1)S(1)}, u32[]{:S(2)}, u32[]{:S(2)}) %collective-permute-start) | collective-permute-done | bytes 262176 | tf_op jit(solution)/shard_map/while/body/eval_jaxpr/ppermute | solution.py:10
  184.2 1.3 collective-permute-start
  185.5 9.9 %collective-permute-done = bf16[16,64,128]{2,1,0:T(8,128)(2,1)S(1)} collective-permute-done((bf16[16,64,128]{2,1,0:T(8,128)(2,1)S(1)}, bf16[16,64,128]{2,1,0:T(8,128)(2,1)S(1)}, u32[]{:S(2)}, u32[]{:S(2)}) %collective-permute-start) | collective-permute-done | bytes 262176 | tf_op jit(solution)/shard_map/while/body/eval_jaxpr/ppermute | solution.py:10
  195.5 1.3 collective-permute-start
  196.8 8.1 %collective-permute-done = bf16[16,64,128]{2,1,0:T(8,128)(2,1)S(1)} collective-permute-done((bf16[16,64,128]{2,1,0:T(8,128)(2,1)S(1)}, bf16[16,64,128]{2,1,0:T(8,128)(2,1)S(1)}, u32[]{:S(2)}, u32[]{:S(2)}) %collective-permute-start) | collective-permute-done | bytes 262176 | tf_op jit(solution)/shard_map/while/body/eval_jaxpr/ppermute | solution.py:10
  205.1 1.3 collective-permute-start
  206.4 7.0 %collective-permute-done = bf16[16,64,128]{2,1,0:T(8,128)(2,1)S(1)} collective-permute-done((bf16[16,64,128]{2,1,0:T(8,128)(2,1)S(1)}, bf16[16,64,128]{2,1,0:T(8,128)(2,1)S(1)}, u32[]{:S(2)}, u32[]{:S(2)}) %collective-permute-start) | collective-permute-done | bytes 262176 | tf_op jit(solution)/shard_map/while/body/eval_jaxpr/ppermute | solution.py:10
  213.6 1.3 collective-permute-start
  214.9 7.1 %collective-permute-done = bf16[16,64,128]{2,1,0:T(8,128)(2,1)S(1)} collective-permute-done((bf16[16,64,128]{2,1,0:T(8,128)(2,1)S(1)}, bf16[16,64,128]{2,1,0:T(8,128)(2,1)S(1)}, u32[]{:S(2)}, u32[]{:S(2)}) %collective-permute-start) | collective-permute-done | bytes 262176 | tf_op jit(solution)/shard_map/while/body/eval_jaxpr/ppermute | solution.py:10
  222.2 1.3 collective-permute-start
  223.5 7.9 %collective-permute-done = bf16[16,64,128]{2,1,0:T(8,128)(2,1)S(1)} collective-permute-done((bf16[16,64,128]{2,1,0:T(8,128)(2,1)S(1)}, bf16[16,64,128]{2,1,0:T(8,128)(2,1)S(1)}, u32[]{:S(2)}, u32[]{:S(2)}) %collective-permute-start) | collective-permute-done | bytes 262176 | tf_op jit(solution)/shard_map/while/body/eval_jaxpr/ppermute | solution.py:10
  231.7 1.3 collective-permute-start
  233.0 7.9 %collective-permute-done = bf16[16,64,128]{2,1,0:T(8,128)(2,1)S(1)} collective-permute-done((bf16[16,64,128]{2,1,0:T(8,128)(2,1)S(1)}, bf16[16,64,128]{2,1,0:T(8,128)(2,1)S(1)}, u32[]{:S(2)}, u32[]{:S(2)}) %collective-permute-start) | collective-permute-done | bytes 262176 | tf_op jit(solution)/shard_map/while/body/eval_jaxpr/ppermute | solution.py:10
  241.5 0.4 fusion.32
  241.9 0.7 copy-done.2
  242.9 6.0 %fusion.11 = bf16[512,1,16,64]{0,3,2,1:T(8,128)(2,1)S(1)} fusion(f32[512,1,16,64]{0,3,2,1:T(8,128)S(1)} %bitcast.133, f32[16,64,512]{2,1,0:T(8,128)S(1)} %fusion.32, f32[16,64,512]{2,1,0:T(8,128)S(1)} %fusion.30, bf16[512,16,64]{0,2,1:T(8,128)(2,1)S(1)} %bitcast.126, f32[16,512]{1,0:T(8,128)S(1)} %bitcast.136, f32[16,512]{1,0:T(8,128)S(1)} %get-tuple-element.103, ...), kind=kOutput, calls=%fused_computation.22 | convolution fusion | flops 565182464 | bytes 9797696 | tf_op jit(solution)/shard_map/ghjt,jghp->tghp/dot_general | solution.py:70
  248.9 6.7 %convert_bitcast_fusion = bf16[4096,1024]{0,1:T(8,128)(2,1)} fusion(bf16[512,1024]{0,1:T(8,128)(2,1)S(1)} %bitcast.138, bf16[512,4096]{1,0:T(8,128)(2,1)S(1)} %copy-done.9), kind=kOutput, calls=%fused_computation.6 | convolution fusion | flops 4299161600 | bytes 13631488 | tf_op jit(solution)/shard_map/dot_general | solution.py:102
  255.9 9.6 %convolution_convert_fusion = bf16[512,4096]{1,0:T(8,128)(2,1)} fusion(bf16[512,1024]{0,1:T(8,128)(2,1)S(1)} %bitcast.139, bf16[4096,1024]{1,0:T(8,128)(2,1)} %param.13), kind=kOutput, calls=%fused_computation.11 | convolution fusion | flops 4297064448 | bytes 13631488 | tf_op jit(solution)/shard_map/dot_general | solution.py:93
  265.5 10.2 %convolution_convert_fusion.1 = bf16[512,1024]{1,0:T(8,128)(2,1)} fusion(bf16[512,4096]{1,0:T(8,128)(2,1)} %param.12, bf16[4096,1024]{1,0:T(8,128)(2,1)} %param.13), kind=kOutput, calls=%fused_computation.27 | convolution fusion | flops 4295491584 | bytes 13631488 | tf_op jit(solution)/shard_map/dot_general | solution.py:38
  275.8 1.5 copy.44
  277.3 0.7 fusion.26
  278.0 1.5 fusion.4
  279.6 1.8 copy.46
  281.4 7.8 %fusion = bf16[512,512]{0,1:T(8,128)(2,1)S(1)} fusion(bf16[512,16,64]{0,2,1:T(8,128)(2,1)S(1)} %bitcast.130, bf16[512,16,64]{0,2,1:T(8,128)(2,1)S(1)} %bitcast.129, f32[16,512]{1,0:T(8,128)S(1)} %bitcast.137, f32[16,512]{1,0:T(8,128)S(1)} %get-tuple-element.103, pred[512,512]{0,1:T(8,128)(4,1)} %iota_compare_fusion), kind=kOutput, calls=%fused_computation.3 | convolution fusion | flops 561774592 | bytes 2949120 | tf_op jit(solution)/shard_map/jghp,tghp->ghjt/dot_general | solution.py:71
  289.2 1.0 fusion.23
  290.2 0.8 fusion.41
  291.0 0.8 fusion.5
  292.0 1.0 fusion.22
  293.0 71.6 %reduce-scatter.5.cloned.1.call-done = bf16[256,1024]{0,1:T(8,128)(2,1)} async-done(((bf16[4096,1024]{0,1:T(8,128)(2,1)}), bf16[256,1024]{0,1:T(8,128)(2,1)}) %reduce-scatter.5.cloned.1.call-update) | async-done | bytes 524304 | tf_op jit(solution)/shard_map/reduce_scatter | solution.py:101
  364.5 1.1 multiply_convert_fusion.6
  365.7 1.0 copy.47
  366.7 36.3 %reduce-scatter.3.cloned.1.call-done = bf16[64,4096]{1,0:T(8,128)(2,1)} async-done(((bf16[512,4096]{1,0:T(8,128)(2,1)}), bf16[64,4096]{1,0:T(8,128)(2,1)}) %reduce-scatter.3.cloned.1.call-update) | async-done | bytes 524304 | tf_op jit(solution)/shard_map/reduce_scatter | solution.py:92
  (66 shorter events, 4.5 us)
Async XLA Ops:
  7.2 14.0 %copy-start = (bf16[512,1,128]{2,0,1:T(8,128)(2,1)S(1)}, bf16[512,1,128]{2,0,1:T(8,128)(2,1)}, u32[]{:S(2)}) copy-start(bf16[512,1,128]{2,0,1:T(8,128)(2,1)} %param.17) | copy-start | bytes 393220
  7.2 91.0 %all-reduce.2.cloned.1.call-start = ((), (), s32[]{:S(2)}) async-start(), calls=%async_computation.2 | async-start | bytes 524288 | tf_op jit(solution)/shard_map/psum | solution.py:50
  9.3 355.2 %reduce-scatter.5.cloned.1.call-start = ((), (), s32[]{:S(2)}) async-start(), calls=%async_computation.4 | async-start | bytes 8912896 | tf_op jit(solution)/shard_map/reduce_scatter | solution.py:101
  13.3 6.1 %copy-start.1 = (bf16[512,1024]{1,0:T(8,128)(2,1)S(1)}, bf16[512,1024]{1,0:T(8,128)(2,1)}, u32[]{:S(2)}) copy-start(bf16[512,1024]{1,0:T(8,128)(2,1)} %param.19) | copy-start | bytes 3145732
  17.3 3.8 copy-start.4
  99.4 7.7 %collective-permute-start = (bf16[16,64,128]{2,1,0:T(8,128)(2,1)S(1)}, bf16[16,64,128]{2,1,0:T(8,128)(2,1)S(1)}, u32[]{:S(2)}, u32[]{:S(2)}) collective-permute-start(bf16[16,64,128]{2,1,0:T(8,128)(2,1)S(1)} %add_convert_fusion.2), channel_id=1, source_target_pairs={{8,0},{16,8},{24,16},{32,24},{40,32},{48,40},{56,48},{64,56},{72,6... | collective-permute-start | bytes 786440 | tf_op jit(solution)/shard_map/while/body/eval_jaxpr/ppermute | solution.py:10
  107.3 7.1 %collective-permute-start = (bf16[16,64,128]{2,1,0:T(8,128)(2,1)S(1)}, bf16[16,64,128]{2,1,0:T(8,128)(2,1)S(1)}, u32[]{:S(2)}, u32[]{:S(2)}) collective-permute-start(bf16[16,64,128]{2,1,0:T(8,128)(2,1)S(1)} %add_convert_fusion.2), channel_id=1, source_target_pairs={{8,0},{16,8},{24,16},{32,24},{40,32},{48,40},{56,48},{64,56},{72,6... | collective-permute-start | bytes 786440 | tf_op jit(solution)/shard_map/while/body/eval_jaxpr/ppermute | solution.py:10
  114.6 7.1 %collective-permute-start = (bf16[16,64,128]{2,1,0:T(8,128)(2,1)S(1)}, bf16[16,64,128]{2,1,0:T(8,128)(2,1)S(1)}, u32[]{:S(2)}, u32[]{:S(2)}) collective-permute-start(bf16[16,64,128]{2,1,0:T(8,128)(2,1)S(1)} %add_convert_fusion.2), channel_id=1, source_target_pairs={{8,0},{16,8},{24,16},{32,24},{40,32},{48,40},{56,48},{64,56},{72,6... | collective-permute-start | bytes 786440 | tf_op jit(solution)/shard_map/while/body/eval_jaxpr/ppermute | solution.py:10
  121.9 7.1 %collective-permute-start = (bf16[16,64,128]{2,1,0:T(8,128)(2,1)S(1)}, bf16[16,64,128]{2,1,0:T(8,128)(2,1)S(1)}, u32[]{:S(2)}, u32[]{:S(2)}) collective-permute-start(bf16[16,64,128]{2,1,0:T(8,128)(2,1)S(1)} %add_convert_fusion.2), channel_id=1, source_target_pairs={{8,0},{16,8},{24,16},{32,24},{40,32},{48,40},{56,48},{64,56},{72,6... | collective-permute-start | bytes 786440 | tf_op jit(solution)/shard_map/while/body/eval_jaxpr/ppermute | solution.py:10
  129.3 8.7 %collective-permute-start = (bf16[16,64,128]{2,1,0:T(8,128)(2,1)S(1)}, bf16[16,64,128]{2,1,0:T(8,128)(2,1)S(1)}, u32[]{:S(2)}, u32[]{:S(2)}) collective-permute-start(bf16[16,64,128]{2,1,0:T(8,128)(2,1)S(1)} %add_convert_fusion.2), channel_id=1, source_target_pairs={{8,0},{16,8},{24,16},{32,24},{40,32},{48,40},{56,48},{64,56},{72,6... | collective-permute-start | bytes 786440 | tf_op jit(solution)/shard_map/while/body/eval_jaxpr/ppermute | solution.py:10
  138.2 9.4 %collective-permute-start = (bf16[16,64,128]{2,1,0:T(8,128)(2,1)S(1)}, bf16[16,64,128]{2,1,0:T(8,128)(2,1)S(1)}, u32[]{:S(2)}, u32[]{:S(2)}) collective-permute-start(bf16[16,64,128]{2,1,0:T(8,128)(2,1)S(1)} %add_convert_fusion.2), channel_id=1, source_target_pairs={{8,0},{16,8},{24,16},{32,24},{40,32},{48,40},{56,48},{64,56},{72,6... | collective-permute-start | bytes 786440 | tf_op jit(solution)/shard_map/while/body/eval_jaxpr/ppermute | solution.py:10
  147.8 10.7 %collective-permute-start = (bf16[16,64,128]{2,1,0:T(8,128)(2,1)S(1)}, bf16[16,64,128]{2,1,0:T(8,128)(2,1)S(1)}, u32[]{:S(2)}, u32[]{:S(2)}) collective-permute-start(bf16[16,64,128]{2,1,0:T(8,128)(2,1)S(1)} %add_convert_fusion.2), channel_id=1, source_target_pairs={{8,0},{16,8},{24,16},{32,24},{40,32},{48,40},{56,48},{64,56},{72,6... | collective-permute-start | bytes 786440 | tf_op jit(solution)/shard_map/while/body/eval_jaxpr/ppermute | solution.py:10
  158.7 12.1 %collective-permute-start = (bf16[16,64,128]{2,1,0:T(8,128)(2,1)S(1)}, bf16[16,64,128]{2,1,0:T(8,128)(2,1)S(1)}, u32[]{:S(2)}, u32[]{:S(2)}) collective-permute-start(bf16[16,64,128]{2,1,0:T(8,128)(2,1)S(1)} %add_convert_fusion.2), channel_id=1, source_target_pairs={{8,0},{16,8},{24,16},{32,24},{40,32},{48,40},{56,48},{64,56},{72,6... | collective-permute-start | bytes 786440 | tf_op jit(solution)/shard_map/while/body/eval_jaxpr/ppermute | solution.py:10
  171.1 12.8 %collective-permute-start = (bf16[16,64,128]{2,1,0:T(8,128)(2,1)S(1)}, bf16[16,64,128]{2,1,0:T(8,128)(2,1)S(1)}, u32[]{:S(2)}, u32[]{:S(2)}) collective-permute-start(bf16[16,64,128]{2,1,0:T(8,128)(2,1)S(1)} %add_convert_fusion.2), channel_id=1, source_target_pairs={{8,0},{16,8},{24,16},{32,24},{40,32},{48,40},{56,48},{64,56},{72,6... | collective-permute-start | bytes 786440 | tf_op jit(solution)/shard_map/while/body/eval_jaxpr/ppermute | solution.py:10
  184.2 11.2 %collective-permute-start = (bf16[16,64,128]{2,1,0:T(8,128)(2,1)S(1)}, bf16[16,64,128]{2,1,0:T(8,128)(2,1)S(1)}, u32[]{:S(2)}, u32[]{:S(2)}) collective-permute-start(bf16[16,64,128]{2,1,0:T(8,128)(2,1)S(1)} %add_convert_fusion.2), channel_id=1, source_target_pairs={{8,0},{16,8},{24,16},{32,24},{40,32},{48,40},{56,48},{64,56},{72,6... | collective-permute-start | bytes 786440 | tf_op jit(solution)/shard_map/while/body/eval_jaxpr/ppermute | solution.py:10
  195.5 9.4 %collective-permute-start = (bf16[16,64,128]{2,1,0:T(8,128)(2,1)S(1)}, bf16[16,64,128]{2,1,0:T(8,128)(2,1)S(1)}, u32[]{:S(2)}, u32[]{:S(2)}) collective-permute-start(bf16[16,64,128]{2,1,0:T(8,128)(2,1)S(1)} %add_convert_fusion.2), channel_id=1, source_target_pairs={{8,0},{16,8},{24,16},{32,24},{40,32},{48,40},{56,48},{64,56},{72,6... | collective-permute-start | bytes 786440 | tf_op jit(solution)/shard_map/while/body/eval_jaxpr/ppermute | solution.py:10
  205.1 8.3 %collective-permute-start = (bf16[16,64,128]{2,1,0:T(8,128)(2,1)S(1)}, bf16[16,64,128]{2,1,0:T(8,128)(2,1)S(1)}, u32[]{:S(2)}, u32[]{:S(2)}) collective-permute-start(bf16[16,64,128]{2,1,0:T(8,128)(2,1)S(1)} %add_convert_fusion.2), channel_id=1, source_target_pairs={{8,0},{16,8},{24,16},{32,24},{40,32},{48,40},{56,48},{64,56},{72,6... | collective-permute-start | bytes 786440 | tf_op jit(solution)/shard_map/while/body/eval_jaxpr/ppermute | solution.py:10
  213.6 8.4 %collective-permute-start = (bf16[16,64,128]{2,1,0:T(8,128)(2,1)S(1)}, bf16[16,64,128]{2,1,0:T(8,128)(2,1)S(1)}, u32[]{:S(2)}, u32[]{:S(2)}) collective-permute-start(bf16[16,64,128]{2,1,0:T(8,128)(2,1)S(1)} %add_convert_fusion.2), channel_id=1, source_target_pairs={{8,0},{16,8},{24,16},{32,24},{40,32},{48,40},{56,48},{64,56},{72,6... | collective-permute-start | bytes 786440 | tf_op jit(solution)/shard_map/while/body/eval_jaxpr/ppermute | solution.py:10
  222.2 9.2 %collective-permute-start = (bf16[16,64,128]{2,1,0:T(8,128)(2,1)S(1)}, bf16[16,64,128]{2,1,0:T(8,128)(2,1)S(1)}, u32[]{:S(2)}, u32[]{:S(2)}) collective-permute-start(bf16[16,64,128]{2,1,0:T(8,128)(2,1)S(1)} %add_convert_fusion.2), channel_id=1, source_target_pairs={{8,0},{16,8},{24,16},{32,24},{40,32},{48,40},{56,48},{64,56},{72,6... | collective-permute-start | bytes 786440 | tf_op jit(solution)/shard_map/while/body/eval_jaxpr/ppermute | solution.py:10
  231.7 9.2 %collective-permute-start = (bf16[16,64,128]{2,1,0:T(8,128)(2,1)S(1)}, bf16[16,64,128]{2,1,0:T(8,128)(2,1)S(1)}, u32[]{:S(2)}, u32[]{:S(2)}) collective-permute-start(bf16[16,64,128]{2,1,0:T(8,128)(2,1)S(1)} %add_convert_fusion.2), channel_id=1, source_target_pairs={{8,0},{16,8},{24,16},{32,24},{40,32},{48,40},{56,48},{64,56},{72,6... | collective-permute-start | bytes 786440 | tf_op jit(solution)/shard_map/while/body/eval_jaxpr/ppermute | solution.py:10
  241.0 1.6 copy-start.2
  241.0 1.8 copy-start.5
  241.0 1.9 copy-start.7
  241.0 1.9 copy-start.8
  241.0 1.9 copy-start.10
  242.9 6.0 %copy-start.9 = (bf16[512,4096]{1,0:T(8,128)(2,1)S(1)}, bf16[512,4096]{1,0:T(8,128)(2,1)}, u32[]{:S(2)}) copy-start(bf16[512,4096]{1,0:T(8,128)(2,1)} %param.12) | copy-start | bytes 12582916
  255.6 147.3 %reduce-scatter.3.cloned.1.call-start = ((), (), s32[]{:S(2)}) async-start(), calls=%async_computation.3 | async-start | bytes 4718592 | tf_op jit(solution)/shard_map/reduce_scatter | solution.py:92
  265.5 11.8 %copy-start.3 = (f32[1,16,64,128]{3,2,1,0:T(8,128)S(1)}, f32[1,16,64,128]{3,2,1,0:T(8,128)}, u32[]{:S(2)}) copy-start(f32[1,16,64,128]{3,2,1,0:T(8,128)} %param.20) | copy-start | bytes 1572868
  281.4 7.8 %copy-start.6 = (f32[512,128]{1,0:T(8,128)S(1)}, f32[512,128]{1,0:T(8,128)}, u32[]{:S(2)}) copy-start(f32[512,128]{1,0:T(8,128)} %copy.46) | copy-start | bytes 786436
Sparse Core Ops, SparseCore 0:
  11.8 86.3 all-reduce.1
  255.8 108.7 reduce-scatter.4
  367.6 35.2 reduce-scatter.2
where the time goes:
time: 413 us; the launch traced here: 409 us
  waiting for transfers between devices  303 us (73%)
  matrix products  51.2 us (12%)
  starting transfers between devices  19.7 us (5%)
  between operations  14 us (3%)
  other arithmetic  12.2 us (3%)
  local copies, waits for them, and re-layouts  9.06 us (2%)
    ppermute x15, waiting for transfers between devices, passed_along(): return lax.ppermute(block, axis, route)  119 us
    psum x1, waiting for transfers between devices, body(): lax.psum(jnp.sum(fork_grad, axis=0).astype(jnp.bfloat16), 'ctx')  75.8 us
    reduce_scatter x1, waiting for transfers between devices, body(): lax.psum_scatter(lax.dot_general(layer_input, x_grad, (((0,), (0,)), ((),...  71.6 us
    reduce_scatter x1, waiting for transfers between devices, body(): lax.psum_scatter(lax.dot_general(x_grad, proj_weight, (((1,), (1,)), ((),...  36.3 us
    ppermute x15, starting transfers between devices, passed_along(): return lax.ppermute(block, axis, route)  19.4 us
    dot_general x1, matrix products, body(): jnp.dot(layer_input, proj_weight, preferred_element_type=jnp.float32)  10.2 us
    dot_general x1, matrix products, body(): lax.dot_general(x_grad, proj_weight, (((1,), (1,)), ((), ())), preferred_...  9.62 us
  transfers between devices with their start and end apart: 18, of which 18 were waited for; matrix products, arithmetic and copies ran while one was open for 13% of the time, Pallas kernels for 0%

commit v1 on v0

v1 whole, which is shorter than its diff:
```python
import jax
import jax.numpy as jnp
from jax import lax
from jax.sharding import PartitionSpec as P

SIDE = 4


def hop(block, dz, dy):
    route = []
    for i in range(SIDE * SIDE):
        z, y = divmod(i, SIDE)
        route.append((i, ((z + dz) % SIDE) * SIDE + (y + dy) % SIDE))
    return lax.ppermute(block, "ctx", route)


def pick(stacked, index):
    return lax.dynamic_index_in_dim(stacked, index % stacked.shape[0], 0, keepdims=False)


def split_product(form, narrow, wide):
    high_part = wide.astype(jnp.bfloat16)
    low_part = (wide - high_part.astype(jnp.float32)).astype(jnp.bfloat16)
    first_term = jnp.einsum(form, narrow, high_part, preferred_element_type=jnp.float32)
    return first_term + jnp.einsum(form, narrow, low_part, preferred_element_type=jnp.float32)


def packed(state, extra, decay):
    high = decay.astype(jnp.bfloat16)
    low = (decay - high.astype(jnp.float32)).astype(jnp.bfloat16)
    tail = jnp.concatenate([high, low, jnp.zeros((8,), jnp.bfloat16)])
    tail = jnp.broadcast_to(tail[:, None], (16, 128))
    return jnp.concatenate(
        [
            state.reshape(-1, 128).astype(jnp.bfloat16),
            extra.reshape(-1, 128).astype(jnp.bfloat16),
            tail,
        ]
    )


def unpacked(message):
    message = message.astype(jnp.float32)
    state = message[:256].reshape(4, 64, 128)
    extra = message[256:512].reshape(4, 64, 128)
    decay = message[512:516, 0] + message[516:520, 0]
    return state, extra, decay[:, None, None]


def relay(local_sum, fork_part, decays, z, y):
    local_q = local_sum.reshape(SIDE, 4, 64, 128)
    fork_q = fork_part.reshape(SIDE, 4, 64, 128)
    decay_q = decays.reshape(SIDE, 4)
    messages = [
        packed(pick(local_q, y + d), pick(fork_q, y + d), pick(decay_q, y + d)) for d in range(SIDE)
    ]
    arrived = [messages[0]] + [hop(messages[d], 0, d) for d in range(1, SIDE)]
    stacked = jnp.stack(arrived)
    by_y = [unpacked(pick(stacked, y - b)) for b in range(SIDE)]
    fork_y = by_y[0][1] + by_y[1][1] + by_y[2][1] + by_y[3][1]
    total, rate = by_y[3][0], by_y[3][2]
    for b in (2, 1, 0):
        total = by_y[b][0] + by_y[b][2] * total
        rate = by_y[b][2] * rate
    message = packed(total, fork_y, rate[:, 0, 0])
    arrived = [message] + [hop(message, d, 0) for d in range(1, SIDE)]
    stacked = jnp.stack(arrived)
    by_z = [unpacked(pick(stacked, z - b)) for b in range(SIDE)]
    carry = by_z[0][1] + by_z[1][1] + by_z[2][1] + by_z[3][1]
    mine = carry
    for b in (3, 2, 1):
        carry = by_z[b][0] + by_z[b][2] * carry
        mine = jnp.where(z == b - 1, carry, mine)
    carried = [None] * SIDE
    carried[3] = mine
    for b in (2, 1, 0):
        carried[b] = by_y[b + 1][0] + by_y[b + 1][2] * carried[b + 1]
    stacked = jnp.stack(carried).astype(jnp.bfloat16).reshape(SIDE, 256, 128)
    arrived = [pick(stacked, y)] + [hop(pick(stacked, y + d), 0, d) for d in range(1, SIDE)]
    stacked = jnp.stack(arrived)
    return jnp.stack([pick(stacked, y - q) for q in range(SIDE)]).reshape(16, 64, 128).astype(
        jnp.float32
    )


def body(
    layer_input,
    proj_weight,
    step_size,
    decay_log,
    skip_gain,
    write_vec,
    read_vec,
    out_grad,
    start_state,
    fork_grad,
):
    length = layer_input.shape[0]
    head_count = step_size.shape[1]
    head_width = out_grad.shape[1] // head_count
    state_size = write_vec.shape[2]
    position = lax.axis_index("ctx")
    z, y = position // SIDE, position % SIDE
    writes = write_vec[:, 0]
    reads = read_vec[:, 0]
    grad_heads = out_grad.reshape(length, head_count, head_width)
    cumulative = jnp.cumsum(step_size * -jnp.exp(decay_log), axis=0)
    decays = jnp.exp(cumulative[length - 1])
    starts = jnp.exp(cumulative)
    weighted = starts[..., None] * reads.astype(jnp.float32)[:, None, :]
    local_sum = split_product("thp,thn->hpn", grad_heads, weighted)
    carried = relay(local_sum, jnp.sum(fork_grad, axis=0), decays, z, y)
    scores = jnp.einsum("jn,tn->jt", reads, writes, preferred_element_type=jnp.float32)
    cum_heads = cumulative.T
    offsets = cum_heads[:, :, None] - cum_heads[:, None, :]
    causal = jnp.arange(length)[:, None] >= jnp.arange(length)[None, :]
    kernel = jnp.where(causal, jnp.exp(jnp.minimum(offsets, 0.0)), 0.0)
    step_cols = step_size.T[:, None, :]
    mixing = (scores[None] * kernel * step_cols).astype(jnp.bfloat16)
    within = jnp.einsum("hjt,jhp->thp", mixing, grad_heads, preferred_element_type=jnp.float32)
    end_weights = step_size * jnp.exp(cumulative[length - 1][None, :] - cumulative)
    to_inputs = split_product("tn,hpn->thp", writes, carried)
    skip_term = skip_gain[None, :, None] * grad_heads.astype(jnp.float32)
    x_wide = within + end_weights[..., None] * to_inputs + skip_term
    x_grad = x_wide.reshape(length, head_count * head_width).astype(jnp.bfloat16)

    columns = layer_input.reshape(length, SIDE, SIDE, 256)
    x_first, x_second = x_grad[:, :512], x_grad[:, 512:]

    def part_a(y_to):
        rows = lax.dynamic_index_in_dim(columns, y_to % SIDE, 2, keepdims=False).reshape(length, 1024)
        return lax.dot_general(
            rows, x_first, (((0,), (0,)), ((), ())), preferred_element_type=jnp.float32
        ).reshape(SIDE, 256, 512)

    def part_b(z_to):
        rows = lax.dynamic_index_in_dim(columns, z_to % SIDE, 1, keepdims=False).reshape(length, 1024)
        return lax.dot_general(
            rows, x_second, (((0,), (0,)), ((), ())), preferred_element_type=jnp.float32
        ).reshape(SIDE, 256, 512)

    def ring(part, here, move):
        half = jnp.bfloat16
        far = part(here + 2).astype(half)
        n = far.shape[0] // 2
        up = move(far[:n], 1)
        down = move(far[n:], -1)
        upper = part(here + 1)
        lower = part(here - 1)
        upper = jnp.concatenate([upper[:n] + up.astype(jnp.float32), upper[n:]]).astype(half)
        lower = jnp.concatenate([lower[:n], lower[n:] + down.astype(jnp.float32)]).astype(half)
        from_below = move(upper, 1)
        from_above = move(lower, -1)
        own = part(here)
        return own + from_below.astype(jnp.float32) + from_above.astype(jnp.float32)

    by_y = lambda b, s: hop(b, 0, s)
    by_z = lambda b, s: hop(b, s, 0)
    sum_a = ring(part_a, y, by_y)
    sum_b = ring(part_b, z, by_z)
    sum_a = ring(lambda i: pick(sum_a, i), z, by_z)
    sum_b = ring(lambda i: pick(sum_b, i), y, by_y)
    scale_factor = (length * lax.axis_size("ctx")) ** (-0.5)
    weight_grad = (jnp.concatenate([sum_a, sum_b], axis=1) * scale_factor).astype(jnp.bfloat16)

    input_grad = lax.psum_scatter(
        lax.dot_general(
            x_grad, proj_weight, (((1,), (1,)), ((), ())), preferred_element_type=jnp.float32
        ).astype(jnp.bfloat16),
        "smp",
        scatter_dimension=0,
        tiled=True,
    )

    projected = jnp.dot(layer_input, proj_weight, preferred_element_type=jnp.float32).astype(
        jnp.bfloat16
    )
    inputs = projected.reshape(length, head_count, head_width)
    intersections = jnp.einsum(
        "jhp,thp->hjt", grad_heads, inputs, preferred_element_type=jnp.float32
    )
    coupling = jnp.sum(step_cols * kernel * intersections, axis=0).astype(jnp.bfloat16)
    input_state = split_product("thp,hpn->thn", inputs, carried)
    from_start = split_product("thp,hpn->thn", grad_heads, start_state[0])
    write_grad = jnp.einsum("jt,jn->tn", coupling, reads, preferred_element_type=jnp.float32) + jnp.sum(
        end_weights[..., None] * input_state, axis=1
    )
    read_grad = jnp.einsum("jt,tn->jn", coupling, writes, preferred_element_type=jnp.float32) + jnp.sum(
        starts[..., None] * from_start, axis=1
    )
    return (input_grad, weight_grad, write_grad[:, None], read_grad[:, None])


def solution(mesh):
    placed = (
        P("ctx", None),
        P(None, "smp"),
        P("ctx", "smp"),
        P("smp"),
        P("smp"),
        P("ctx", "smp", None),
        P("ctx", "smp", None),
        P("ctx", "smp"),
        P("ctx", "smp", None, None),
        P("ctx", "smp", None, None),
    )
    return jax.shard_map(
        body,
        mesh=mesh,
        in_specs=placed,
        out_specs=(
            P(("ctx", "smp"), None),
            P("ctx", "smp"),
            P("ctx", "smp", None),
            P("ctx", "smp", None),
        ),
        check_vma=False,
    )
```

time: 413 us -> 181 us (0.44)
  the two profiles are of different devices: /device:TPU:1 before, /device:TPU:22 now
where the time goes in v1:
time: 181 us; the launch traced here: 180 us
  matrix products  52.2 us (29%)
  starting transfers between devices  38 us (21%)
  other arithmetic  32.1 us (18%)
  local copies, waits for them, and re-layouts  22.1 us (12%)
  waiting for transfers between devices  20 us (11%)
  between operations  15.1 us (8%)
    ppermute x25, starting transfers between devices, hop(): return lax.ppermute(block, 'ctx', route)  38 us
    ppermute x25, waiting for transfers between devices, hop(): return lax.ppermute(block, 'ctx', route)  20 us
    dot_general x1, matrix products, body(): jnp.dot(layer_input, proj_weight, preferred_element_type=jnp.float32)  10.2 us
    unnamed x62, local copies, waits for them, and re-layouts  9.9 us
    dot_general x1, matrix products, body(): jnp.einsum('jhp,thp->hjt', grad_heads, inputs, preferred_element_type=jnp...  7.79 us
    dot_general x1, matrix products, body(): jnp.einsum('hjt,jhp->thp', mixing, grad_heads, preferred_element_type=jnp...  7.13 us
    dot_general x1, matrix products, body(): lax.dot_general(x_grad, proj_weight, (((1,), (1,)), ((), ())), preferred_...  6.38 us
    dot_general x4, matrix products, part_b(): lax.dot_general(rows, x_second, (((0,), (0,)), ((), ())), preferred_eleme...  5.49 us
  transfers between devices with their start and end apart: 26, of which 7 were waited for; matrix products, arithmetic and copies ran while one was open for 35% of the time, Pallas kernels for 0%

profile of v1, /device:TPU:22, one launch (start us, length us, event | category | flops | bytes accessed | tf_op | source)
XLA Modules:
  0.0 179.5 jit_solution(16717646666341171712)
XLA Ops:
  8.8 1.1 reduce-window.6
  11.2 1.5 exponential_multiply_fusion
  12.6 1.5 copy.65
  14.1 1.0 bitcast_convert_fusion.3
  16.1 0.9 fusion.16
  18.7 1.3 collective-permute-start
  22.2 1.1 collective-permute-start.2
  23.4 1.3 fusion.78
  24.7 6.5 %copy.70 = bf16[512,4096]{0,1:T(8,128)(2,1)} copy(bf16[512,4096]{1,0:T(8,128)(2,1)} %param.10) | data formatting | bytes 8388608 | tf_op args[0]
  31.2 10.2 %convolution_convert_fusion.1 = bf16[512,1024]{1,0:T(8,128)(2,1)} fusion(bf16[512,4096]{1,0:T(8,128)(2,1)} %param.10, bf16[4096,1024]{1,0:T(8,128)(2,1)} %param.11), kind=kOutput, calls=%fused_computation.26 | convolution fusion | flops 4295491584 | bytes 13631488 | tf_op jit(solution)/shard_map/dot_general | solution.py:175
  41.4 1.5 copy.73
  44.7 7.8 %fusion = bf16[512,512]{0,1:T(8,128)(2,1)S(1)} fusion(bf16[512,16,64]{0,2,1:T(8,128)(2,1)S(1)} %bitcast.383, bf16[512,16,64]{0,2,1:T(8,128)(2,1)S(1)} %bitcast.381, f32[16,512]{1,0:T(8,128)} %bitcast.418, f32[16,512]{1,0:T(8,128)} %get-tuple-element.83, pred[512,512]{0,1:T(8,128)(4,1)S(1)} %iota_compare_fusion), kind=kOutput, calls=%fused_computation.1 | convolution fusion | flops 561774592 | bytes 2949120 | tf_op jit(solution)/shard_map/jhp,thp->hjt/dot_general | solution.py:179
  52.5 1.0 convolution_add_fusion
  53.7 1.1 pad_maximum_fusion.4
  54.8 1.1 fusion.87
  56.2 0.9 fusion.100
  57.3 0.9 fusion.98
  58.3 0.9 fusion.99
  59.3 1.0 fusion.83
  60.3 1.1 fusion.72
  61.6 2.0 %collective-permute-start.3 = (bf16[528,128]{1,0:T(8,128)(2,1)S(1)}, bf16[528,128]{1,0:T(8,128)(2,1)S(1)}, u32[]{:S(2)}, u32[]{:S(2)}) collective-permute-start(bf16[528,128]{1,0:T(8,128)(2,1)S(1)} %get-tuple-element.78), channel_id=1, source_target_pairs={{0,32},{8,40},{16,48},{24,56},{32,64},{40,72},{48,80},{56,88},{64,... | collective-permute-start | bytes 405512 | tf_op jit(solution)/shard_map/ppermute | solution.py:14
  63.6 3.6 %collective-permute-start.4 = (bf16[528,128]{1,0:T(8,128)(2,1)S(1)}, bf16[528,128]{1,0:T(8,128)(2,1)S(1)}, u32[]{:S(2)}, u32[]{:S(2)}) collective-permute-start(bf16[528,128]{1,0:T(8,128)(2,1)S(1)} %get-tuple-element.78), channel_id=1, source_target_pairs={{0,64},{8,72},{16,80},{24,88},{32,96},{40,104},{48,112},{56,120},{... | collective-permute-start | bytes 405512 | tf_op jit(solution)/shard_map/ppermute | solution.py:14
  67.1 1.0 collective-permute-start.5
  68.1 3.0 %constant_dynamic-slice_fusion.3 = (bf16[512,4,1,256]{0,3,2,1:T(8,128)(2,1)}, bf16[512,4,1,256]{0,3,2,1:T(8,128)(2,1)}) fusion(bf16[512,4,4,256]{0,3,2,1:T(8,128)(2,1)} %bitcast.362, s32[]{:T(128)S(6)} %select_n.275, s32[]{:T(128)S(6)} %select_n.281), kind=kLoop, calls=%fused_computation.201 | loop fusion | bytes 4194312 | tf_op jit(solution)/shard_map/jit(dynamic_index_in_dim)/dynamic_slice | solution.py:131
  71.4 1.2 collective-permute-done.4
  73.3 1.1 pad_maximum_fusion.5
  74.4 1.1 fusion.88
  75.8 0.9 fusion.96
  76.8 0.9 fusion.95
  77.8 1.5 fusion.82
  79.5 1.4 collective-permute-start.6
  81.0 2.5 %collective-permute-start.7 = (bf16[256,128]{1,0:T(8,128)(2,1)S(1)}, bf16[256,128]{1,0:T(8,128)(2,1)S(1)}, u32[]{:S(2)}, u32[]{:S(2)}) collective-permute-start(bf16[256,128]{1,0:T(8,128)(2,1)S(1)} %get-tuple-element.67), channel_id=1, source_target_pairs={{0,16},{8,24},{16,0},{24,8},{32,48},{40,56},{48,32},{56,40},{64,80... | collective-permute-start | bytes 196616 | tf_op jit(solution)/shard_map/ppermute | solution.py:14
  83.4 2.0 %collective-permute-start.8 = (bf16[256,128]{1,0:T(8,128)(2,1)S(1)}, bf16[256,128]{1,0:T(8,128)(2,1)S(1)}, u32[]{:S(2)}, u32[]{:S(2)}) collective-permute-start(bf16[256,128]{1,0:T(8,128)(2,1)S(1)} %get-tuple-element.66), channel_id=1, source_target_pairs={{0,24},{8,0},{16,8},{24,16},{32,56},{40,32},{48,40},{56,48},{64,88... | collective-permute-start | bytes 196616 | tf_op jit(solution)/shard_map/ppermute | solution.py:14
  85.4 3.0 %constant_dynamic-slice_fusion.1 = (bf16[512,1,4,256]{0,3,2,1:T(8,128)(2,1)}, bf16[512,1,4,256]{0,3,2,1:T(8,128)(2,1)}) fusion(bf16[512,4,4,256]{0,3,2,1:T(8,128)(2,1)} %bitcast.363, s32[]{:T(128)S(6)} %select_n.303, s32[]{:T(128)S(6)} %select_n.289), kind=kLoop, calls=%fused_computation.197 | loop fusion | bytes 4194312 | tf_op jit(solution)/shard_map/jit(dynamic_index_in_dim)/dynamic_slice | solution.py:137
  89.5 7.1 %fusion.11 = bf16[512,16,64]{0,2,1:T(8,128)(2,1)S(1)} fusion(bf16[512,16,64]{0,2,1:T(8,128)(2,1)S(1)} %bitcast.382, f32[16,64,512]{2,1,0:T(8,128)S(1)} %fusion.75, f32[16,64,512]{2,1,0:T(8,128)S(1)} %fusion.73, f32[16,512]{1,0:T(8,128)} %bitcast.419, f32[16,512]{1,0:T(8,128)} %get-tuple-element.83, f32[512,512]{0,1:T(8,128)} %fusion.78, ...), kind=kOutput, calls=%fused_computation.19 | convolution fusion | flops 565706752 | bytes 7700544 | tf_op jit(solution)/shard_map/hjt,jhp->thp/dot_general | solution.py:120
  96.7 2.0 %convolution_convert_fusion.3 = bf16[4,256,512]{2,1,0:T(8,128)(2,1)S(1)} fusion(bf16[512,4,4,256]{0,3,2,1:T(8,128)(2,1)} %bitcast.364, s32[]{:T(128)S(6)} %select_n.277, bf16[512,1024]{0,1:T(8,128)(2,1)S(1)} %bitcast.368), kind=kOutput, calls=%fused_computation.28 | convolution fusion | flops 537395200 | bytes 2621444 | tf_op jit(solution)/shard_map/dot_general | solution.py:132
  98.7 6.4 %convolution_convert_fusion = bf16[512,4096]{1,0:T(8,128)(2,1)} fusion(bf16[512,1024]{0,1:T(8,128)(2,1)S(1)} %bitcast.369, bf16[4096,1024]{1,0:T(8,128)(2,1)S(1)} %bitcast.424), kind=kOutput, calls=%fused_computation.8 | convolution fusion | flops 4297064448 | bytes 13631488 | tf_op jit(solution)/shard_map/dot_general | solution.py:167
  105.2 1.9 %collective-permute-start.9 = (bf16[2,256,512]{2,1,0:T(8,128)(2,1)S(1)}, bf16[2,256,512]{2,1,0:T(8,128)(2,1)S(1)}, u32[]{:S(2)}, u32[]{:S(2)}) collective-permute-start(bf16[2,256,512]{2,1,0:T(8,128)(2,1)S(1)} %get-tuple-element.39), channel_id=1, source_target_pairs={{0,8},{8,16},{16,24},{24,0},{32,40},{40,48},{48,56},{56,32},{64,72... | collective-permute-start | bytes 1572872 | tf_op jit(solution)/shard_map/ppermute | solution.py:14
  107.3 2.0 %convolution_convert_fusion.2 = bf16[4,256,512]{2,1,0:T(8,128)(2,1)S(1)} fusion(bf16[512,4,4,256]{0,3,2,1:T(8,128)(2,1)} %bitcast.365, s32[]{:T(128)S(6)} %select_n.305, bf16[512,1024]{0,1:T(8,128)(2,1)S(1)} %bitcast.370), kind=kOutput, calls=%fused_computation.27 | convolution fusion | flops 537395200 | bytes 2621444 | tf_op jit(solution)/shard_map/dot_general | solution.py:138
  109.4 1.2 collective-permute-start.17
  110.6 2.1 %collective-permute-start.19 = (bf16[2,256,512]{2,1,0:T(8,128)(2,1)S(1)}, bf16[2,256,512]{2,1,0:T(8,128)(2,1)S(1)}, u32[]{:S(2)}, u32[]{:S(2)}) collective-permute-start(bf16[2,256,512]{2,1,0:T(8,128)(2,1)S(1)} %get-tuple-element.42), channel_id=1, source_target_pairs={{0,96},{8,104},{16,112},{24,120},{32,0},{40,8},{48,16},{56,24},{64... | collective-permute-start | bytes 1572872 | tf_op jit(solution)/shard_map/ppermute | solution.py:14
  115.0 1.5 fusion.5
  120.2 1.1 pad_maximum_fusion
  121.3 1.8 collective-permute-start.10
  123.3 1.1 pad_maximum_fusion.1
  124.9 1.1 pad_maximum_fusion.2
  126.2 1.1 pad_maximum_fusion.3
  127.3 3.2 %collective-permute-start.20 = (bf16[4,256,512]{2,1,0:T(8,128)(2,1)}, bf16[4,256,512]{2,1,0:T(8,128)(2,1)}, u32[]{:S(2)}, u32[]{:S(2)}) collective-permute-start(bf16[4,256,512]{2,1,0:T(8,128)(2,1)} %pad_maximum_fusion.3), channel_id=1, source_target_pairs={{0,96},{8,104},{16,112},{24,120},{32,0},{40,8},{48,16},{56,24},{64... | collective-permute-start | bytes 3145736 | tf_op jit(solution)/shard_map/ppermute | solution.py:14
  130.5 2.0 %fusion.24 = f32[4,256,512]{2,1,0:T(8,128)S(1)} fusion(bf16[512,4,4,256]{0,3,2,1:T(8,128)(2,1)} %bitcast.366, s32[]{:T(128)S(6)} %select_n.273, bf16[512,1024]{0,1:T(8,128)(2,1)S(1)} %bitcast.375), kind=kOutput, calls=%fused_computation.46 | convolution fusion | flops 536870912 | bytes 3670020 | tf_op jit(solution)/shard_map/dot_general | solution.py:132
  132.5 0.8 copy.74
  133.3 2.0 %fusion.21 = f32[4,256,512]{2,1,0:T(8,128)S(1)} fusion(bf16[512,4,4,256]{0,3,2,1:T(8,128)(2,1)} %bitcast.367, s32[]{:T(128)S(6)} %select_n.295, bf16[512,1024]{0,1:T(8,128)(2,1)S(1)} %bitcast.376), kind=kOutput, calls=%fused_computation.43 | convolution fusion | flops 536870912 | bytes 3670020 | tf_op jit(solution)/shard_map/dot_general | solution.py:138
  135.3 8.1 %collective-permute-done.10 = bf16[4,256,512]{2,1,0:T(8,128)(2,1)} collective-permute-done((bf16[4,256,512]{2,1,0:T(8,128)(2,1)}, bf16[4,256,512]{2,1,0:T(8,128)(2,1)}, u32[]{:S(2)}, u32[]{:S(2)}) %collective-permute-start.10) | collective-permute-done | bytes 1048608 | tf_op jit(solution)/shard_map/ppermute | solution.py:14
  143.4 2.6 %collective-permute-done.12 = bf16[4,256,512]{2,1,0:T(8,128)(2,1)} collective-permute-done((bf16[4,256,512]{2,1,0:T(8,128)(2,1)}, bf16[4,256,512]{2,1,0:T(8,128)(2,1)}, u32[]{:S(2)}, u32[]{:S(2)}) %collective-permute-start.12) | collective-permute-done | bytes 1048608 | tf_op jit(solution)/shard_map/ppermute | solution.py:14
  146.0 1.9 %convert_add_fusion.1 = f32[4,256,512]{2,1,0:T(8,128)S(1)} fusion(bf16[4,256,512]{2,1,0:T(8,128)(2,1)} %collective-permute-done.12, f32[4,256,512]{2,1,0:T(8,128)S(1)} %fusion.24, bf16[4,256,512]{2,1,0:T(8,128)(2,1)} %collective-permute-done.10), kind=kLoop, calls=%fused_computation.21 | loop fusion | flops 2097152 | bytes 6291456 | tf_op jit(solution)/shard_map/add | solution.py:155
  148.7 2.6 %collective-permute-start.15 = (bf16[128,512]{1,0:T(8,128)(2,1)S(1)}, bf16[128,512]{1,0:T(8,128)(2,1)S(1)}, u32[]{:S(2)}, u32[]{:S(2)}) collective-permute-start(bf16[128,512]{1,0:T(8,128)(2,1)S(1)} %get-tuple-element.58), channel_id=1, source_target_pairs={{0,96},{8,104},{16,112},{24,120},{32,0},{40,8},{48,16},{56,24},{64... | collective-permute-start | bytes 393224 | tf_op jit(solution)/shard_map/ppermute | solution.py:14
  151.4 2.0 %convert_add_fusion = f32[4,256,512]{2,1,0:T(8,128)S(1)} fusion(bf16[4,256,512]{2,1,0:T(8,128)(2,1)} %collective-permute-done.20, f32[4,256,512]{2,1,0:T(8,128)S(1)} %fusion.21, bf16[4,256,512]{2,1,0:T(8,128)(2,1)} %collective-permute-done.18), kind=kLoop, calls=%fused_computation.20 | loop fusion | flops 2097152 | bytes 6291456 | tf_op jit(solution)/shard_map/add | solution.py:155
  153.5 3.0 %collective-permute-start.21 = (bf16[128,512]{1,0:T(8,128)(2,1)S(1)}, bf16[128,512]{1,0:T(8,128)(2,1)S(1)}, u32[]{:S(2)}, u32[]{:S(2)}) collective-permute-start(bf16[128,512]{1,0:T(8,128)(2,1)S(1)} %get-tuple-element.59), channel_id=1, source_target_pairs={{0,8},{8,16},{16,24},{24,0},{32,40},{40,48},{48,56},{56,32},{64,72... | collective-permute-start | bytes 393224 | tf_op jit(solution)/shard_map/ppermute | solution.py:14
  156.8 3.3 %collective-permute-start.16 = (bf16[256,512]{1,0:T(8,128)(2,1)S(1)}, bf16[256,512]{1,0:T(8,128)(2,1)S(1)}, u32[]{:S(2)}, u32[]{:S(2)}) collective-permute-start(bf16[256,512]{1,0:T(8,128)(2,1)S(1)} %pad_maximum_fusion.10), channel_id=1, source_target_pairs={{0,96},{8,104},{16,112},{24,120},{32,0},{40,8},{48,16},{56,24},{64... | collective-permute-start | bytes 786440 | tf_op jit(solution)/shard_map/ppermute | solution.py:14
  160.4 2.5 %collective-permute-done.23 = bf16[128,512]{1,0:T(8,128)(2,1)S(1)} collective-permute-done((bf16[128,512]{1,0:T(8,128)(2,1)S(1)}, bf16[128,512]{1,0:T(8,128)(2,1)S(1)}, u32[]{:S(2)}, u32[]{:S(2)}) %collective-permute-start.23) | collective-permute-done | bytes 131104 | tf_op jit(solution)/shard_map/ppermute | solution.py:14
  163.0 2.2 %collective-permute-start.22 = (bf16[256,512]{1,0:T(8,128)(2,1)S(1)}, bf16[256,512]{1,0:T(8,128)(2,1)S(1)}, u32[]{:S(2)}, u32[]{:S(2)}) collective-permute-start(bf16[256,512]{1,0:T(8,128)(2,1)S(1)} %pad_maximum_fusion.11), channel_id=1, source_target_pairs={{0,8},{8,16},{16,24},{24,0},{32,40},{40,48},{48,56},{56,32},{64,72... | collective-permute-start | bytes 786440 | tf_op jit(solution)/shard_map/ppermute | solution.py:14
  165.3 1.0 convolution_add_fusion.1
  166.5 3.0 %collective-permute-done.22 = bf16[256,512]{1,0:T(8,128)(2,1)S(1)} collective-permute-done((bf16[256,512]{1,0:T(8,128)(2,1)S(1)}, bf16[256,512]{1,0:T(8,128)(2,1)S(1)}, u32[]{:S(2)}, u32[]{:S(2)}) %collective-permute-start.22) | collective-permute-done | bytes 262176 | tf_op jit(solution)/shard_map/ppermute | solution.py:14
  169.4 2.2 %collective-permute-done.24 = bf16[256,512]{1,0:T(8,128)(2,1)S(1)} collective-permute-done((bf16[256,512]{1,0:T(8,128)(2,1)S(1)}, bf16[256,512]{1,0:T(8,128)(2,1)S(1)}, u32[]{:S(2)}, u32[]{:S(2)}) %collective-permute-start.24) | collective-permute-done | bytes 262176 | tf_op jit(solution)/shard_map/ppermute | solution.py:14
  171.8 0.9 fusion.19
  (186 shorter events, 21.9 us)
Async XLA Ops:
  7.2 16.2 %copy-start = (bf16[512,1,128]{2,0,1:T(8,128)(2,1)S(1)}, bf16[512,1,128]{2,0,1:T(8,128)(2,1)}, u32[]{:S(2)}) copy-start(bf16[512,1,128]{2,0,1:T(8,128)(2,1)} %param.15) | copy-start | bytes 393220
  7.2 165.5 %reduce-scatter.2.cloned.1.call-start = ((), (), s32[]{:S(2)}) async-start(), calls=%async_computation.1 | async-start | bytes 4718592 | tf_op jit(solution)/shard_map/reduce_scatter | solution.py:166
  12.6 4.4 %copy-start.25 = (f32[512,16]{0,1:T(8,128)}, f32[512,16]{0,1:T(8,128)S(1)}, u32[]{:S(2)}) copy-start(f32[512,16]{0,1:T(8,128)S(1)} %get-tuple-element.82) | copy-start | bytes 98308
  14.1 2.9 %copy-start.16 = (f32[2,16,64,128]{3,2,1,0:T(8,128)S(1)}, f32[2,16,64,128]{3,2,1,0:T(8,128)}, u32[]{:S(2)}) copy-start(f32[2,16,64,128]{3,2,1,0:T(8,128)} %param.19) | copy-start | bytes 3145732
  16.1 7.3 %copy-start.13 = (bf16[512,1,128]{2,0,1:T(8,128)(2,1)S(1)}, bf16[512,1,128]{2,0,1:T(8,128)(2,1)}, u32[]{:S(2)}) copy-start(bf16[512,1,128]{2,0,1:T(8,128)(2,1)} %param.16) | copy-start | bytes 393220
  18.7 35.0 %collective-permute-start = (bf16[528,128]{1,0:T(8,128)(2,1)}, bf16[528,128]{1,0:T(8,128)(2,1)}, u32[]{:S(2)}, u32[]{:S(2)}) collective-permute-start(bf16[528,128]{1,0:T(8,128)(2,1)} %maximum_maximum_fusion), channel_id=1, source_target_pairs={{0,8},{8,16},{16,24},{24,0},{32,40},{40,48},{48,56},{56,32},{64,72... | collective-permute-start | bytes 405512 | tf_op jit(solution)/shard_map/ppermute | solution.py:14
  20.8 32.9 %collective-permute-start.1 = (bf16[528,128]{1,0:T(8,128)(2,1)}, bf16[528,128]{1,0:T(8,128)(2,1)}, u32[]{:S(2)}, u32[]{:S(2)}) collective-permute-start(bf16[528,128]{1,0:T(8,128)(2,1)} %maximum_maximum_fusion.1), channel_id=1, source_target_pairs={{0,16},{8,24},{16,0},{24,8},{32,48},{40,56},{48,32},{56,40},{64,80... | collective-permute-start | bytes 405512 | tf_op jit(solution)/shard_map/ppermute | solution.py:14
  22.2 31.5 %collective-permute-start.2 = (bf16[528,128]{1,0:T(8,128)(2,1)}, bf16[528,128]{1,0:T(8,128)(2,1)}, u32[]{:S(2)}, u32[]{:S(2)}) collective-permute-start(bf16[528,128]{1,0:T(8,128)(2,1)} %maximum_maximum_fusion.2), channel_id=1, source_target_pairs={{0,24},{8,0},{16,8},{24,16},{32,56},{40,32},{48,40},{56,48},{64,88... | collective-permute-start | bytes 405512 | tf_op jit(solution)/shard_map/ppermute | solution.py:14
  23.3 21.3 %copy-start.18 = (pred[512,512]{0,1:T(8,128)(4,1)}, pred[512,512]{0,1:T(8,128)(4,1)S(1)}, u32[]{:S(2)}) copy-start(pred[512,512]{0,1:T(8,128)(4,1)S(1)} %iota_compare_fusion) | copy-start | bytes 786436
  31.2 11.7 %copy-start.12 = (f32[1,16,64,128]{3,2,1,0:T(8,128)S(1)}, f32[1,16,64,128]{3,2,1,0:T(8,128)}, u32[]{:S(2)}) copy-start(f32[1,16,64,128]{3,2,1,0:T(8,128)} %param.18) | copy-start | bytes 1572868
  41.4 2.3 %copy-start.26 = (f32[512,16]{0,1:T(8,128)S(1)}, f32[512,16]{0,1:T(8,128)}, u32[]{:S(2)}) copy-start(f32[512,16]{0,1:T(8,128)} %copy-done.25) | copy-start | bytes 98308
  44.7 8.9 %copy-start.19 = (bf16[1,4,64,128]{3,2,1,0:T(8,128)(2,1)S(1)}, bf16[1,4,64,128]{3,2,1,0:T(8,128)(2,1)}, u32[]{:S(2)}) copy-start(bf16[1,4,64,128]{3,2,1,0:T(8,128)(2,1)} %get-tuple-element.73) | copy-start | bytes 196612
  44.7 8.9 %copy-start.20 = (bf16[1,4,64,128]{3,2,1,0:T(8,128)(2,1)S(1)}, bf16[1,4,64,128]{3,2,1,0:T(8,128)(2,1)}, u32[]{:S(2)}) copy-start(bf16[1,4,64,128]{3,2,1,0:T(8,128)(2,1)} %get-tuple-element.100) | copy-start | bytes 196612
  52.5 3.5 %copy-start.10 = (bf16[512,512]{0,1:T(8,128)(2,1)}, bf16[512,512]{0,1:T(8,128)(2,1)S(1)}, u32[]{:S(2)}) copy-start(bf16[512,512]{0,1:T(8,128)(2,1)S(1)} %fusion) | copy-start | bytes 1572868
  61.6 9.8 %collective-permute-start.3 = (bf16[528,128]{1,0:T(8,128)(2,1)S(1)}, bf16[528,128]{1,0:T(8,128)(2,1)S(1)}, u32[]{:S(2)}, u32[]{:S(2)}) collective-permute-start(bf16[528,128]{1,0:T(8,128)(2,1)S(1)} %get-tuple-element.78), channel_id=1, source_target_pairs={{0,32},{8,40},{16,48},{24,56},{32,64},{40,72},{48,80},{56,88},{64,... | collective-permute-start | bytes 405512 | tf_op jit(solution)/shard_map/ppermute | solution.py:14
  63.6 9.0 %collective-permute-start.4 = (bf16[528,128]{1,0:T(8,128)(2,1)S(1)}, bf16[528,128]{1,0:T(8,128)(2,1)S(1)}, u32[]{:S(2)}, u32[]{:S(2)}) collective-permute-start(bf16[528,128]{1,0:T(8,128)(2,1)S(1)} %get-tuple-element.78), channel_id=1, source_target_pairs={{0,64},{8,72},{16,80},{24,88},{32,96},{40,104},{48,112},{56,120},{... | collective-permute-start | bytes 405512 | tf_op jit(solution)/shard_map/ppermute | solution.py:14
  67.1 5.4 %collective-permute-start.5 = (bf16[528,128]{1,0:T(8,128)(2,1)S(1)}, bf16[528,128]{1,0:T(8,128)(2,1)S(1)}, u32[]{:S(2)}, u32[]{:S(2)}) collective-permute-start(bf16[528,128]{1,0:T(8,128)(2,1)S(1)} %get-tuple-element.78), channel_id=1, source_target_pairs={{0,96},{8,104},{16,112},{24,120},{32,0},{40,8},{48,16},{56,24},{64... | collective-permute-start | bytes 405512 | tf_op jit(solution)/shard_map/ppermute | solution.py:14
  71.3 1.2 copy-start.21
  72.6 0.7 copy-start.22
  72.6 0.7 copy-start.23
  79.5 8.9 %collective-permute-start.6 = (bf16[256,128]{1,0:T(8,128)(2,1)S(1)}, bf16[256,128]{1,0:T(8,128)(2,1)S(1)}, u32[]{:S(2)}, u32[]{:S(2)}) collective-permute-start(bf16[256,128]{1,0:T(8,128)(2,1)S(1)} %get-tuple-element.68), channel_id=1, source_target_pairs={{0,8},{8,16},{16,24},{24,0},{32,40},{40,48},{48,56},{56,32},{64,72... | collective-permute-start | bytes 196616 | tf_op jit(solution)/shard_map/ppermute | solution.py:14
  81.0 7.4 %collective-permute-start.7 = (bf16[256,128]{1,0:T(8,128)(2,1)S(1)}, bf16[256,128]{1,0:T(8,128)(2,1)S(1)}, u32[]{:S(2)}, u32[]{:S(2)}) collective-permute-start(bf16[256,128]{1,0:T(8,128)(2,1)S(1)} %get-tuple-element.67), channel_id=1, source_target_pairs={{0,16},{8,24},{16,0},{24,8},{32,48},{40,56},{48,32},{56,40},{64,80... | collective-permute-start | bytes 196616 | tf_op jit(solution)/shard_map/ppermute | solution.py:14
  83.4 5.0 %collective-permute-start.8 = (bf16[256,128]{1,0:T(8,128)(2,1)S(1)}, bf16[256,128]{1,0:T(8,128)(2,1)S(1)}, u32[]{:S(2)}, u32[]{:S(2)}) collective-permute-start(bf16[256,128]{1,0:T(8,128)(2,1)S(1)} %get-tuple-element.66), channel_id=1, source_target_pairs={{0,24},{8,0},{16,8},{24,16},{32,56},{40,32},{48,40},{56,48},{64,88... | collective-permute-start | bytes 196616 | tf_op jit(solution)/shard_map/ppermute | solution.py:14
  88.4 1.1 copy-start.27
  89.0 9.6 %slice-start.4 = ((s8[8388608]{0:T(1024)(128)(4,1)}), s8[4194304]{0:T(1024)(128)(4,1)S(1)}, s32[]{:S(2)}) async-start(s8[8388608]{0:T(1024)(128)(4,1)} %bitcast.423), calls=%async_computation.6 | async-start | bytes 8388608
  89.5 9.1 %slice-start.5 = ((s8[8388608]{0:T(1024)(128)(4,1)}), s8[4194304]{0:T(1024)(128)(4,1)S(1)}, s32[]{:S(2)}) async-start(s8[8388608]{0:T(1024)(128)(4,1)} %bitcast.423), calls=%async_computation.7 | async-start | bytes 8388608
  105.1 7.6 %copy-start.7 = (bf16[512,4,1,256]{0,3,2,1:T(8,128)(2,1)S(1)}, bf16[512,4,1,256]{0,3,2,1:T(8,128)(2,1)}, u32[]{:S(2)}) copy-start(bf16[512,4,1,256]{0,3,2,1:T(8,128)(2,1)} %get-tuple-element.27) | copy-start | bytes 3145732
  105.2 14.3 %collective-permute-start.9 = (bf16[2,256,512]{2,1,0:T(8,128)(2,1)S(1)}, bf16[2,256,512]{2,1,0:T(8,128)(2,1)S(1)}, u32[]{:S(2)}, u32[]{:S(2)}) collective-permute-start(bf16[2,256,512]{2,1,0:T(8,128)(2,1)S(1)} %get-tuple-element.39), channel_id=1, source_target_pairs={{0,8},{8,16},{16,24},{24,0},{32,40},{40,48},{48,56},{56,32},{64,72... | collective-permute-start | bytes 1572872 | tf_op jit(solution)/shard_map/ppermute | solution.py:14
  107.1 6.3 %copy-start.6 = (bf16[512,4,1,256]{0,3,2,1:T(8,128)(2,1)S(1)}, bf16[512,4,1,256]{0,3,2,1:T(8,128)(2,1)}, u32[]{:S(2)}) copy-start(bf16[512,4,1,256]{0,3,2,1:T(8,128)(2,1)} %get-tuple-element.28) | copy-start | bytes 3145732
  107.1 16.0 %collective-permute-start.11 = (bf16[2,256,512]{2,1,0:T(8,128)(2,1)S(1)}, bf16[2,256,512]{2,1,0:T(8,128)(2,1)S(1)}, u32[]{:S(2)}, u32[]{:S(2)}) collective-permute-start(bf16[2,256,512]{2,1,0:T(8,128)(2,1)S(1)} %get-tuple-element.40), channel_id=1, source_target_pairs={{0,24},{8,0},{16,8},{24,16},{32,56},{40,32},{48,40},{56,48},{64,88... | collective-permute-start | bytes 1572872 | tf_op jit(solution)/shard_map/ppermute | solution.py:14
  109.4 15.3 %collective-permute-start.17 = (bf16[2,256,512]{2,1,0:T(8,128)(2,1)S(1)}, bf16[2,256,512]{2,1,0:T(8,128)(2,1)S(1)}, u32[]{:S(2)}, u32[]{:S(2)}) collective-permute-start(bf16[2,256,512]{2,1,0:T(8,128)(2,1)S(1)} %get-tuple-element.41), channel_id=1, source_target_pairs={{0,32},{8,40},{16,48},{24,56},{32,64},{40,72},{48,80},{56,88},{64,... | collective-permute-start | bytes 1572872 | tf_op jit(solution)/shard_map/ppermute | solution.py:14
  110.6 15.3 %collective-permute-start.19 = (bf16[2,256,512]{2,1,0:T(8,128)(2,1)S(1)}, bf16[2,256,512]{2,1,0:T(8,128)(2,1)S(1)}, u32[]{:S(2)}, u32[]{:S(2)}) collective-permute-start(bf16[2,256,512]{2,1,0:T(8,128)(2,1)S(1)} %get-tuple-element.42), channel_id=1, source_target_pairs={{0,96},{8,104},{16,112},{24,120},{32,0},{40,8},{48,16},{56,24},{64... | collective-permute-start | bytes 1572872 | tf_op jit(solution)/shard_map/ppermute | solution.py:14
  113.4 4.6 %copy-start.2 = (f32[1024,512]{1,0:T(8,128)}, f32[1024,512]{1,0:T(8,128)S(1)}, u32[]{:S(2)}) copy-start(f32[1024,512]{1,0:T(8,128)S(1)} %fusion.44) | copy-start | bytes 6291460
  113.5 1.5 copy-start.24
  114.2 3.9 %copy-start.4 = (f32[1024,512]{1,0:T(8,128)}, f32[1024,512]{1,0:T(8,128)S(1)}, u32[]{:S(2)}) copy-start(f32[1024,512]{1,0:T(8,128)S(1)} %fusion.47) | copy-start | bytes 6291460
  115.0 1.6 copy-start.9
  115.0 2.3 %copy-start.8 = (bf16[512,1,4,256]{0,3,2,1:T(8,128)(2,1)S(1)}, bf16[512,1,4,256]{0,3,2,1:T(8,128)(2,1)}, u32[]{:S(2)}) copy-start(bf16[512,1,4,256]{0,3,2,1:T(8,128)(2,1)} %get-tuple-element.30) | copy-start | bytes 3145732
  117.3 1.4 copy-start.3
  118.1 1.4 copy-start.5
  118.2 1.9 %slice-start = ((f32[1024,512]{1,0:T(8,128)}), f32[512,512]{1,0:T(8,128)S(1)}, s32[]{:S(2)}) async-start(f32[1024,512]{1,0:T(8,128)} %copy-done.2), calls=%async_computation.2 | async-start | bytes 2097152 | tf_op jit(solution)/shard_map/slice | solution.py:150
  118.7 4.4 %slice-start.2 = ((f32[1024,512]{1,0:T(8,128)}), f32[512,512]{1,0:T(8,128)S(1)}, s32[]{:S(2)}) async-start(f32[1024,512]{1,0:T(8,128)} %copy-done.4), calls=%async_computation.4 | async-start | bytes 2097152 | tf_op jit(solution)/shard_map/slice | solution.py:151
  120.1 4.6 %slice-start.1 = ((f32[1024,512]{1,0:T(8,128)}), f32[512,512]{1,0:T(8,128)S(1)}, s32[]{:S(2)}) async-start(f32[1024,512]{1,0:T(8,128)} %copy-done.3), calls=%async_computation.3 | async-start | bytes 2097152 | tf_op jit(solution)/shard_map/slice | solution.py:150
  121.3 22.1 %collective-permute-start.10 = (bf16[4,256,512]{2,1,0:T(8,128)(2,1)}, bf16[4,256,512]{2,1,0:T(8,128)(2,1)}, u32[]{:S(2)}, u32[]{:S(2)}) collective-permute-start(bf16[4,256,512]{2,1,0:T(8,128)(2,1)} %pad_maximum_fusion), channel_id=1, source_target_pairs={{0,8},{8,16},{16,24},{24,0},{32,40},{40,48},{48,56},{56,32},{64,72... | collective-permute-start | bytes 3145736 | tf_op jit(solution)/shard_map/ppermute | solution.py:14
  123.1 2.9 %slice-start.3 = ((f32[1024,512]{1,0:T(8,128)}), f32[512,512]{1,0:T(8,128)S(1)}, s32[]{:S(2)}) async-start(f32[1024,512]{1,0:T(8,128)} %copy-done.5), calls=%async_computation.5 | async-start | bytes 2097152 | tf_op jit(solution)/shard_map/slice | solution.py:151
  124.4 21.6 %collective-permute-start.12 = (bf16[4,256,512]{2,1,0:T(8,128)(2,1)}, bf16[4,256,512]{2,1,0:T(8,128)(2,1)}, u32[]{:S(2)}, u32[]{:S(2)}) collective-permute-start(bf16[4,256,512]{2,1,0:T(8,128)(2,1)} %pad_maximum_fusion.1), channel_id=1, source_target_pairs={{0,24},{8,0},{16,8},{24,16},{32,56},{40,32},{48,40},{56,48},{64,88... | collective-permute-start | bytes 3145736 | tf_op jit(solution)/shard_map/ppermute | solution.py:14
  126.0 6.5 %copy-start.15 = (f32[512,128]{0,1:T(8,128)S(1)}, f32[512,128]{0,1:T(8,128)}, u32[]{:S(2)}) copy-start(f32[512,128]{0,1:T(8,128)} %fusion.5) | copy-start | bytes 786436
  126.0 25.4 %collective-permute-start.18 = (bf16[4,256,512]{2,1,0:T(8,128)(2,1)}, bf16[4,256,512]{2,1,0:T(8,128)(2,1)}, u32[]{:S(2)}, u32[]{:S(2)}) collective-permute-start(bf16[4,256,512]{2,1,0:T(8,128)(2,1)} %pad_maximum_fusion.2), channel_id=1, source_target_pairs={{0,32},{8,40},{16,48},{24,56},{32,64},{40,72},{48,80},{56,88},{64,... | collective-permute-start | bytes 3145736 | tf_op jit(solution)/shard_map/ppermute | solution.py:14
  127.3 24.1 %collective-permute-start.20 = (bf16[4,256,512]{2,1,0:T(8,128)(2,1)}, bf16[4,256,512]{2,1,0:T(8,128)(2,1)}, u32[]{:S(2)}, u32[]{:S(2)}) collective-permute-start(bf16[4,256,512]{2,1,0:T(8,128)(2,1)} %pad_maximum_fusion.3), channel_id=1, source_target_pairs={{0,96},{8,104},{16,112},{24,120},{32,0},{40,8},{48,16},{56,24},{64... | collective-permute-start | bytes 3145736 | tf_op jit(solution)/shard_map/ppermute | solution.py:14
  148.1 8.5 %collective-permute-start.13 = (bf16[128,512]{1,0:T(8,128)(2,1)S(1)}, bf16[128,512]{1,0:T(8,128)(2,1)S(1)}, u32[]{:S(2)}, u32[]{:S(2)}) collective-permute-start(bf16[128,512]{1,0:T(8,128)(2,1)S(1)} %get-tuple-element.57), channel_id=1, source_target_pairs={{0,32},{8,40},{16,48},{24,56},{32,64},{40,72},{48,80},{56,88},{64,... | collective-permute-start | bytes 393224 | tf_op jit(solution)/shard_map/ppermute | solution.py:14
  148.7 7.9 %collective-permute-start.15 = (bf16[128,512]{1,0:T(8,128)(2,1)S(1)}, bf16[128,512]{1,0:T(8,128)(2,1)S(1)}, u32[]{:S(2)}, u32[]{:S(2)}) collective-permute-start(bf16[128,512]{1,0:T(8,128)(2,1)S(1)} %get-tuple-element.58), channel_id=1, source_target_pairs={{0,96},{8,104},{16,112},{24,120},{32,0},{40,8},{48,16},{56,24},{64... | collective-permute-start | bytes 393224 | tf_op jit(solution)/shard_map/ppermute | solution.py:14
  153.4 12.0 %copy-start.11 = (bf16[512,512]{0,1:T(8,128)(2,1)S(1)}, bf16[512,512]{0,1:T(8,128)(2,1)}, u32[]{:S(2)}) copy-start(bf16[512,512]{0,1:T(8,128)(2,1)} %copy-done.10) | copy-start | bytes 1572868
  153.4 12.0 %copy-start.14 = (bf16[512,1,128]{2,0,1:T(8,128)(2,1)S(1)}, bf16[512,1,128]{2,0,1:T(8,128)(2,1)}, u32[]{:S(2)}) copy-start(bf16[512,1,128]{2,0,1:T(8,128)(2,1)} %param.16) | copy-start | bytes 393220
  153.4 12.0 %copy-start.17 = (f32[512,128]{1,0:T(8,128)S(1)}, f32[512,128]{1,0:T(8,128)}, u32[]{:S(2)}) copy-start(f32[512,128]{1,0:T(8,128)} %copy.74) | copy-start | bytes 786436
  153.5 6.9 %collective-permute-start.21 = (bf16[128,512]{1,0:T(8,128)(2,1)S(1)}, bf16[128,512]{1,0:T(8,128)(2,1)S(1)}, u32[]{:S(2)}, u32[]{:S(2)}) collective-permute-start(bf16[128,512]{1,0:T(8,128)(2,1)S(1)} %get-tuple-element.59), channel_id=1, source_target_pairs={{0,8},{8,16},{16,24},{24,0},{32,40},{40,48},{48,56},{56,32},{64,72... | collective-permute-start | bytes 393224 | tf_op jit(solution)/shard_map/ppermute | solution.py:14
  156.5 6.4 %collective-permute-start.23 = (bf16[128,512]{1,0:T(8,128)(2,1)S(1)}, bf16[128,512]{1,0:T(8,128)(2,1)S(1)}, u32[]{:S(2)}, u32[]{:S(2)}) collective-permute-start(bf16[128,512]{1,0:T(8,128)(2,1)S(1)} %get-tuple-element.60), channel_id=1, source_target_pairs={{0,24},{8,0},{16,8},{24,16},{32,56},{40,32},{48,40},{56,48},{64,88... | collective-permute-start | bytes 393224 | tf_op jit(solution)/shard_map/ppermute | solution.py:14
  156.7 9.6 %collective-permute-start.14 = (bf16[256,512]{1,0:T(8,128)(2,1)S(1)}, bf16[256,512]{1,0:T(8,128)(2,1)S(1)}, u32[]{:S(2)}, u32[]{:S(2)}) collective-permute-start(bf16[256,512]{1,0:T(8,128)(2,1)S(1)} %pad_maximum_fusion.9), channel_id=1, source_target_pairs={{0,32},{8,40},{16,48},{24,56},{32,64},{40,72},{48,80},{56,88},{64,... | collective-permute-start | bytes 786440 | tf_op jit(solution)/shard_map/ppermute | solution.py:14
  156.8 15.9 %copy-start.1 = (bf16[512,1,128]{2,0,1:T(8,128)(2,1)S(1)}, bf16[512,1,128]{2,0,1:T(8,128)(2,1)}, u32[]{:S(2)}) copy-start(bf16[512,1,128]{2,0,1:T(8,128)(2,1)} %param.15) | copy-start | bytes 393220
  156.8 9.5 %collective-permute-start.16 = (bf16[256,512]{1,0:T(8,128)(2,1)S(1)}, bf16[256,512]{1,0:T(8,128)(2,1)S(1)}, u32[]{:S(2)}, u32[]{:S(2)}) collective-permute-start(bf16[256,512]{1,0:T(8,128)(2,1)S(1)} %pad_maximum_fusion.10), channel_id=1, source_target_pairs={{0,96},{8,104},{16,112},{24,120},{32,0},{40,8},{48,16},{56,24},{64... | collective-permute-start | bytes 786440 | tf_op jit(solution)/shard_map/ppermute | solution.py:14
  163.0 6.4 %collective-permute-start.22 = (bf16[256,512]{1,0:T(8,128)(2,1)S(1)}, bf16[256,512]{1,0:T(8,128)(2,1)S(1)}, u32[]{:S(2)}, u32[]{:S(2)}) collective-permute-start(bf16[256,512]{1,0:T(8,128)(2,1)S(1)} %pad_maximum_fusion.11), channel_id=1, source_target_pairs={{0,8},{8,16},{16,24},{24,0},{32,40},{40,48},{48,56},{56,32},{64,72... | collective-permute-start | bytes 786440 | tf_op jit(solution)/shard_map/ppermute | solution.py:14
  165.2 6.4 %collective-permute-start.24 = (bf16[256,512]{1,0:T(8,128)(2,1)S(1)}, bf16[256,512]{1,0:T(8,128)(2,1)S(1)}, u32[]{:S(2)}, u32[]{:S(2)}) collective-permute-start(bf16[256,512]{1,0:T(8,128)(2,1)S(1)} %pad_maximum_fusion.12), channel_id=1, source_target_pairs={{0,24},{8,0},{16,8},{24,16},{32,56},{40,32},{48,40},{56,48},{64,88... | collective-permute-start | bytes 786440 | tf_op jit(solution)/shard_map/ppermute | solution.py:14
Sparse Core Ops, SparseCore 0:
  105.2 35.7 reduce-scatter.1

commit v2 on v0

v2 whole, which is shorter than its diff:
```python
import functools

import jax
import jax.numpy as jnp
from jax import lax
from jax.experimental import pallas as pl
from jax.experimental.pallas import tpu as pltpu
from jax.sharding import PartitionSpec as P

SIDE = 4
CHUNK = 128
CHUNKS = 4
HEADS = 16
WIDE = 1024
QUARTER = WIDE // SIDE
TAIL = 16
F32 = jnp.float32
BF16 = jnp.bfloat16
ORDER = (2, 1, 3, 0)
VMEM_LIMIT = 48 * 1024 * 1024


def params(**kw):
    return pltpu.CompilerParams(vmem_limit_bytes=VMEM_LIMIT, **kw)


def cost(flops, moved, exps=0):
    return pl.CostEstimate(flops=flops, bytes_accessed=moved, transcendentals=exps)


def whole(space=pltpu.VMEM):
    return pl.BlockSpec(memory_space=space)


def hop(block, dz, dy):
    route = []
    for i in range(SIDE * SIDE):
        z, y = divmod(i, SIDE)
        route.append((i, ((z + dz) % SIDE) * SIDE + (y + dy) % SIDE))
    return lax.ppermute(block, "ctx", route)


def hop_smp(block, dx, dc):
    route = []
    for i in range(SIDE * 2):
        x, c = divmod(i, 2)
        route.append((i, ((x + dx) % SIDE) * 2 + (c + dc) % 2))
    return lax.ppermute(block, "smp", route)


def dot(a, b):
    return lax.dot_general(a, b, (((1,), (0,)), ((), ())), preferred_element_type=F32)


def dot_nt(a, b):
    return lax.dot_general(a, b, (((1,), (1,)), ((), ())), preferred_element_type=F32)


def dot_tn(a, b):
    return lax.dot_general(a, b, (((0,), (0,)), ((), ())), preferred_element_type=F32)


def halves(v):
    high = v.astype(BF16)
    return high, (v - high.astype(F32)).astype(BF16)


def spread_matrix():
    lane = lax.broadcasted_iota(jnp.int32, (HEADS, WIDE), 1)
    head = lax.broadcasted_iota(jnp.int32, (HEADS, WIDE), 0)
    return ((lane >= head * 64) & (lane < head * 64 + 64)).astype(F32).astype(BF16)


def spread(v, matrix):
    high, low = halves(v)
    return dot(high, matrix) + dot(low, matrix)


def spread_row(v, matrix):
    return spread(jnp.broadcast_to(v, (8, HEADS)), matrix)[0:1]


def tail_rows(row):
    high, low = halves(row)
    at = lax.broadcasted_iota(jnp.int32, (TAIL, row.shape[1]), 0)
    wide = jnp.where(at == 0, high.astype(F32), jnp.where(at == 1, low.astype(F32), 0.0))
    return wide.astype(BF16)


def tail_value(rows):
    rows = rows.astype(F32)
    return rows[0:1] + rows[1:2]


def turn(a, b):
    return lax.rem(a + b + 2 * SIDE, SIDE)


def pre_kernel(
    y_ref, step_ref, dlog_ref, grad_ref, read_ref, fork_ref,
    rel_ref, scaled_ref, state_ref, m0, m1, m2, m3, message,
):
    y = y_ref[0]
    row = lax.broadcasted_iota(jnp.int32, (CHUNK, CHUNK), 0)
    col = lax.broadcasted_iota(jnp.int32, (CHUNK, CHUNK), 1)
    lower = jnp.where(row >= col, 1.0, 0.0).astype(BF16)
    matrix = spread_matrix()
    rates = step_ref[...] * -jnp.exp(dlog_ref[...])
    totals = []
    for c in range(CHUNKS):
        here = slice(c * CHUNK, (c + 1) * CHUNK)
        part = rates[here]
        high, rest = part.astype(BF16), None
        rest = part - high.astype(F32)
        middle, low = halves(rest)
        rel = dot(lower, high) + dot(lower, middle) + dot(lower, low)
        rel_ref[c] = rel
        totals.append(rel[CHUNK - 1 : CHUNK])
        scaled_ref[here] = (spread(jnp.exp(rel), matrix) * grad_ref[here].astype(F32)).astype(BF16)
    state = None
    for c in reversed(range(CHUNKS)):
        here = slice(c * CHUNK, (c + 1) * CHUNK)
        local = dot_tn(read_ref[here], scaled_ref[here])
        if state is None:
            state = local
        else:
            state = local + spread_row(jnp.exp(totals[c]), matrix) * state
        if c > 0:
            state_ref[c - 1] = state.astype(BF16)
    message[0:128] = state.astype(BF16)
    message[128:256] = (fork_ref[0] + fork_ref[1]).T.astype(BF16)
    decay = spread_row(jnp.exp(totals[0] + totals[1] + totals[2] + totals[3]), matrix)
    message[256 : 256 + TAIL] = tail_rows(decay)
    for d, out in enumerate((m0, m1, m2, m3)):
        start = pl.multiple_of(turn(y, d) * QUARTER, QUARTER)
        out[...] = message[:, pl.ds(start, QUARTER)]


def pre(y, step_size, decay_log, out_grad, reads, fork_grad):
    sent = jax.ShapeDtypeStruct((256 + TAIL, QUARTER), BF16)
    return pl.pallas_call(
        pre_kernel,
        out_shape=[
            jax.ShapeDtypeStruct((CHUNKS, CHUNK, HEADS), F32),
            jax.ShapeDtypeStruct((CHUNKS * CHUNK, WIDE), BF16),
            jax.ShapeDtypeStruct((CHUNKS - 1, 128, WIDE), BF16),
        ]
        + [sent] * 4,
        in_specs=[whole(pltpu.SMEM)] + [whole()] * 5,
        out_specs=[whole()] * 7,
        scratch_shapes=[pltpu.VMEM((256 + TAIL, WIDE), BF16)],
        compiler_params=params(),
        cost_estimate=cost(400_000_000, 5_000_000),
    )(y, step_size, decay_log, out_grad, reads, fork_grad)


def group_kernel(y_ref, a0, a1, a2, a3, out_ref, stack):
    y = y_ref[0]
    for d, ref in enumerate((a0, a1, a2, a3)):
        stack[d] = ref[...]
    total = rate = fork = None
    for b in reversed(range(SIDE)):
        at = turn(y, -b)
        local = stack[at, 0:128].astype(F32)
        decay = tail_value(stack[at, 256 : 256 + TAIL])
        share = stack[at, 128:256].astype(F32)
        if total is None:
            total, rate, fork = local, decay, share
        else:
            total, rate, fork = local + decay * total, rate * decay, fork + share
    out_ref[0:128] = total.astype(BF16)
    out_ref[128:256] = fork.astype(BF16)
    out_ref[256 : 256 + TAIL] = tail_rows(rate)


def group(y, arrived):
    return pl.pallas_call(
        group_kernel,
        out_shape=jax.ShapeDtypeStruct((256 + TAIL, QUARTER), BF16),
        in_specs=[whole(pltpu.SMEM)] + [whole()] * 4,
        out_specs=whole(),
        scratch_shapes=[pltpu.VMEM((SIDE, 256 + TAIL, QUARTER), BF16)],
        compiler_params=params(),
        cost_estimate=cost(1_000_000, 600_000),
    )(y, *arrived)


def carry_kernel(y_ref, z_ref, a0, a1, a2, a3, b0, b1, b2, b3, c0, c1, c2, c3, first, second, out):
    y, z = y_ref[0], z_ref[0]
    for d, ref in enumerate((a0, a1, a2, a3)):
        first[d] = ref[...]
    for d, ref in enumerate((b0, b1, b2, b3)):
        second[d] = ref[...]
    carry = jnp.zeros((128, QUARTER), F32)
    for d in range(SIDE):
        carry = carry + second[d, 128:256].astype(F32)
    mine = carry
    for b in (3, 2, 1):
        at = turn(z, -b)
        decay = tail_value(second[at, 256 : 256 + TAIL])
        carry = second[at, 0:128].astype(F32) + decay * carry
        mine = jnp.where(z == b - 1, carry, mine)
    out[SIDE - 1] = mine.astype(BF16)
    for b in (3, 2, 1):
        at = turn(y, -b)
        decay = tail_value(first[at, 256 : 256 + TAIL])
        mine = first[at, 0:128].astype(F32) + decay * mine
        out[b - 1] = mine.astype(BF16)
    for d, ref in enumerate((c0, c1, c2, c3)):
        ref[...] = out[turn(y, d)]


def carry_over(y, z, first, second):
    return pl.pallas_call(
        carry_kernel,
        out_shape=[jax.ShapeDtypeStruct((128, QUARTER), BF16)] * 4,
        in_specs=[whole(pltpu.SMEM)] * 2 + [whole()] * 8,
        out_specs=[whole()] * 4,
        scratch_shapes=[
            pltpu.VMEM((SIDE, 256 + TAIL, QUARTER), BF16),
            pltpu.VMEM((SIDE, 256 + TAIL, QUARTER), BF16),
            pltpu.VMEM((SIDE, 128, QUARTER), BF16),
        ],
        compiler_params=params(),
        cost_estimate=cost(1_000_000, 1_400_000),
    )(y, z, *first, *second)


def diag_kernel(rel_ref, relt_ref, step_ref, skip_ref, read_ref, write_ref, grad_ref, out_ref):
    matrix = spread_matrix()
    row = lax.broadcasted_iota(jnp.int32, (CHUNK, CHUNK), 0)
    col = lax.broadcasted_iota(jnp.int32, (CHUNK, CHUNK), 1)
    scores = jnp.where(col >= row, dot_nt(write_ref[...], read_ref[...]), 0.0)
    rel, relt = rel_ref[0], relt_ref[0]
    parts = []
    for pair in range(HEADS // 2):
        grads = grad_ref[:, pair * 128 : pair * 128 + 128]
        both = []
        for h in (2 * pair, 2 * pair + 1):
            kernel = jnp.exp(jnp.minimum(relt[h : h + 1] - rel[:, h : h + 1], 0.0))
            both.append(dot((scores * kernel).astype(BF16), grads))
        parts.append(jnp.where(col < 64, both[0], both[1]))
    steps = spread(step_ref[...], matrix)
    for pair in range(HEADS // 2):
        at = slice(pair * 128, pair * 128 + 128)
        out_ref[:, at] = steps[:, at] * parts[pair] + skip_ref[:, at] * grad_ref[:, at].astype(F32)


def diag(rel, relt, step_size, skip_row, reads, writes, out_grad):
    by_chunk = lambda c: (c, 0)
    return pl.pallas_call(
        diag_kernel,
        grid=(CHUNKS,),
        out_shape=jax.ShapeDtypeStruct((CHUNKS * CHUNK, WIDE), F32),
        in_specs=[
            pl.BlockSpec((1, CHUNK, HEADS), lambda c: (c, 0, 0)),
            pl.BlockSpec((1, HEADS, CHUNK), lambda c: (c, 0, 0)),
            pl.BlockSpec((CHUNK, HEADS), by_chunk),
            pl.BlockSpec((1, WIDE), lambda c: (0, 0)),
            pl.BlockSpec((CHUNK, 128), by_chunk),
            pl.BlockSpec((CHUNK, 128), by_chunk),
            pl.BlockSpec((CHUNK, WIDE), by_chunk),
        ],
        out_specs=pl.BlockSpec((CHUNK, WIDE), by_chunk),
        compiler_params=params(),
        cost_estimate=cost(1_500_000_000, 3_500_000, 1_000_000),
    )(rel, relt, step_size, skip_row, reads, writes, out_grad)


def x_kernel(
    y_ref, q0, q1, q2, q3, state_ref, rel_ref, step_ref, write_ref, base_ref,
    x_ref, full_ref, carried,
):
    y, c = y_ref[0], pl.program_id(0)
    matrix = spread_matrix()

    @pl.when(c == 0)
    def _():
        for d, ref in enumerate((q0, q1, q2, q3)):
            start = pl.multiple_of(turn(y, -d) * QUARTER, QUARTER)
            carried[:, pl.ds(start, QUARTER)] = ref[...]

    later = jnp.zeros((1, HEADS), F32)
    for k in range(CHUNKS):
        later = later + jnp.where(k > c, rel_ref[k, CHUNK - 1 : CHUNK], 0.0)
    share = spread_row(jnp.exp(later), matrix) * carried[...].astype(F32)
    full = jnp.where(c < CHUNKS - 1, state_ref[0].astype(F32) + share, share).astype(BF16)
    full_ref[0] = full
    rel = rel_ref[c]
    weights = spread(step_ref[...] * jnp.exp(rel[CHUNK - 1 : CHUNK] - rel), matrix)
    x_ref[...] = (base_ref[...] + weights * dot(write_ref[...], full)).astype(BF16)


def x_final(y, quarters, states, rel, step_size, writes, base):
    by_chunk = lambda c: (c, 0)
    return pl.pallas_call(
        x_kernel,
        grid=(CHUNKS,),
        out_shape=[
            jax.ShapeDtypeStruct((CHUNKS * CHUNK, WIDE), BF16),
            jax.ShapeDtypeStruct((CHUNKS, 128, WIDE), BF16),
        ],
        in_specs=[whole(pltpu.SMEM)]
        + [pl.BlockSpec((128, QUARTER), lambda c: (0, 0))] * 4
        + [
            pl.BlockSpec((1, 128, WIDE), lambda c: (jnp.minimum(c, CHUNKS - 2), 0, 0)),
            pl.BlockSpec((CHUNKS, CHUNK, HEADS), lambda c: (0, 0, 0)),
            pl.BlockSpec((CHUNK, HEADS), by_chunk),
            pl.BlockSpec((CHUNK, 128), by_chunk),
            pl.BlockSpec((CHUNK, WIDE), by_chunk),
        ],
        out_specs=[
            pl.BlockSpec((CHUNK, WIDE), by_chunk),
            pl.BlockSpec((1, 128, WIDE), lambda c: (c, 0, 0)),
        ],
        scratch_shapes=[pltpu.VMEM((128, WIDE), BF16)],
        compiler_params=params(),
        cost_estimate=cost(300_000_000, 5_500_000),
    )(y, *quarters, states, rel, step_size, writes, base)


def vector_kernel(
    rel_ref, relt_ref, step_ref, read_ref, write_ref, grad_ref, scaled_ref, inputs_ref, full_ref,
    start_ref, wgrad_ref, rgrad_ref, state,
):
    matrix = spread_matrix()

    @pl.when(pl.program_id(0) == 0)
    def _():
        state[...] = start_ref[...].T

    row = lax.broadcasted_iota(jnp.int32, (CHUNK, CHUNK), 0)
    col = lax.broadcasted_iota(jnp.int32, (CHUNK, CHUNK), 1)
    rel, relt, step = rel_ref[0], relt_ref[0], step_ref[...]
    coupling = jnp.zeros((CHUNK, CHUNK), F32)
    for pair in range(HEADS // 2):
        at = slice(pair * 128, pair * 128 + 128)
        grads = grad_ref[:, at]
        inputs = inputs_ref[:, at]
        for k in range(2):
            h = 2 * pair + k
            own = jnp.where((col >= 64) == (k == 1), inputs.astype(F32), 0.0).astype(BF16)
            kernel = jnp.exp(jnp.minimum(relt[h : h + 1] - rel[:, h : h + 1], 0.0))
            coupling = coupling + step[:, h : h + 1] * kernel * dot_nt(own, grads)
    coupling = jnp.where(col >= row, coupling, 0.0).astype(BF16)
    last = rel[CHUNK - 1 : CHUNK]
    weights = spread(step * jnp.exp(last - rel), matrix)
    weighted = (weights * inputs_ref[...].astype(F32)).astype(BF16)
    wgrad_ref[...] = dot_nt(weighted, full_ref[0]) + dot(coupling, read_ref[...])
    rgrad_ref[...] = dot_nt(scaled_ref[...], state[...].astype(BF16)) + dot_tn(
        coupling, write_ref[...]
    )
    state[...] = spread_row(jnp.exp(last), matrix) * state[...] + dot_tn(write_ref[...], weighted)


def vectors(rel, relt, step_size, reads, writes, out_grad, scaled, inputs, full, start_state):
    by_chunk = lambda c: (c, 0)
    return pl.pallas_call(
        vector_kernel,
        grid=(CHUNKS,),
        out_shape=[jax.ShapeDtypeStruct((CHUNKS * CHUNK, 128), F32)] * 2,
        in_specs=[
            pl.BlockSpec((1, CHUNK, HEADS), lambda c: (c, 0, 0)),
            pl.BlockSpec((1, HEADS, CHUNK), lambda c: (c, 0, 0)),
            pl.BlockSpec((CHUNK, HEADS), by_chunk),
            pl.BlockSpec((CHUNK, 128), by_chunk),
            pl.BlockSpec((CHUNK, 128), by_chunk),
            pl.BlockSpec((CHUNK, WIDE), by_chunk),
            pl.BlockSpec((CHUNK, WIDE), by_chunk),
            pl.BlockSpec((CHUNK, WIDE), by_chunk),
            pl.BlockSpec((1, 128, WIDE), lambda c: (c, 0, 0)),
            pl.BlockSpec((WIDE, 128), lambda c: (0, 0)),
        ],
        out_specs=[pl.BlockSpec((CHUNK, 128), by_chunk)] * 2,
        scratch_shapes=[pltpu.VMEM((128, WIDE), F32)],
        compiler_params=params(),
        cost_estimate=cost(3_000_000_000, 5_000_000, 1_000_000),
    )(rel, relt, step_size, reads, writes, out_grad, scaled, inputs, full, start_state)


def project_kernel(x_ref, w_ref, out_ref):
    out_ref[...] = dot(x_ref[...], w_ref[...]).astype(BF16)


def project(layer_input, proj_weight):
    rows, depth = layer_input.shape
    wide = proj_weight.shape[1]
    tile = 256
    return pl.pallas_call(
        project_kernel,
        grid=(wide // tile,),
        out_shape=jax.ShapeDtypeStruct((rows, wide), BF16),
        in_specs=[
            pl.BlockSpec((rows, depth), lambda i: (0, 0)),
            pl.BlockSpec((depth, tile), lambda i: (0, i)),
        ],
        out_specs=pl.BlockSpec((rows, tile), lambda i: (0, i)),
        compiler_params=params(),
        cost_estimate=cost(2 * rows * depth * wide, 2 * (rows * depth + depth * wide + rows * wide)),
    )(layer_input, proj_weight)


def pair_kernel(idx_ref, up_ref, down_ref, x_ref, *refs):
    more, (up_out, down_out) = refs[:-2], refs[-2:]
    up = dot_tn(up_ref[...], x_ref[...])
    down = dot_tn(down_ref[...], x_ref[...])
    if more:
        up = up + more[0][0].astype(F32)
        down = down + more[1][0].astype(F32)
    up_out[0] = up.astype(BF16)
    down_out[0] = down.astype(BF16)


def pair_product(idx, layer_input, x_grad, side, more=()):
    rows = layer_input.shape[0]
    block = pl.BlockSpec((1, 256, 512), lambda g, s: (g, 0, 0))
    return pl.pallas_call(
        pair_kernel,
        grid_spec=pltpu.PrefetchScalarGridSpec(
            num_scalar_prefetch=1,
            grid=(2,),
            in_specs=[
                pl.BlockSpec((rows, 256), lambda g, s: (0, s[g])),
                pl.BlockSpec((rows, 256), lambda g, s: (0, s[g + 2])),
                pl.BlockSpec((rows, 512), lambda g, s: (0, side)),
            ]
            + [block] * len(more),
            out_specs=[block] * 2,
        ),
        out_shape=[jax.ShapeDtypeStruct((2, 256, 512), BF16)] * 2,
        compiler_params=params(),
        cost_estimate=cost(2 * 1024 * 512 * rows, 2 * (1024 * rows + 512 * rows + 1024 * 512)),
    )(idx, layer_input, layer_input, x_grad, *more)


def own_kernel(
    idx_ref, cols_ref, x_ref, below_add, below_plain, above_plain, above_add,
    up_out, down_out, up_keep, down_keep, own_out,
):
    g = pl.program_id(0)
    product = dot_tn(cols_ref[...], x_ref[...])
    below = jnp.where(g < 2, below_add[0].astype(F32), below_plain[0].astype(F32))
    above = jnp.where(g < 2, above_plain[0].astype(F32), above_add[0].astype(F32))
    total = product + below + above

    @pl.when(g == 0)
    def _():
        up_out[0:128] = total[0:128].astype(BF16)
        down_out[0:128] = total[128:256].astype(BF16)

    @pl.when(g == 1)
    def _():
        up_keep[...] = total[0:128].astype(BF16)
        up_out[128:256] = total[128:256].astype(BF16)

    @pl.when(g == 2)
    def _():
        down_out[128:256] = total[0:128].astype(BF16)
        down_keep[...] = total[128:256].astype(BF16)

    @pl.when(g == 3)
    def _():
        own_out[...] = total


def own_product(idx, layer_input, x_grad, side, below_add, below_plain, above_plain, above_add):
    rows = layer_input.shape[0]
    first = pl.BlockSpec((1, 256, 512), lambda g, s: (jnp.minimum(g, 1), 0, 0))
    second = pl.BlockSpec((1, 256, 512), lambda g, s: (jnp.maximum(g - 2, 0), 0, 0))
    kept = lambda n: pl.BlockSpec((n, 512), lambda g, s: (0, 0))
    return pl.pallas_call(
        own_kernel,
        grid_spec=pltpu.PrefetchScalarGridSpec(
            num_scalar_prefetch=1,
            grid=(4,),
            in_specs=[
                pl.BlockSpec((rows, 256), lambda g, s: (0, s[g])),
                pl.BlockSpec((rows, 512), lambda g, s: (0, side)),
                first,
                second,
                first,
                second,
            ],
            out_specs=[kept(256), kept(256), kept(128), kept(128), kept(256)],
        ),
        out_shape=[
            jax.ShapeDtypeStruct((256, 512), BF16),
            jax.ShapeDtypeStruct((256, 512), BF16),
            jax.ShapeDtypeStruct((128, 512), BF16),
            jax.ShapeDtypeStruct((128, 512), BF16),
            jax.ShapeDtypeStruct((256, 512), F32),
        ],
        compiler_params=params(),
        cost_estimate=cost(2 * 1024 * 512 * rows, 2 * (1024 * rows + 512 * rows + 3 * 1024 * 512)),
    )(idx, layer_input, x_grad, below_add, below_plain, above_plain, above_add)


def add_kernel(up_keep, down_keep, from_below, from_above, up_out, down_out):
    n = up_keep.shape[0]
    up_out[...] = (up_keep[...].astype(F32) + from_below[0:n].astype(F32)).astype(BF16)
    down_out[...] = (down_keep[...].astype(F32) + from_above[0:n].astype(F32)).astype(BF16)


def add_two(up_keep, down_keep, from_below, from_above):
    size = up_keep.shape
    return pl.pallas_call(
        add_kernel,
        out_shape=[jax.ShapeDtypeStruct(size, BF16)] * 2,
        in_specs=[whole()] * 4,
        out_specs=[whole()] * 2,
        compiler_params=params(),
        cost_estimate=cost(2 * size[0] * size[1], 12 * size[0] * size[1]),
    )(up_keep, down_keep, from_below, from_above)


def weight_kernel(scale, *refs):
    out = refs[-1]
    for side in range(2):
        own, below, above, below_add, above_add = refs[5 * side : 5 * side + 5]
        at = slice(512 * side, 512 * side + 512)
        top = own[0:128] + below_add[...].astype(F32) + above[128:256].astype(F32)
        bottom = own[128:256] + below[128:256].astype(F32) + above_add[...].astype(F32)
        out[0:128, at] = (top * scale).astype(BF16)
        out[128:256, at] = (bottom * scale).astype(BF16)


def weight_final(scale, first, second):
    return pl.pallas_call(
        functools.partial(weight_kernel, scale),
        out_shape=jax.ShapeDtypeStruct((256, WIDE), BF16),
        in_specs=[whole()] * 10,
        out_specs=whole(),
        compiler_params=params(),
        cost_estimate=cost(1_000_000, 3_000_000),
    )(*first, *second)


def weight_grad_of(layer_input, x_grad, z, y, scale):
    def blocks(side, to, groups):
        out = []
        for g in groups:
            if side == 0:
                out.append(turn(z, ORDER[g]) * SIDE + turn(y, to))
            else:
                out.append(turn(z, to) * SIDE + turn(y, ORDER[g]))
        return out

    moves = (lambda b, s: hop(b, 0, s), lambda b, s: hop(b, s, 0))
    arrived = []
    for side in range(2):
        idx = jnp.stack(blocks(side, 2, (0, 1)) + blocks(side, 2, (2, 3)))
        up, down = pair_product(idx, layer_input, x_grad, side)
        arrived.append((moves[side](up, 1), moves[side](down, -1)))
    plain = []
    for side in range(2):
        idx = jnp.stack(blocks(side, 1, (2, 3)) + blocks(side, -1, (0, 1)))
        up, down = pair_product(idx, layer_input, x_grad, side)
        plain.append((moves[side](up, 1), moves[side](down, -1)))
    added = []
    for side in range(2):
        idx = jnp.stack(blocks(side, 1, (0, 1)) + blocks(side, -1, (2, 3)))
        up, down = pair_product(idx, layer_input, x_grad, side, arrived[side])
        added.append((moves[side](up, 1), moves[side](down, -1)))
    results = []
    for side in range(2):
        idx = jnp.stack(blocks(side, 0, (0, 1, 2, 3)))
        move = moves[1 - side]
        up, down, up_keep, down_keep, own = own_product(
            idx, layer_input, x_grad, side,
            added[side][0], plain[side][0], plain[side][1], added[side][1],
        )
        below, above = move(up, 1), move(down, -1)
        up, down = add_two(up_keep, down_keep, below, above)
        results.append((own, below, above, move(up, 1), move(down, -1)))
    return weight_final(scale, *results)


def theirs_kernel(c_ref, x_ref, w_ref, out_ref):
    rows = x_ref[...].reshape(256, WIDE)
    out_ref[...] = dot_nt(rows, w_ref[...]).astype(BF16)


def theirs(other, x_rows, proj_weight):
    depth, tile = proj_weight.shape[0], 512
    return pl.pallas_call(
        theirs_kernel,
        grid_spec=pltpu.PrefetchScalarGridSpec(
            num_scalar_prefetch=1,
            grid=(depth // tile,),
            in_specs=[
                pl.BlockSpec((SIDE, 1, 64, WIDE), lambda i, s: (0, s[0], 0, 0)),
                pl.BlockSpec((tile, WIDE), lambda i, s: (i, 0)),
            ],
            out_specs=pl.BlockSpec((256, tile), lambda i, s: (0, i)),
        ),
        out_shape=jax.ShapeDtypeStruct((256, depth), BF16),
        compiler_params=params(),
        cost_estimate=cost(2 * 256 * depth * WIDE, 2 * depth * WIDE + 512 * depth),
    )(other, x_rows, proj_weight)


def mine_kernel(at_ref, x_ref, w_ref, add_ref, up_out, down_out, up_keep, down_keep, own_out, total):
    x = at_ref[1]
    rows = x_ref[...].reshape(256, WIDE)
    total[...] = (dot_nt(rows, w_ref[...]) + add_ref[...].astype(F32)).reshape(SIDE, 64, -1)
    far, after, before = turn(x, 2), turn(x, 1), turn(x, -1)
    up_out[0:32] = total[far, 0:32].astype(BF16)
    up_out[32:64] = total[after, 32:64].astype(BF16)
    up_keep[...] = total[after, 0:32].astype(BF16)
    down_out[0:32] = total[far, 32:64].astype(BF16)
    down_out[32:64] = total[before, 0:32].astype(BF16)
    down_keep[...] = total[before, 32:64].astype(BF16)
    own_out[...] = total[x]


def mine(at, x_rows, proj_weight, add):
    depth, tile = proj_weight.shape[0], 512
    out = lambda n: pl.BlockSpec((n, tile), lambda i, s: (0, i))
    return pl.pallas_call(
        mine_kernel,
        grid_spec=pltpu.PrefetchScalarGridSpec(
            num_scalar_prefetch=1,
            grid=(depth // tile,),
            in_specs=[
                pl.BlockSpec((SIDE, 1, 64, WIDE), lambda i, s: (0, s[0], 0, 0)),
                pl.BlockSpec((tile, WIDE), lambda i, s: (i, 0)),
                pl.BlockSpec((256, tile), lambda i, s: (0, i)),
            ],
            out_specs=[out(64), out(64), out(32), out(32), out(64)],
            scratch_shapes=[pltpu.VMEM((SIDE, 64, tile), F32)],
        ),
        out_shape=[
            jax.ShapeDtypeStruct((64, depth), BF16),
            jax.ShapeDtypeStruct((64, depth), BF16),
            jax.ShapeDtypeStruct((32, depth), BF16),
            jax.ShapeDtypeStruct((32, depth), BF16),
            jax.ShapeDtypeStruct((64, depth), F32),
        ],
        compiler_params=params(),
        cost_estimate=cost(2 * 256 * depth * WIDE, 2 * depth * WIDE + 1536 * depth),
    )(at, x_rows, proj_weight, add)


def input_kernel(own, below, above, below_add, above_add, out):
    top = own[0:32] + below_add[...].astype(F32) + above[32:64].astype(F32)
    bottom = own[32:64] + below[32:64].astype(F32) + above_add[...].astype(F32)
    out[0:32] = top.astype(BF16)
    out[32:64] = bottom.astype(BF16)


def input_grad_of(x_grad, proj_weight, x, core):
    x_rows = x_grad.reshape(SIDE, 2, 64, WIDE)
    sent = theirs((1 - core).reshape(1), x_rows, proj_weight)
    at = jnp.stack([core, x])
    up, down, up_keep, down_keep, own = mine(at, x_rows, proj_weight, hop_smp(sent, 0, 1))
    below, above = hop_smp(up, 1, 0), hop_smp(down, -1, 0)
    up, down = add_two(up_keep, down_keep, below, above)
    below_add, above_add = hop_smp(up, 1, 0), hop_smp(down, -1, 0)
    return pl.pallas_call(
        input_kernel,
        out_shape=jax.ShapeDtypeStruct((64, proj_weight.shape[0]), BF16),
        in_specs=[whole()] * 5,
        out_specs=whole(),
        compiler_params=params(),
        cost_estimate=cost(1_000_000, 3_000_000),
    )(own, below, above, below_add, above_add)


def body(
    layer_input,
    proj_weight,
    step_size,
    decay_log,
    skip_gain,
    write_vec,
    read_vec,
    out_grad,
    start_state,
    fork_grad,
):
    length = layer_input.shape[0]
    position = lax.axis_index("ctx")
    z, y = position // SIDE, position % SIDE
    column = lax.axis_index("smp")
    x, core = column // 2, column % 2
    y_at, z_at = y.reshape(1), z.reshape(1)
    writes = write_vec[:, 0]
    reads = read_vec[:, 0]
    rel, scaled, states, *messages = pre(
        y_at, step_size, decay_log[None], out_grad, reads, fork_grad.reshape(2, WIDE, 128)
    )
    first = [messages[0]] + [hop(messages[d], 0, d) for d in range(1, SIDE)]
    message = group(y_at, first)
    second = [message] + [hop(message, d, 0) for d in range(1, SIDE)]
    sent = carry_over(y_at, z_at, first, second)
    quarters = [sent[0]] + [hop(sent[d], 0, d) for d in range(1, SIDE)]
    relt = rel.transpose(0, 2, 1)
    skip_row = jnp.repeat(skip_gain, 64)[None]
    base = diag(rel, relt, step_size, skip_row, reads, writes, out_grad)
    inputs = project(layer_input, proj_weight)
    x_grad, full = x_final(y_at, quarters, states, rel, step_size, writes, base)
    scale = (length * lax.axis_size("ctx")) ** (-0.5)
    weight_grad = weight_grad_of(layer_input, x_grad, z, y, scale)
    input_grad = input_grad_of(x_grad, proj_weight, x, core)
    write_grad, read_grad = vectors(
        rel, relt, step_size, reads, writes, out_grad, scaled, inputs, full,
        start_state.reshape(WIDE, 128),
    )
    return (input_grad, weight_grad, write_grad[:, None], read_grad[:, None])


def solution(mesh):
    placed = (
        P("ctx", None),
        P(None, "smp"),
        P("ctx", "smp"),
        P("smp"),
        P("smp"),
        P("ctx", "smp", None),
        P("ctx", "smp", None),
        P("ctx", "smp"),
        P("ctx", "smp", None, None),
        P("ctx", "smp", None, None),
    )
    return jax.shard_map(
        body,
        mesh=mesh,
        in_specs=placed,
        out_specs=(
            P(("ctx", "smp"), None),
            P("ctx", "smp"),
            P("ctx", "smp", None),
            P("ctx", "smp", None),
        ),
        check_vma=False,
    )
```

time: 413 us -> 170 us (0.41)
  the two profiles are of different devices: /device:TPU:1 before, /device:TPU:0 now
where the time goes in v2:
time: 170 us; the launch traced here: 169 us
  Pallas kernels  70.3 us (41%)
  starting transfers between devices  52.3 us (31%)
  waiting for transfers between devices  23 us (14%)
  local copies, waits for them, and re-layouts  21.4 us (13%)
    ppermute x29, starting transfers between devices, hop(): return lax.ppermute(block, 'ctx', route)  45.7 us
    ppermute x29, waiting for transfers between devices, hop(): return lax.ppermute(block, 'ctx', route)  23 us
    unnamed x79, local copies, waits for them, and re-layouts  20.5 us
    pallas_call x6, Pallas kernels, pair_product(): pl.pallas_call(pair_kernel, grid_spec=pltpu.PrefetchScalarGridSpec(num_sc...  19.7 us
    pallas_call x2, Pallas kernels, own_product(): pl.pallas_call(own_kernel, grid_spec=pltpu.PrefetchScalarGridSpec(num_sca...  9.56 us
    pallas_call x1, Pallas kernels, mine(): pl.pallas_call(mine_kernel, grid_spec=pltpu.PrefetchScalarGridSpec(num_sc...  9.2 us
    pallas_call x1, Pallas kernels, theirs(): pl.pallas_call(theirs_kernel, grid_spec=pltpu.PrefetchScalarGridSpec(num_...  8.7 us
    pallas_call x1, Pallas kernels, project(): pl.pallas_call(project_kernel, grid=(wide // tile,), out_shape=jax.ShapeD...  7.25 us
  transfers between devices with their start and end apart: 34, of which 9 were waited for; matrix products, arithmetic and copies ran while one was open for 1% of the time, Pallas kernels for 33%

profile of v2, /device:TPU:0, one launch (start us, length us, event | category | flops | bytes accessed | tf_op | source)
XLA Modules:
  0.0 168.6 jit_solution(3073971790424596759)
XLA Ops:
  0.7 0.9 copy.14.step_ref
  1.6 1.2 copy-done.4
  2.8 1.2 copy-done.5
  4.0 0.9 copy-done.14
  5.6 2.0 %shard_map.129 = (f32[4,128,16]{2,1,0:T(8,128)S(1)}, bf16[512,1024]{1,0:T(8,128)(2,1)S(1)}, bf16[3,128,1024]{2,1,0:T(8,128)(2,1)S(1)}, bf16[272,256]{1,0:T(8,128...) custom-call(s32[1]{0:T(128)} %bitcast.2.y_ref, ...), custom_call_target="tpu_custom_call" | custom-call | flops 400000000 | bytes 5000000 | tf_op jit(solution)/shard_map/pallas_call | solution.py:141
  7.6 0.9 copy-done.8
  8.5 0.9 copy-done.30
  9.4 1.7 collective-permute-start
  11.1 2.9 %collective-permute-start.1 = (bf16[272,256]{1,0:T(8,128)(2,1)S(1)}, bf16[272,256]{1,0:T(8,128)(2,1)S(1)}, u32[]{:S(2)}, u32[]{:S(2)}) collective-permute-start(bf16[272,256]{1,0:T(8,128)(2,1)S(1)} %get-tuple-element.54), channel_id=1, source_target_pairs={{0,16},{8,24},{16,0},{24,8},{32,48},{40,56},{48,32},{56,40},{64,80... | collective-permute-start | bytes 417800 | tf_op jit(solution)/shard_map/ppermute | solution.py:40
  14.0 1.3 collective-permute-start.2
  15.3 0.9 collective-permute-done.a1
  16.2 4.2 %collective-permute-done.1.a2 = bf16[272,256]{1,0:T(8,128)(2,1)S(1)} collective-permute-done((bf16[272,256]{1,0:T(8,128)(2,1)S(1)}, bf16[272,256]{1,0:T(8,128)(2,1)S(1)}, u32[]{:S(2)}, u32[]{:S(2)}) %collective-permute-start.1) | collective-permute-done | bytes 139296 | tf_op jit(solution)/shard_map/ppermute | solution.py:40
  20.5 4.1 %collective-permute-start.5 = (bf16[272,256]{1,0:T(8,128)(2,1)S(1)}, bf16[272,256]{1,0:T(8,128)(2,1)S(1)}, u32[]{:S(2)}, u32[]{:S(2)}) collective-permute-start(bf16[272,256]{1,0:T(8,128)(2,1)S(1)} %shard_map.130.b0), channel_id=1, source_target_pairs={{0,96},{8,104},{16,112},{24,120},{32,0},{40,8},{48,16},{56,24},{64... | collective-permute-start | bytes 417800 | tf_op jit(solution)/shard_map/ppermute | solution.py:40
  24.6 1.3 collective-permute-start.3
  26.7 2.9 %collective-permute-done.5.b3 = bf16[272,256]{1,0:T(8,128)(2,1)S(1)} collective-permute-done((bf16[272,256]{1,0:T(8,128)(2,1)S(1)}, bf16[272,256]{1,0:T(8,128)(2,1)S(1)}, u32[]{:S(2)}, u32[]{:S(2)}) %collective-permute-start.5) | collective-permute-done | bytes 139296 | tf_op jit(solution)/shard_map/ppermute | solution.py:40
  29.6 2.3 %collective-permute-done.4.b2 = bf16[272,256]{1,0:T(8,128)(2,1)S(1)} collective-permute-done((bf16[272,256]{1,0:T(8,128)(2,1)S(1)}, bf16[272,256]{1,0:T(8,128)(2,1)S(1)}, u32[]{:S(2)}, u32[]{:S(2)}) %collective-permute-start.4) | collective-permute-done | bytes 139296 | tf_op jit(solution)/shard_map/ppermute | solution.py:40
  31.9 1.1 collective-permute-done.3.b1
  33.0 0.9 shard_map.131
  33.9 1.1 collective-permute-start.6
  35.1 2.7 %collective-permute-start.7 = (bf16[128,256]{1,0:T(8,128)(2,1)}, bf16[128,256]{1,0:T(8,128)(2,1)S(1)}, u32[]{:S(2)}, u32[]{:S(2)}) collective-permute-start(bf16[128,256]{1,0:T(8,128)(2,1)} %get-tuple-element.58), channel_id=1, source_target_pairs={{0,16},{8,24},{16,0},{24,8},{32,48},{40,56},{48,32},{56,40},{64,80... | collective-permute-start | bytes 196616 | tf_op jit(solution)/shard_map/ppermute | solution.py:40
  37.7 1.1 collective-permute-start.8
  38.9 1.2 copy-done.6
  40.1 0.9 copy-done.16
  41.8 3.0 %shard_map.132.base_ref = f32[512,1024]{1,0:T(8,128)S(1)} custom-call(f32[4,128,16]{2,1,0:T(8,128)S(1)} %get-tuple-element.61.rel_ref, f32[4,16,128]{2,1,0:T(8,128)S(1)} %bitcast.50, f32[512,16]{1,0:T(8,128)S(1)} %copy.14.step_ref, f32[1,1024]{1,0:T(1,128)S(1)} %broadcast_in_dim_reshape.3.skip_ref, bf16[512,128]{1,0:T(8,128)(2,1)S(1)} %bitcast.45, ...), custom_call_target="tpu_custom_call" | custom-call | flops 1500000000 | bytes 3500000 | tf_op jit(solution)/shard_map/pallas_call | solution.py:251
  46.7 0.9 copy-done.2
  47.7 1.1 copy-done.9
  48.8 0.9 copy-done.17
  49.7 0.8 copy-done.20
  53.1 1.7 %shard_map.133 = (bf16[512,1024]{1,0:T(8,128)(2,1)S(1)}, bf16[4,128,1024]{2,1,0:T(8,128)(2,1)S(1)}) custom-call(s32[1]{0:T(128)} %bitcast.2.y_ref, bf16[128,256]{1,0:T(8,128)(2,1)S(1)} %copy-done.20, bf16[128,256]{1,0:T(8,128)(2,1)S(1)} %copy-done.22, bf16[128,256]{1,0:T(8,128)(2,1)S(1)} %copy-done.24, bf16[128,256]{1,0:T(8,128)(2,1)S(1)} %copy-done.26, ...), custom_call_target="tpu_custom_call" | custom-call | flops 300000000 | bytes 5500000 | tf_op jit(solution)/shard_map/pallas_call | solution.py:296
  54.8 1.0 copy-done.32
  55.8 8.7 %shard_map.134 = bf16[256,4096]{1,0:T(8,128)(2,1)} custom-call(s32[1]{0:T(128)} %bitcast.10.c_ref, bf16[4,2,64,1024]{3,2,1,0:T(8,128)(2,1)S(1)} %bitcast.41, bf16[4096,1024]{1,0:T(8,128)(2,1)} %w_ref.5), custom_call_target="tpu_custom_call" | custom-call | flops 2147483648 | bytes 10485760 | tf_op jit(solution)/shard_map/pallas_call | solution.py:585
  64.6 3.1 %shard_map.143 = (bf16[2,256,512]{2,1,0:T(8,128)(2,1)}, bf16[2,256,512]{2,1,0:T(8,128)(2,1)S(1)}) custom-call(s32[4]{0:T(128)S(1)} %get-tuple-element.105.idx_ref, bf16[512,4096]{1,0:T(8,128)(2,1)} %x_ref.1, bf16[512,4096]{1,0:T(8,128)(2,1)} %x_ref.1, bf16[512,1024]{1,0:T(8,128)(2,1)S(1)} %get-tuple-element.62.x_ref), custom_call_target="tpu_custom_call" | custom-call | flops 536870912 | bytes 2621440 | tf_op jit(solution)/shard_map/pallas_call | solution.py:417
  67.7 0.8 copy-done.37
  68.6 3.2 %collective-permute-start.25 = (bf16[2,256,512]{2,1,0:T(8,128)(2,1)}, bf16[2,256,512]{2,1,0:T(8,128)(2,1)}, u32[]{:S(2)}, u32[]{:S(2)}) collective-permute-start(bf16[2,256,512]{2,1,0:T(8,128)(2,1)} %copy-done.37), channel_id=1, source_target_pairs={{0,96},{8,104},{16,112},{24,120},{32,0},{40,8},{48,16},{56,24},{64... | collective-permute-start | bytes 1572872 | tf_op jit(solution)/shard_map/ppermute | solution.py:40
  71.9 3.2 %shard_map.145 = (bf16[2,256,512]{2,1,0:T(8,128)(2,1)}, bf16[2,256,512]{2,1,0:T(8,128)(2,1)S(1)}) custom-call(s32[4]{0:T(128)S(1)} %pad_add_fusion.6.idx_ref, bf16[512,4096]{1,0:T(8,128)(2,1)} %x_ref.1, bf16[512,4096]{1,0:T(8,128)(2,1)} %x_ref.1, bf16[512,1024]{1,0:T(8,128)(2,1)S(1)} %get-tuple-element.62.x_ref), custom_call_target="tpu_custom_call" | custom-call | flops 536870912 | bytes 2621440 | tf_op jit(solution)/shard_map/pallas_call | solution.py:417
  75.0 3.3 %shard_map.138 = (bf16[2,256,512]{2,1,0:T(8,128)(2,1)}, bf16[2,256,512]{2,1,0:T(8,128)(2,1)}) custom-call(s32[4]{0:T(128)S(1)} %get-tuple-element.104.idx_ref, bf16[512,4096]{1,0:T(8,128)(2,1)} %x_ref.1, bf16[512,4096]{1,0:T(8,128)(2,1)} %x_ref.1, bf16[512,1024]{1,0:T(8,128)(2,1)S(1)} %get-tuple-element.62.x_ref), custom_call_target="tpu_custom_call" | custom-call | flops 536870912 | bytes 2621440 | tf_op jit(solution)/shard_map/pallas_call | solution.py:417
  78.3 0.9 collective-permute-start.14
  79.2 5.6 %collective-permute-done.24.refs_0_ = bf16[2,256,512]{2,1,0:T(8,128)(2,1)} collective-permute-done((bf16[2,256,512]{2,1,0:T(8,128)(2,1)}, bf16[2,256,512]{2,1,0:T(8,128)(2,1)}, u32[]{:S(2)}, u32[]{:S(2)}) %collective-permute-start.24) | collective-permute-done | bytes 524320 | tf_op jit(solution)/shard_map/ppermute | solution.py:40
  85.2 2.3 %collective-permute-start.28 = (bf16[2,256,512]{2,1,0:T(8,128)(2,1)}, bf16[2,256,512]{2,1,0:T(8,128)(2,1)}, u32[]{:S(2)}, u32[]{:S(2)}) collective-permute-start(bf16[2,256,512]{2,1,0:T(8,128)(2,1)} %copy-done.36), channel_id=1, source_target_pairs={{0,96},{8,104},{16,112},{24,120},{32,0},{40,8},{48,16},{56,24},{64... | collective-permute-start | bytes 1572872 | tf_op jit(solution)/shard_map/ppermute | solution.py:40
  87.4 3.5 %shard_map.144 = (bf16[2,256,512]{2,1,0:T(8,128)(2,1)}, bf16[2,256,512]{2,1,0:T(8,128)(2,1)}) custom-call(s32[4]{0:T(128)S(1)} %pad_add_fusion.4.idx_ref, bf16[512,4096]{1,0:T(8,128)(2,1)} %x_ref.1, bf16[512,4096]{1,0:T(8,128)(2,1)} %x_ref.1, bf16[512,1024]{1,0:T(8,128)(2,1)S(1)} %get-tuple-element.62.x_ref, ...), custom_call_target="tpu_custom_call" | custom-call | flops 536870912 | bytes 2621440 | tf_op jit(solution)/shard_map/pallas_call | solution.py:417
  90.9 4.7 %collective-permute-done.27.below_plain = bf16[2,256,512]{2,1,0:T(8,128)(2,1)} collective-permute-done((bf16[2,256,512]{2,1,0:T(8,128)(2,1)}, bf16[2,256,512]{2,1,0:T(8,128)(2,1)}, u32[]{:S(2)}, u32[]{:S(2)}) %collective-permute-start.27) | collective-permute-done | bytes 524320 | tf_op jit(solution)/shard_map/ppermute | solution.py:40
  95.7 3.2 %collective-permute-start.29 = (bf16[2,256,512]{2,1,0:T(8,128)(2,1)}, bf16[2,256,512]{2,1,0:T(8,128)(2,1)}, u32[]{:S(2)}, u32[]{:S(2)}) collective-permute-start(bf16[2,256,512]{2,1,0:T(8,128)(2,1)} %get-tuple-element.88), channel_id=1, source_target_pairs={{0,96},{8,104},{16,112},{24,120},{32,0},{40,8},{48,16},{56,24},{64... | collective-permute-start | bytes 1572872 | tf_op jit(solution)/shard_map/ppermute | solution.py:40
  99.0 3.3 %shard_map.140 = (bf16[2,256,512]{2,1,0:T(8,128)(2,1)}, bf16[2,256,512]{2,1,0:T(8,128)(2,1)}) custom-call(s32[4]{0:T(128)S(1)} %pad_add_fusion.3.idx_ref, bf16[512,4096]{1,0:T(8,128)(2,1)} %x_ref.1, bf16[512,4096]{1,0:T(8,128)(2,1)} %x_ref.1, bf16[512,1024]{1,0:T(8,128)(2,1)S(1)} %get-tuple-element.62.x_ref), custom_call_target="tpu_custom_call" | custom-call | flops 536870912 | bytes 2621440 | tf_op jit(solution)/shard_map/pallas_call | solution.py:417
  102.3 0.9 collective-permute-start.17
  103.2 3.3 %shard_map.139 = (bf16[2,256,512]{2,1,0:T(8,128)(2,1)}, bf16[2,256,512]{2,1,0:T(8,128)(2,1)S(1)}) custom-call(s32[4]{0:T(128)S(1)} %pad_add_fusion.1.idx_ref, bf16[512,4096]{1,0:T(8,128)(2,1)} %x_ref.1, bf16[512,4096]{1,0:T(8,128)(2,1)} %x_ref.1, bf16[512,1024]{1,0:T(8,128)(2,1)S(1)} %get-tuple-element.62.x_ref, ...), custom_call_target="tpu_custom_call" | custom-call | flops 536870912 | bytes 2621440 | tf_op jit(solution)/shard_map/pallas_call | solution.py:417
  107.3 2.3 %collective-permute-start.18 = (bf16[2,256,512]{2,1,0:T(8,128)(2,1)}, bf16[2,256,512]{2,1,0:T(8,128)(2,1)}, u32[]{:S(2)}, u32[]{:S(2)}) collective-permute-start(bf16[2,256,512]{2,1,0:T(8,128)(2,1)} %get-tuple-element.74), channel_id=1, source_target_pairs={{0,24},{8,0},{16,8},{24,16},{32,56},{40,32},{48,40},{56,48},{64,88... | collective-permute-start | bytes 1572872 | tf_op jit(solution)/shard_map/ppermute | solution.py:40
  109.7 1.0 collective-permute-done.26.below_add
  110.7 0.9 collective-permute-start.16
  111.6 2.3 %collective-permute-start.19 = (bf16[2,256,512]{2,1,0:T(8,128)(2,1)}, bf16[2,256,512]{2,1,0:T(8,128)(2,1)}, u32[]{:S(2)}, u32[]{:S(2)}) collective-permute-start(bf16[2,256,512]{2,1,0:T(8,128)(2,1)} %copy-done.35), channel_id=1, source_target_pairs={{0,24},{8,0},{16,8},{24,16},{32,56},{40,32},{48,40},{56,48},{64,88... | collective-permute-start | bytes 1572872 | tf_op jit(solution)/shard_map/ppermute | solution.py:40
  114.1 4.2 %shard_map.146 = (bf16[256,512]{1,0:T(8,128)(2,1)S(1)}, bf16[256,512]{1,0:T(8,128)(2,1)S(1)}, bf16[128,512]{1,0:T(8,128)(2,1)S(1)}, bf16[128,512]{1,0:T(8,128)(2,1)S(1)}, f32[256,512]{1,0:T(8,128)S(1)}) custom-call(s32[4]{0:T(128)S(1)} %add_add_fusion.1.idx_ref, bf16[512,4096]{1,0:T(8,128)(2,1)} %x_ref.1, bf16[512,1024]{1,0:T(8,128)(2,1)S(1)} %get-tuple-element.62.x_ref, ...), custom_call_target="tpu_custom_call" | custom-call | flops 536870912 | bytes 4718592 | tf_op jit(solution)/shard_map/pallas_call | solution.py:471
  118.7 3.2 %collective-permute-start.31 = (bf16[256,512]{1,0:T(8,128)(2,1)S(1)}, bf16[256,512]{1,0:T(8,128)(2,1)S(1)}, u32[]{:S(2)}, u32[]{:S(2)}) collective-permute-start(bf16[256,512]{1,0:T(8,128)(2,1)S(1)} %get-tuple-element.91), channel_id=1, source_target_pairs={{0,24},{8,0},{16,8},{24,16},{32,56},{40,32},{48,40},{56,48},{64,88... | collective-permute-start | bytes 786440 | tf_op jit(solution)/shard_map/ppermute | solution.py:40
  121.9 9.2 %shard_map.135 = (bf16[64,4096]{1,0:T(8,128)(2,1)}, bf16[64,4096]{1,0:T(8,128)(2,1)}, bf16[32,4096]{1,0:T(8,128)(2,1)S(1)}, bf16[32,4096]{1,0:T(8,128)(2,1)S(1)}, f32[64,4096]{1,0:T(8,128)S(1)}) custom-call(s32[2]{0:T(128)S(1)} %pad_add_fusion.at_ref, bf16[4,2,64,1024]{3,2,1,0:T(8,128)(2,1)S(1)} %bitcast.42, bf16[4096,1024]{1,0:T(8,128)(2,1)} %w_ref.5, ...), custom_call_target="tpu_custom_call" | custom-call | flops 2147483648 | bytes 14680064 | tf_op jit(solution)/shard_map/pallas_call | solution.py:619
  131.1 1.6 collective-permute-start.10
  132.7 1.7 %collective-permute-start.11 = (bf16[64,4096]{1,0:T(8,128)(2,1)}, bf16[64,4096]{1,0:T(8,128)(2,1)S(1)}, u32[]{:S(2)}, u32[]{:S(2)}) collective-permute-start(bf16[64,4096]{1,0:T(8,128)(2,1)} %get-tuple-element.65), channel_id=1, source_target_pairs={{0,6},{1,7},{2,0},{3,1},{4,2},{5,3},{6,4},{7,5},{8,14},{9,15},{10,... | collective-permute-start | bytes 1572872 | tf_op jit(solution)/shard_map/ppermute | solution.py:48
  134.5 5.3 %shard_map.141 = (bf16[256,512]{1,0:T(8,128)(2,1)}, bf16[256,512]{1,0:T(8,128)(2,1)}, bf16[128,512]{1,0:T(8,128)(2,1)S(1)}, bf16[128,512]{1,0:T(8,128)(2,1)S(1)}, f32[256,512]{1,0:T(8,128)S(1)}) custom-call(s32[4]{0:T(128)S(1)} %add_add_fusion.idx_ref, bf16[512,4096]{1,0:T(8,128)(2,1)} %x_ref.1, bf16[512,1024]{1,0:T(8,128)(2,1)S(1)} %get-tuple-element.62.x_ref, ...), custom_call_target="tpu_custom_call" | custom-call | flops 536870912 | bytes 4718592 | tf_op jit(solution)/shard_map/pallas_call | solution.py:471
  139.8 3.2 %collective-permute-start.21 = (bf16[256,512]{1,0:T(8,128)(2,1)}, bf16[256,512]{1,0:T(8,128)(2,1)S(1)}, u32[]{:S(2)}, u32[]{:S(2)}) collective-permute-start(bf16[256,512]{1,0:T(8,128)(2,1)} %get-tuple-element.78), channel_id=1, source_target_pairs={{0,96},{8,104},{16,112},{24,120},{32,0},{40,8},{48,16},{56,24},{64... | collective-permute-start | bytes 786440 | tf_op jit(solution)/shard_map/ppermute | solution.py:40
  143.2 7.2 %shard_map.149.inputs_ref = bf16[512,1024]{1,0:T(8,128)(2,1)S(1)} custom-call(bf16[512,4096]{1,0:T(8,128)(2,1)S(1)} %copy-done, bf16[4096,1024]{1,0:T(8,128)(2,1)} %w_ref.5), custom_call_target="tpu_custom_call" | custom-call | flops 4294967296 | bytes 13631488 | tf_op jit(solution)/shard_map/pallas_call | solution.py:389
  150.6 3.3 %collective-permute-start.33 = (bf16[128,512]{1,0:T(8,128)(2,1)S(1)}, bf16[128,512]{1,0:T(8,128)(2,1)S(1)}, u32[]{:S(2)}, u32[]{:S(2)}) collective-permute-start(bf16[128,512]{1,0:T(8,128)(2,1)S(1)} %get-tuple-element.95), channel_id=1, source_target_pairs={{0,24},{8,0},{16,8},{24,16},{32,56},{40,32},{48,40},{56,48},{64,88... | collective-permute-start | bytes 393224 | tf_op jit(solution)/shard_map/ppermute | solution.py:40
  154.0 3.2 %collective-permute-start.23 = (bf16[128,512]{1,0:T(8,128)(2,1)S(1)}, bf16[128,512]{1,0:T(8,128)(2,1)S(1)}, u32[]{:S(2)}, u32[]{:S(2)}) collective-permute-start(bf16[128,512]{1,0:T(8,128)(2,1)S(1)} %get-tuple-element.82), channel_id=1, source_target_pairs={{0,96},{8,104},{16,112},{24,120},{32,0},{40,8},{48,16},{56,24},{64... | collective-permute-start | bytes 393224 | tf_op jit(solution)/shard_map/ppermute | solution.py:40
  157.3 0.9 collective-permute-start.12
  158.2 2.4 %collective-permute-start.13 = (bf16[32,4096]{1,0:T(8,128)(2,1)S(1)}, bf16[32,4096]{1,0:T(8,128)(2,1)S(1)}, u32[]{:S(2)}, u32[]{:S(2)}) collective-permute-start(bf16[32,4096]{1,0:T(8,128)(2,1)S(1)} %get-tuple-element.69), channel_id=1, source_target_pairs={{0,6},{1,7},{2,0},{3,1},{4,2},{5,3},{6,4},{7,5},{8,14},{9,15},{10,... | collective-permute-start | bytes 786440 | tf_op jit(solution)/shard_map/ppermute | solution.py:48
  160.7 5.9 %shard_map.150 = (f32[512,128]{1,0:T(8,128)}, f32[512,128]{1,0:T(8,128)}) custom-call(f32[4,128,16]{2,1,0:T(8,128)S(1)} %copy-done.3, f32[4,16,128]{2,1,0:T(8,128)S(1)} %bitcast.51, f32[512,16]{1,0:T(8,128)S(1)} %copy.14.step_ref, bf16[512,128]{1,0:T(8,128)(2,1)S(1)} %bitcast.46, bf16[512,128]{1,0:T(8,128)(2,1)S(1)} %bitcast.49, ...), custom_call_target="tpu_custom_call" | custom-call | flops 3000000000 | bytes 5000000 | tf_op jit(solution)/shard_map/pallas_call | solution.py:358
  166.7 1.0 shard_map.148
  167.7 0.9 shard_map.137
  (116 shorter events, 9.4 us)
Async XLA Ops:
  0.6 25.2 %copy-start.38 = (f32[16]{0:T(128)S(1)}, f32[16]{0:T(128)}, u32[]{:S(2)}) copy-start(f32[16]{0:T(128)} %param.14) | copy-start | bytes 196
  1.6 1.2 copy-start.4
  2.8 1.2 copy-start.5
  4.0 0.9 copy-start.14
  5.6 33.3 %copy-start.15 = (bf16[512,1,128]{2,0,1:T(8,128)(2,1)S(1)}, bf16[512,1,128]{2,0,1:T(8,128)(2,1)}, u32[]{:S(2)}) copy-start(bf16[512,1,128]{2,0,1:T(8,128)(2,1)} %param.16) | copy-start | bytes 393220
  7.6 0.9 copy-start.8
  8.4 0.9 copy-start.30
  9.4 35.4 %copy-start.1 = (f32[4,128,16]{2,1,0:T(8,128)}, f32[4,128,16]{2,1,0:T(8,128)S(1)}, u32[]{:S(2)}) copy-start(f32[4,128,16]{2,1,0:T(8,128)S(1)} %get-tuple-element.61.rel_ref) | copy-start | bytes 98308
  9.4 6.8 %collective-permute-start = (bf16[272,256]{1,0:T(8,128)(2,1)S(1)}, bf16[272,256]{1,0:T(8,128)(2,1)S(1)}, u32[]{:S(2)}, u32[]{:S(2)}) collective-permute-start(bf16[272,256]{1,0:T(8,128)(2,1)S(1)} %get-tuple-element.53), channel_id=1, source_target_pairs={{0,8},{8,16},{16,24},{24,0},{32,40},{40,48},{48,56},{56,32},{64,72... | collective-permute-start | bytes 417800 | tf_op jit(solution)/shard_map/ppermute | solution.py:40
  11.1 9.3 %collective-permute-start.1 = (bf16[272,256]{1,0:T(8,128)(2,1)S(1)}, bf16[272,256]{1,0:T(8,128)(2,1)S(1)}, u32[]{:S(2)}, u32[]{:S(2)}) collective-permute-start(bf16[272,256]{1,0:T(8,128)(2,1)S(1)} %get-tuple-element.54), channel_id=1, source_target_pairs={{0,16},{8,24},{16,0},{24,8},{32,48},{40,56},{48,32},{56,40},{64,80... | collective-permute-start | bytes 417800 | tf_op jit(solution)/shard_map/ppermute | solution.py:40
  14.0 6.4 %collective-permute-start.2 = (bf16[272,256]{1,0:T(8,128)(2,1)S(1)}, bf16[272,256]{1,0:T(8,128)(2,1)S(1)}, u32[]{:S(2)}, u32[]{:S(2)}) collective-permute-start(bf16[272,256]{1,0:T(8,128)(2,1)S(1)} %get-tuple-element.55), channel_id=1, source_target_pairs={{0,24},{8,0},{16,8},{24,16},{32,56},{40,32},{48,40},{56,48},{64,88... | collective-permute-start | bytes 417800 | tf_op jit(solution)/shard_map/ppermute | solution.py:40
  20.5 9.1 %collective-permute-start.5 = (bf16[272,256]{1,0:T(8,128)(2,1)S(1)}, bf16[272,256]{1,0:T(8,128)(2,1)S(1)}, u32[]{:S(2)}, u32[]{:S(2)}) collective-permute-start(bf16[272,256]{1,0:T(8,128)(2,1)S(1)} %shard_map.130.b0), channel_id=1, source_target_pairs={{0,96},{8,104},{16,112},{24,120},{32,0},{40,8},{48,16},{56,24},{64... | collective-permute-start | bytes 417800 | tf_op jit(solution)/shard_map/ppermute | solution.py:40
  24.6 7.3 %collective-permute-start.4 = (bf16[272,256]{1,0:T(8,128)(2,1)S(1)}, bf16[272,256]{1,0:T(8,128)(2,1)S(1)}, u32[]{:S(2)}, u32[]{:S(2)}) collective-permute-start(bf16[272,256]{1,0:T(8,128)(2,1)S(1)} %shard_map.130.b0), channel_id=1, source_target_pairs={{0,64},{8,72},{16,80},{24,88},{32,96},{40,104},{48,112},{56,120},{... | collective-permute-start | bytes 417800 | tf_op jit(solution)/shard_map/ppermute | solution.py:40
  24.6 8.4 %collective-permute-start.3 = (bf16[272,256]{1,0:T(8,128)(2,1)S(1)}, bf16[272,256]{1,0:T(8,128)(2,1)S(1)}, u32[]{:S(2)}, u32[]{:S(2)}) collective-permute-start(bf16[272,256]{1,0:T(8,128)(2,1)S(1)} %shard_map.130.b0), channel_id=1, source_target_pairs={{0,32},{8,40},{16,48},{24,56},{32,64},{40,72},{48,80},{56,88},{64,... | collective-permute-start | bytes 417800 | tf_op jit(solution)/shard_map/ppermute | solution.py:40
  33.9 10.8 %copy-start.19 = (bf16[128,256]{1,0:T(8,128)(2,1)}, bf16[128,256]{1,0:T(8,128)(2,1)S(1)}, u32[]{:S(2)}) copy-start(bf16[128,256]{1,0:T(8,128)(2,1)S(1)} %get-tuple-element.56.q0) | copy-start | bytes 196612
  33.9 10.9 %collective-permute-start.6 = (bf16[128,256]{1,0:T(8,128)(2,1)}, bf16[128,256]{1,0:T(8,128)(2,1)S(1)}, u32[]{:S(2)}, u32[]{:S(2)}) collective-permute-start(bf16[128,256]{1,0:T(8,128)(2,1)} %get-tuple-element.57), channel_id=1, source_target_pairs={{0,8},{8,16},{16,24},{24,0},{32,40},{40,48},{48,56},{56,32},{64,72... | collective-permute-start | bytes 196616 | tf_op jit(solution)/shard_map/ppermute | solution.py:40
  35.1 10.4 %collective-permute-start.7 = (bf16[128,256]{1,0:T(8,128)(2,1)}, bf16[128,256]{1,0:T(8,128)(2,1)S(1)}, u32[]{:S(2)}, u32[]{:S(2)}) collective-permute-start(bf16[128,256]{1,0:T(8,128)(2,1)} %get-tuple-element.58), channel_id=1, source_target_pairs={{0,16},{8,24},{16,0},{24,8},{32,48},{40,56},{48,32},{56,40},{64,80... | collective-permute-start | bytes 196616 | tf_op jit(solution)/shard_map/ppermute | solution.py:40
  37.7 8.3 %collective-permute-start.8 = (bf16[128,256]{1,0:T(8,128)(2,1)}, bf16[128,256]{1,0:T(8,128)(2,1)S(1)}, u32[]{:S(2)}, u32[]{:S(2)}) collective-permute-start(bf16[128,256]{1,0:T(8,128)(2,1)} %get-tuple-element.59), channel_id=1, source_target_pairs={{0,24},{8,0},{16,8},{24,16},{32,56},{40,32},{48,40},{56,48},{64,88... | collective-permute-start | bytes 196616 | tf_op jit(solution)/shard_map/ppermute | solution.py:40
  38.9 1.2 copy-start.6
  40.1 0.9 copy-start.16
  46.7 0.9 copy-start.2
  47.7 1.1 copy-start.9
  48.8 0.9 copy-start.17
  49.7 0.8 copy-start.20
  54.8 1.0 copy-start.32
  64.5 54.2 %collective-permute-start.9 = (bf16[256,4096]{1,0:T(8,128)(2,1)}, bf16[256,4096]{1,0:T(8,128)(2,1)S(1)}, u32[]{:S(2)}, u32[]{:S(2)}) collective-permute-start(bf16[256,4096]{1,0:T(8,128)(2,1)} %shard_map.134), channel_id=1, source_target_pairs={{0,1},{1,0},{2,3},{3,2},{4,5},{5,4},{6,7},{7,6},{8,9},{9,8},{10,11... | collective-permute-start | bytes 6291464 | tf_op jit(solution)/shard_map/ppermute | solution.py:48
  67.7 0.9 copy-start.37
  68.6 16.2 %collective-permute-start.24 = (bf16[2,256,512]{2,1,0:T(8,128)(2,1)}, bf16[2,256,512]{2,1,0:T(8,128)(2,1)}, u32[]{:S(2)}, u32[]{:S(2)}) collective-permute-start(bf16[2,256,512]{2,1,0:T(8,128)(2,1)} %get-tuple-element.83), channel_id=1, source_target_pairs={{0,32},{8,40},{16,48},{24,56},{32,64},{40,72},{48,80},{56,88},{64,... | collective-permute-start | bytes 1572872 | tf_op jit(solution)/shard_map/ppermute | solution.py:40
  68.6 16.5 %collective-permute-start.25 = (bf16[2,256,512]{2,1,0:T(8,128)(2,1)}, bf16[2,256,512]{2,1,0:T(8,128)(2,1)}, u32[]{:S(2)}, u32[]{:S(2)}) collective-permute-start(bf16[2,256,512]{2,1,0:T(8,128)(2,1)} %copy-done.37), channel_id=1, source_target_pairs={{0,96},{8,104},{16,112},{24,120},{32,0},{40,8},{48,16},{56,24},{64... | collective-permute-start | bytes 1572872 | tf_op jit(solution)/shard_map/ppermute | solution.py:40
  75.0 3.3 %copy-start.36 = (bf16[2,256,512]{2,1,0:T(8,128)(2,1)}, bf16[2,256,512]{2,1,0:T(8,128)(2,1)S(1)}, u32[]{:S(2)}) copy-start(bf16[2,256,512]{2,1,0:T(8,128)(2,1)S(1)} %get-tuple-element.87) | copy-start | bytes 1572868
  75.0 20.6 %collective-permute-start.27 = (bf16[2,256,512]{2,1,0:T(8,128)(2,1)}, bf16[2,256,512]{2,1,0:T(8,128)(2,1)}, u32[]{:S(2)}, u32[]{:S(2)}) collective-permute-start(bf16[2,256,512]{2,1,0:T(8,128)(2,1)} %get-tuple-element.86), channel_id=1, source_target_pairs={{0,32},{8,40},{16,48},{24,56},{32,64},{40,72},{48,80},{56,88},{64,... | collective-permute-start | bytes 1572872 | tf_op jit(solution)/shard_map/ppermute | solution.py:40
  78.3 17.3 %collective-permute-start.14 = (bf16[2,256,512]{2,1,0:T(8,128)(2,1)}, bf16[2,256,512]{2,1,0:T(8,128)(2,1)}, u32[]{:S(2)}, u32[]{:S(2)}) collective-permute-start(bf16[2,256,512]{2,1,0:T(8,128)(2,1)} %get-tuple-element.70), channel_id=1, source_target_pairs={{0,8},{8,16},{16,24},{24,0},{32,40},{40,48},{48,56},{56,32},{64,72... | collective-permute-start | bytes 1572872 | tf_op jit(solution)/shard_map/ppermute | solution.py:40
  84.8 17.5 %collective-permute-start.15 = (bf16[2,256,512]{2,1,0:T(8,128)(2,1)}, bf16[2,256,512]{2,1,0:T(8,128)(2,1)}, u32[]{:S(2)}, u32[]{:S(2)}) collective-permute-start(bf16[2,256,512]{2,1,0:T(8,128)(2,1)} %get-tuple-element.71), channel_id=1, source_target_pairs={{0,24},{8,0},{16,8},{24,16},{32,56},{40,32},{48,40},{56,48},{64,88... | collective-permute-start | bytes 1572872 | tf_op jit(solution)/shard_map/ppermute | solution.py:40
  85.2 22.2 %collective-permute-start.28 = (bf16[2,256,512]{2,1,0:T(8,128)(2,1)}, bf16[2,256,512]{2,1,0:T(8,128)(2,1)}, u32[]{:S(2)}, u32[]{:S(2)}) collective-permute-start(bf16[2,256,512]{2,1,0:T(8,128)(2,1)} %copy-done.36), channel_id=1, source_target_pairs={{0,96},{8,104},{16,112},{24,120},{32,0},{40,8},{48,16},{56,24},{64... | collective-permute-start | bytes 1572872 | tf_op jit(solution)/shard_map/ppermute | solution.py:40
  95.6 15.1 %collective-permute-start.26 = (bf16[2,256,512]{2,1,0:T(8,128)(2,1)}, bf16[2,256,512]{2,1,0:T(8,128)(2,1)}, u32[]{:S(2)}, u32[]{:S(2)}) collective-permute-start(bf16[2,256,512]{2,1,0:T(8,128)(2,1)} %get-tuple-element.85), channel_id=1, source_target_pairs={{0,32},{8,40},{16,48},{24,56},{32,64},{40,72},{48,80},{56,88},{64,... | collective-permute-start | bytes 1572872 | tf_op jit(solution)/shard_map/ppermute | solution.py:40
  95.7 16.0 %collective-permute-start.29 = (bf16[2,256,512]{2,1,0:T(8,128)(2,1)}, bf16[2,256,512]{2,1,0:T(8,128)(2,1)}, u32[]{:S(2)}, u32[]{:S(2)}) collective-permute-start(bf16[2,256,512]{2,1,0:T(8,128)(2,1)} %get-tuple-element.88), channel_id=1, source_target_pairs={{0,96},{8,104},{16,112},{24,120},{32,0},{40,8},{48,16},{56,24},{64... | collective-permute-start | bytes 1572872 | tf_op jit(solution)/shard_map/ppermute | solution.py:40
  102.3 16.4 %collective-permute-start.17 = (bf16[2,256,512]{2,1,0:T(8,128)(2,1)}, bf16[2,256,512]{2,1,0:T(8,128)(2,1)}, u32[]{:S(2)}, u32[]{:S(2)}) collective-permute-start(bf16[2,256,512]{2,1,0:T(8,128)(2,1)} %get-tuple-element.73), channel_id=1, source_target_pairs={{0,8},{8,16},{16,24},{24,0},{32,40},{40,48},{48,56},{56,32},{64,72... | collective-permute-start | bytes 1572872 | tf_op jit(solution)/shard_map/ppermute | solution.py:40
  107.3 23.8 %collective-permute-start.18 = (bf16[2,256,512]{2,1,0:T(8,128)(2,1)}, bf16[2,256,512]{2,1,0:T(8,128)(2,1)}, u32[]{:S(2)}, u32[]{:S(2)}) collective-permute-start(bf16[2,256,512]{2,1,0:T(8,128)(2,1)} %get-tuple-element.74), channel_id=1, source_target_pairs={{0,24},{8,0},{16,8},{24,16},{32,56},{40,32},{48,40},{56,48},{64,88... | collective-permute-start | bytes 1572872 | tf_op jit(solution)/shard_map/ppermute | solution.py:40
  110.7 21.9 %collective-permute-start.16 = (bf16[2,256,512]{2,1,0:T(8,128)(2,1)}, bf16[2,256,512]{2,1,0:T(8,128)(2,1)}, u32[]{:S(2)}, u32[]{:S(2)}) collective-permute-start(bf16[2,256,512]{2,1,0:T(8,128)(2,1)} %get-tuple-element.72), channel_id=1, source_target_pairs={{0,8},{8,16},{16,24},{24,0},{32,40},{40,48},{48,56},{56,32},{64,72... | collective-permute-start | bytes 1572872 | tf_op jit(solution)/shard_map/ppermute | solution.py:40
  111.6 22.9 %collective-permute-start.19 = (bf16[2,256,512]{2,1,0:T(8,128)(2,1)}, bf16[2,256,512]{2,1,0:T(8,128)(2,1)}, u32[]{:S(2)}, u32[]{:S(2)}) collective-permute-start(bf16[2,256,512]{2,1,0:T(8,128)(2,1)} %copy-done.35), channel_id=1, source_target_pairs={{0,24},{8,0},{16,8},{24,16},{32,56},{40,32},{48,40},{56,48},{64,88... | collective-permute-start | bytes 1572872 | tf_op jit(solution)/shard_map/ppermute | solution.py:40
  118.4 12.7 %copy-start.10 = (f32[256,512]{1,0:T(8,128)}, f32[256,512]{1,0:T(8,128)S(1)}, u32[]{:S(2)}) copy-start(f32[256,512]{1,0:T(8,128)S(1)} %get-tuple-element.89.refs_5_) | copy-start | bytes 1572868
  118.6 21.2 %collective-permute-start.30 = (bf16[256,512]{1,0:T(8,128)(2,1)S(1)}, bf16[256,512]{1,0:T(8,128)(2,1)S(1)}, u32[]{:S(2)}, u32[]{:S(2)}) collective-permute-start(bf16[256,512]{1,0:T(8,128)(2,1)S(1)} %get-tuple-element.90), channel_id=1, source_target_pairs={{0,8},{8,16},{16,24},{24,0},{32,40},{40,48},{48,56},{56,32},{64,72... | collective-permute-start | bytes 786440 | tf_op jit(solution)/shard_map/ppermute | solution.py:40
  118.7 24.4 %collective-permute-start.31 = (bf16[256,512]{1,0:T(8,128)(2,1)S(1)}, bf16[256,512]{1,0:T(8,128)(2,1)S(1)}, u32[]{:S(2)}, u32[]{:S(2)}) collective-permute-start(bf16[256,512]{1,0:T(8,128)(2,1)S(1)} %get-tuple-element.91), channel_id=1, source_target_pairs={{0,24},{8,0},{16,8},{24,16},{32,56},{40,32},{48,40},{56,48},{64,88... | collective-permute-start | bytes 786440 | tf_op jit(solution)/shard_map/ppermute | solution.py:40
  131.1 8.7 %copy-start.12 = (bf16[32,4096]{1,0:T(8,128)(2,1)}, bf16[32,4096]{1,0:T(8,128)(2,1)S(1)}, u32[]{:S(2)}) copy-start(bf16[32,4096]{1,0:T(8,128)(2,1)S(1)} %get-tuple-element.67.down_keep) | copy-start | bytes 786436
  131.1 22.9 %collective-permute-start.10 = (bf16[64,4096]{1,0:T(8,128)(2,1)}, bf16[64,4096]{1,0:T(8,128)(2,1)S(1)}, u32[]{:S(2)}, u32[]{:S(2)}) collective-permute-start(bf16[64,4096]{1,0:T(8,128)(2,1)} %get-tuple-element.64), channel_id=1, source_target_pairs={{0,2},{1,3},{2,4},{3,5},{4,6},{5,7},{6,0},{7,1},{8,10},{9,11},{10,... | collective-permute-start | bytes 1572872 | tf_op jit(solution)/shard_map/ppermute | solution.py:48
  132.7 24.6 %collective-permute-start.11 = (bf16[64,4096]{1,0:T(8,128)(2,1)}, bf16[64,4096]{1,0:T(8,128)(2,1)S(1)}, u32[]{:S(2)}, u32[]{:S(2)}) collective-permute-start(bf16[64,4096]{1,0:T(8,128)(2,1)} %get-tuple-element.65), channel_id=1, source_target_pairs={{0,6},{1,7},{2,0},{3,1},{4,2},{5,3},{6,4},{7,5},{8,14},{9,15},{10,... | collective-permute-start | bytes 1572872 | tf_op jit(solution)/shard_map/ppermute | solution.py:48
  134.5 8.7 %copy-start = (bf16[512,4096]{1,0:T(8,128)(2,1)S(1)}, bf16[512,4096]{1,0:T(8,128)(2,1)}, u32[]{:S(2)}) copy-start(bf16[512,4096]{1,0:T(8,128)(2,1)} %x_ref.1) | copy-start | bytes 12582916
  139.8 10.8 %collective-permute-start.20 = (bf16[256,512]{1,0:T(8,128)(2,1)}, bf16[256,512]{1,0:T(8,128)(2,1)S(1)}, u32[]{:S(2)}, u32[]{:S(2)}) collective-permute-start(bf16[256,512]{1,0:T(8,128)(2,1)} %get-tuple-element.77), channel_id=1, source_target_pairs={{0,32},{8,40},{16,48},{24,56},{32,64},{40,72},{48,80},{56,88},{64,... | collective-permute-start | bytes 786440 | tf_op jit(solution)/shard_map/ppermute | solution.py:40
  139.8 14.0 %collective-permute-start.21 = (bf16[256,512]{1,0:T(8,128)(2,1)}, bf16[256,512]{1,0:T(8,128)(2,1)S(1)}, u32[]{:S(2)}, u32[]{:S(2)}) collective-permute-start(bf16[256,512]{1,0:T(8,128)(2,1)} %get-tuple-element.78), channel_id=1, source_target_pairs={{0,96},{8,104},{16,112},{24,120},{32,0},{40,8},{48,16},{56,24},{64... | collective-permute-start | bytes 786440 | tf_op jit(solution)/shard_map/ppermute | solution.py:40
  143.1 14.1 %copy-start.13 = (bf16[32,4096]{1,0:T(8,128)(2,1)S(1)}, bf16[32,4096]{1,0:T(8,128)(2,1)}, u32[]{:S(2)}) copy-start(bf16[32,4096]{1,0:T(8,128)(2,1)} %copy-done.12) | copy-start | bytes 786436
  143.1 15.1 %collective-permute-start.32 = (bf16[128,512]{1,0:T(8,128)(2,1)S(1)}, bf16[128,512]{1,0:T(8,128)(2,1)S(1)}, u32[]{:S(2)}, u32[]{:S(2)}) collective-permute-start(bf16[128,512]{1,0:T(8,128)(2,1)S(1)} %get-tuple-element.94), channel_id=1, source_target_pairs={{0,8},{8,16},{16,24},{24,0},{32,40},{40,48},{48,56},{56,32},{64,72... | collective-permute-start | bytes 393224 | tf_op jit(solution)/shard_map/ppermute | solution.py:40
  143.2 17.4 %copy-start.31 = (bf16[512,1024]{1,0:T(8,128)(2,1)S(1)}, bf16[512,1024]{1,0:T(8,128)(2,1)}, u32[]{:S(2)}) copy-start(bf16[512,1024]{1,0:T(8,128)(2,1)} %copy-done.30) | copy-start | bytes 3145732
  143.2 17.4 %copy-start.33 = (bf16[4,128,1024]{2,1,0:T(8,128)(2,1)S(1)}, bf16[4,128,1024]{2,1,0:T(8,128)(2,1)}, u32[]{:S(2)}) copy-start(bf16[4,128,1024]{2,1,0:T(8,128)(2,1)} %copy-done.32) | copy-start | bytes 3145732
  150.5 10.2 %copy-start.3 = (f32[4,128,16]{2,1,0:T(8,128)S(1)}, f32[4,128,16]{2,1,0:T(8,128)}, u32[]{:S(2)}) copy-start(f32[4,128,16]{2,1,0:T(8,128)} %copy-done.1) | copy-start | bytes 98308
  150.5 10.2 %copy-start.7 = (bf16[512,1024]{1,0:T(8,128)(2,1)S(1)}, bf16[512,1024]{1,0:T(8,128)(2,1)}, u32[]{:S(2)}) copy-start(bf16[512,1024]{1,0:T(8,128)(2,1)} %grad_ref.5) | copy-start | bytes 3145732
  150.5 10.1 %copy-start.18 = (bf16[512,1,128]{2,0,1:T(8,128)(2,1)S(1)}, bf16[512,1,128]{2,0,1:T(8,128)(2,1)}, u32[]{:S(2)}) copy-start(bf16[512,1,128]{2,0,1:T(8,128)(2,1)} %param.15) | copy-start | bytes 393220
  150.5 10.1 %copy-start.28 = (f32[4,128,16]{1,2,0:T(8,128)S(1)}, f32[4,128,16]{1,2,0:T(8,128)}, u32[]{:S(2)}) copy-start(f32[4,128,16]{1,2,0:T(8,128)} %copy.15) | copy-start | bytes 98308
  150.5 10.1 %copy-start.34 = (f32[1,16,64,128]{3,2,1,0:T(8,128)S(1)}, f32[1,16,64,128]{3,2,1,0:T(8,128)}, u32[]{:S(2)}) copy-start(f32[1,16,64,128]{3,2,1,0:T(8,128)} %param.18) | copy-start | bytes 1572868
  150.6 16.1 %collective-permute-start.33 = (bf16[128,512]{1,0:T(8,128)(2,1)S(1)}, bf16[128,512]{1,0:T(8,128)(2,1)S(1)}, u32[]{:S(2)}, u32[]{:S(2)}) collective-permute-start(bf16[128,512]{1,0:T(8,128)(2,1)S(1)} %get-tuple-element.95), channel_id=1, source_target_pairs={{0,24},{8,0},{16,8},{24,16},{32,56},{40,32},{48,40},{56,48},{64,88... | collective-permute-start | bytes 393224 | tf_op jit(solution)/shard_map/ppermute | solution.py:40
  153.9 12.8 %collective-permute-start.22 = (bf16[128,512]{1,0:T(8,128)(2,1)S(1)}, bf16[128,512]{1,0:T(8,128)(2,1)S(1)}, u32[]{:S(2)}, u32[]{:S(2)}) collective-permute-start(bf16[128,512]{1,0:T(8,128)(2,1)S(1)} %get-tuple-element.81), channel_id=1, source_target_pairs={{0,32},{8,40},{16,48},{24,56},{32,64},{40,72},{48,80},{56,88},{64,... | collective-permute-start | bytes 393224 | tf_op jit(solution)/shard_map/ppermute | solution.py:40
  154.0 12.7 %collective-permute-start.23 = (bf16[128,512]{1,0:T(8,128)(2,1)S(1)}, bf16[128,512]{1,0:T(8,128)(2,1)S(1)}, u32[]{:S(2)}, u32[]{:S(2)}) collective-permute-start(bf16[128,512]{1,0:T(8,128)(2,1)S(1)} %get-tuple-element.82), channel_id=1, source_target_pairs={{0,96},{8,104},{16,112},{24,120},{32,0},{40,8},{48,16},{56,24},{64... | collective-permute-start | bytes 393224 | tf_op jit(solution)/shard_map/ppermute | solution.py:40
  157.3 10.3 %collective-permute-start.12 = (bf16[32,4096]{1,0:T(8,128)(2,1)S(1)}, bf16[32,4096]{1,0:T(8,128)(2,1)S(1)}, u32[]{:S(2)}, u32[]{:S(2)}) collective-permute-start(bf16[32,4096]{1,0:T(8,128)(2,1)S(1)} %get-tuple-element.68), channel_id=1, source_target_pairs={{0,2},{1,3},{2,4},{3,5},{4,6},{5,7},{6,0},{7,1},{8,10},{9,11},{10,... | collective-permute-start | bytes 786440 | tf_op jit(solution)/shard_map/ppermute | solution.py:48
  158.2 9.4 %collective-permute-start.13 = (bf16[32,4096]{1,0:T(8,128)(2,1)S(1)}, bf16[32,4096]{1,0:T(8,128)(2,1)S(1)}, u32[]{:S(2)}, u32[]{:S(2)}) collective-permute-start(bf16[32,4096]{1,0:T(8,128)(2,1)S(1)} %get-tuple-element.69), channel_id=1, source_target_pairs={{0,6},{1,7},{2,0},{3,1},{4,2},{5,3},{6,4},{7,5},{8,14},{9,15},{10,... | collective-permute-start | bytes 786440 | tf_op jit(solution)/shard_map/ppermute | solution.py:48
  160.7 6.0 %copy-start.11 = (f32[256,512]{1,0:T(8,128)S(1)}, f32[256,512]{1,0:T(8,128)}, u32[]{:S(2)}) copy-start(f32[256,512]{1,0:T(8,128)} %copy-done.10) | copy-start | bytes 1572868
  (9 other events, 6.6 us)

commit v3 on v0

v3 whole, which is shorter than its diff:
```python
import functools

import jax
import jax.numpy as jnp
from jax import lax
from jax.experimental import pallas as pl
from jax.experimental.pallas import tpu as pltpu
from jax.sharding import PartitionSpec as P

SIDE = 4
CHUNK = 128
CHUNKS = 4
HEADS = 16
WIDE = 1024
QUARTER = WIDE // SIDE
TAIL = 16
F32 = jnp.float32
BF16 = jnp.bfloat16
ORDER = (2, 1, 3, 0)
VMEM_LIMIT = 64 * 1024 * 1024


def params(limit=VMEM_LIMIT):
    return pltpu.CompilerParams(vmem_limit_bytes=limit)


COST = pl.CostEstimate(flops=1, bytes_accessed=1, transcendentals=0)


def whole(space=pltpu.VMEM):
    return pl.BlockSpec(memory_space=space)


def full_block(*shape):
    return pl.BlockSpec(shape, lambda *_: (0,) * len(shape))


def routed(block, move):
    route = []
    for i in range(SIDE**3 * 2):
        z, y, x, core = i // 32, i // 8 % 4, i // 2 % 4, i % 2
        z, y, x, core = move(z, y, x, core)
        route.append((i, ((z % SIDE * SIDE + y % SIDE) * SIDE + x % SIDE) * 2 + core % 2))
    return lax.ppermute(block, ("ctx", "smp"), route)


def hop(block, dz, dy):
    return routed(block, lambda z, y, x, core: (z + dz, y + dy, x, core))


def hop_smp(block, dx, dc):
    return routed(block, lambda z, y, x, core: (z, y, x + dx, core + dc))


def first_hop(block, d, to_other):
    def move(z, y, x, core):
        core = core ^ to_other
        return (z, y + d, x, core) if core == 0 else (z + d, y, x, core)

    return routed(block, move)


def second_hop(block, d, to_other):
    def move(z, y, x, core):
        return (z + d, y, x, core ^ to_other) if core == 0 else (z, y + d, x, core ^ to_other)

    return routed(block, move)


def dot(a, b):
    return lax.dot_general(a, b, (((1,), (0,)), ((), ())), preferred_element_type=F32)


def dot_nt(a, b):
    return lax.dot_general(a, b, (((1,), (1,)), ((), ())), preferred_element_type=F32)


def dot_tn(a, b):
    return lax.dot_general(a, b, (((0,), (0,)), ((), ())), preferred_element_type=F32)


def halves(v):
    high = v.astype(BF16)
    return high, (v - high.astype(F32)).astype(BF16)


def spread_matrix():
    lane = lax.broadcasted_iota(jnp.int32, (HEADS, WIDE), 1)
    head = lax.broadcasted_iota(jnp.int32, (HEADS, WIDE), 0)
    return ((lane >= head * 64) & (lane < head * 64 + 64)).astype(F32).astype(BF16)


def spread(v, matrix):
    high, low = halves(v)
    return dot(high, matrix) + dot(low, matrix)


def spread_row(v, matrix):
    return spread(jnp.broadcast_to(v, (8, HEADS)), matrix)[0:1]


def tail_rows(row):
    high, low = halves(row)
    at = lax.broadcasted_iota(jnp.int32, (TAIL, row.shape[1]), 0)
    wide = jnp.where(at == 0, high.astype(F32), jnp.where(at == 1, low.astype(F32), 0.0))
    return wide.astype(BF16)


def tail_value(rows):
    rows = rows.astype(F32)
    return rows[0:1] + rows[1:2]


def turn(a, b):
    return lax.rem(a + b + 2 * SIDE, SIDE)


def pieces(v):
    high = v.astype(BF16)
    middle, low = halves(v - high.astype(F32))
    return high, middle, low


def pre_kernel(
    at_ref, dlog_ref, stept_ref, grad_ref, read_ref, fork_ref,
    rel_ref, relt_ref, step_ref, scaled_ref, state_ref, m0, m1, m2, m3, message,
):
    y = at_ref[1]
    row = lax.broadcasted_iota(jnp.int32, (CHUNK, CHUNK), 0)
    col = lax.broadcasted_iota(jnp.int32, (CHUNK, CHUNK), 1)
    lower = jnp.where(row >= col, 1.0, 0.0).astype(BF16)
    upper = jnp.where(row <= col, 1.0, 0.0).astype(BF16)
    same = jnp.where(row == col, 1.0, 0.0).astype(BF16)
    matrix = spread_matrix()
    head = lax.broadcasted_iota(jnp.int32, (HEADS, CHUNK), 0)
    decay_log = jnp.zeros((HEADS, CHUNK), F32)
    for h in range(HEADS):
        decay_log = jnp.where(head == h, dlog_ref[h], decay_log)
    decay_rate = -jnp.exp(decay_log)
    totals = []
    for c in range(CHUNKS):
        here = slice(c * CHUNK, (c + 1) * CHUNK)
        steps = stept_ref[:, here]
        rates = pieces(steps * decay_rate)
        rel = dot_nt(lower, rates[0]) + dot_nt(lower, rates[1]) + dot_nt(lower, rates[2])
        rel_ref[c] = rel
        relt_ref[c] = dot(rates[0], upper) + dot(rates[1], upper) + dot(rates[2], upper)
        cut = pieces(steps)
        step_ref[here] = dot_nt(same, cut[0]) + dot_nt(same, cut[1]) + dot_nt(same, cut[2])
        totals.append(rel[CHUNK - 1 : CHUNK])
        scaled_ref[here] = (spread(jnp.exp(rel), matrix) * grad_ref[here].astype(F32)).astype(BF16)
    state = None
    for c in reversed(range(CHUNKS)):
        here = slice(c * CHUNK, (c + 1) * CHUNK)
        local = dot_tn(read_ref[here], scaled_ref[here])
        if state is None:
            state = local
        else:
            state = local + spread_row(jnp.exp(totals[c]), matrix) * state
        if c > 0:
            state_ref[c - 1] = state.astype(BF16)
    message[0:128] = state.astype(BF16)
    message[128:256] = (fork_ref[0] + fork_ref[1]).T.astype(BF16)
    decay = spread_row(jnp.exp(totals[0] + totals[1] + totals[2] + totals[3]), matrix)
    message[256 : 256 + TAIL] = tail_rows(decay)
    for d, out in enumerate((m0, m1, m2, m3)):
        start = pl.multiple_of(turn(y, d) * QUARTER, QUARTER)
        out[...] = message[:, pl.ds(start, QUARTER)]


def pre(at, decay_log, stept, out_grad, reads, fork_grad):
    length = CHUNKS * CHUNK
    sent = jax.ShapeDtypeStruct((256 + TAIL, QUARTER), BF16)
    return pl.pallas_call(
        pre_kernel,
        grid=(1,),
        out_shape=[
            jax.ShapeDtypeStruct((CHUNKS, CHUNK, HEADS), F32),
            jax.ShapeDtypeStruct((CHUNKS, HEADS, CHUNK), F32),
            jax.ShapeDtypeStruct((length, HEADS), F32),
            jax.ShapeDtypeStruct((length, WIDE), BF16),
            jax.ShapeDtypeStruct((CHUNKS - 1, 128, WIDE), BF16),
        ]
        + [sent] * 4,
        in_specs=[
            whole(pltpu.SMEM),
            whole(pltpu.SMEM),
            full_block(HEADS, length),
            full_block(length, WIDE),
            full_block(length, 128),
            full_block(2, WIDE, 128),
        ],
        out_specs=[
            full_block(CHUNKS, CHUNK, HEADS),
            full_block(CHUNKS, HEADS, CHUNK),
            full_block(length, HEADS),
            full_block(length, WIDE),
            full_block(CHUNKS - 1, 128, WIDE),
        ]
        + [full_block(256 + TAIL, QUARTER)] * 4,
        scratch_shapes=[pltpu.VMEM((256 + TAIL, WIDE), BF16)],
        compiler_params=params(),
        cost_estimate=COST,
    )(at, decay_log, stept, out_grad, reads, fork_grad)


def group_kernel(at_ref, a0, a1, a2, a3, out_ref, stack):
    y = at_ref[1]
    for d, ref in enumerate((a0, a1, a2, a3)):
        stack[d] = ref[...]
    total = rate = fork = None
    for b in reversed(range(SIDE)):
        at = turn(y, -b)
        local = stack[at, 0:128].astype(F32)
        decay = tail_value(stack[at, 256 : 256 + TAIL])
        share = stack[at, 128:256].astype(F32)
        if total is None:
            total, rate, fork = local, decay, share
        else:
            total, rate, fork = local + decay * total, rate * decay, fork + share
    out_ref[0:128] = total.astype(BF16)
    out_ref[128:256] = fork.astype(BF16)
    out_ref[256 : 256 + TAIL] = tail_rows(rate)


def group(at, arrived):
    return pl.pallas_call(
        group_kernel,
        grid=(1,),
        out_shape=jax.ShapeDtypeStruct((256 + TAIL, QUARTER), BF16),
        in_specs=[whole(pltpu.SMEM)] + [full_block(256 + TAIL, QUARTER)] * 4,
        out_specs=full_block(256 + TAIL, QUARTER),
        scratch_shapes=[pltpu.VMEM((SIDE, 256 + TAIL, QUARTER), BF16)],
        compiler_params=params(),
        cost_estimate=COST,
    )(at, *arrived)


def carry_kernel(at_ref, a0, a1, a2, a3, b0, b1, b2, b3, c0, c1, c2, c3, first, second, out):
    z, y = at_ref[0], at_ref[1]
    for d, ref in enumerate((a0, a1, a2, a3)):
        first[d] = ref[...]
    for d, ref in enumerate((b0, b1, b2, b3)):
        second[d] = ref[...]
    carry = jnp.zeros((128, QUARTER), F32)
    for d in range(SIDE):
        carry = carry + second[d, 128:256].astype(F32)
    mine = carry
    for b in (3, 2, 1):
        at = turn(z, -b)
        decay = tail_value(second[at, 256 : 256 + TAIL])
        carry = second[at, 0:128].astype(F32) + decay * carry
        mine = jnp.where(z == b - 1, carry, mine)
    out[SIDE - 1] = mine.astype(BF16)
    for b in (3, 2, 1):
        at = turn(y, -b)
        decay = tail_value(first[at, 256 : 256 + TAIL])
        mine = first[at, 0:128].astype(F32) + decay * mine
        out[b - 1] = mine.astype(BF16)
    for d, ref in enumerate((c0, c1, c2, c3)):
        ref[...] = out[turn(y, d)]


def carry_over(at, first, second):
    return pl.pallas_call(
        carry_kernel,
        grid=(1,),
        out_shape=[jax.ShapeDtypeStruct((128, QUARTER), BF16)] * 4,
        in_specs=[whole(pltpu.SMEM)] + [full_block(256 + TAIL, QUARTER)] * 8,
        out_specs=[full_block(128, QUARTER)] * 4,
        scratch_shapes=[
            pltpu.VMEM((SIDE, 256 + TAIL, QUARTER), BF16),
            pltpu.VMEM((SIDE, 256 + TAIL, QUARTER), BF16),
            pltpu.VMEM((SIDE, 128, QUARTER), BF16),
        ],
        compiler_params=params(),
        cost_estimate=COST,
    )(at, *first, *second)


def diag_kernel(skip_ref, rel_ref, relt_ref, step_ref, read_ref, write_ref, grad_ref, out_ref):
    matrix = spread_matrix()
    row = lax.broadcasted_iota(jnp.int32, (CHUNK, CHUNK), 0)
    col = lax.broadcasted_iota(jnp.int32, (CHUNK, CHUNK), 1)
    for c in range(2):
        here = slice(c * CHUNK, (c + 1) * CHUNK)
        scores = jnp.where(col >= row, dot_nt(write_ref[here], read_ref[here]), 0.0)
        rel, relt = rel_ref[c], relt_ref[c]
        steps = spread(step_ref[here], matrix)
        for pair in range(HEADS // 2):
            at = slice(pair * 128, pair * 128 + 128)
            grads = grad_ref[here, at]
            both = []
            for h in (2 * pair, 2 * pair + 1):
                kernel = jnp.exp(jnp.minimum(relt[h : h + 1] - rel[:, h : h + 1], 0.0))
                both.append(dot((scores * kernel).astype(BF16), grads))
            part = steps[:, at] * jnp.where(col < 64, both[0], both[1])
            skip = jnp.where(col < 64, skip_ref[2 * pair], skip_ref[2 * pair + 1])
            out_ref[here, at] = (part + skip * grads.astype(F32)).astype(BF16)


def diag(skip_gain, rel, relt, step_size, reads, writes, out_grad):
    by_two = lambda c: (c, 0)
    rows = 2 * CHUNK
    return pl.pallas_call(
        diag_kernel,
        grid=(CHUNKS // 2,),
        out_shape=jax.ShapeDtypeStruct((CHUNKS * CHUNK, WIDE), BF16),
        in_specs=[
            whole(pltpu.SMEM),
            pl.BlockSpec((2, CHUNK, HEADS), lambda c: (c, 0, 0)),
            pl.BlockSpec((2, HEADS, CHUNK), lambda c: (c, 0, 0)),
            pl.BlockSpec((rows, HEADS), by_two),
            pl.BlockSpec((rows, 128), by_two),
            pl.BlockSpec((rows, 128), by_two),
            pl.BlockSpec((rows, WIDE), by_two),
        ],
        out_specs=pl.BlockSpec((rows, WIDE), by_two),
        compiler_params=params(),
        cost_estimate=COST,
    )(skip_gain, rel, relt, step_size, reads, writes, out_grad)


def x_kernel(
    at_ref, q0, q1, q2, q3, state_ref, rel_ref, step_ref, write_ref, base_ref,
    keep_ref, give_ref, mine_ref, theirs_ref, full_ref, carried, x_ref,
):
    y, core = at_ref[1], at_ref[3]
    matrix = spread_matrix()
    for d, ref in enumerate((q0, q1, q2, q3)):
        start = pl.multiple_of(turn(y, -d) * QUARTER, QUARTER)
        carried[:, pl.ds(start, QUARTER)] = ref[...]
    later = jnp.zeros((1, HEADS), F32)
    for c in reversed(range(CHUNKS)):
        here = slice(c * CHUNK, (c + 1) * CHUNK)
        rel = rel_ref[c]
        last = rel[CHUNK - 1 : CHUNK]
        if c == CHUNKS - 1:
            full = carried[...]
        else:
            share = spread_row(jnp.exp(later), matrix) * carried[...].astype(F32)
            full = (state_ref[c].astype(F32) + share).astype(BF16)
        full_ref[c] = full
        weights = spread(step_ref[here] * jnp.exp(last - rel), matrix)
        x = (base_ref[here].astype(F32) + weights * dot(write_ref[here], full)).astype(BF16)
        for k in range(2):
            x_ref[c, k] = x[k * 64 : k * 64 + 64]
        later = later + last
    start = pl.multiple_of(core * 512, 512)
    other = pl.multiple_of((1 - core) * 512, 512)
    for c in range(CHUNKS):
        for k in range(2):
            here = slice(c * CHUNK + k * 64, c * CHUNK + k * 64 + 64)
            keep_ref[here] = x_ref[c, k, :, pl.ds(start, 512)]
            give_ref[here] = x_ref[c, k, :, pl.ds(other, 512)]
        there = slice(c * 64, c * 64 + 64)
        mine_ref[there] = x_ref[c, core]
        theirs_ref[there] = x_ref[c, 1 - core]


def x_final(at, quarters, states, rel, step_size, writes, base):
    rows = CHUNKS * CHUNK
    half, rest = (rows, 512), (rows // 2, WIDE)
    return pl.pallas_call(
        x_kernel,
        grid=(1,),
        in_specs=[whole(pltpu.SMEM)]
        + [full_block(128, QUARTER)] * 4
        + [
            full_block(CHUNKS - 1, 128, WIDE),
            full_block(CHUNKS, CHUNK, HEADS),
            full_block(rows, HEADS),
            full_block(rows, 128),
            full_block(rows, WIDE),
        ],
        out_specs=[full_block(*half)] * 2 + [full_block(*rest)] * 2 + [full_block(CHUNKS, 128, WIDE)],
        scratch_shapes=[pltpu.VMEM((128, WIDE), BF16), pltpu.VMEM((CHUNKS, 2, 64, WIDE), BF16)],
        out_shape=[jax.ShapeDtypeStruct(half, BF16)] * 2
        + [jax.ShapeDtypeStruct(rest, BF16)] * 2
        + [jax.ShapeDtypeStruct((CHUNKS, 128, WIDE), BF16)],
        compiler_params=params(),
        cost_estimate=COST,
    )(at, *quarters, states, rel, step_size, writes, base)


def vector_kernel(
    rel_ref, relt_ref, step_ref, read_ref, write_ref, grad_ref, scaled_ref, first_ref, second_ref,
    full_ref, start_ref, wgrad_ref, rgrad_ref, state, inputs_ref,
):
    matrix = spread_matrix()
    inputs_ref[:, : WIDE // 2] = first_ref[...]
    inputs_ref[:, WIDE // 2 :] = second_ref[...]

    @pl.when(pl.program_id(0) == 0)
    def _():
        state[...] = start_ref[...].T

    row = lax.broadcasted_iota(jnp.int32, (CHUNK, CHUNK), 0)
    col = lax.broadcasted_iota(jnp.int32, (CHUNK, CHUNK), 1)
    rel, relt, step = rel_ref[0], relt_ref[0], step_ref[...]
    coupling = jnp.zeros((CHUNK, CHUNK), F32)
    for pair in range(HEADS // 2):
        at = slice(pair * 128, pair * 128 + 128)
        grads = grad_ref[:, at]
        inputs = inputs_ref[:, at]
        for k in range(2):
            h = 2 * pair + k
            own = jnp.where((col >= 64) == (k == 1), inputs.astype(F32), 0.0).astype(BF16)
            kernel = jnp.exp(jnp.minimum(relt[h : h + 1] - rel[:, h : h + 1], 0.0))
            coupling = coupling + step[:, h : h + 1] * kernel * dot_nt(own, grads)
    coupling = jnp.where(col >= row, coupling, 0.0).astype(BF16)
    last = rel[CHUNK - 1 : CHUNK]
    weights = spread(step * jnp.exp(last - rel), matrix)
    weighted = (weights * inputs_ref[...].astype(F32)).astype(BF16)
    wgrad_ref[...] = dot_nt(weighted, full_ref[0]) + dot(coupling, read_ref[...])
    rgrad_ref[...] = dot_nt(scaled_ref[...], state[...].astype(BF16)) + dot_tn(
        coupling, write_ref[...]
    )
    state[...] = spread_row(jnp.exp(last), matrix) * state[...] + dot_tn(write_ref[...], weighted)


def vectors(rel, relt, step_size, reads, writes, out_grad, scaled, first, second, full, start_state):
    by_chunk = lambda c: (c, 0)
    return pl.pallas_call(
        vector_kernel,
        grid=(CHUNKS,),
        out_shape=[jax.ShapeDtypeStruct((CHUNKS * CHUNK, 128), F32)] * 2,
        in_specs=[
            pl.BlockSpec((1, CHUNK, HEADS), lambda c: (c, 0, 0)),
            pl.BlockSpec((1, HEADS, CHUNK), lambda c: (c, 0, 0)),
            pl.BlockSpec((CHUNK, HEADS), by_chunk),
            pl.BlockSpec((CHUNK, 128), by_chunk),
            pl.BlockSpec((CHUNK, 128), by_chunk),
            pl.BlockSpec((CHUNK, WIDE), by_chunk),
            pl.BlockSpec((CHUNK, WIDE), by_chunk),
            pl.BlockSpec((CHUNK, WIDE // 2), by_chunk),
            pl.BlockSpec((CHUNK, WIDE // 2), by_chunk),
            pl.BlockSpec((1, 128, WIDE), lambda c: (c, 0, 0)),
            pl.BlockSpec((WIDE, 128), lambda c: (0, 0)),
        ],
        out_specs=[pl.BlockSpec((CHUNK, 128), by_chunk)] * 2,
        scratch_shapes=[pltpu.VMEM((128, WIDE), F32), pltpu.VMEM((CHUNK, WIDE), BF16)],
        compiler_params=params(),
        cost_estimate=COST,
    )(rel, relt, step_size, reads, writes, out_grad, scaled, first, second, full, start_state)


def project_kernel(x_ref, w_ref, out_ref, total):
    step = pl.program_id(0)
    product = dot(x_ref[...], w_ref[...])

    @pl.when(step == 0)
    def _():
        total[...] = product

    @pl.when(step == 1)
    def _():
        out_ref[...] = (total[...] + product).astype(BF16)


def project(layer_input, proj_weight, part):
    rows, depth = layer_input.shape
    wide = WIDE // 2
    return pl.pallas_call(
        project_kernel,
        grid=(2,),
        out_shape=jax.ShapeDtypeStruct((rows, wide), BF16),
        in_specs=[
            pl.BlockSpec((rows, depth // 2), lambda i: (0, i)),
            pl.BlockSpec((depth // 2, wide), lambda i: (i, part)),
        ],
        out_specs=pl.BlockSpec((rows, wide), lambda i: (0, 0)),
        scratch_shapes=[pltpu.VMEM((rows, wide), F32)],
        compiler_params=params(),
        cost_estimate=COST,
    )(layer_input, proj_weight)


FAR = ((2, (0, 1)), (2, (2, 3)))
PLAIN = ((1, (2, 3)), (-1, (0, 1)))
ADDED = ((1, (0, 1)), (-1, (2, 3)))


def column_block(s, d, part):
    for_y = turn(s[0], part) * SIDE + turn(s[1], d)
    for_z = turn(s[0], d) * SIDE + turn(s[1], part)
    return jnp.where(s[3] == 0, for_y, for_z)


def columns_spec(d, parts):
    def index(g, s):
        return 0, column_block(s, d, jnp.where(g == 0, ORDER[parts[0]], ORDER[parts[1]]))

    return pl.BlockSpec((CHUNKS * CHUNK, 256), index)


def ring_kernel(at_ref, up_ref, down_ref, keep_ref, got_ref, *refs):
    more, outs = refs[:-2], refs[-2:]
    for k, cols in enumerate((up_ref, down_ref)):
        turned = cols[...].T
        for half, x_ref in enumerate((keep_ref, got_ref)):
            at = slice(512 * half, 512 * half + 512)
            product = dot(turned, x_ref[...])
            if more:
                product = product + more[k][0, :, at].astype(F32)
            outs[k][0, :, at] = product.astype(BF16)


def ring_product(at, way, layer_input, keep, got, more=()):
    rows = layer_input.shape[0]
    (up_to, up_parts), (down_to, down_parts) = way
    block = pl.BlockSpec((1, 256, WIDE), lambda g, s: (g, 0, 0))
    return pl.pallas_call(
        ring_kernel,
        grid_spec=pltpu.PrefetchScalarGridSpec(
            num_scalar_prefetch=1,
            grid=(2,),
            in_specs=[columns_spec(up_to, up_parts), columns_spec(down_to, down_parts)]
            + [full_block(rows, 512)] * 2
            + [block] * len(more),
            out_specs=[block] * 2,
        ),
        out_shape=[jax.ShapeDtypeStruct((2, 256, WIDE), BF16)] * 2,
        compiler_params=params(),
        cost_estimate=COST,
    )(at, layer_input, layer_input, keep, got, *more)


def own_kernel(
    at_ref, first_ref, second_ref, keep_ref, got_ref,
    below_add, below_plain, above_plain, above_add, *outs,
):
    g = pl.program_id(0)
    for k, cols in enumerate((first_ref, second_ref)):
        turned = cols[...].T
        for half, x_ref in enumerate((keep_ref, got_ref)):
            at = slice(512 * half, 512 * half + 512)
            product = dot(turned, x_ref[...])
            early, late = outs[SIDE * half + k], outs[SIDE * half + 2 + k]

            @pl.when(g == 0)
            def _():
                total = product + below_add[k, :, at].astype(F32) + above_plain[k, :, at].astype(F32)
                early[...] = total.astype(early.dtype)

            @pl.when(g == 1)
            def _():
                total = product + below_plain[k, :, at].astype(F32) + above_add[k, :, at].astype(F32)
                late[...] = total.astype(late.dtype)


def own_product(at, layer_input, keep, got, arrived):
    rows = layer_input.shape[0]
    shape = lambda dtype: jax.ShapeDtypeStruct((256, 512), dtype)
    return pl.pallas_call(
        own_kernel,
        grid_spec=pltpu.PrefetchScalarGridSpec(
            num_scalar_prefetch=1,
            grid=(2,),
            in_specs=[columns_spec(0, (0, 2)), columns_spec(0, (1, 3))]
            + [full_block(rows, 512)] * 2
            + [full_block(2, 256, WIDE)] * 4,
            out_specs=[full_block(256, 512)] * 8,
        ),
        out_shape=[shape(BF16)] * 3 + [shape(F32)] + [shape(BF16)] * 4,
        compiler_params=params(),
        cost_estimate=COST,
    )(at, layer_input, layer_input, keep, got, *arrived)


def weight_kernel(scale, at_ref, *refs):
    same, cross, out = refs[:4], refs[4:8], refs[8]
    for terms, place in ((same, at_ref[3]), (cross, 1 - at_ref[3])):
        total = terms[0][...].astype(F32)
        for term in terms[1:]:
            total = total + term[...].astype(F32)
        out[:, pl.ds(pl.multiple_of(place * 512, 512), 512)] = (total * scale).astype(BF16)


def weight_final(at, scale, terms):
    return pl.pallas_call(
        functools.partial(weight_kernel, scale),
        grid=(1,),
        out_shape=jax.ShapeDtypeStruct((256, WIDE), BF16),
        in_specs=[whole(pltpu.SMEM)] + [full_block(256, 512)] * 8,
        out_specs=full_block(256, WIDE),
        compiler_params=params(),
        cost_estimate=COST,
    )(at, *terms)


def theirs_kernel(at_ref, x_ref, w_ref, out_ref):
    out_ref[...] = dot_nt(x_ref[...], w_ref[...]).astype(BF16)


def theirs(at, x_rows, proj_weight):
    depth, tile = proj_weight.shape[0], 2048
    return pl.pallas_call(
        theirs_kernel,
        grid_spec=pltpu.PrefetchScalarGridSpec(
            num_scalar_prefetch=1,
            grid=(depth // tile,),
            in_specs=[
                full_block(256, WIDE),
                pl.BlockSpec((tile, WIDE), lambda i, s: (i, 0)),
            ],
            out_specs=pl.BlockSpec((256, tile), lambda i, s: (0, i)),
        ),
        out_shape=jax.ShapeDtypeStruct((256, depth), BF16),
        compiler_params=params(),
        cost_estimate=COST,
    )(at, x_rows, proj_weight)


def mine_kernel(at_ref, x_ref, w_ref, add_ref, up_out, down_out, up_keep, down_keep, own_out, total):
    x = at_ref[2]
    total[...] = (dot_nt(x_ref[...], w_ref[...]) + add_ref[...].astype(F32)).reshape(SIDE, 64, -1)
    far, above, below = turn(x, 2), turn(x, 1), turn(x, -1)
    up_out[0:32] = total[far, 0:32].astype(BF16)
    up_out[32:64] = total[above, 32:64].astype(BF16)
    up_keep[...] = total[above, 0:32].astype(BF16)
    down_out[0:32] = total[far, 32:64].astype(BF16)
    down_out[32:64] = total[below, 0:32].astype(BF16)
    down_keep[...] = total[below, 32:64].astype(BF16)
    own_out[...] = total[x]


def mine(at, x_rows, proj_weight, add):
    depth, tile = proj_weight.shape[0], 2048
    out = lambda n: pl.BlockSpec((n, tile), lambda i, s: (0, i))
    shape = lambda n, dtype: jax.ShapeDtypeStruct((n, depth), dtype)
    return pl.pallas_call(
        mine_kernel,
        grid_spec=pltpu.PrefetchScalarGridSpec(
            num_scalar_prefetch=1,
            grid=(depth // tile,),
            in_specs=[
                full_block(256, WIDE),
                pl.BlockSpec((tile, WIDE), lambda i, s: (i, 0)),
                pl.BlockSpec((256, tile), lambda i, s: (0, i)),
            ],
            out_specs=[out(64), out(64), out(32), out(32), out(64)],
            scratch_shapes=[pltpu.VMEM((SIDE, 64, tile), F32)],
        ),
        out_shape=[shape(64, BF16), shape(64, BF16), shape(32, BF16), shape(32, BF16), shape(64, F32)],
        compiler_params=params(),
        cost_estimate=COST,
    )(at, x_rows, proj_weight, add)


def add_kernel(up_keep, down_keep, from_below, from_above, up_out, down_out):
    n = up_keep.shape[0]
    up_out[...] = (up_keep[...].astype(F32) + from_below[0:n].astype(F32)).astype(BF16)
    down_out[...] = (down_keep[...].astype(F32) + from_above[0:n].astype(F32)).astype(BF16)


def add_two(up_keep, down_keep, from_below, from_above):
    n, depth = up_keep.shape
    return pl.pallas_call(
        add_kernel,
        grid=(1,),
        out_shape=[jax.ShapeDtypeStruct((n, depth), BF16)] * 2,
        in_specs=[full_block(n, depth)] * 4,
        out_specs=[full_block(n, depth)] * 2,
        compiler_params=params(),
        cost_estimate=COST,
    )(up_keep, down_keep, from_below, from_above)


def input_kernel(own, below, above, below_add, above_add, out):
    top = own[0:32] + below_add[...].astype(F32) + above[32:64].astype(F32)
    bottom = own[32:64] + below[32:64].astype(F32) + above_add[...].astype(F32)
    out[0:32] = top.astype(BF16)
    out[32:64] = bottom.astype(BF16)


def input_final(own, below, above, below_add, above_add):
    rows, depth = own.shape
    full, part = full_block(rows, depth), full_block(rows // 2, depth)
    return pl.pallas_call(
        input_kernel,
        grid=(1,),
        out_shape=jax.ShapeDtypeStruct((rows, depth), BF16),
        in_specs=[full, full, full, part, part],
        out_specs=full,
        compiler_params=params(),
        cost_estimate=COST,
    )(own, below, above, below_add, above_add)


def after(value, *earlier):
    return lax.optimization_barrier((value, earlier))[0]


def body(
    layer_input,
    proj_weight,
    step_size,
    decay_log,
    skip_gain,
    write_vec,
    read_vec,
    out_grad,
    start_state,
    fork_grad,
):
    length = layer_input.shape[0]
    position = lax.axis_index("ctx")
    z, y = position // SIDE, position % SIDE
    column = lax.axis_index("smp")
    x, core = column // 2, column % 2
    at = jnp.stack([z, y, x, core])
    writes = write_vec[:, 0]
    reads = read_vec[:, 0]
    rel, relt, steps, scaled, states, *messages = pre(
        at, decay_log, step_size.T, out_grad, reads, fork_grad.reshape(2, WIDE, 128)
    )
    far, above, below = (hop(messages[d], 0, d) for d in (2, 1, 3))
    inputs_a = project(after(layer_input, *messages), proj_weight, 0)
    first = after([messages[0], above, far, below], inputs_a)
    message = group(at, first)
    far, above, below = (hop(message, d, 0) for d in (2, 1, 3))
    base = diag(skip_gain, rel, relt, steps, reads, writes, after(out_grad, message))
    second = after([message, above, far, below], base)
    sent = carry_over(at, first, second)
    far, above, below = (hop(sent[d], 0, d) for d in (2, 1, 3))
    inputs_b = project(after(layer_input, sent[0]), proj_weight, 1)
    quarters = after([sent[0], above, far, below], inputs_b)
    keep, give, x_mine, x_theirs, full = x_final(at, quarters, states, rel, steps, writes, base)
    got = first_hop(give, 0, 1)
    other = theirs(at, x_theirs, proj_weight)
    far = ring_product(at, FAR, layer_input, keep, after(got, other))
    far_in = first_hop(far[0], 1, 0), first_hop(far[1], -1, 0)
    other_in = hop_smp(other, 0, 1)
    plain = ring_product(at, PLAIN, layer_input, after(keep, *far), got)
    plain_in = first_hop(plain[0], 1, 0), first_hop(plain[1], -1, 0)
    up, down, up_keep, down_keep, own = mine(at, after(x_mine, *plain), proj_weight, other_in)
    added = ring_product(at, ADDED, layer_input, keep, got, after(far_in, own))
    added_in = first_hop(added[0], 1, 0), first_hop(added[1], -1, 0)
    below_x, above_x = hop_smp(up, 1, 0), hop_smp(down, -1, 0)
    write_grad, read_grad = vectors(
        rel, relt, steps, reads, writes, out_grad, scaled, inputs_a, inputs_b, after(full, *added),
        start_state.reshape(WIDE, 128),
    )
    up, down = add_two(up_keep, down_keep, below_x, after(above_x, write_grad))
    below_add, above_add = hop_smp(up, 1, 0), hop_smp(down, -1, 0)
    arrived = after((added_in[0], plain_in[0], plain_in[1], added_in[1]), up)
    sums = own_product(at, layer_input, keep, got, arrived)
    same, cross = list(sums[:4]), list(sums[4:])
    for g in range(3):
        same[g] = second_hop(same[g], ORDER[g], 0)
        cross[g] = second_hop(cross[g], ORDER[g], 1)
    cross[3] = second_hop(cross[3], 0, 1)
    input_grad = input_final(after(own, *sums), below_x, above_x, below_add, above_add)
    scale = (length * lax.axis_size("ctx")) ** (-0.5)
    weight_grad = weight_final(at, scale, same + cross)
    return (input_grad, weight_grad, write_grad[:, None], read_grad[:, None])


def solution(mesh):
    placed = (
        P("ctx", None),
        P(None, "smp"),
        P("ctx", "smp"),
        P("smp"),
        P("smp"),
        P("ctx", "smp", None),
        P("ctx", "smp", None),
        P("ctx", "smp"),
        P("ctx", "smp", None, None),
        P("ctx", "smp", None, None),
    )
    return jax.shard_map(
        body,
        mesh=mesh,
        in_specs=placed,
        out_specs=(
            P(("ctx", "smp"), None),
            P("ctx", "smp"),
            P("ctx", "smp", None),
            P("ctx", "smp", None),
        ),
        check_vma=False,
    )
```

time: 413 us -> 142 us (0.34)
  waiting for transfers between devices: 303 us -> 18.1 us
  Pallas kernels: 0 us -> 79.1 us
  matrix products: 51.2 us -> 0 us
  starting transfers between devices: 19.7 us -> 42.8 us
  between operations: 14 us -> 0.73 us
  other arithmetic: 12.2 us -> 0.67 us
  local copies, waits for them, and re-layouts: 9.06 us -> 0 us
    reduce_scatter x2 -> x0, waiting for transfers between devices: 108 us -> none  [the longest x1 71.6 us: body(): lax.psum_scatter(lax.dot_general(layer_input, x_grad, (((0,), (0,)), ((),...]
    ppermute x15 -> x28, waiting for transfers between devices: 119 us -> 18.1 us  [routed(): return lax.ppermute(block, ('ctx', 'smp'), route)]
    pallas_call x0 -> x17, Pallas kernels: none -> 79.1 us  [the longest x3 13.6 us: ring_product(): pl.pallas_call(ring_kernel, grid_spec=pltpu.PrefetchScalarGridSpec(num_sc...]
    psum x1 -> x0, waiting for transfers between devices: 75.8 us -> none  [body(): lax.psum(jnp.sum(fork_grad, axis=0).astype(jnp.bfloat16), 'ctx')]
    dot_general x16 -> x0, matrix products: 51.2 us -> none  [the longest x1 10.2 us: body(): jnp.dot(layer_input, proj_weight, preferred_element_type=jnp.float32)]
    ppermute x15 -> x28, starting transfers between devices: 19.4 us -> 42.8 us  [routed(): return lax.ppermute(block, ('ctx', 'smp'), route)]
  transfers between devices with their start and end apart: 18 -> 28, of which waited for: 18 -> 7; matrix products, arithmetic and copies ran while one was open for 13% -> 0% of each run, Pallas kernels for 0% -> 40%
where the time goes in v3:
time: 142 us; the launch traced here: 141 us
  Pallas kernels  79.1 us (56%)
  starting transfers between devices  42.8 us (30%)
  waiting for transfers between devices  18.1 us (13%)
    ppermute x28, starting transfers between devices, routed(): return lax.ppermute(block, ('ctx', 'smp'), route)  42.8 us
    ppermute x28, waiting for transfers between devices, routed(): return lax.ppermute(block, ('ctx', 'smp'), route)  18.1 us
    pallas_call x3, Pallas kernels, ring_product(): pl.pallas_call(ring_kernel, grid_spec=pltpu.PrefetchScalarGridSpec(num_sc...  13.6 us
    pallas_call x2, Pallas kernels, project(): pl.pallas_call(project_kernel, grid=(2,), out_shape=jax.ShapeDtypeStruct(...  11.4 us
    pallas_call x1, Pallas kernels, own_product(): pl.pallas_call(own_kernel, grid_spec=pltpu.PrefetchScalarGridSpec(num_sca...  7.98 us
    pallas_call x1, Pallas kernels, vectors(): pl.pallas_call(vector_kernel, grid=(CHUNKS,), out_shape=[jax.ShapeDtypeSt...  7.78 us
    pallas_call x1, Pallas kernels, mine(): pl.pallas_call(mine_kernel, grid_spec=pltpu.PrefetchScalarGridSpec(num_sc...  7.39 us
    pallas_call x1, Pallas kernels, theirs(): pl.pallas_call(theirs_kernel, grid_spec=pltpu.PrefetchScalarGridSpec(num_...  6.57 us
  transfers between devices with their start and end apart: 28, of which 7 were waited for; matrix products, arithmetic and copies ran while one was open for 0% of the time, Pallas kernels for 40%

profile of v3, /device:TPU:1, one launch (start us, length us, event | category | flops | bytes accessed | tf_op | source)
XLA Modules:
  0.0 141.4 jit_solution(712834104541496368)
XLA Ops:
  0.7 0.7 pad_add_fusion.at_ref
  1.3 4.3 %shard_map.129 = (f32[4,128,16]{2,1,0:T(8,128)}, f32[4,16,128]{2,1,0:T(8,128)}, f32[512,16]{1,0:T(8,128)}, bf16[512,1024]{1,0:T(8,128)(2,1)}, bf16[3,128,1024]{2...) custom-call(s32[4]{0:T(128)} %pad_add_fusion.at_ref, ...), custom_call_target="tpu_custom_call" | custom-call | flops 1 | bytes 1 | tf_op jit(solution)/shard_map/pallas_call | solution.py:174
  5.7 2.1 %collective-permute-start = (bf16[272,256]{1,0:T(8,128)(2,1)}, bf16[272,256]{1,0:T(8,128)(2,1)}, u32[]{:S(2)}, u32[]{:S(2)}) collective-permute-start(bf16[272,256]{1,0:T(8,128)(2,1)} %get-tuple-element.73), channel_id=1, source_target_pairs={{0,8},{1,9},{2,10},{3,11},{4,12},{5,13},{6,14},{7,15},{8,16},{9,17... | collective-permute-start | bytes 417800 | tf_op jit(solution)/shard_map/ppermute | solution.py:44
  7.8 2.6 %collective-permute-start.1 = (bf16[272,256]{1,0:T(8,128)(2,1)}, bf16[272,256]{1,0:T(8,128)(2,1)}, u32[]{:S(2)}, u32[]{:S(2)}) collective-permute-start(bf16[272,256]{1,0:T(8,128)(2,1)} %get-tuple-element.74), channel_id=1, source_target_pairs={{0,16},{1,17},{2,18},{3,19},{4,20},{5,21},{6,22},{7,23},{8,24},{9,... | collective-permute-start | bytes 417800 | tf_op jit(solution)/shard_map/ppermute | solution.py:44
  10.4 1.1 collective-permute-start.2
  11.5 5.7 %shard_map.130.first_ref = bf16[512,512]{1,0:T(8,128)(2,1)} custom-call(bf16[512,4096]{1,0:T(8,128)(2,1)} %second_ref.1, bf16[4096,1024]{1,0:T(8,128)(2,1)} %w_ref.7), custom_call_target="tpu_custom_call" | custom-call | flops 1 | bytes 1 | tf_op jit(solution)/shard_map/pallas_call | solution.py:464
  17.2 0.0 collective-permute-done.2.a3
  17.2 1.9 %shard_map.131.b0 = bf16[272,256]{1,0:T(8,128)(2,1)} custom-call(s32[4]{0:T(128)} %pad_add_fusion.at_ref, bf16[272,256]{1,0:T(8,128)(2,1)} %get-tuple-element.77.a0, bf16[272,256]{1,0:T(8,128)(2,1)} %collective-permute-done.a1, bf16[272,256]{1,0:T(8,128)(2,1)} %collective-permute-done.1.a2, bf16[272,256]{1,0:T(8,128)(2,1)} %collective-permute-done.2.a3), custom_call_target="tpu_custom_call" | custom-call | flops 1 | bytes 1 | tf_op jit(solution)/shard_map/pallas_call | solution.py:227
  19.1 3.8 %collective-permute-start.5 = (bf16[272,256]{1,0:T(8,128)(2,1)}, bf16[272,256]{1,0:T(8,128)(2,1)}, u32[]{:S(2)}, u32[]{:S(2)}) collective-permute-start(bf16[272,256]{1,0:T(8,128)(2,1)} %shard_map.131.b0), channel_id=1, source_target_pairs={{0,96},{1,97},{2,98},{3,99},{4,100},{5,101},{6,102},{7,103},{8,104... | collective-permute-start | bytes 417800 | tf_op jit(solution)/shard_map/ppermute | solution.py:44
  22.9 0.0 collective-permute-start.4
  22.9 0.7 collective-permute-start.3
  23.6 3.9 %shard_map.132.base_ref = bf16[512,1024]{1,0:T(8,128)(2,1)} custom-call(f32[16]{0:T(128)} %skip_ref.1, f32[4,128,16]{2,1,0:T(8,128)} %get-tuple-element.81.rel_ref, f32[4,16,128]{2,1,0:T(8,128)} %get-tuple-element.82.relt_ref, f32[512,16]{1,0:T(8,128)} %get-tuple-element.83.step_ref, bf16[512,128]{1,0:T(8,128)(2,1)} %bitcast.16, bf16[512,128]{1,0:T(8,128)(2,1)} %bitcast.18, ...), custom_call_target="tpu_custom_call" | custom-call | flops 1 | bytes 1 | tf_op jit(solution)/shard_map/pallas_call | solution.py:305
  27.5 1.0 collective-permute-done.5.b3
  28.5 0.2 collective-permute-done.4.b2
  28.7 3.5 %collective-permute-done.3.b1 = bf16[272,256]{1,0:T(8,128)(2,1)} collective-permute-done((bf16[272,256]{1,0:T(8,128)(2,1)}, bf16[272,256]{1,0:T(8,128)(2,1)}, u32[]{:S(2)}, u32[]{:S(2)}) %collective-permute-start.3) | collective-permute-done | bytes 139296 | tf_op jit(solution)/shard_map/ppermute | solution.py:44
  32.3 2.2 %shard_map.133 = (bf16[128,256]{1,0:T(8,128)(2,1)}, bf16[128,256]{1,0:T(8,128)(2,1)}, bf16[128,256]{1,0:T(8,128)(2,1)}, bf16[128,256]{1,0:T(8,128)(2,1)}) custom-call(s32[4]{0:T(128)} %pad_add_fusion.at_ref, bf16[272,256]{1,0:T(8,128)(2,1)} %get-tuple-element.77.a0, bf16[272,256]{1,0:T(8,128)(2,1)} %collective-permute-done.a1, ...), custom_call_target="tpu_custom_call" | custom-call | flops 1 | bytes 1 | tf_op jit(solution)/shard_map/pallas_call | solution.py:265
  34.5 0.9 collective-permute-start.6
  35.4 2.2 %collective-permute-start.7 = (bf16[128,256]{1,0:T(8,128)(2,1)}, bf16[128,256]{1,0:T(8,128)(2,1)}, u32[]{:S(2)}, u32[]{:S(2)}) collective-permute-start(bf16[128,256]{1,0:T(8,128)(2,1)} %get-tuple-element.91), channel_id=1, source_target_pairs={{0,16},{1,17},{2,18},{3,19},{4,20},{5,21},{6,22},{7,23},{8,24},{9,... | collective-permute-start | bytes 196616 | tf_op jit(solution)/shard_map/ppermute | solution.py:44
  37.6 0.2 collective-permute-start.8
  37.9 5.7 %shard_map.134.second_ref = bf16[512,512]{1,0:T(8,128)(2,1)} custom-call(bf16[512,4096]{1,0:T(8,128)(2,1)} %second_ref.1, bf16[4096,1024]{1,0:T(8,128)(2,1)} %w_ref.7), custom_call_target="tpu_custom_call" | custom-call | flops 1 | bytes 1 | tf_op jit(solution)/shard_map/pallas_call | solution.py:464
  43.6 0.0 collective-permute-done.6.q1
  43.6 0.0 collective-permute-done.7.q2
  43.6 0.0 collective-permute-done.8.q3
  43.6 4.7 %shard_map.135 = (bf16[512,512]{1,0:T(8,128)(2,1)}, bf16[512,512]{1,0:T(8,128)(2,1)}, bf16[256,1024]{1,0:T(8,128)(2,1)}, bf16[256,1024]{1,0:T(8,128)(2,1)}, bf16[4,128,1024]{2,1,0:T(8,128)(2,1)}) custom-call(s32[4]{0:T(128)} %pad_add_fusion.at_ref, bf16[128,256]{1,0:T(8,128)(2,1)} %get-tuple-element.94.q0, bf16[128,256]{1,0:T(8,128)(2,1)} %collective-permute-done.6.q1, ...), custom_call_target="tpu_custom_call" | custom-call | flops 1 | bytes 1 | tf_op jit(solution)/shard_map/pallas_call | solution.py:364
  48.3 6.6 %shard_map.136 = bf16[256,4096]{1,0:T(8,128)(2,1)} custom-call(s32[4]{0:T(128)} %pad_add_fusion.at_ref, bf16[256,1024]{1,0:T(8,128)(2,1)} %get-tuple-element.102.x_ref, bf16[4096,1024]{1,0:T(8,128)(2,1)} %w_ref.7), custom_call_target="tpu_custom_call" | custom-call | flops 1 | bytes 1 | tf_op jit(solution)/shard_map/pallas_call | solution.py:598
  54.9 2.4 %collective-permute-start.10 = (bf16[256,4096]{1,0:T(8,128)(2,1)}, bf16[256,4096]{1,0:T(8,128)(2,1)}, u32[]{:S(2)}, u32[]{:S(2)}) collective-permute-start(bf16[256,4096]{1,0:T(8,128)(2,1)} %shard_map.136), channel_id=1, source_target_pairs={{0,1},{1,0},{2,3},{3,2},{4,5},{5,4},{6,7},{7,6},{8,9},{9,8},{10,11... | collective-permute-start | bytes 6291464 | tf_op jit(solution)/shard_map/ppermute | solution.py:44
  57.2 4.9 %collective-permute-done.9.got_ref = bf16[512,512]{1,0:T(8,128)(2,1)} collective-permute-done((bf16[512,512]{1,0:T(8,128)(2,1)}, bf16[512,512]{1,0:T(8,128)(2,1)}, u32[]{:S(2)}, u32[]{:S(2)}) %collective-permute-start.9) | collective-permute-done | bytes 524320 | tf_op jit(solution)/shard_map/ppermute | solution.py:44
  62.1 4.4 %shard_map.137 = (bf16[2,256,1024]{2,1,0:T(8,128)(2,1)}, bf16[2,256,1024]{2,1,0:T(8,128)(2,1)}) custom-call(s32[4]{0:T(128)} %pad_add_fusion.at_ref, bf16[512,4096]{1,0:T(8,128)(2,1)} %second_ref.1, bf16[512,4096]{1,0:T(8,128)(2,1)} %second_ref.1, bf16[512,512]{1,0:T(8,128)(2,1)} %get-tuple-element.106.keep_ref, bf16[512,512]{1,0:T(8,128)(2,1)} %collective-permute-done.9.got_ref), custom_call_target="tpu_custom_call" | custom-call | flops 1 | bytes 1 | tf_op jit(solution)/shard_map/pallas_call | solution.py:513
  66.5 0.0 collective-permute-start.11
  66.5 2.7 %collective-permute-start.12 = (bf16[2,256,1024]{2,1,0:T(8,128)(2,1)}, bf16[2,256,1024]{2,1,0:T(8,128)(2,1)}, u32[]{:S(2)}, u32[]{:S(2)}) collective-permute-start(bf16[2,256,1024]{2,1,0:T(8,128)(2,1)} %get-tuple-element.105), channel_id=1, source_target_pairs={{0,24},{1,97},{2,26},{3,99},{4,28},{5,101},{6,30},{7,103},{8,0},{9... | collective-permute-start | bytes 3145736 | tf_op jit(solution)/shard_map/ppermute | solution.py:44
  69.2 4.4 %shard_map.138 = (bf16[2,256,1024]{2,1,0:T(8,128)(2,1)}, bf16[2,256,1024]{2,1,0:T(8,128)(2,1)}) custom-call(s32[4]{0:T(128)} %pad_add_fusion.at_ref, bf16[512,4096]{1,0:T(8,128)(2,1)} %second_ref.1, bf16[512,4096]{1,0:T(8,128)(2,1)} %second_ref.1, bf16[512,512]{1,0:T(8,128)(2,1)} %get-tuple-element.106.keep_ref, bf16[512,512]{1,0:T(8,128)(2,1)} %collective-permute-done.9.got_ref), custom_call_target="tpu_custom_call" | custom-call | flops 1 | bytes 1 | tf_op jit(solution)/shard_map/pallas_call | solution.py:513
  73.6 0.0 collective-permute-done.10.add_ref
  73.6 7.4 %shard_map.139 = (bf16[64,4096]{1,0:T(8,128)(2,1)}, bf16[64,4096]{1,0:T(8,128)(2,1)}, bf16[32,4096]{1,0:T(8,128)(2,1)}, bf16[32,4096]{1,0:T(8,128)(2,1)}, f32[64,4096]{1,0:T(8,128)}) custom-call(s32[4]{0:T(128)} %pad_add_fusion.at_ref, bf16[256,1024]{1,0:T(8,128)(2,1)} %get-tuple-element.109.x_ref, bf16[4096,1024]{1,0:T(8,128)(2,1)} %w_ref.7, ...), custom_call_target="tpu_custom_call" | custom-call | flops 1 | bytes 1 | tf_op jit(solution)/shard_map/pallas_call | solution.py:632
  80.9 2.5 %collective-permute-start.18 = (bf16[64,4096]{1,0:T(8,128)(2,1)}, bf16[64,4096]{1,0:T(8,128)(2,1)}, u32[]{:S(2)}, u32[]{:S(2)}) collective-permute-start(bf16[64,4096]{1,0:T(8,128)(2,1)} %get-tuple-element.118), channel_id=1, source_target_pairs={{0,6},{1,7},{2,0},{3,1},{4,2},{5,3},{6,4},{7,5},{8,14},{9,15},{10,... | collective-permute-start | bytes 1572872 | tf_op jit(solution)/shard_map/ppermute | solution.py:44
  83.4 2.7 %collective-permute-start.15 = (bf16[2,256,1024]{2,1,0:T(8,128)(2,1)}, bf16[2,256,1024]{2,1,0:T(8,128)(2,1)}, u32[]{:S(2)}, u32[]{:S(2)}) collective-permute-start(bf16[2,256,1024]{2,1,0:T(8,128)(2,1)} %get-tuple-element.108), channel_id=1, source_target_pairs={{0,24},{1,97},{2,26},{3,99},{4,28},{5,101},{6,30},{7,103},{8,0},{9... | collective-permute-start | bytes 3145736 | tf_op jit(solution)/shard_map/ppermute | solution.py:44
  86.1 0.0 collective-permute-done.11.refs_0_
  86.1 4.8 %shard_map.140 = (bf16[2,256,1024]{2,1,0:T(8,128)(2,1)}, bf16[2,256,1024]{2,1,0:T(8,128)(2,1)}) custom-call(s32[4]{0:T(128)} %pad_add_fusion.at_ref, bf16[512,4096]{1,0:T(8,128)(2,1)} %second_ref.1, bf16[512,4096]{1,0:T(8,128)(2,1)} %second_ref.1, bf16[512,512]{1,0:T(8,128)(2,1)} %get-tuple-element.106.keep_ref, ...), custom_call_target="tpu_custom_call" | custom-call | flops 1 | bytes 1 | tf_op jit(solution)/shard_map/pallas_call | solution.py:513
  90.9 0.0 collective-permute-start.13
  90.9 2.7 %collective-permute-start.16 = (bf16[2,256,1024]{2,1,0:T(8,128)(2,1)}, bf16[2,256,1024]{2,1,0:T(8,128)(2,1)}, u32[]{:S(2)}, u32[]{:S(2)}) collective-permute-start(bf16[2,256,1024]{2,1,0:T(8,128)(2,1)} %get-tuple-element.114), channel_id=1, source_target_pairs={{0,24},{1,97},{2,26},{3,99},{4,28},{5,101},{6,30},{7,103},{8,0},{9... | collective-permute-start | bytes 3145736 | tf_op jit(solution)/shard_map/ppermute | solution.py:44
  93.6 0.4 collective-permute-done.18.from_above.above
  94.0 0.9 collective-permute-start.17
  94.9 7.8 %shard_map.141 = (f32[512,128]{1,0:T(8,128)}, f32[512,128]{1,0:T(8,128)}) custom-call(f32[4,128,16]{2,1,0:T(8,128)} %get-tuple-element.81.rel_ref, f32[4,16,128]{2,1,0:T(8,128)} %get-tuple-element.82.relt_ref, f32[512,16]{1,0:T(8,128)} %get-tuple-element.83.step_ref, bf16[512,128]{1,0:T(8,128)(2,1)} %bitcast.17, bf16[512,128]{1,0:T(8,128)(2,1)} %bitcast.20, ...), custom_call_target="tpu_custom_call" | custom-call | flops 1 | bytes 1 | tf_op jit(solution)/shard_map/pallas_call | solution.py:424
  102.7 5.4 %collective-permute-done.17.from_below.below = bf16[64,4096]{1,0:T(8,128)(2,1)} collective-permute-done((bf16[64,4096]{1,0:T(8,128)(2,1)}, bf16[64,4096]{1,0:T(8,128)(2,1)}, u32[]{:S(2)}, u32[]{:S(2)}) %collective-permute-start.17) | collective-permute-done | bytes 524320 | tf_op jit(solution)/shard_map/ppermute | solution.py:44
  108.1 2.1 %shard_map.142 = (bf16[32,4096]{1,0:T(8,128)(2,1)}, bf16[32,4096]{1,0:T(8,128)(2,1)}) custom-call(bf16[32,4096]{1,0:T(8,128)(2,1)} %get-tuple-element.115.up_keep, bf16[32,4096]{1,0:T(8,128)(2,1)} %get-tuple-element.116.down_keep, bf16[64,4096]{1,0:T(8,128)(2,1)} %collective-permute-done.17.from_below.below, ...), custom_call_target="tpu_custom_call" | custom-call | flops 1 | bytes 1 | tf_op jit(solution)/shard_map/pallas_call | solution.py:659
  110.2 1.2 collective-permute-start.20
  111.4 0.0 collective-permute-done.14.below_plain
  111.4 0.3 collective-permute-start.19
  111.7 0.0 collective-permute-done.15.above_plain
  111.7 0.0 collective-permute-done.13.below_add
  111.7 0.0 collective-permute-done.16.above_add
  111.7 8.0 %shard_map.143 = (bf16[256,512]{1,0:T(8,128)(2,1)}, bf16[256,512]{1,0:T(8,128)(2,1)}, bf16[256,512]{1,0:T(8,128)(2,1)}, f32[256,512]{1,0:T(8,128)}, bf16[256,512...) custom-call(s32[4]{0:T(128)} %pad_add_fusion.at_ref, ...), custom_call_target="tpu_custom_call" | custom-call | flops 1 | bytes 1 | tf_op jit(solution)/shard_map/pallas_call | solution.py:555
  119.7 4.0 %collective-permute-start.21 = (bf16[256,512]{1,0:T(8,128)(2,1)}, bf16[256,512]{1,0:T(8,128)(2,1)}, u32[]{:S(2)}, u32[]{:S(2)}) collective-permute-start(bf16[256,512]{1,0:T(8,128)(2,1)} %get-tuple-element.129), channel_id=1, source_target_pairs={{0,64},{1,17},{2,66},{3,19},{4,68},{5,21},{6,70},{7,23},{8,72},{9,... | collective-permute-start | bytes 786440 | tf_op jit(solution)/shard_map/ppermute | solution.py:44
  123.7 2.7 %collective-permute-start.23 = (bf16[256,512]{1,0:T(8,128)(2,1)}, bf16[256,512]{1,0:T(8,128)(2,1)}, u32[]{:S(2)}, u32[]{:S(2)}) collective-permute-start(bf16[256,512]{1,0:T(8,128)(2,1)} %get-tuple-element.131), channel_id=1, source_target_pairs={{0,96},{1,25},{2,98},{3,27},{4,100},{5,29},{6,102},{7,31},{8,104},... | collective-permute-start | bytes 786440 | tf_op jit(solution)/shard_map/ppermute | solution.py:44
  126.3 0.0 collective-permute-done.20.above_add
  126.3 2.2 %collective-permute-start.24 = (bf16[256,512]{1,0:T(8,128)(2,1)}, bf16[256,512]{1,0:T(8,128)(2,1)}, u32[]{:S(2)}, u32[]{:S(2)}) collective-permute-start(bf16[256,512]{1,0:T(8,128)(2,1)} %get-tuple-element.133), channel_id=1, source_target_pairs={{0,65},{1,16},{2,67},{3,18},{4,69},{5,20},{6,71},{7,22},{8,73},{9,... | collective-permute-start | bytes 786440 | tf_op jit(solution)/shard_map/ppermute | solution.py:44
  128.6 0.0 collective-permute-done.19.below_add
  128.6 0.0 collective-permute-start.25
  128.6 3.4 %collective-permute-start.26 = (bf16[256,512]{1,0:T(8,128)(2,1)}, bf16[256,512]{1,0:T(8,128)(2,1)}, u32[]{:S(2)}, u32[]{:S(2)}) collective-permute-start(bf16[256,512]{1,0:T(8,128)(2,1)} %get-tuple-element.135), channel_id=1, source_target_pairs={{0,97},{1,24},{2,99},{3,26},{4,101},{5,28},{6,103},{7,30},{8,105},... | collective-permute-start | bytes 786440 | tf_op jit(solution)/shard_map/ppermute | solution.py:44
  131.9 0.0 collective-permute-done.22.refs_1_
  131.9 1.6 %collective-permute-start.27 = (bf16[256,512]{1,0:T(8,128)(2,1)}, bf16[256,512]{1,0:T(8,128)(2,1)}, u32[]{:S(2)}, u32[]{:S(2)}) collective-permute-start(bf16[256,512]{1,0:T(8,128)(2,1)} %get-tuple-element.136), channel_id=1, source_target_pairs={{0,1},{1,0},{2,3},{3,2},{4,5},{5,4},{6,7},{7,6},{8,9},{9,8},{10,11... | collective-permute-start | bytes 786440 | tf_op jit(solution)/shard_map/ppermute | solution.py:44
  133.5 2.6 %shard_map.144 = bf16[64,4096]{1,0:T(8,128)(2,1)} custom-call(f32[64,4096]{1,0:T(8,128)} %get-tuple-element.137.own, bf16[64,4096]{1,0:T(8,128)(2,1)} %collective-permute-done.17.from_below.below, bf16[64,4096]{1,0:T(8,128)(2,1)} %collective-permute-done.18.from_above.above, bf16[32,4096]{1,0:T(8,128)(2,1)} %collective-permute-done.19.below_add, ...), custom_call_target="tpu_custom_call" | custom-call | flops 1 | bytes 1 | tf_op jit(solution)/shard_map/pallas_call | solution.py:680
  136.1 2.6 %collective-permute-done.25.refs_5_ = bf16[256,512]{1,0:T(8,128)(2,1)} collective-permute-done((bf16[256,512]{1,0:T(8,128)(2,1)}, bf16[256,512]{1,0:T(8,128)(2,1)}, u32[]{:S(2)}, u32[]{:S(2)}) %collective-permute-start.25) | collective-permute-done | bytes 262176 | tf_op jit(solution)/shard_map/ppermute | solution.py:44
  138.7 0.0 collective-permute-done.26.refs_6_
  138.7 2.7 %shard_map.145 = bf16[256,1024]{1,0:T(8,128)(2,1)} custom-call(s32[4]{0:T(128)} %pad_add_fusion.at_ref, bf16[256,512]{1,0:T(8,128)(2,1)} %collective-permute-done.21.refs_0_, bf16[256,512]{1,0:T(8,128)(2,1)} %collective-permute-done.22.refs_1_, bf16[256,512]{1,0:T(8,128)(2,1)} %collective-permute-done.23.refs_2_, f32[256,512]{1,0:T(8,128)} %get-tuple-element.132.refs_3_, ...), custom_call_target="tpu_custom_call" | custom-call | flops 1 | bytes 1 | tf_op jit(solution)/shard_map/pallas_call | solution.py:581
  (10 shorter events, 0.0 us)
Async XLA Ops:
  5.7 11.5 %collective-permute-start = (bf16[272,256]{1,0:T(8,128)(2,1)}, bf16[272,256]{1,0:T(8,128)(2,1)}, u32[]{:S(2)}, u32[]{:S(2)}) collective-permute-start(bf16[272,256]{1,0:T(8,128)(2,1)} %get-tuple-element.73), channel_id=1, source_target_pairs={{0,8},{1,9},{2,10},{3,11},{4,12},{5,13},{6,14},{7,15},{8,16},{9,17... | collective-permute-start | bytes 417800 | tf_op jit(solution)/shard_map/ppermute | solution.py:44
  7.8 9.4 %collective-permute-start.1 = (bf16[272,256]{1,0:T(8,128)(2,1)}, bf16[272,256]{1,0:T(8,128)(2,1)}, u32[]{:S(2)}, u32[]{:S(2)}) collective-permute-start(bf16[272,256]{1,0:T(8,128)(2,1)} %get-tuple-element.74), channel_id=1, source_target_pairs={{0,16},{1,17},{2,18},{3,19},{4,20},{5,21},{6,22},{7,23},{8,24},{9,... | collective-permute-start | bytes 417800 | tf_op jit(solution)/shard_map/ppermute | solution.py:44
  10.4 6.8 %collective-permute-start.2 = (bf16[272,256]{1,0:T(8,128)(2,1)}, bf16[272,256]{1,0:T(8,128)(2,1)}, u32[]{:S(2)}, u32[]{:S(2)}) collective-permute-start(bf16[272,256]{1,0:T(8,128)(2,1)} %get-tuple-element.75), channel_id=1, source_target_pairs={{0,24},{1,25},{2,26},{3,27},{4,28},{5,29},{6,30},{7,31},{8,0},{9,1... | collective-permute-start | bytes 417800 | tf_op jit(solution)/shard_map/ppermute | solution.py:44
  19.1 9.3 %collective-permute-start.5 = (bf16[272,256]{1,0:T(8,128)(2,1)}, bf16[272,256]{1,0:T(8,128)(2,1)}, u32[]{:S(2)}, u32[]{:S(2)}) collective-permute-start(bf16[272,256]{1,0:T(8,128)(2,1)} %shard_map.131.b0), channel_id=1, source_target_pairs={{0,96},{1,97},{2,98},{3,99},{4,100},{5,101},{6,102},{7,103},{8,104... | collective-permute-start | bytes 417800 | tf_op jit(solution)/shard_map/ppermute | solution.py:44
  22.9 5.8 %collective-permute-start.4 = (bf16[272,256]{1,0:T(8,128)(2,1)}, bf16[272,256]{1,0:T(8,128)(2,1)}, u32[]{:S(2)}, u32[]{:S(2)}) collective-permute-start(bf16[272,256]{1,0:T(8,128)(2,1)} %shard_map.131.b0), channel_id=1, source_target_pairs={{0,64},{1,65},{2,66},{3,67},{4,68},{5,69},{6,70},{7,71},{8,72},{9,... | collective-permute-start | bytes 417800 | tf_op jit(solution)/shard_map/ppermute | solution.py:44
  22.9 9.4 %collective-permute-start.3 = (bf16[272,256]{1,0:T(8,128)(2,1)}, bf16[272,256]{1,0:T(8,128)(2,1)}, u32[]{:S(2)}, u32[]{:S(2)}) collective-permute-start(bf16[272,256]{1,0:T(8,128)(2,1)} %shard_map.131.b0), channel_id=1, source_target_pairs={{0,32},{1,33},{2,34},{3,35},{4,36},{5,37},{6,38},{7,39},{8,40},{9,... | collective-permute-start | bytes 417800 | tf_op jit(solution)/shard_map/ppermute | solution.py:44
  34.5 9.1 %collective-permute-start.6 = (bf16[128,256]{1,0:T(8,128)(2,1)}, bf16[128,256]{1,0:T(8,128)(2,1)}, u32[]{:S(2)}, u32[]{:S(2)}) collective-permute-start(bf16[128,256]{1,0:T(8,128)(2,1)} %get-tuple-element.90), channel_id=1, source_target_pairs={{0,8},{1,9},{2,10},{3,11},{4,12},{5,13},{6,14},{7,15},{8,16},{9,17... | collective-permute-start | bytes 196616 | tf_op jit(solution)/shard_map/ppermute | solution.py:44
  35.4 8.2 %collective-permute-start.7 = (bf16[128,256]{1,0:T(8,128)(2,1)}, bf16[128,256]{1,0:T(8,128)(2,1)}, u32[]{:S(2)}, u32[]{:S(2)}) collective-permute-start(bf16[128,256]{1,0:T(8,128)(2,1)} %get-tuple-element.91), channel_id=1, source_target_pairs={{0,16},{1,17},{2,18},{3,19},{4,20},{5,21},{6,22},{7,23},{8,24},{9,... | collective-permute-start | bytes 196616 | tf_op jit(solution)/shard_map/ppermute | solution.py:44
  37.6 5.9 %collective-permute-start.8 = (bf16[128,256]{1,0:T(8,128)(2,1)}, bf16[128,256]{1,0:T(8,128)(2,1)}, u32[]{:S(2)}, u32[]{:S(2)}) collective-permute-start(bf16[128,256]{1,0:T(8,128)(2,1)} %get-tuple-element.92), channel_id=1, source_target_pairs={{0,24},{1,25},{2,26},{3,27},{4,28},{5,29},{6,30},{7,31},{8,0},{9,1... | collective-permute-start | bytes 196616 | tf_op jit(solution)/shard_map/ppermute | solution.py:44
  54.9 18.7 %collective-permute-start.10 = (bf16[256,4096]{1,0:T(8,128)(2,1)}, bf16[256,4096]{1,0:T(8,128)(2,1)}, u32[]{:S(2)}, u32[]{:S(2)}) collective-permute-start(bf16[256,4096]{1,0:T(8,128)(2,1)} %shard_map.136), channel_id=1, source_target_pairs={{0,1},{1,0},{2,3},{3,2},{4,5},{5,4},{6,7},{7,6},{8,9},{9,8},{10,11... | collective-permute-start | bytes 6291464 | tf_op jit(solution)/shard_map/ppermute | solution.py:44
  57.2 4.9 %collective-permute-start.9 = (bf16[512,512]{1,0:T(8,128)(2,1)}, bf16[512,512]{1,0:T(8,128)(2,1)}, u32[]{:S(2)}, u32[]{:S(2)}) collective-permute-start(bf16[512,512]{1,0:T(8,128)(2,1)} %get-tuple-element.101), channel_id=1, source_target_pairs={{0,1},{1,0},{2,3},{3,2},{4,5},{5,4},{6,7},{7,6},{8,9},{9,8},{10,11... | collective-permute-start | bytes 1572872 | tf_op jit(solution)/shard_map/ppermute | solution.py:44
  66.5 19.6 %collective-permute-start.11 = (bf16[2,256,1024]{2,1,0:T(8,128)(2,1)}, bf16[2,256,1024]{2,1,0:T(8,128)(2,1)}, u32[]{:S(2)}, u32[]{:S(2)}) collective-permute-start(bf16[2,256,1024]{2,1,0:T(8,128)(2,1)} %get-tuple-element.104), channel_id=1, source_target_pairs={{0,8},{1,33},{2,10},{3,35},{4,12},{5,37},{6,14},{7,39},{8,16},{9,4... | collective-permute-start | bytes 3145736 | tf_op jit(solution)/shard_map/ppermute | solution.py:44
  66.5 19.6 %collective-permute-start.12 = (bf16[2,256,1024]{2,1,0:T(8,128)(2,1)}, bf16[2,256,1024]{2,1,0:T(8,128)(2,1)}, u32[]{:S(2)}, u32[]{:S(2)}) collective-permute-start(bf16[2,256,1024]{2,1,0:T(8,128)(2,1)} %get-tuple-element.105), channel_id=1, source_target_pairs={{0,24},{1,97},{2,26},{3,99},{4,28},{5,101},{6,30},{7,103},{8,0},{9... | collective-permute-start | bytes 3145736 | tf_op jit(solution)/shard_map/ppermute | solution.py:44
  80.9 13.1 %collective-permute-start.18 = (bf16[64,4096]{1,0:T(8,128)(2,1)}, bf16[64,4096]{1,0:T(8,128)(2,1)}, u32[]{:S(2)}, u32[]{:S(2)}) collective-permute-start(bf16[64,4096]{1,0:T(8,128)(2,1)} %get-tuple-element.118), channel_id=1, source_target_pairs={{0,6},{1,7},{2,0},{3,1},{4,2},{5,3},{6,4},{7,5},{8,14},{9,15},{10,... | collective-permute-start | bytes 1572872 | tf_op jit(solution)/shard_map/ppermute | solution.py:44
  83.4 28.0 %collective-permute-start.14 = (bf16[2,256,1024]{2,1,0:T(8,128)(2,1)}, bf16[2,256,1024]{2,1,0:T(8,128)(2,1)}, u32[]{:S(2)}, u32[]{:S(2)}) collective-permute-start(bf16[2,256,1024]{2,1,0:T(8,128)(2,1)} %get-tuple-element.107), channel_id=1, source_target_pairs={{0,8},{1,33},{2,10},{3,35},{4,12},{5,37},{6,14},{7,39},{8,16},{9,4... | collective-permute-start | bytes 3145736 | tf_op jit(solution)/shard_map/ppermute | solution.py:44
  83.4 28.2 %collective-permute-start.15 = (bf16[2,256,1024]{2,1,0:T(8,128)(2,1)}, bf16[2,256,1024]{2,1,0:T(8,128)(2,1)}, u32[]{:S(2)}, u32[]{:S(2)}) collective-permute-start(bf16[2,256,1024]{2,1,0:T(8,128)(2,1)} %get-tuple-element.108), channel_id=1, source_target_pairs={{0,24},{1,97},{2,26},{3,99},{4,28},{5,101},{6,30},{7,103},{8,0},{9... | collective-permute-start | bytes 3145736 | tf_op jit(solution)/shard_map/ppermute | solution.py:44
  90.9 20.8 %collective-permute-start.13 = (bf16[2,256,1024]{2,1,0:T(8,128)(2,1)}, bf16[2,256,1024]{2,1,0:T(8,128)(2,1)}, u32[]{:S(2)}, u32[]{:S(2)}) collective-permute-start(bf16[2,256,1024]{2,1,0:T(8,128)(2,1)} %get-tuple-element.113), channel_id=1, source_target_pairs={{0,8},{1,33},{2,10},{3,35},{4,12},{5,37},{6,14},{7,39},{8,16},{9,4... | collective-permute-start | bytes 3145736 | tf_op jit(solution)/shard_map/ppermute | solution.py:44
  90.9 20.8 %collective-permute-start.16 = (bf16[2,256,1024]{2,1,0:T(8,128)(2,1)}, bf16[2,256,1024]{2,1,0:T(8,128)(2,1)}, u32[]{:S(2)}, u32[]{:S(2)}) collective-permute-start(bf16[2,256,1024]{2,1,0:T(8,128)(2,1)} %get-tuple-element.114), channel_id=1, source_target_pairs={{0,24},{1,97},{2,26},{3,99},{4,28},{5,101},{6,30},{7,103},{8,0},{9... | collective-permute-start | bytes 3145736 | tf_op jit(solution)/shard_map/ppermute | solution.py:44
  94.0 14.1 %collective-permute-start.17 = (bf16[64,4096]{1,0:T(8,128)(2,1)}, bf16[64,4096]{1,0:T(8,128)(2,1)}, u32[]{:S(2)}, u32[]{:S(2)}) collective-permute-start(bf16[64,4096]{1,0:T(8,128)(2,1)} %get-tuple-element.117), channel_id=1, source_target_pairs={{0,2},{1,3},{2,4},{3,5},{4,6},{5,7},{6,0},{7,1},{8,10},{9,11},{10,... | collective-permute-start | bytes 1572872 | tf_op jit(solution)/shard_map/ppermute | solution.py:44
  110.2 16.1 %collective-permute-start.20 = (bf16[32,4096]{1,0:T(8,128)(2,1)}, bf16[32,4096]{1,0:T(8,128)(2,1)}, u32[]{:S(2)}, u32[]{:S(2)}) collective-permute-start(bf16[32,4096]{1,0:T(8,128)(2,1)} %get-tuple-element.138), channel_id=1, source_target_pairs={{0,6},{1,7},{2,0},{3,1},{4,2},{5,3},{6,4},{7,5},{8,14},{9,15},{10,... | collective-permute-start | bytes 786440 | tf_op jit(solution)/shard_map/ppermute | solution.py:44
  111.4 17.2 %collective-permute-start.19 = (bf16[32,4096]{1,0:T(8,128)(2,1)}, bf16[32,4096]{1,0:T(8,128)(2,1)}, u32[]{:S(2)}, u32[]{:S(2)}) collective-permute-start(bf16[32,4096]{1,0:T(8,128)(2,1)} %get-tuple-element.124), channel_id=1, source_target_pairs={{0,2},{1,3},{2,4},{3,5},{4,6},{5,7},{6,0},{7,1},{8,10},{9,11},{10,... | collective-permute-start | bytes 786440 | tf_op jit(solution)/shard_map/ppermute | solution.py:44
  119.7 8.9 %collective-permute-start.21 = (bf16[256,512]{1,0:T(8,128)(2,1)}, bf16[256,512]{1,0:T(8,128)(2,1)}, u32[]{:S(2)}, u32[]{:S(2)}) collective-permute-start(bf16[256,512]{1,0:T(8,128)(2,1)} %get-tuple-element.129), channel_id=1, source_target_pairs={{0,64},{1,17},{2,66},{3,19},{4,68},{5,21},{6,70},{7,23},{8,72},{9,... | collective-permute-start | bytes 786440 | tf_op jit(solution)/shard_map/ppermute | solution.py:44
  123.7 8.3 %collective-permute-start.22 = (bf16[256,512]{1,0:T(8,128)(2,1)}, bf16[256,512]{1,0:T(8,128)(2,1)}, u32[]{:S(2)}, u32[]{:S(2)}) collective-permute-start(bf16[256,512]{1,0:T(8,128)(2,1)} %get-tuple-element.130), channel_id=1, source_target_pairs={{0,32},{1,9},{2,34},{3,11},{4,36},{5,13},{6,38},{7,15},{8,40},{9,1... | collective-permute-start | bytes 786440 | tf_op jit(solution)/shard_map/ppermute | solution.py:44
  123.7 12.5 %collective-permute-start.23 = (bf16[256,512]{1,0:T(8,128)(2,1)}, bf16[256,512]{1,0:T(8,128)(2,1)}, u32[]{:S(2)}, u32[]{:S(2)}) collective-permute-start(bf16[256,512]{1,0:T(8,128)(2,1)} %get-tuple-element.131), channel_id=1, source_target_pairs={{0,96},{1,25},{2,98},{3,27},{4,100},{5,29},{6,102},{7,31},{8,104},... | collective-permute-start | bytes 786440 | tf_op jit(solution)/shard_map/ppermute | solution.py:44
  126.3 9.8 %collective-permute-start.24 = (bf16[256,512]{1,0:T(8,128)(2,1)}, bf16[256,512]{1,0:T(8,128)(2,1)}, u32[]{:S(2)}, u32[]{:S(2)}) collective-permute-start(bf16[256,512]{1,0:T(8,128)(2,1)} %get-tuple-element.133), channel_id=1, source_target_pairs={{0,65},{1,16},{2,67},{3,18},{4,69},{5,20},{6,71},{7,22},{8,73},{9,... | collective-permute-start | bytes 786440 | tf_op jit(solution)/shard_map/ppermute | solution.py:44
  128.6 10.1 %collective-permute-start.25 = (bf16[256,512]{1,0:T(8,128)(2,1)}, bf16[256,512]{1,0:T(8,128)(2,1)}, u32[]{:S(2)}, u32[]{:S(2)}) collective-permute-start(bf16[256,512]{1,0:T(8,128)(2,1)} %get-tuple-element.134), channel_id=1, source_target_pairs={{0,33},{1,8},{2,35},{3,10},{4,37},{5,12},{6,39},{7,14},{8,41},{9,1... | collective-permute-start | bytes 786440 | tf_op jit(solution)/shard_map/ppermute | solution.py:44
  128.6 10.1 %collective-permute-start.26 = (bf16[256,512]{1,0:T(8,128)(2,1)}, bf16[256,512]{1,0:T(8,128)(2,1)}, u32[]{:S(2)}, u32[]{:S(2)}) collective-permute-start(bf16[256,512]{1,0:T(8,128)(2,1)} %get-tuple-element.135), channel_id=1, source_target_pairs={{0,97},{1,24},{2,99},{3,26},{4,101},{5,28},{6,103},{7,30},{8,105},... | collective-permute-start | bytes 786440 | tf_op jit(solution)/shard_map/ppermute | solution.py:44
  131.9 6.8 %collective-permute-start.27 = (bf16[256,512]{1,0:T(8,128)(2,1)}, bf16[256,512]{1,0:T(8,128)(2,1)}, u32[]{:S(2)}, u32[]{:S(2)}) collective-permute-start(bf16[256,512]{1,0:T(8,128)(2,1)} %get-tuple-element.136), channel_id=1, source_target_pairs={{0,1},{1,0},{2,3},{3,2},{4,5},{5,4},{6,7},{7,6},{8,9},{9,8},{10,11... | collective-permute-start | bytes 786440 | tf_op jit(solution)/shard_map/ppermute | solution.py:44

commit v4 on v3

--- a/solution.py
+++ b/solution.py
@@ -18,6 +18,8 @@
 BF16 = jnp.bfloat16
 ORDER = (2, 1, 3, 0)
 VMEM_LIMIT = 64 * 1024 * 1024
+ROOMY_LIMIT = 61 * 1024 * 1024
+SMALL_LIMIT = 8 * 1024 * 1024
 
 
 def params(limit=VMEM_LIMIT):
@@ -52,6 +54,10 @@
     return routed(block, lambda z, y, x, core: (z, y, x + dx, core + dc))
 
 
+def x_hop(block, d):
+    return routed(block, lambda z, y, x, core: (z, y, x + (d if core == 0 else -d), core))
+
+
 def first_hop(block, d, to_other):
     def move(z, y, x, core):
         core = core ^ to_other
@@ -122,10 +128,10 @@
 
 
 def pre_kernel(
-    at_ref, dlog_ref, stept_ref, grad_ref, read_ref, fork_ref,
+    dlog_ref, stept_ref, grad_ref, read_ref, fork_ref,
     rel_ref, relt_ref, step_ref, scaled_ref, state_ref, m0, m1, m2, m3, message,
 ):
-    y = at_ref[1]
+    y = lax.rem(lax.axis_index("ctx"), SIDE)
     row = lax.broadcasted_iota(jnp.int32, (CHUNK, CHUNK), 0)
     col = lax.broadcasted_iota(jnp.int32, (CHUNK, CHUNK), 1)
     lower = jnp.where(row >= col, 1.0, 0.0).astype(BF16)
@@ -168,7 +174,7 @@
         out[...] = message[:, pl.ds(start, QUARTER)]
 
 
-def pre(at, decay_log, stept, out_grad, reads, fork_grad):
+def pre(decay_log, stept, out_grad, reads, fork_grad):
     length = CHUNKS * CHUNK
     sent = jax.ShapeDtypeStruct((256 + TAIL, QUARTER), BF16)
     return pl.pallas_call(
@@ -183,7 +189,6 @@
         ]
         + [sent] * 4,
         in_specs=[
-            whole(pltpu.SMEM),
             whole(pltpu.SMEM),
             full_block(HEADS, length),
             full_block(length, WIDE),
@@ -201,7 +206,7 @@
         scratch_shapes=[pltpu.VMEM((256 + TAIL, WIDE), BF16)],
         compiler_params=params(),
         cost_estimate=COST,
-    )(at, decay_log, stept, out_grad, reads, fork_grad)
+    )(decay_log, stept, out_grad, reads, fork_grad)
 
 
 def group_kernel(at_ref, a0, a1, a2, a3, out_ref, stack):
@@ -226,12 +231,11 @@
 def group(at, arrived):
     return pl.pallas_call(
         group_kernel,
-        grid=(1,),
         out_shape=jax.ShapeDtypeStruct((256 + TAIL, QUARTER), BF16),
-        in_specs=[whole(pltpu.SMEM)] + [full_block(256 + TAIL, QUARTER)] * 4,
-        out_specs=full_block(256 + TAIL, QUARTER),
+        in_specs=[whole(pltpu.SMEM)] + [whole()] * 4,
+        out_specs=whole(),
         scratch_shapes=[pltpu.VMEM((SIDE, 256 + TAIL, QUARTER), BF16)],
-        compiler_params=params(),
+        compiler_params=params(SMALL_LIMIT),
         cost_estimate=COST,
     )(at, *arrived)
 
@@ -264,16 +268,15 @@
 def carry_over(at, first, second):
     return pl.pallas_call(
         carry_kernel,
-        grid=(1,),
         out_shape=[jax.ShapeDtypeStruct((128, QUARTER), BF16)] * 4,
-        in_specs=[whole(pltpu.SMEM)] + [full_block(256 + TAIL, QUARTER)] * 8,
-        out_specs=[full_block(128, QUARTER)] * 4,
+        in_specs=[whole(pltpu.SMEM)] + [whole()] * 8,
+        out_specs=[whole()] * 4,
         scratch_shapes=[
             pltpu.VMEM((SIDE, 256 + TAIL, QUARTER), BF16),
             pltpu.VMEM((SIDE, 256 + TAIL, QUARTER), BF16),
             pltpu.VMEM((SIDE, 128, QUARTER), BF16),
         ],
-        compiler_params=params(),
+        compiler_params=params(SMALL_LIMIT),
         cost_estimate=COST,
     )(at, *first, *second)
 
@@ -316,14 +319,14 @@
             pl.BlockSpec((rows, WIDE), by_two),
         ],
         out_specs=pl.BlockSpec((rows, WIDE), by_two),
-        compiler_params=params(),
+        compiler_params=params(ROOMY_LIMIT),
         cost_estimate=COST,
     )(skip_gain, rel, relt, step_size, reads, writes, out_grad)
 
 
 def x_kernel(
     at_ref, q0, q1, q2, q3, state_ref, rel_ref, step_ref, write_ref, base_ref,
-    keep_ref, give_ref, mine_ref, theirs_ref, full_ref, carried, x_ref,
+    keep_ref, give_ref, mine_ref, full_ref, carried, x_ref,
 ):
     y, core = at_ref[1], at_ref[3]
     matrix = spread_matrix()
@@ -355,12 +358,14 @@
             give_ref[here] = x_ref[c, k, :, pl.ds(other, 512)]
         there = slice(c * 64, c * 64 + 64)
         mine_ref[there] = x_ref[c, core]
-        theirs_ref[there] = x_ref[c, 1 - core]
+        for k in range(2):
+            there = slice(512 + k * 256 + c * 64, 512 + k * 256 + c * 64 + 64)
+            give_ref[there] = x_ref[c, 1 - core, :, k * 512 : k * 512 + 512]
 
 
 def x_final(at, quarters, states, rel, step_size, writes, base):
     rows = CHUNKS * CHUNK
-    half, rest = (rows, 512), (rows // 2, WIDE)
+    shapes = (rows, 512), (2 * rows, 512), (rows // 2, WIDE)
     return pl.pallas_call(
         x_kernel,
         grid=(1,),
@@ -373,23 +378,20 @@
             full_block(rows, 128),
             full_block(rows, WIDE),
         ],
-        out_specs=[full_block(*half)] * 2 + [full_block(*rest)] * 2 + [full_block(CHUNKS, 128, WIDE)],
+        out_specs=[full_block(*shape) for shape in shapes] + [full_block(CHUNKS, 128, WIDE)],
         scratch_shapes=[pltpu.VMEM((128, WIDE), BF16), pltpu.VMEM((CHUNKS, 2, 64, WIDE), BF16)],
-        out_shape=[jax.ShapeDtypeStruct(half, BF16)] * 2
-        + [jax.ShapeDtypeStruct(rest, BF16)] * 2
+        out_shape=[jax.ShapeDtypeStruct(shape, BF16) for shape in shapes]
         + [jax.ShapeDtypeStruct((CHUNKS, 128, WIDE), BF16)],
-        compiler_params=params(),
+        compiler_params=params(ROOMY_LIMIT),
         cost_estimate=COST,
     )(at, *quarters, states, rel, step_size, writes, base)
 
 
 def vector_kernel(
     rel_ref, relt_ref, step_ref, read_ref, write_ref, grad_ref, scaled_ref, first_ref, second_ref,
-    full_ref, start_ref, wgrad_ref, rgrad_ref, state, inputs_ref,
+    full_ref, start_ref, wgrad_ref, rgrad_ref, state,
 ):
     matrix = spread_matrix()
-    inputs_ref[:, : WIDE // 2] = first_ref[...]
-    inputs_ref[:, WIDE // 2 :] = second_ref[...]
 
     @pl.when(pl.program_id(0) == 0)
     def _():
@@ -397,51 +399,69 @@
 
     row = lax.broadcasted_iota(jnp.int32, (CHUNK, CHUNK), 0)
     col = lax.broadcasted_iota(jnp.int32, (CHUNK, CHUNK), 1)
-    rel, relt, step = rel_ref[0], relt_ref[0], step_ref[...]
-    coupling = jnp.zeros((CHUNK, CHUNK), F32)
-    for pair in range(HEADS // 2):
-        at = slice(pair * 128, pair * 128 + 128)
-        grads = grad_ref[:, at]
-        inputs = inputs_ref[:, at]
-        for k in range(2):
-            h = 2 * pair + k
-            own = jnp.where((col >= 64) == (k == 1), inputs.astype(F32), 0.0).astype(BF16)
-            kernel = jnp.exp(jnp.minimum(relt[h : h + 1] - rel[:, h : h + 1], 0.0))
-            coupling = coupling + step[:, h : h + 1] * kernel * dot_nt(own, grads)
-    coupling = jnp.where(col >= row, coupling, 0.0).astype(BF16)
-    last = rel[CHUNK - 1 : CHUNK]
-    weights = spread(step * jnp.exp(last - rel), matrix)
-    weighted = (weights * inputs_ref[...].astype(F32)).astype(BF16)
-    wgrad_ref[...] = dot_nt(weighted, full_ref[0]) + dot(coupling, read_ref[...])
-    rgrad_ref[...] = dot_nt(scaled_ref[...], state[...].astype(BF16)) + dot_tn(
-        coupling, write_ref[...]
-    )
-    state[...] = spread_row(jnp.exp(last), matrix) * state[...] + dot_tn(write_ref[...], weighted)
+    later = jnp.where(col >= 64, 1.0, 0.0).astype(BF16)
+    for c in range(2):
+        here = slice(c * CHUNK, (c + 1) * CHUNK)
+        rel, relt, step = rel_ref[c], relt_ref[c], step_ref[here]
+        last = rel[CHUNK - 1 : CHUNK]
+        steps = spread(step, matrix)
+        weights = spread(step * jnp.exp(last - rel), matrix)
+        weighted, coupling = [], None
+        for half, inputs_ref in enumerate((first_ref, second_ref)):
+            inputs = inputs_ref[here].astype(F32)
+            wide = slice(half * 512, half * 512 + 512)
+            weighted.append((weights[:, wide] * inputs).astype(BF16))
+            stepped = (steps[:, wide] * inputs).astype(BF16)
+            for pair in range(HEADS // 4):
+                at = slice(pair * 128, pair * 128 + 128)
+                grads = grad_ref[here, half * 512 + pair * 128 : half * 512 + pair * 128 + 128].T
+                for k in range(2):
+                    h = half * HEADS // 2 + 2 * pair + k
+                    own = stepped[:, at] * (later if k == 1 else 1 - later)
+                    kernel = jnp.exp(jnp.minimum(relt[h : h + 1] - rel[:, h : h + 1], 0.0))
+                    term = kernel * dot(own, grads)
+                    coupling = term if coupling is None else coupling + term
+        coupling = jnp.where(col >= row, coupling, 0.0).astype(BF16)
+        full, scaled = full_ref[c], scaled_ref[here]
+        wgrad = dot(coupling, read_ref[here])
+        new_state = []
+        for half in range(2):
+            wide = slice(half * 512, half * 512 + 512)
+            wgrad = wgrad + dot_nt(weighted[half], full[:, wide])
+            new_state.append(dot_tn(write_ref[here], weighted[half]))
+        wgrad_ref[here] = wgrad
+        rgrad_ref[here] = dot_nt(scaled, state[...].astype(BF16)) + dot_tn(coupling, write_ref[here])
+        decay = spread_row(jnp.exp(last), matrix)
+        for half in range(2):
+            wide = slice(half * 512, half * 512 + 512)
+            state[:, wide] = decay[:, wide] * state[:, wide] + new_state[half]
 
 
 def vectors(rel, relt, step_size, reads, writes, out_grad, scaled, first, second, full, start_state):
-    by_chunk = lambda c: (c, 0)
+    by_two = lambda c: (c, 0)
+    by_first = lambda c: (c, 0, 0)
+    rows = 2 * CHUNK
     return pl.pallas_call(
         vector_kernel,
-        grid=(CHUNKS,),
+        grid=(CHUNKS // 2,),
         out_shape=[jax.ShapeDtypeStruct((CHUNKS * CHUNK, 128), F32)] * 2,
         in_specs=[
-            pl.BlockSpec((1, CHUNK, HEADS), lambda c: (c, 0, 0)),
-            pl.BlockSpec((1, HEADS, CHUNK), lambda c: (c, 0, 0)),
-            pl.BlockSpec((CHUNK, HEADS), by_chunk),
-            pl.BlockSpec((CHUNK, 128), by_chunk),
-            pl.BlockSpec((CHUNK, 128), by_chunk),
-            pl.BlockSpec((CHUNK, WIDE), by_chunk),
-            pl.BlockSpec((CHUNK, WIDE), by_chunk),
-            pl.BlockSpec((CHUNK, WIDE // 2), by_chunk),
-            pl.BlockSpec((CHUNK, WIDE // 2), by_chunk),
-            pl.BlockSpec((1, 128, WIDE), lambda c: (c, 0, 0)),
+            pl.BlockSpec((2, CHUNK, HEADS), by_first),
+            pl.BlockSpec((2, HEADS, CHUNK), by_first),
+            pl.BlockSpec((rows, HEADS), by_two),
+            pl.BlockSpec((rows, 128), by_two),
+            pl.BlockSpec((rows, 128), by_two),
+            pl.BlockSpec((rows, WIDE), by_two),
+            pl.BlockSpec((rows, WIDE), by_two),
+            pl.BlockSpec((rows, WIDE // 2), by_two),
+            pl.BlockSpec((rows, WIDE // 2), by_two),
+            pl.BlockSpec((2, 128, WIDE), by_first),
             pl.BlockSpec((WIDE, 128), lambda c: (0, 0)),
         ],
-        out_specs=[pl.BlockSpec((CHUNK, 128), by_chunk)] * 2,
-        scratch_shapes=[pltpu.VMEM((128, WIDE), F32), pltpu.VMEM((CHUNK, WIDE), BF16)],
-        compiler_params=params(),
-        cost_estimate=COST,
+        out_specs=[pl.BlockSpec((rows, 128), by_two)] * 2,
+        scratch_shapes=[pltpu.VMEM((128, WIDE), F32)],
+        compiler_params=params(),
+        cost_estimate=pl.CostEstimate(flops=50000000000, bytes_accessed=1, transcendentals=0),
     )(rel, relt, step_size, reads, writes, out_grad, scaled, first, second, full, start_state)
 
 
@@ -471,7 +491,7 @@
         ],
         out_specs=pl.BlockSpec((rows, wide), lambda i: (0, 0)),
         scratch_shapes=[pltpu.VMEM((rows, wide), F32)],
-        compiler_params=params(),
+        compiler_params=params(ROOMY_LIMIT),
         cost_estimate=COST,
     )(layer_input, proj_weight)
 
@@ -516,7 +536,7 @@
             num_scalar_prefetch=1,
             grid=(2,),
             in_specs=[columns_spec(up_to, up_parts), columns_spec(down_to, down_parts)]
-            + [full_block(rows, 512)] * 2
+            + [pl.BlockSpec((rows, 512), lambda g, s: (0, 0))] * 2
             + [block] * len(more),
             out_specs=[block] * 2,
         ),
@@ -526,46 +546,61 @@
     )(at, layer_input, layer_input, keep, got, *more)
 
 
-def own_kernel(
-    at_ref, first_ref, second_ref, keep_ref, got_ref,
-    below_add, below_plain, above_plain, above_add, *outs,
-):
+def own_kernel(at_ref, first_ref, second_ref, keep_ref, got_ref, below_plain, above_plain, out):
     g = pl.program_id(0)
     for k, cols in enumerate((first_ref, second_ref)):
         turned = cols[...].T
         for half, x_ref in enumerate((keep_ref, got_ref)):
             at = slice(512 * half, 512 * half + 512)
-            product = dot(turned, x_ref[...])
-            early, late = outs[SIDE * half + k], outs[SIDE * half + 2 + k]
-
-            @pl.when(g == 0)
-            def _():
-                total = product + below_add[k, :, at].astype(F32) + above_plain[k, :, at].astype(F32)
-                early[...] = total.astype(early.dtype)
-
-            @pl.when(g == 1)
-            def _():
-                total = product + below_plain[k, :, at].astype(F32) + above_add[k, :, at].astype(F32)
-                late[...] = total.astype(late.dtype)
-
-
-def own_product(at, layer_input, keep, got, arrived):
+            plain = jnp.where(g == 0, above_plain[k, :, at], below_plain[k, :, at])
+            out[k, :, at] = (dot(turned, x_ref[...]) + plain.astype(F32)).astype(BF16)
+
+
+def own_product(at, layer_input, keep, got, below_plain, above_plain):
     rows = layer_input.shape[0]
-    shape = lambda dtype: jax.ShapeDtypeStruct((256, 512), dtype)
     return pl.pallas_call(
         own_kernel,
         grid_spec=pltpu.PrefetchScalarGridSpec(
             num_scalar_prefetch=1,
             grid=(2,),
             in_specs=[columns_spec(0, (0, 2)), columns_spec(0, (1, 3))]
-            + [full_block(rows, 512)] * 2
-            + [full_block(2, 256, WIDE)] * 4,
-            out_specs=[full_block(256, 512)] * 8,
+            + [pl.BlockSpec((rows, 512), lambda g, s: (0, 0))] * 2
+            + [full_block(2, 256, WIDE)] * 2,
+            out_specs=pl.BlockSpec((2, 256, WIDE), lambda g, s: (g, 0, 0)),
         ),
+        out_shape=jax.ShapeDtypeStruct((4, 256, WIDE), BF16),
+        compiler_params=params(),
+        cost_estimate=COST,
+    )(at, layer_input, layer_input, keep, got, below_plain, above_plain)
+
+
+def total_kernel(own_ref, below_add, above_add, *outs):
+    g = pl.program_id(0)
+    for k in range(2):
+        for half in range(2):
+            at = slice(512 * half, 512 * half + 512)
+            early, late = outs[SIDE * half + k], outs[SIDE * half + 2 + k]
+
+            @pl.when(g == 0)
+            def _():
+                early[...] = (own_ref[k, :, at].astype(F32) + below_add[k, :, at].astype(F32)).astype(early.dtype)
+
+            @pl.when(g == 1)
+            def _():
+                late[...] = (own_ref[k, :, at].astype(F32) + above_add[k, :, at].astype(F32)).astype(late.dtype)
+
+
+def own_total(own, below_add, above_add):
+    shape = lambda dtype: jax.ShapeDtypeStruct((256, 512), dtype)
+    return pl.pallas_call(
+        total_kernel,
+        grid=(2,),
+        in_specs=[pl.BlockSpec((2, 256, WIDE), lambda g: (g, 0, 0))] + [full_block(2, 256, WIDE)] * 2,
+        out_specs=[full_block(256, 512)] * 8,
         out_shape=[shape(BF16)] * 3 + [shape(F32)] + [shape(BF16)] * 4,
         compiler_params=params(),
         cost_estimate=COST,
-    )(at, layer_input, layer_input, keep, got, *arrived)
+    )(own, below_add, above_add)
 
 
 def weight_kernel(scale, at_ref, *refs):
@@ -589,103 +624,72 @@
     )(at, *terms)
 
 
-def theirs_kernel(at_ref, x_ref, w_ref, out_ref):
+def input_kernel(x_ref, w_ref, out_ref):
     out_ref[...] = dot_nt(x_ref[...], w_ref[...]).astype(BF16)
 
 
-def theirs(at, x_rows, proj_weight):
+def input_product(x_rows, proj_weight):
     depth, tile = proj_weight.shape[0], 2048
     return pl.pallas_call(
-        theirs_kernel,
+        input_kernel,
+        grid=(depth // tile,),
+        in_specs=[full_block(256, WIDE), pl.BlockSpec((tile, WIDE), lambda i: (i, 0))],
+        out_specs=pl.BlockSpec((256, tile), lambda i: (0, i)),
+        out_shape=jax.ShapeDtypeStruct((256, depth), BF16),
+        compiler_params=params(),
+        cost_estimate=COST,
+    )(x_rows, proj_weight)
+
+
+def rest_kernel(at_ref, left_ref, right_ref, w_ref, part_ref, far, next_out, last_out, own, total):
+    x, core = at_ref[2], at_ref[3]
+    product = dot_nt(left_ref[...], w_ref[:, :512]) + dot_nt(right_ref[...], w_ref[:, 512:])
+    total[...] = (product + part_ref[...].astype(F32)).reshape(SIDE, 64, -1)
+    step = 1 - 2 * core
+    for d, out in ((2, far), (step, next_out), (-step, last_out), (0, own)):
+        out[...] = total[turn(x, d)].astype(out.dtype)
+
+
+def input_rest(at, got, other_weight, part):
+    depth, tile = other_weight.shape[0], 2048
+    out = pl.BlockSpec((64, tile), lambda i, s: (0, i))
+    shape = lambda dtype: jax.ShapeDtypeStruct((64, depth), dtype)
+    return pl.pallas_call(
+        rest_kernel,
         grid_spec=pltpu.PrefetchScalarGridSpec(
             num_scalar_prefetch=1,
             grid=(depth // tile,),
             in_specs=[
-                full_block(256, WIDE),
-                pl.BlockSpec((tile, WIDE), lambda i, s: (i, 0)),
-            ],
-            out_specs=pl.BlockSpec((256, tile), lambda i, s: (0, i)),
-        ),
-        out_shape=jax.ShapeDtypeStruct((256, depth), BF16),
-        compiler_params=params(),
-        cost_estimate=COST,
-    )(at, x_rows, proj_weight)
-
-
-def mine_kernel(at_ref, x_ref, w_ref, add_ref, up_out, down_out, up_keep, down_keep, own_out, total):
-    x = at_ref[2]
-    total[...] = (dot_nt(x_ref[...], w_ref[...]) + add_ref[...].astype(F32)).reshape(SIDE, 64, -1)
-    far, above, below = turn(x, 2), turn(x, 1), turn(x, -1)
-    up_out[0:32] = total[far, 0:32].astype(BF16)
-    up_out[32:64] = total[above, 32:64].astype(BF16)
-    up_keep[...] = total[above, 0:32].astype(BF16)
-    down_out[0:32] = total[far, 32:64].astype(BF16)
-    down_out[32:64] = total[below, 0:32].astype(BF16)
-    down_keep[...] = total[below, 32:64].astype(BF16)
-    own_out[...] = total[x]
-
-
-def mine(at, x_rows, proj_weight, add):
-    depth, tile = proj_weight.shape[0], 2048
-    out = lambda n: pl.BlockSpec((n, tile), lambda i, s: (0, i))
-    shape = lambda n, dtype: jax.ShapeDtypeStruct((n, depth), dtype)
-    return pl.pallas_call(
-        mine_kernel,
-        grid_spec=pltpu.PrefetchScalarGridSpec(
-            num_scalar_prefetch=1,
-            grid=(depth // tile,),
-            in_specs=[
-                full_block(256, WIDE),
+                pl.BlockSpec((256, 512), lambda i, s: (2, 0)),
+                pl.BlockSpec((256, 512), lambda i, s: (3, 0)),
                 pl.BlockSpec((tile, WIDE), lambda i, s: (i, 0)),
                 pl.BlockSpec((256, tile), lambda i, s: (0, i)),
             ],
-            out_specs=[out(64), out(64), out(32), out(32), out(64)],
+            out_specs=[out] * 4,
             scratch_shapes=[pltpu.VMEM((SIDE, 64, tile), F32)],
         ),
-        out_shape=[shape(64, BF16), shape(64, BF16), shape(32, BF16), shape(32, BF16), shape(64, F32)],
-        compiler_params=params(),
-        cost_estimate=COST,
-    )(at, x_rows, proj_weight, add)
-
-
-def add_kernel(up_keep, down_keep, from_below, from_above, up_out, down_out):
-    n = up_keep.shape[0]
-    up_out[...] = (up_keep[...].astype(F32) + from_below[0:n].astype(F32)).astype(BF16)
-    down_out[...] = (down_keep[...].astype(F32) + from_above[0:n].astype(F32)).astype(BF16)
-
-
-def add_two(up_keep, down_keep, from_below, from_above):
-    n, depth = up_keep.shape
-    return pl.pallas_call(
-        add_kernel,
-        grid=(1,),
-        out_shape=[jax.ShapeDtypeStruct((n, depth), BF16)] * 2,
-        in_specs=[full_block(n, depth)] * 4,
-        out_specs=[full_block(n, depth)] * 2,
-        compiler_params=params(),
-        cost_estimate=COST,
-    )(up_keep, down_keep, from_below, from_above)
-
-
-def input_kernel(own, below, above, below_add, above_add, out):
-    top = own[0:32] + below_add[...].astype(F32) + above[32:64].astype(F32)
-    bottom = own[32:64] + below[32:64].astype(F32) + above_add[...].astype(F32)
-    out[0:32] = top.astype(BF16)
-    out[32:64] = bottom.astype(BF16)
-
-
-def input_final(own, below, above, below_add, above_add):
+        out_shape=[shape(BF16), shape(BF16), shape(BF16), shape(F32)],
+        compiler_params=params(),
+        cost_estimate=COST,
+    )(at, got, got, other_weight, part)
+
+
+def sum_kernel(own, first, second, third, out):
+    total = own[...] + first[...].astype(F32) + second[...].astype(F32) + third[...].astype(F32)
+    out[...] = total.astype(BF16)
+
+
+def input_final(own, *arrived):
     rows, depth = own.shape
-    full, part = full_block(rows, depth), full_block(rows // 2, depth)
-    return pl.pallas_call(
-        input_kernel,
+    return pl.pallas_call(
+        sum_kernel,
         grid=(1,),
         out_shape=jax.ShapeDtypeStruct((rows, depth), BF16),
-        in_specs=[full, full, full, part, part],
-        out_specs=full,
-        compiler_params=params(),
-        cost_estimate=COST,
-    )(own, below, above, below_add, above_add)
+        in_specs=[full_block(rows, depth)] * 4,
+        out_specs=full_block(rows, depth),
+        compiler_params=params(),
+        cost_estimate=COST,
+    )(own, *arrived)
 
 
 def after(value, *earlier):
@@ -709,49 +713,48 @@
     z, y = position // SIDE, position % SIDE
     column = lax.axis_index("smp")
     x, core = column // 2, column % 2
-    at = jnp.stack([z, y, x, core])
     writes = write_vec[:, 0]
     reads = read_vec[:, 0]
     rel, relt, steps, scaled, states, *messages = pre(
-        at, decay_log, step_size.T, out_grad, reads, fork_grad.reshape(2, WIDE, 128)
+        decay_log, step_size.T, out_grad, reads, fork_grad.reshape(2, WIDE, 128)
     )
+    at = jnp.stack(after([z, y, x, core], *messages))
     far, above, below = (hop(messages[d], 0, d) for d in (2, 1, 3))
+    other_weight = hop_smp(proj_weight, 0, 1)
     inputs_a = project(after(layer_input, *messages), proj_weight, 0)
     first = after([messages[0], above, far, below], inputs_a)
     message = group(at, first)
     far, above, below = (hop(message, d, 0) for d in (2, 1, 3))
-    base = diag(skip_gain, rel, relt, steps, reads, writes, after(out_grad, message))
-    second = after([message, above, far, below], base)
+    inputs_b = project(after(layer_input, message), proj_weight, 1)
+    second = after([message, above, far, below], inputs_b, other_weight)
     sent = carry_over(at, first, second)
     far, above, below = (hop(sent[d], 0, d) for d in (2, 1, 3))
-    inputs_b = project(after(layer_input, sent[0]), proj_weight, 1)
-    quarters = after([sent[0], above, far, below], inputs_b)
-    keep, give, x_mine, x_theirs, full = x_final(at, quarters, states, rel, steps, writes, base)
+    base = diag(skip_gain, rel, relt, steps, reads, writes, after(out_grad, sent[0]))
+    quarters = [sent[0], above, far, below]
+    keep, give, x_mine, full = x_final(at, quarters, states, rel, steps, writes, base)
     got = first_hop(give, 0, 1)
-    other = theirs(at, x_theirs, proj_weight)
-    far = ring_product(at, FAR, layer_input, keep, after(got, other))
+    part = input_product(x_mine, proj_weight)
+    far = ring_product(at, FAR, layer_input, keep, after(got, part))
     far_in = first_hop(far[0], 1, 0), first_hop(far[1], -1, 0)
-    other_in = hop_smp(other, 0, 1)
     plain = ring_product(at, PLAIN, layer_input, after(keep, *far), got)
     plain_in = first_hop(plain[0], 1, 0), first_hop(plain[1], -1, 0)
-    up, down, up_keep, down_keep, own = mine(at, after(x_mine, *plain), proj_weight, other_in)
-    added = ring_product(at, ADDED, layer_input, keep, got, after(far_in, own))
+    sums = input_rest(at, after(got, *plain), other_weight, part)
+    near_terms = x_hop(sums[1], 1), x_hop(after(sums[2], plain_in), -1)
+    added = ring_product(at, ADDED, layer_input, keep, got, after(far_in, *sums))
     added_in = first_hop(added[0], 1, 0), first_hop(added[1], -1, 0)
-    below_x, above_x = hop_smp(up, 1, 0), hop_smp(down, -1, 0)
+    far_term = x_hop(after(sums[0], plain_in), 2)
     write_grad, read_grad = vectors(
         rel, relt, steps, reads, writes, out_grad, scaled, inputs_a, inputs_b, after(full, *added),
         start_state.reshape(WIDE, 128),
     )
-    up, down = add_two(up_keep, down_keep, below_x, after(above_x, write_grad))
-    below_add, above_add = hop_smp(up, 1, 0), hop_smp(down, -1, 0)
-    arrived = after((added_in[0], plain_in[0], plain_in[1], added_in[1]), up)
-    sums = own_product(at, layer_input, keep, got, arrived)
-    same, cross = list(sums[:4]), list(sums[4:])
+    own = own_product(at, layer_input, keep, got, *after(plain_in, write_grad))
+    totals = own_total(own, *after(added_in, own, near_terms[0]))
+    same, cross = list(totals[:4]), list(totals[4:])
     for g in range(3):
         same[g] = second_hop(same[g], ORDER[g], 0)
         cross[g] = second_hop(cross[g], ORDER[g], 1)
     cross[3] = second_hop(cross[3], 0, 1)
-    input_grad = input_final(after(own, *sums), below_x, above_x, below_add, above_add)
+    input_grad = input_final(after(sums[3], *totals), *near_terms, far_term)
     scale = (length * lax.axis_size("ctx")) ** (-0.5)
     weight_grad = weight_final(at, scale, same + cross)
     return (input_grad, weight_grad, write_grad[:, None], read_grad[:, None])

time: 142 us -> 125 us (0.88)
  waiting for transfers between devices: 18.1 us -> 6.89 us
  Pallas kernels: 79.1 us -> 74.7 us
  starting transfers between devices: 42.8 us -> 41.2 us
    ppermute x28 -> x27, waiting for transfers between devices: 18.1 us -> 6.89 us  [routed(): return lax.ppermute(block, ('ctx', 'smp'), route)]
    pallas_call x1, Pallas kernels: 7.98 us -> 5.24 us  [own_product(): pl.pallas_call(own_kernel, grid_spec=pltpu.PrefetchScalarGridSpec(num_sca...]
    pallas_call x7, Pallas kernels: 30.6 us -> 28.6 us  [the longest x1 7.48 us: input_rest(): pl.pallas_call(rest_kernel, grid_spec=pltpu.PrefetchScalarGridSpec(num_sc...]
    ppermute x28 -> x27, starting transfers between devices: 42.8 us -> 41.2 us  [routed(): return lax.ppermute(block, ('ctx', 'smp'), route)]
  transfers between devices with their start and end apart: 28 -> 27, of which waited for: 7 -> 4; matrix products, arithmetic and copies ran while one was open for 0% -> 0% of each run, Pallas kernels for 40% -> 50%
where the time goes in v4:
time: 125 us
  Pallas kernels  74.7 us (60%)
  starting transfers between devices  41.2 us (33%)
  waiting for transfers between devices  6.89 us (6%)
  local copies, waits for them, and re-layouts  1.25 us (1%)
    ppermute x27, starting transfers between devices, routed(): return lax.ppermute(block, ('ctx', 'smp'), route)  41.2 us
    pallas_call x3, Pallas kernels, ring_product(): pl.pallas_call(ring_kernel, grid_spec=pltpu.PrefetchScalarGridSpec(num_sc...  13.7 us
    pallas_call x2, Pallas kernels, project(): pl.pallas_call(project_kernel, grid=(2,), out_shape=jax.ShapeDtypeStruct(...  11.4 us
    pallas_call x1, Pallas kernels, input_rest(): pl.pallas_call(rest_kernel, grid_spec=pltpu.PrefetchScalarGridSpec(num_sc...  7.48 us
    pallas_call x1, Pallas kernels, vectors(): pl.pallas_call(vector_kernel, grid=(CHUNKS // 2,), out_shape=[jax.ShapeDt...  7.3 us
    ppermute x27, waiting for transfers between devices, routed(): return lax.ppermute(block, ('ctx', 'smp'), route)  6.89 us
    pallas_call x1, Pallas kernels, input_product(): pl.pallas_call(input_kernel, grid=(depth // tile,), in_specs=[full_block(...  5.87 us
    pallas_call x1, Pallas kernels, own_product(): pl.pallas_call(own_kernel, grid_spec=pltpu.PrefetchScalarGridSpec(num_sca...  5.24 us
  transfers between devices with their start and end apart: 27, of which 4 were waited for; matrix products, arithmetic and copies ran while one was open for 0% of the time, Pallas kernels for 50%

profile of v4, /device:TPU:1, one launch (start us, length us, event | category | flops | bytes accessed | tf_op | source)
XLA Modules:
  0.0 124.8 jit_solution(5017022441420869503)
XLA Ops:
  0.6 1.5 %collective-permute-start.6 = (bf16[4096,1024]{1,0:T(8,128)(2,1)}, bf16[4096,1024]{1,0:T(8,128)(2,1)}, u32[]{:S(2)}, u32[]{:S(2)}) collective-permute-start(bf16[4096,1024]{1,0:T(8,128)(2,1)} %w_ref.5), channel_id=1, source_target_pairs={{0,1},{1,0},{2,3},{3,2},{4,5},{5,4},{6,7},{7,6},{8,9},{9,8},{10,11... | collective-permute-start | bytes 25165832 | tf_op jit(solution)/shard_map/ppermute | solution.py:46
  2.1 4.3 %shard_map.129 = (f32[4,128,16]{2,1,0:T(8,128)}, f32[4,16,128]{2,1,0:T(8,128)}, f32[512,16]{1,0:T(8,128)}, bf16[512,1024]{1,0:T(8,128)(2,1)}, bf16[3,128,1024]{2...) custom-call(f32[16]{0:T(128)} %dlog_ref.1, ...), custom_call_target="tpu_custom_call" | custom-call | flops 1 | bytes 1 | tf_op jit(solution)/shard_map/pallas_call | solution.py:180
  6.5 1.4 %collective-permute-start = (bf16[272,256]{1,0:T(8,128)(2,1)}, bf16[272,256]{1,0:T(8,128)(2,1)S(1)}, u32[]{:S(2)}, u32[]{:S(2)}) collective-permute-start(bf16[272,256]{1,0:T(8,128)(2,1)} %get-tuple-element.70), channel_id=1, source_target_pairs={{0,8},{1,9},{2,10},{3,11},{4,12},{5,13},{6,14},{7,15},{8,16},{9,17... | collective-permute-start | bytes 417800 | tf_op jit(solution)/shard_map/ppermute | solution.py:46
  7.8 2.6 %collective-permute-start.1 = (bf16[272,256]{1,0:T(8,128)(2,1)}, bf16[272,256]{1,0:T(8,128)(2,1)S(1)}, u32[]{:S(2)}, u32[]{:S(2)}) collective-permute-start(bf16[272,256]{1,0:T(8,128)(2,1)} %get-tuple-element.71), channel_id=1, source_target_pairs={{0,16},{1,17},{2,18},{3,19},{4,20},{5,21},{6,22},{7,23},{8,24},{9,... | collective-permute-start | bytes 417800 | tf_op jit(solution)/shard_map/ppermute | solution.py:46
  10.5 1.1 collective-permute-start.2
  11.5 5.7 %shard_map.130.first_ref = bf16[512,512]{1,0:T(8,128)(2,1)} custom-call(bf16[512,4096]{1,0:T(8,128)(2,1)} %second_ref.1, bf16[4096,1024]{1,0:T(8,128)(2,1)} %w_ref.5), custom_call_target="tpu_custom_call" | custom-call | flops 1 | bytes 1 | tf_op jit(solution)/shard_map/pallas_call | solution.py:484
  17.2 0.1 pad_add_fusion.at_ref
  17.3 0.2 collective-permute-done.1.a2
  17.5 0.0 collective-permute-done.2.a3
  17.5 0.7 shard_map.131.b0
  18.2 3.8 %collective-permute-start.5 = (bf16[272,256]{1,0:T(8,128)(2,1)S(1)}, bf16[272,256]{1,0:T(8,128)(2,1)S(1)}, u32[]{:S(2)}, u32[]{:S(2)}) collective-permute-start(bf16[272,256]{1,0:T(8,128)(2,1)S(1)} %shard_map.131.b0), channel_id=1, source_target_pairs={{0,96},{1,97},{2,98},{3,99},{4,100},{5,101},{6,102},{7,103},{8,104... | collective-permute-start | bytes 417800 | tf_op jit(solution)/shard_map/ppermute | solution.py:46
  22.0 0.0 collective-permute-start.4
  22.0 0.7 collective-permute-start.3
  22.7 5.7 %shard_map.132.second_ref = bf16[512,512]{1,0:T(8,128)(2,1)} custom-call(bf16[512,4096]{1,0:T(8,128)(2,1)} %second_ref.1, bf16[4096,1024]{1,0:T(8,128)(2,1)} %w_ref.5), custom_call_target="tpu_custom_call" | custom-call | flops 1 | bytes 1 | tf_op jit(solution)/shard_map/pallas_call | solution.py:484
  28.5 3.0 %collective-permute-done.3.b1 = bf16[272,256]{1,0:T(8,128)(2,1)S(1)} collective-permute-done((bf16[272,256]{1,0:T(8,128)(2,1)S(1)}, bf16[272,256]{1,0:T(8,128)(2,1)S(1)}, u32[]{:S(2)}, u32[]{:S(2)}) %collective-permute-start.3) | collective-permute-done | bytes 139296 | tf_op jit(solution)/shard_map/ppermute | solution.py:46
  31.5 0.0 collective-permute-done.6.w_ref
  31.5 0.8 shard_map.133
  32.2 0.0 copy-start.1
  32.2 0.6 copy-done.1
  32.9 0.5 collective-permute-start.7
  33.3 2.7 %collective-permute-start.8 = (bf16[128,256]{1,0:T(8,128)(2,1)S(1)}, bf16[128,256]{1,0:T(8,128)(2,1)S(1)}, u32[]{:S(2)}, u32[]{:S(2)}) collective-permute-start(bf16[128,256]{1,0:T(8,128)(2,1)S(1)} %get-tuple-element.89), channel_id=1, source_target_pairs={{0,16},{1,17},{2,18},{3,19},{4,20},{5,21},{6,22},{7,23},{8,24},{9,... | collective-permute-start | bytes 196616 | tf_op jit(solution)/shard_map/ppermute | solution.py:46
  36.1 0.9 collective-permute-start.9
  36.9 3.9 %shard_map.134.base_ref = bf16[512,1024]{1,0:T(8,128)(2,1)} custom-call(f32[16]{0:T(128)} %skip_ref.1, f32[4,128,16]{2,1,0:T(8,128)} %get-tuple-element.92.rel_ref, f32[4,16,128]{2,1,0:T(8,128)} %get-tuple-element.94.relt_ref, f32[512,16]{1,0:T(8,128)} %get-tuple-element.93.step_ref, bf16[512,128]{1,0:T(8,128)(2,1)} %bitcast.17, bf16[512,128]{1,0:T(8,128)(2,1)} %bitcast.19, ...), custom_call_target="tpu_custom_call" | custom-call | flops 1 | bytes 1 | tf_op jit(solution)/shard_map/pallas_call | solution.py:308
  40.8 0.0 collective-permute-done.7.q1
  40.8 0.0 copy-start.3
  40.9 0.0 collective-permute-done.9.q3
  40.9 0.6 copy-done.3
  41.5 0.0 copy-done.4
  41.5 0.0 copy-done.5
  41.5 4.8 %shard_map.135 = (bf16[512,512]{1,0:T(8,128)(2,1)}, bf16[1024,512]{1,0:T(8,128)(2,1)}, bf16[256,1024]{1,0:T(8,128)(2,1)}, bf16[4,128,1024]{2,1,0:T(8,128)(2,1)}) custom-call(s32[4]{0:T(128)} %copy-done.2, bf16[128,256]{1,0:T(8,128)(2,1)} %copy-done.1, bf16[128,256]{1,0:T(8,128)(2,1)} %copy-done.3, bf16[128,256]{1,0:T(8,128)(2,1)} %copy-done.4, ...), custom_call_target="tpu_custom_call" | custom-call | flops 1 | bytes 1 | tf_op jit(solution)/shard_map/pallas_call | solution.py:369
  46.3 1.7 %collective-permute-start.10 = (bf16[1024,512]{1,0:T(8,128)(2,1)}, bf16[1024,512]{1,0:T(8,128)(2,1)}, u32[]{:S(2)}, u32[]{:S(2)}) collective-permute-start(bf16[1024,512]{1,0:T(8,128)(2,1)} %get-tuple-element.96), channel_id=1, source_target_pairs={{0,1},{1,0},{2,3},{3,2},{4,5},{5,4},{6,7},{7,6},{8,9},{9,8},{10,11... | collective-permute-start | bytes 3145736 | tf_op jit(solution)/shard_map/ppermute | solution.py:46
  47.9 5.9 %shard_map.136.part_ref = bf16[256,4096]{1,0:T(8,128)(2,1)} custom-call(bf16[256,1024]{1,0:T(8,128)(2,1)} %get-tuple-element.98.x_ref, bf16[4096,1024]{1,0:T(8,128)(2,1)} %w_ref.5), custom_call_target="tpu_custom_call" | custom-call | flops 1 | bytes 1 | tf_op jit(solution)/shard_map/pallas_call | solution.py:633
  53.8 0.0 collective-permute-done.10.got_ref.left_ref.right_ref
  53.8 4.4 %shard_map.137 = (bf16[2,256,1024]{2,1,0:T(8,128)(2,1)}, bf16[2,256,1024]{2,1,0:T(8,128)(2,1)}) custom-call(s32[4]{0:T(128)} %copy-done.2, bf16[512,4096]{1,0:T(8,128)(2,1)} %second_ref.1, bf16[512,4096]{1,0:T(8,128)(2,1)} %second_ref.1, bf16[512,512]{1,0:T(8,128)(2,1)} %get-tuple-element.102.keep_ref, ...), custom_call_target="tpu_custom_call" | custom-call | flops 1 | bytes 1 | tf_op jit(solution)/shard_map/pallas_call | solution.py:533
  58.2 0.1 collective-permute-start.13
  58.3 2.6 %collective-permute-start.14 = (bf16[2,256,1024]{2,1,0:T(8,128)(2,1)}, bf16[2,256,1024]{2,1,0:T(8,128)(2,1)}, u32[]{:S(2)}, u32[]{:S(2)}) collective-permute-start(bf16[2,256,1024]{2,1,0:T(8,128)(2,1)} %get-tuple-element.101), channel_id=1, source_target_pairs={{0,24},{1,97},{2,26},{3,99},{4,28},{5,101},{6,30},{7,103},{8,0},{9... | collective-permute-start | bytes 3145736 | tf_op jit(solution)/shard_map/ppermute | solution.py:46
  60.9 4.4 %shard_map.138 = (bf16[2,256,1024]{2,1,0:T(8,128)(2,1)}, bf16[2,256,1024]{2,1,0:T(8,128)(2,1)}) custom-call(s32[4]{0:T(128)} %copy-done.2, bf16[512,4096]{1,0:T(8,128)(2,1)} %second_ref.1, bf16[512,4096]{1,0:T(8,128)(2,1)} %second_ref.1, bf16[512,512]{1,0:T(8,128)(2,1)} %get-tuple-element.102.keep_ref, ...), custom_call_target="tpu_custom_call" | custom-call | flops 1 | bytes 1 | tf_op jit(solution)/shard_map/pallas_call | solution.py:533
  65.3 2.7 %collective-permute-start.12 = (bf16[2,256,1024]{2,1,0:T(8,128)(2,1)}, bf16[2,256,1024]{2,1,0:T(8,128)(2,1)}, u32[]{:S(2)}, u32[]{:S(2)}) collective-permute-start(bf16[2,256,1024]{2,1,0:T(8,128)(2,1)} %get-tuple-element.104), channel_id=1, source_target_pairs={{0,24},{1,97},{2,26},{3,99},{4,28},{5,101},{6,30},{7,103},{8,0},{9... | collective-permute-start | bytes 3145736 | tf_op jit(solution)/shard_map/ppermute | solution.py:46
  68.0 7.5 %shard_map.139 = (bf16[64,4096]{1,0:T(8,128)(2,1)}, bf16[64,4096]{1,0:T(8,128)(2,1)}, bf16[64,4096]{1,0:T(8,128)(2,1)}, f32[64,4096]{1,0:T(8,128)}) custom-call(s32[4]{0:T(128)} %copy-done.2, bf16[1024,512]{1,0:T(8,128)(2,1)} %collective-permute-done.10.got_ref.left_ref.right_ref, bf16[1024,512]{1,0:T(8,128)(2,1)} %collective-permute-done.10.got_ref.left_ref.right_ref, ...), custom_call_target="tpu_custom_call" | custom-call | flops 1 | bytes 1 | tf_op jit(solution)/shard_map/pallas_call | solution.py:657
  75.5 2.5 %collective-permute-start.17 = (bf16[64,4096]{1,0:T(8,128)(2,1)}, bf16[64,4096]{1,0:T(8,128)(2,1)}, u32[]{:S(2)}, u32[]{:S(2)}) collective-permute-start(bf16[64,4096]{1,0:T(8,128)(2,1)} %get-tuple-element.110), channel_id=1, source_target_pairs={{0,2},{1,7},{2,4},{3,1},{4,6},{5,3},{6,0},{7,5},{8,10},{9,15},{10,... | collective-permute-start | bytes 1572872 | tf_op jit(solution)/shard_map/ppermute | solution.py:46
  78.0 0.0 collective-permute-done.13.refs_0_
  78.0 0.0 collective-permute-done.14.refs_1_
  78.0 4.9 %shard_map.140 = (bf16[2,256,1024]{2,1,0:T(8,128)(2,1)}, bf16[2,256,1024]{2,1,0:T(8,128)(2,1)}) custom-call(s32[4]{0:T(128)} %copy-done.2, bf16[512,4096]{1,0:T(8,128)(2,1)} %second_ref.1, bf16[512,4096]{1,0:T(8,128)(2,1)} %second_ref.1, bf16[512,512]{1,0:T(8,128)(2,1)} %get-tuple-element.102.keep_ref, ...), custom_call_target="tpu_custom_call" | custom-call | flops 1 | bytes 1 | tf_op jit(solution)/shard_map/pallas_call | solution.py:533
  82.9 2.7 %collective-permute-start.16 = (bf16[2,256,1024]{2,1,0:T(8,128)(2,1)}, bf16[2,256,1024]{2,1,0:T(8,128)(2,1)}, u32[]{:S(2)}, u32[]{:S(2)}) collective-permute-start(bf16[2,256,1024]{2,1,0:T(8,128)(2,1)} %get-tuple-element.115), channel_id=1, source_target_pairs={{0,24},{1,97},{2,26},{3,99},{4,28},{5,101},{6,30},{7,103},{8,0},{9... | collective-permute-start | bytes 3145736 | tf_op jit(solution)/shard_map/ppermute | solution.py:46
  85.6 0.0 collective-permute-done.11.below_plain
  85.6 0.0 collective-permute-done.12.above_plain
  85.6 0.6 collective-permute-start.18
  86.2 2.5 %collective-permute-start.19 = (bf16[64,4096]{1,0:T(8,128)(2,1)}, bf16[64,4096]{1,0:T(8,128)(2,1)}, u32[]{:S(2)}, u32[]{:S(2)}) collective-permute-start(bf16[64,4096]{1,0:T(8,128)(2,1)} %get-tuple-element.132), channel_id=1, source_target_pairs={{0,4},{1,5},{2,6},{3,7},{4,0},{5,1},{6,2},{7,3},{8,12},{9,13},{10,... | collective-permute-start | bytes 1572872 | tf_op jit(solution)/shard_map/ppermute | solution.py:46
  88.6 7.3 %shard_map.141 = (f32[512,128]{1,0:T(8,128)}, f32[512,128]{1,0:T(8,128)}) custom-call(f32[4,128,16]{2,1,0:T(8,128)} %get-tuple-element.92.rel_ref, f32[4,16,128]{2,1,0:T(8,128)} %get-tuple-element.94.relt_ref, f32[512,16]{1,0:T(8,128)} %get-tuple-element.93.step_ref, bf16[512,128]{1,0:T(8,128)(2,1)} %bitcast.18, bf16[512,128]{1,0:T(8,128)(2,1)} %bitcast.21, ...), custom_call_target="tpu_custom_call" | custom-call | flops 49999998976 | bytes 1 | tf_op jit(solution)/shard_map/pallas_call | solution.py:444
  95.9 5.2 %shard_map.142.own_ref = bf16[4,256,1024]{2,1,0:T(8,128)(2,1)} custom-call(s32[4]{0:T(128)} %copy-done.2, bf16[512,4096]{1,0:T(8,128)(2,1)} %second_ref.1, bf16[512,4096]{1,0:T(8,128)(2,1)} %second_ref.1, bf16[512,512]{1,0:T(8,128)(2,1)} %get-tuple-element.102.keep_ref, bf16[1024,512]{1,0:T(8,128)(2,1)} %collective-permute-done.10.got_ref.left_ref.right_ref, ...), custom_call_target="tpu_custom_call" | custom-call | flops 1 | bytes 1 | tf_op jit(solution)/shard_map/pallas_call | solution.py:561
  101.2 0.0 collective-permute-done.17.first
  101.2 0.0 collective-permute-done.15.below_add
  101.2 0.0 collective-permute-done.16.above_add
  101.2 3.8 %shard_map.143 = (bf16[256,512]{1,0:T(8,128)(2,1)}, bf16[256,512]{1,0:T(8,128)(2,1)}, bf16[256,512]{1,0:T(8,128)(2,1)}, f32[256,512]{1,0:T(8,128)}, bf16[256,512...) custom-call(bf16[4,256,1024]{2,1,0:T(8,128)(2,1)} %shard_map.142.own_ref, ...), custom_call_target="tpu_custom_call" | custom-call | flops 1 | bytes 1 | tf_op jit(solution)/shard_map/pallas_call | solution.py:595
  105.0 0.7 collective-permute-start.20
  105.7 1.1 collective-permute-start.21
  106.8 1.6 %collective-permute-start.22 = (bf16[256,512]{1,0:T(8,128)(2,1)}, bf16[256,512]{1,0:T(8,128)(2,1)}, u32[]{:S(2)}, u32[]{:S(2)}) collective-permute-start(bf16[256,512]{1,0:T(8,128)(2,1)} %get-tuple-element.124), channel_id=1, source_target_pairs={{0,96},{1,25},{2,98},{3,27},{4,100},{5,29},{6,102},{7,31},{8,104},... | collective-permute-start | bytes 786440 | tf_op jit(solution)/shard_map/ppermute | solution.py:46
  108.4 2.5 %collective-permute-start.23 = (bf16[256,512]{1,0:T(8,128)(2,1)}, bf16[256,512]{1,0:T(8,128)(2,1)}, u32[]{:S(2)}, u32[]{:S(2)}) collective-permute-start(bf16[256,512]{1,0:T(8,128)(2,1)} %get-tuple-element.126), channel_id=1, source_target_pairs={{0,65},{1,16},{2,67},{3,18},{4,69},{5,20},{6,71},{7,22},{8,73},{9,... | collective-permute-start | bytes 786440 | tf_op jit(solution)/shard_map/ppermute | solution.py:46
  110.9 1.4 %collective-permute-done.20.refs_0_ = bf16[256,512]{1,0:T(8,128)(2,1)} collective-permute-done((bf16[256,512]{1,0:T(8,128)(2,1)}, bf16[256,512]{1,0:T(8,128)(2,1)}, u32[]{:S(2)}, u32[]{:S(2)}) %collective-permute-start.20) | collective-permute-done | bytes 262176 | tf_op jit(solution)/shard_map/ppermute | solution.py:46
  112.4 4.5 %collective-permute-start.25 = (bf16[256,512]{1,0:T(8,128)(2,1)}, bf16[256,512]{1,0:T(8,128)(2,1)}, u32[]{:S(2)}, u32[]{:S(2)}) collective-permute-start(bf16[256,512]{1,0:T(8,128)(2,1)} %get-tuple-element.128), channel_id=1, source_target_pairs={{0,97},{1,24},{2,99},{3,26},{4,101},{5,28},{6,103},{7,30},{8,105},... | collective-permute-start | bytes 786440 | tf_op jit(solution)/shard_map/ppermute | solution.py:46
  116.9 0.3 collective-permute-start.26
  117.2 2.7 %shard_map.144 = bf16[64,4096]{1,0:T(8,128)(2,1)} custom-call(f32[64,4096]{1,0:T(8,128)} %get-tuple-element.130.own, bf16[64,4096]{1,0:T(8,128)(2,1)} %collective-permute-done.17.first, bf16[64,4096]{1,0:T(8,128)(2,1)} %collective-permute-done.18.second, bf16[64,4096]{1,0:T(8,128)(2,1)} %collective-permute-done.19.third), custom_call_target="tpu_custom_call" | custom-call | flops 1 | bytes 1 | tf_op jit(solution)/shard_map/pallas_call | solution.py:684
  119.9 2.2 %collective-permute-done.24.refs_5_ = bf16[256,512]{1,0:T(8,128)(2,1)} collective-permute-done((bf16[256,512]{1,0:T(8,128)(2,1)}, bf16[256,512]{1,0:T(8,128)(2,1)}, u32[]{:S(2)}, u32[]{:S(2)}) %collective-permute-start.24) | collective-permute-done | bytes 262176 | tf_op jit(solution)/shard_map/ppermute | solution.py:46
  122.2 2.7 %shard_map.145 = bf16[256,1024]{1,0:T(8,128)(2,1)} custom-call(s32[4]{0:T(128)} %copy-done.2, bf16[256,512]{1,0:T(8,128)(2,1)} %collective-permute-done.20.refs_0_, bf16[256,512]{1,0:T(8,128)(2,1)} %collective-permute-done.21.refs_1_, bf16[256,512]{1,0:T(8,128)(2,1)} %collective-permute-done.22.refs_2_, f32[256,512]{1,0:T(8,128)} %get-tuple-element.125.refs_3_, ...), custom_call_target="tpu_custom_call" | custom-call | flops 1 | bytes 1 | tf_op jit(solution)/shard_map/pallas_call | solution.py:616
  (20 shorter events, 0.0 us)
Async XLA Ops:
  0.6 30.8 %collective-permute-start.6 = (bf16[4096,1024]{1,0:T(8,128)(2,1)}, bf16[4096,1024]{1,0:T(8,128)(2,1)}, u32[]{:S(2)}, u32[]{:S(2)}) collective-permute-start(bf16[4096,1024]{1,0:T(8,128)(2,1)} %w_ref.5), channel_id=1, source_target_pairs={{0,1},{1,0},{2,3},{3,2},{4,5},{5,4},{6,7},{7,6},{8,9},{9,8},{10,11... | collective-permute-start | bytes 25165832 | tf_op jit(solution)/shard_map/ppermute | solution.py:46
  6.5 10.9 %collective-permute-start = (bf16[272,256]{1,0:T(8,128)(2,1)}, bf16[272,256]{1,0:T(8,128)(2,1)S(1)}, u32[]{:S(2)}, u32[]{:S(2)}) collective-permute-start(bf16[272,256]{1,0:T(8,128)(2,1)} %get-tuple-element.70), channel_id=1, source_target_pairs={{0,8},{1,9},{2,10},{3,11},{4,12},{5,13},{6,14},{7,15},{8,16},{9,17... | collective-permute-start | bytes 417800 | tf_op jit(solution)/shard_map/ppermute | solution.py:46
  7.8 9.6 %collective-permute-start.1 = (bf16[272,256]{1,0:T(8,128)(2,1)}, bf16[272,256]{1,0:T(8,128)(2,1)S(1)}, u32[]{:S(2)}, u32[]{:S(2)}) collective-permute-start(bf16[272,256]{1,0:T(8,128)(2,1)} %get-tuple-element.71), channel_id=1, source_target_pairs={{0,16},{1,17},{2,18},{3,19},{4,20},{5,21},{6,22},{7,23},{8,24},{9,... | collective-permute-start | bytes 417800 | tf_op jit(solution)/shard_map/ppermute | solution.py:46
  10.5 7.0 %collective-permute-start.2 = (bf16[272,256]{1,0:T(8,128)(2,1)}, bf16[272,256]{1,0:T(8,128)(2,1)S(1)}, u32[]{:S(2)}, u32[]{:S(2)}) collective-permute-start(bf16[272,256]{1,0:T(8,128)(2,1)} %get-tuple-element.72), channel_id=1, source_target_pairs={{0,24},{1,25},{2,26},{3,27},{4,28},{5,29},{6,30},{7,31},{8,0},{9,1... | collective-permute-start | bytes 417800 | tf_op jit(solution)/shard_map/ppermute | solution.py:46
  11.5 6.0 %copy-start = (bf16[272,256]{1,0:T(8,128)(2,1)S(1)}, bf16[272,256]{1,0:T(8,128)(2,1)}, u32[]{:S(2)}) copy-start(bf16[272,256]{1,0:T(8,128)(2,1)} %get-tuple-element.78.a0) | copy-start | bytes 417796
  17.3 14.1 %copy-start.2 = (s32[4]{0:T(128)}, s32[4]{0:T(128)S(1)}, u32[]{:S(2)}) copy-start(s32[4]{0:T(128)S(1)} %pad_add_fusion.at_ref) | copy-start | bytes 52
  18.2 10.3 %collective-permute-start.5 = (bf16[272,256]{1,0:T(8,128)(2,1)S(1)}, bf16[272,256]{1,0:T(8,128)(2,1)S(1)}, u32[]{:S(2)}, u32[]{:S(2)}) collective-permute-start(bf16[272,256]{1,0:T(8,128)(2,1)S(1)} %shard_map.131.b0), channel_id=1, source_target_pairs={{0,96},{1,97},{2,98},{3,99},{4,100},{5,101},{6,102},{7,103},{8,104... | collective-permute-start | bytes 417800 | tf_op jit(solution)/shard_map/ppermute | solution.py:46
  22.0 6.4 %collective-permute-start.4 = (bf16[272,256]{1,0:T(8,128)(2,1)S(1)}, bf16[272,256]{1,0:T(8,128)(2,1)S(1)}, u32[]{:S(2)}, u32[]{:S(2)}) collective-permute-start(bf16[272,256]{1,0:T(8,128)(2,1)S(1)} %shard_map.131.b0), channel_id=1, source_target_pairs={{0,64},{1,65},{2,66},{3,67},{4,68},{5,69},{6,70},{7,71},{8,72},{9,... | collective-permute-start | bytes 417800 | tf_op jit(solution)/shard_map/ppermute | solution.py:46
  22.0 9.4 %collective-permute-start.3 = (bf16[272,256]{1,0:T(8,128)(2,1)S(1)}, bf16[272,256]{1,0:T(8,128)(2,1)S(1)}, u32[]{:S(2)}, u32[]{:S(2)}) collective-permute-start(bf16[272,256]{1,0:T(8,128)(2,1)S(1)} %shard_map.131.b0), channel_id=1, source_target_pairs={{0,32},{1,33},{2,34},{3,35},{4,36},{5,37},{6,38},{7,39},{8,40},{9,... | collective-permute-start | bytes 417800 | tf_op jit(solution)/shard_map/ppermute | solution.py:46
  32.2 0.6 copy-start.1
  32.9 8.0 %collective-permute-start.7 = (bf16[128,256]{1,0:T(8,128)(2,1)S(1)}, bf16[128,256]{1,0:T(8,128)(2,1)S(1)}, u32[]{:S(2)}, u32[]{:S(2)}) collective-permute-start(bf16[128,256]{1,0:T(8,128)(2,1)S(1)} %get-tuple-element.88), channel_id=1, source_target_pairs={{0,8},{1,9},{2,10},{3,11},{4,12},{5,13},{6,14},{7,15},{8,16},{9,17... | collective-permute-start | bytes 196616 | tf_op jit(solution)/shard_map/ppermute | solution.py:46
  33.3 7.5 %collective-permute-start.8 = (bf16[128,256]{1,0:T(8,128)(2,1)S(1)}, bf16[128,256]{1,0:T(8,128)(2,1)S(1)}, u32[]{:S(2)}, u32[]{:S(2)}) collective-permute-start(bf16[128,256]{1,0:T(8,128)(2,1)S(1)} %get-tuple-element.89), channel_id=1, source_target_pairs={{0,16},{1,17},{2,18},{3,19},{4,20},{5,21},{6,22},{7,23},{8,24},{9,... | collective-permute-start | bytes 196616 | tf_op jit(solution)/shard_map/ppermute | solution.py:46
  36.1 4.8 %collective-permute-start.9 = (bf16[128,256]{1,0:T(8,128)(2,1)S(1)}, bf16[128,256]{1,0:T(8,128)(2,1)S(1)}, u32[]{:S(2)}, u32[]{:S(2)}) collective-permute-start(bf16[128,256]{1,0:T(8,128)(2,1)S(1)} %get-tuple-element.90), channel_id=1, source_target_pairs={{0,24},{1,25},{2,26},{3,27},{4,28},{5,29},{6,30},{7,31},{8,0},{9,1... | collective-permute-start | bytes 196616 | tf_op jit(solution)/shard_map/ppermute | solution.py:46
  40.8 0.6 copy-start.3
  40.9 0.6 copy-start.4
  40.9 0.6 copy-start.5
  46.3 7.5 %collective-permute-start.10 = (bf16[1024,512]{1,0:T(8,128)(2,1)}, bf16[1024,512]{1,0:T(8,128)(2,1)}, u32[]{:S(2)}, u32[]{:S(2)}) collective-permute-start(bf16[1024,512]{1,0:T(8,128)(2,1)} %get-tuple-element.96), channel_id=1, source_target_pairs={{0,1},{1,0},{2,3},{3,2},{4,5},{5,4},{6,7},{7,6},{8,9},{9,8},{10,11... | collective-permute-start | bytes 3145736 | tf_op jit(solution)/shard_map/ppermute | solution.py:46
  58.2 19.8 %collective-permute-start.13 = (bf16[2,256,1024]{2,1,0:T(8,128)(2,1)}, bf16[2,256,1024]{2,1,0:T(8,128)(2,1)}, u32[]{:S(2)}, u32[]{:S(2)}) collective-permute-start(bf16[2,256,1024]{2,1,0:T(8,128)(2,1)} %get-tuple-element.100), channel_id=1, source_target_pairs={{0,8},{1,33},{2,10},{3,35},{4,12},{5,37},{6,14},{7,39},{8,16},{9,4... | collective-permute-start | bytes 3145736 | tf_op jit(solution)/shard_map/ppermute | solution.py:46
  58.3 19.7 %collective-permute-start.14 = (bf16[2,256,1024]{2,1,0:T(8,128)(2,1)}, bf16[2,256,1024]{2,1,0:T(8,128)(2,1)}, u32[]{:S(2)}, u32[]{:S(2)}) collective-permute-start(bf16[2,256,1024]{2,1,0:T(8,128)(2,1)} %get-tuple-element.101), channel_id=1, source_target_pairs={{0,24},{1,97},{2,26},{3,99},{4,28},{5,101},{6,30},{7,103},{8,0},{9... | collective-permute-start | bytes 3145736 | tf_op jit(solution)/shard_map/ppermute | solution.py:46
  65.3 20.2 %collective-permute-start.11 = (bf16[2,256,1024]{2,1,0:T(8,128)(2,1)}, bf16[2,256,1024]{2,1,0:T(8,128)(2,1)}, u32[]{:S(2)}, u32[]{:S(2)}) collective-permute-start(bf16[2,256,1024]{2,1,0:T(8,128)(2,1)} %get-tuple-element.103), channel_id=1, source_target_pairs={{0,8},{1,33},{2,10},{3,35},{4,12},{5,37},{6,14},{7,39},{8,16},{9,4... | collective-permute-start | bytes 3145736 | tf_op jit(solution)/shard_map/ppermute | solution.py:46
  65.3 20.2 %collective-permute-start.12 = (bf16[2,256,1024]{2,1,0:T(8,128)(2,1)}, bf16[2,256,1024]{2,1,0:T(8,128)(2,1)}, u32[]{:S(2)}, u32[]{:S(2)}) collective-permute-start(bf16[2,256,1024]{2,1,0:T(8,128)(2,1)} %get-tuple-element.104), channel_id=1, source_target_pairs={{0,24},{1,97},{2,26},{3,99},{4,28},{5,101},{6,30},{7,103},{8,0},{9... | collective-permute-start | bytes 3145736 | tf_op jit(solution)/shard_map/ppermute | solution.py:46
  75.5 25.7 %collective-permute-start.17 = (bf16[64,4096]{1,0:T(8,128)(2,1)}, bf16[64,4096]{1,0:T(8,128)(2,1)}, u32[]{:S(2)}, u32[]{:S(2)}) collective-permute-start(bf16[64,4096]{1,0:T(8,128)(2,1)} %get-tuple-element.110), channel_id=1, source_target_pairs={{0,2},{1,7},{2,4},{3,1},{4,6},{5,3},{6,0},{7,5},{8,10},{9,15},{10,... | collective-permute-start | bytes 1572872 | tf_op jit(solution)/shard_map/ppermute | solution.py:46
  82.9 18.3 %collective-permute-start.15 = (bf16[2,256,1024]{2,1,0:T(8,128)(2,1)}, bf16[2,256,1024]{2,1,0:T(8,128)(2,1)}, u32[]{:S(2)}, u32[]{:S(2)}) collective-permute-start(bf16[2,256,1024]{2,1,0:T(8,128)(2,1)} %get-tuple-element.114), channel_id=1, source_target_pairs={{0,8},{1,33},{2,10},{3,35},{4,12},{5,37},{6,14},{7,39},{8,16},{9,4... | collective-permute-start | bytes 3145736 | tf_op jit(solution)/shard_map/ppermute | solution.py:46
  82.9 18.3 %collective-permute-start.16 = (bf16[2,256,1024]{2,1,0:T(8,128)(2,1)}, bf16[2,256,1024]{2,1,0:T(8,128)(2,1)}, u32[]{:S(2)}, u32[]{:S(2)}) collective-permute-start(bf16[2,256,1024]{2,1,0:T(8,128)(2,1)} %get-tuple-element.115), channel_id=1, source_target_pairs={{0,24},{1,97},{2,26},{3,99},{4,28},{5,101},{6,30},{7,103},{8,0},{9... | collective-permute-start | bytes 3145736 | tf_op jit(solution)/shard_map/ppermute | solution.py:46
  85.6 22.8 %collective-permute-start.18 = (bf16[64,4096]{1,0:T(8,128)(2,1)}, bf16[64,4096]{1,0:T(8,128)(2,1)}, u32[]{:S(2)}, u32[]{:S(2)}) collective-permute-start(bf16[64,4096]{1,0:T(8,128)(2,1)} %get-tuple-element.131), channel_id=1, source_target_pairs={{0,6},{1,3},{2,0},{3,5},{4,2},{5,7},{6,4},{7,1},{8,14},{9,11},{10,... | collective-permute-start | bytes 1572872 | tf_op jit(solution)/shard_map/ppermute | solution.py:46
  86.2 24.8 %collective-permute-start.19 = (bf16[64,4096]{1,0:T(8,128)(2,1)}, bf16[64,4096]{1,0:T(8,128)(2,1)}, u32[]{:S(2)}, u32[]{:S(2)}) collective-permute-start(bf16[64,4096]{1,0:T(8,128)(2,1)} %get-tuple-element.132), channel_id=1, source_target_pairs={{0,4},{1,5},{2,6},{3,7},{4,0},{5,1},{6,2},{7,3},{8,12},{9,13},{10,... | collective-permute-start | bytes 1572872 | tf_op jit(solution)/shard_map/ppermute | solution.py:46
  105.0 7.4 %collective-permute-start.20 = (bf16[256,512]{1,0:T(8,128)(2,1)}, bf16[256,512]{1,0:T(8,128)(2,1)}, u32[]{:S(2)}, u32[]{:S(2)}) collective-permute-start(bf16[256,512]{1,0:T(8,128)(2,1)} %get-tuple-element.122), channel_id=1, source_target_pairs={{0,64},{1,17},{2,66},{3,19},{4,68},{5,21},{6,70},{7,23},{8,72},{9,... | collective-permute-start | bytes 786440 | tf_op jit(solution)/shard_map/ppermute | solution.py:46
  105.7 11.2 %collective-permute-start.21 = (bf16[256,512]{1,0:T(8,128)(2,1)}, bf16[256,512]{1,0:T(8,128)(2,1)}, u32[]{:S(2)}, u32[]{:S(2)}) collective-permute-start(bf16[256,512]{1,0:T(8,128)(2,1)} %get-tuple-element.123), channel_id=1, source_target_pairs={{0,32},{1,9},{2,34},{3,11},{4,36},{5,13},{6,38},{7,15},{8,40},{9,1... | collective-permute-start | bytes 786440 | tf_op jit(solution)/shard_map/ppermute | solution.py:46
  106.8 13.1 %collective-permute-start.22 = (bf16[256,512]{1,0:T(8,128)(2,1)}, bf16[256,512]{1,0:T(8,128)(2,1)}, u32[]{:S(2)}, u32[]{:S(2)}) collective-permute-start(bf16[256,512]{1,0:T(8,128)(2,1)} %get-tuple-element.124), channel_id=1, source_target_pairs={{0,96},{1,25},{2,98},{3,27},{4,100},{5,29},{6,102},{7,31},{8,104},... | collective-permute-start | bytes 786440 | tf_op jit(solution)/shard_map/ppermute | solution.py:46
  108.4 11.5 %collective-permute-start.23 = (bf16[256,512]{1,0:T(8,128)(2,1)}, bf16[256,512]{1,0:T(8,128)(2,1)}, u32[]{:S(2)}, u32[]{:S(2)}) collective-permute-start(bf16[256,512]{1,0:T(8,128)(2,1)} %get-tuple-element.126), channel_id=1, source_target_pairs={{0,65},{1,16},{2,67},{3,18},{4,69},{5,20},{6,71},{7,22},{8,73},{9,... | collective-permute-start | bytes 786440 | tf_op jit(solution)/shard_map/ppermute | solution.py:46
  110.9 11.2 %collective-permute-start.24 = (bf16[256,512]{1,0:T(8,128)(2,1)}, bf16[256,512]{1,0:T(8,128)(2,1)}, u32[]{:S(2)}, u32[]{:S(2)}) collective-permute-start(bf16[256,512]{1,0:T(8,128)(2,1)} %get-tuple-element.127), channel_id=1, source_target_pairs={{0,33},{1,8},{2,35},{3,10},{4,37},{5,12},{6,39},{7,14},{8,41},{9,1... | collective-permute-start | bytes 786440 | tf_op jit(solution)/shard_map/ppermute | solution.py:46
  112.4 9.8 %collective-permute-start.25 = (bf16[256,512]{1,0:T(8,128)(2,1)}, bf16[256,512]{1,0:T(8,128)(2,1)}, u32[]{:S(2)}, u32[]{:S(2)}) collective-permute-start(bf16[256,512]{1,0:T(8,128)(2,1)} %get-tuple-element.128), channel_id=1, source_target_pairs={{0,97},{1,24},{2,99},{3,26},{4,101},{5,28},{6,103},{7,30},{8,105},... | collective-permute-start | bytes 786440 | tf_op jit(solution)/shard_map/ppermute | solution.py:46
  116.9 5.3 %collective-permute-start.26 = (bf16[256,512]{1,0:T(8,128)(2,1)}, bf16[256,512]{1,0:T(8,128)(2,1)}, u32[]{:S(2)}, u32[]{:S(2)}) collective-permute-start(bf16[256,512]{1,0:T(8,128)(2,1)} %get-tuple-element.129), channel_id=1, source_target_pairs={{0,1},{1,0},{2,3},{3,2},{4,5},{5,4},{6,7},{7,6},{8,9},{9,8},{10,11... | collective-permute-start | bytes 786440 | tf_op jit(solution)/shard_map/ppermute | solution.py:46

commit v5 on v4

--- a/solution.py
+++ b/solution.py
@@ -17,9 +17,10 @@
 F32 = jnp.float32
 BF16 = jnp.bfloat16
 ORDER = (2, 1, 3, 0)
-VMEM_LIMIT = 64 * 1024 * 1024
-ROOMY_LIMIT = 61 * 1024 * 1024
-SMALL_LIMIT = 8 * 1024 * 1024
+MIB = 1024 * 1024
+VMEM_LIMIT = 24 * MIB
+ROOMY_LIMIT = 24 * MIB
+SMALL_LIMIT = 8 * MIB
 
 
 def params(limit=VMEM_LIMIT):
@@ -204,7 +205,7 @@
         ]
         + [full_block(256 + TAIL, QUARTER)] * 4,
         scratch_shapes=[pltpu.VMEM((256 + TAIL, WIDE), BF16)],
-        compiler_params=params(),
+        compiler_params=params(64 * MIB),
         cost_estimate=COST,
     )(decay_log, stept, out_grad, reads, fork_grad)
 
@@ -491,7 +492,7 @@
         ],
         out_specs=pl.BlockSpec((rows, wide), lambda i: (0, 0)),
         scratch_shapes=[pltpu.VMEM((rows, wide), F32)],
-        compiler_params=params(ROOMY_LIMIT),
+        compiler_params=params(61 * MIB),
         cost_estimate=COST,
     )(layer_input, proj_weight)
 
@@ -546,61 +547,67 @@
     )(at, layer_input, layer_input, keep, got, *more)
 
 
-def own_kernel(at_ref, first_ref, second_ref, keep_ref, got_ref, below_plain, above_plain, out):
-    g = pl.program_id(0)
-    for k, cols in enumerate((first_ref, second_ref)):
+def plain_kernel(
+    at_ref, up_ref, down_ref, first_ref, second_ref, keep_ref, got_ref, up_out, down_out, own_out
+):
+    outs = (up_out.at[0], down_out.at[0], own_out.at[0], own_out.at[1])
+    for cols, out in zip((up_ref, down_ref, first_ref, second_ref), outs):
         turned = cols[...].T
         for half, x_ref in enumerate((keep_ref, got_ref)):
-            at = slice(512 * half, 512 * half + 512)
-            plain = jnp.where(g == 0, above_plain[k, :, at], below_plain[k, :, at])
-            out[k, :, at] = (dot(turned, x_ref[...]) + plain.astype(F32)).astype(BF16)
-
-
-def own_product(at, layer_input, keep, got, below_plain, above_plain):
+            out[:, 512 * half : 512 * half + 512] = dot(turned, x_ref[...]).astype(BF16)
+
+
+def plain_product(at, layer_input, keep, got):
     rows = layer_input.shape[0]
-    return pl.pallas_call(
-        own_kernel,
+    (up_to, up_parts), (down_to, down_parts) = PLAIN
+    return pl.pallas_call(
+        plain_kernel,
         grid_spec=pltpu.PrefetchScalarGridSpec(
             num_scalar_prefetch=1,
             grid=(2,),
-            in_specs=[columns_spec(0, (0, 2)), columns_spec(0, (1, 3))]
-            + [pl.BlockSpec((rows, 512), lambda g, s: (0, 0))] * 2
-            + [full_block(2, 256, WIDE)] * 2,
-            out_specs=pl.BlockSpec((2, 256, WIDE), lambda g, s: (g, 0, 0)),
+            in_specs=[columns_spec(up_to, up_parts), columns_spec(down_to, down_parts)]
+            + [columns_spec(0, (0, 2)), columns_spec(0, (1, 3))]
+            + [pl.BlockSpec((rows, 512), lambda g, s: (0, 0))] * 2,
+            out_specs=[pl.BlockSpec((1, 256, WIDE), lambda g, s: (g, 0, 0))] * 2
+            + [pl.BlockSpec((2, 256, WIDE), lambda g, s: (g, 0, 0))],
         ),
-        out_shape=jax.ShapeDtypeStruct((4, 256, WIDE), BF16),
+        out_shape=[jax.ShapeDtypeStruct((2, 256, WIDE), BF16)] * 2
+        + [jax.ShapeDtypeStruct((4, 256, WIDE), BF16)],
         compiler_params=params(),
         cost_estimate=COST,
-    )(at, layer_input, layer_input, keep, got, below_plain, above_plain)
-
-
-def total_kernel(own_ref, below_add, above_add, *outs):
+    )(at, *[layer_input] * 4, keep, got)
+
+
+def total_kernel(own_ref, below_add, below_plain, above_plain, above_add, *outs):
     g = pl.program_id(0)
     for k in range(2):
         for half in range(2):
             at = slice(512 * half, 512 * half + 512)
             early, late = outs[SIDE * half + k], outs[SIDE * half + 2 + k]
+            own = own_ref[k, :, at].astype(F32)
 
             @pl.when(g == 0)
             def _():
-                early[...] = (own_ref[k, :, at].astype(F32) + below_add[k, :, at].astype(F32)).astype(early.dtype)
+                total = own + below_add[k, :, at].astype(F32) + above_plain[k, :, at].astype(F32)
+                early[...] = total.astype(early.dtype)
 
             @pl.when(g == 1)
             def _():
-                late[...] = (own_ref[k, :, at].astype(F32) + above_add[k, :, at].astype(F32)).astype(late.dtype)
-
-
-def own_total(own, below_add, above_add):
+                total = own + below_plain[k, :, at].astype(F32) + above_add[k, :, at].astype(F32)
+                late[...] = total.astype(late.dtype)
+
+
+def own_total(own, arrived):
     shape = lambda dtype: jax.ShapeDtypeStruct((256, 512), dtype)
     return pl.pallas_call(
         total_kernel,
         grid=(2,),
-        in_specs=[pl.BlockSpec((2, 256, WIDE), lambda g: (g, 0, 0))] + [full_block(2, 256, WIDE)] * 2,
+        in_specs=[pl.BlockSpec((2, 256, WIDE), lambda g: (g, 0, 0))] + [full_block(2, 256, WIDE)] * 4,
         out_specs=[full_block(256, 512)] * 8,
         out_shape=[shape(BF16)] * 3 + [shape(F32)] + [shape(BF16)] * 4,
         compiler_params=params(),
         cost_estimate=COST,
-    )(own, below_add, above_add)
+    )(own, *arrived)
 
 
 def weight_kernel(scale, at_ref, *refs):
@@ -736,7 +743,7 @@
     part = input_product(x_mine, proj_weight)
     far = ring_product(at, FAR, layer_input, keep, after(got, part))
     far_in = first_hop(far[0], 1, 0), first_hop(far[1], -1, 0)
-    plain = ring_product(at, PLAIN, layer_input, after(keep, *far), got)
+    *plain, own = plain_product(at, layer_input, after(keep, *far), got)
     plain_in = first_hop(plain[0], 1, 0), first_hop(plain[1], -1, 0)
     sums = input_rest(at, after(got, *plain), other_weight, part)
     near_terms = x_hop(sums[1], 1), x_hop(after(sums[2], plain_in), -1)
@@ -747,8 +754,8 @@
         rel, relt, steps, reads, writes, out_grad, scaled, inputs_a, inputs_b, after(full, *added),
         start_state.reshape(WIDE, 128),
     )
-    own = own_product(at, layer_input, keep, got, *after(plain_in, write_grad))
-    totals = own_total(own, *after(added_in, own, near_terms[0]))
+    arrived = added_in[0], plain_in[0], plain_in[1], added_in[1]
+    totals = own_total(own, after(arrived, write_grad, near_terms[0]))
     same, cross = list(totals[:4]), list(totals[4:])
     for g in range(3):
         same[g] = second_hop(same[g], ORDER[g], 0)

time: 125 us -> 111 us (0.89)
  Pallas kernels: 74.7 us -> 47.7 us
  waiting for transfers between devices: 6.89 us -> 13.4 us
  starting transfers between devices: 41.2 us -> 44.1 us
  local copies, waits for them, and re-layouts: 1.25 us -> 3.45 us
    pallas_call x3 -> x2, Pallas kernels: 13.7 us -> 4.83 us  [ring_product(): pl.pallas_call(ring_kernel, grid_spec=pltpu.PrefetchScalarGridSpec(num_sc...]
    ppermute x27, waiting for transfers between devices: 6.89 us -> 13.4 us  [routed(): return lax.ppermute(block, ('ctx', 'smp'), route)]
    pallas_call x1, Pallas kernels: 5.87 us -> 2.7 us  [input_product(): pl.pallas_call(input_kernel, grid=(depth // tile,), in_specs=[full_block(...]
    pallas_call x1, Pallas kernels: 4.76 us -> 1.86 us  [x_final(): pl.pallas_call(x_kernel, grid=(1,), in_specs=[whole(pltpu.SMEM)] + [full_...]
    ppermute x27, starting transfers between devices: 41.2 us -> 44.1 us  [routed(): return lax.ppermute(block, ('ctx', 'smp'), route)]
    pallas_call x1, Pallas kernels: 3.83 us -> 0.95 us  [own_total(): pl.pallas_call(total_kernel, grid=(2,), in_specs=[pl.BlockSpec((2, 256, W...]
    unnamed x12 -> x30, local copies, waits for them, and re-layouts: 1.25 us -> 3.45 us
    pallas_call x1, Pallas kernels: 7.3 us -> 5.18 us  [vectors(): pl.pallas_call(vector_kernel, grid=(CHUNKS // 2,), out_shape=[jax.ShapeDt...]
  transfers between devices with their start and end apart: 27 -> 27, of which waited for: 4 -> 8; matrix products, arithmetic and copies ran while one was open for 0% -> 0% of each run, Pallas kernels for 50% -> 37%
where the time goes in v5:
time: 111 us; the launch traced here: 110 us
  Pallas kernels  47.7 us (43%)
  starting transfers between devices  44.1 us (40%)
  waiting for transfers between devices  13.4 us (12%)
  local copies, waits for them, and re-layouts  3.45 us (3%)
    ppermute x27, starting transfers between devices, routed(): return lax.ppermute(block, ('ctx', 'smp'), route)  44.1 us
    ppermute x27, waiting for transfers between devices, routed(): return lax.ppermute(block, ('ctx', 'smp'), route)  13.4 us
    pallas_call x2, Pallas kernels, project(): pl.pallas_call(project_kernel, grid=(2,), out_shape=jax.ShapeDtypeStruct(...  11.3 us
    pallas_call x1, Pallas kernels, input_rest(): pl.pallas_call(rest_kernel, grid_spec=pltpu.PrefetchScalarGridSpec(num_sc...  6.07 us
    pallas_call x1, Pallas kernels, vectors(): pl.pallas_call(vector_kernel, grid=(CHUNKS // 2,), out_shape=[jax.ShapeDt...  5.18 us
    pallas_call x2, Pallas kernels, ring_product(): pl.pallas_call(ring_kernel, grid_spec=pltpu.PrefetchScalarGridSpec(num_sc...  4.83 us
    pallas_call x1, Pallas kernels, pre(): pl.pallas_call(pre_kernel, grid=(1,), out_shape=[jax.ShapeDtypeStruct((CH...  4.34 us
    pallas_call x1, Pallas kernels, plain_product(): pl.pallas_call(plain_kernel, grid_spec=pltpu.PrefetchScalarGridSpec(num_s...  3.87 us
  transfers between devices with their start and end apart: 27, of which 8 were waited for; matrix products, arithmetic and copies ran while one was open for 0% of the time, Pallas kernels for 37%

profile of v5, /device:TPU:1, one launch (start us, length us, event | category | flops | bytes accessed | tf_op | source)
XLA Modules:
  0.0 109.6 jit_solution(14790515506599302966)
XLA Ops:
  0.6 1.5 %collective-permute-start.6 = (bf16[4096,1024]{1,0:T(8,128)(2,1)}, bf16[4096,1024]{1,0:T(8,128)(2,1)}, u32[]{:S(2)}, u32[]{:S(2)}) collective-permute-start(bf16[4096,1024]{1,0:T(8,128)(2,1)} %w_ref.5), channel_id=1, source_target_pairs={{0,1},{1,0},{2,3},{3,2},{4,5},{5,4},{6,7},{7,6},{8,9},{9,8},{10,11... | collective-permute-start | bytes 25165832 | tf_op jit(solution)/shard_map/ppermute | solution.py:47
  2.1 4.3 %shard_map.129 = (f32[4,128,16]{2,1,0:T(8,128)}, f32[4,16,128]{2,1,0:T(8,128)}, f32[512,16]{1,0:T(8,128)}, bf16[512,1024]{1,0:T(8,128)(2,1)}, bf16[3,128,1024]{2...) custom-call(f32[16]{0:T(128)} %dlog_ref.1, ...), custom_call_target="tpu_custom_call" | custom-call | flops 1 | bytes 1 | tf_op jit(solution)/shard_map/pallas_call | solution.py:181
  6.5 1.4 %collective-permute-start = (bf16[272,256]{1,0:T(8,128)(2,1)}, bf16[272,256]{1,0:T(8,128)(2,1)S(1)}, u32[]{:S(2)}, u32[]{:S(2)}) collective-permute-start(bf16[272,256]{1,0:T(8,128)(2,1)} %get-tuple-element.71), channel_id=1, source_target_pairs={{0,8},{1,9},{2,10},{3,11},{4,12},{5,13},{6,14},{7,15},{8,16},{9,17... | collective-permute-start | bytes 417800 | tf_op jit(solution)/shard_map/ppermute | solution.py:47
  7.9 2.6 %collective-permute-start.1 = (bf16[272,256]{1,0:T(8,128)(2,1)}, bf16[272,256]{1,0:T(8,128)(2,1)S(1)}, u32[]{:S(2)}, u32[]{:S(2)}) collective-permute-start(bf16[272,256]{1,0:T(8,128)(2,1)} %get-tuple-element.72), channel_id=1, source_target_pairs={{0,16},{1,17},{2,18},{3,19},{4,20},{5,21},{6,22},{7,23},{8,24},{9,... | collective-permute-start | bytes 417800 | tf_op jit(solution)/shard_map/ppermute | solution.py:47
  10.5 1.1 collective-permute-start.2
  11.5 5.7 %shard_map.130.first_ref = bf16[512,512]{1,0:T(8,128)(2,1)} custom-call(bf16[512,4096]{1,0:T(8,128)(2,1)} %down_ref.5, bf16[4096,1024]{1,0:T(8,128)(2,1)} %w_ref.5), custom_call_target="tpu_custom_call" | custom-call | flops 1 | bytes 1 | tf_op jit(solution)/shard_map/pallas_call | solution.py:485
  17.2 0.1 pad_add_fusion.at_ref
  17.3 0.0 collective-permute-done.a1
  17.3 0.2 collective-permute-done.1.a2
  17.5 0.7 shard_map.131.b0
  18.2 0.0 copy-start.2
  18.2 0.0 copy-start.3
  18.2 0.0 copy-start.4
  18.2 0.0 copy-start.9
  18.3 0.0 copy-start.10
  18.3 0.0 copy-start.12
  18.3 3.8 %collective-permute-start.5 = (bf16[272,256]{1,0:T(8,128)(2,1)S(1)}, bf16[272,256]{1,0:T(8,128)(2,1)S(1)}, u32[]{:S(2)}, u32[]{:S(2)}) collective-permute-start(bf16[272,256]{1,0:T(8,128)(2,1)S(1)} %shard_map.131.b0), channel_id=1, source_target_pairs={{0,96},{1,97},{2,98},{3,99},{4,100},{5,101},{6,102},{7,103},{8,104... | collective-permute-start | bytes 417800 | tf_op jit(solution)/shard_map/ppermute | solution.py:47
  22.1 0.0 collective-permute-start.4
  22.1 0.7 collective-permute-start.3
  22.8 5.7 %shard_map.132.second_ref = bf16[512,512]{1,0:T(8,128)(2,1)} custom-call(bf16[512,4096]{1,0:T(8,128)(2,1)} %down_ref.5, bf16[4096,1024]{1,0:T(8,128)(2,1)} %w_ref.5), custom_call_target="tpu_custom_call" | custom-call | flops 1 | bytes 1 | tf_op jit(solution)/shard_map/pallas_call | solution.py:485
  28.5 0.0 collective-permute-done.5.b3
  28.5 0.0 collective-permute-done.4.b2
  28.5 3.0 %collective-permute-done.3.b1 = bf16[272,256]{1,0:T(8,128)(2,1)S(1)} collective-permute-done((bf16[272,256]{1,0:T(8,128)(2,1)S(1)}, bf16[272,256]{1,0:T(8,128)(2,1)S(1)}, u32[]{:S(2)}, u32[]{:S(2)}) %collective-permute-start.3) | collective-permute-done | bytes 139296 | tf_op jit(solution)/shard_map/ppermute | solution.py:47
  31.5 0.8 shard_map.133
  32.3 0.5 collective-permute-start.7
  32.8 2.7 %collective-permute-start.8 = (bf16[128,256]{1,0:T(8,128)(2,1)S(1)}, bf16[128,256]{1,0:T(8,128)(2,1)S(1)}, u32[]{:S(2)}, u32[]{:S(2)}) collective-permute-start(bf16[128,256]{1,0:T(8,128)(2,1)S(1)} %get-tuple-element.90), channel_id=1, source_target_pairs={{0,16},{1,17},{2,18},{3,19},{4,20},{5,21},{6,22},{7,23},{8,24},{9,... | collective-permute-start | bytes 196616 | tf_op jit(solution)/shard_map/ppermute | solution.py:47
  35.6 0.9 collective-permute-start.9
  36.5 2.4 %shard_map.134.base_ref = bf16[512,1024]{1,0:T(8,128)(2,1)S(1)} custom-call(f32[16]{0:T(128)S(1)} %copy-done.12, f32[4,128,16]{2,1,0:T(8,128)S(1)} %copy-done.3, f32[4,16,128]{2,1,0:T(8,128)S(1)} %copy-done.11, f32[512,16]{1,0:T(8,128)S(1)} %copy-done.4, bf16[512,128]{1,0:T(8,128)(2,1)S(1)} %bitcast.16, bf16[512,128]{1,0:T(8,128)(2,1)S(1)} %bitcast.18, ...), custom_call_target="tpu_custom_call" | custom-call | flops 1 | bytes 1 | tf_op jit(solution)/shard_map/pallas_call | solution.py:309
  38.9 0.0 collective-permute-done.8.q2
  38.9 0.6 collective-permute-done.9.q3
  39.5 1.9 %shard_map.135 = (bf16[512,512]{1,0:T(8,128)(2,1)S(1)}, bf16[1024,512]{1,0:T(8,128)(2,1)S(1)}, bf16[256,1024]{1,0:T(8,128)(2,1)S(1)}, bf16[4,128,1024]{2,1,0:T(8,128)(2,1)S(1)}) custom-call(s32[4]{0:T(128)S(1)} %pad_add_fusion.at_ref, bf16[128,256]{1,0:T(8,128)(2,1)S(1)} %get-tuple-element.88.q0, bf16[128,256]{1,0:T(8,128)(2,1)S(1)} %collective-permute-done.7.q1, ...), custom_call_target="tpu_custom_call" | custom-call | flops 1 | bytes 1 | tf_op jit(solution)/shard_map/pallas_call | solution.py:370
  41.4 1.8 %collective-permute-start.10 = (bf16[1024,512]{1,0:T(8,128)(2,1)S(1)}, bf16[1024,512]{1,0:T(8,128)(2,1)S(1)}, u32[]{:S(2)}, u32[]{:S(2)}) collective-permute-start(bf16[1024,512]{1,0:T(8,128)(2,1)S(1)} %get-tuple-element.97), channel_id=1, source_target_pairs={{0,1},{1,0},{2,3},{3,2},{4,5},{5,4},{6,7},{7,6},{8,9},{9,8},{10,11... | collective-permute-start | bytes 3145736 | tf_op jit(solution)/shard_map/ppermute | solution.py:47
  43.2 3.4 %copy-done.1 = bf16[4096,1024]{1,0:T(8,128)(2,1)S(1)} copy-done((bf16[4096,1024]{1,0:T(8,128)(2,1)S(1)}, bf16[4096,1024]{1,0:T(8,128)(2,1)}, u32[]{:S(2)}) %copy-start.1) | copy-done | bytes 8388632
  46.6 2.7 %shard_map.136.part_ref = bf16[256,4096]{1,0:T(8,128)(2,1)S(1)} custom-call(bf16[256,1024]{1,0:T(8,128)(2,1)S(1)} %get-tuple-element.99.x_ref, bf16[4096,1024]{1,0:T(8,128)(2,1)S(1)} %copy-done.1), custom_call_target="tpu_custom_call" | custom-call | flops 1 | bytes 1 | tf_op jit(solution)/shard_map/pallas_call | solution.py:640
  49.3 2.4 %shard_map.137 = (bf16[2,256,1024]{2,1,0:T(8,128)(2,1)S(1)}, bf16[2,256,1024]{2,1,0:T(8,128)(2,1)S(1)}) custom-call(s32[4]{0:T(128)S(1)} %pad_add_fusion.at_ref, bf16[512,4096]{1,0:T(8,128)(2,1)S(1)} %copy-done, bf16[512,4096]{1,0:T(8,128)(2,1)S(1)} %copy-done, bf16[512,512]{1,0:T(8,128)(2,1)S(1)} %get-tuple-element.103.keep_ref, ...), custom_call_target="tpu_custom_call" | custom-call | flops 1 | bytes 1 | tf_op jit(solution)/shard_map/pallas_call | solution.py:534
  51.7 0.1 collective-permute-start.11
  51.8 2.7 %collective-permute-start.12 = (bf16[2,256,1024]{2,1,0:T(8,128)(2,1)S(1)}, bf16[2,256,1024]{2,1,0:T(8,128)(2,1)S(1)}, u32[]{:S(2)}, u32[]{:S(2)}) collective-permute-start(bf16[2,256,1024]{2,1,0:T(8,128)(2,1)S(1)} %get-tuple-element.102), channel_id=1, source_target_pairs={{0,24},{1,97},{2,26},{3,99},{4,28},{5,101},{6,30},{7,103},{8,0},{9... | collective-permute-start | bytes 3145736 | tf_op jit(solution)/shard_map/ppermute | solution.py:47
  54.5 3.9 %shard_map.138 = (bf16[2,256,1024]{2,1,0:T(8,128)(2,1)S(1)}, bf16[2,256,1024]{2,1,0:T(8,128)(2,1)S(1)}, bf16[4,256,1024]{2,1,0:T(8,128)(2,1)S(1)}) custom-call(s32[4]{0:T(128)S(1)} %pad_add_fusion.at_ref, bf16[512,4096]{1,0:T(8,128)(2,1)S(1)} %copy-done, bf16[512,4096]{1,0:T(8,128)(2,1)S(1)} %copy-done, bf16[512,4096]{1,0:T(8,128)(2,1)S(1)} %copy-done, ...), custom_call_target="tpu_custom_call" | custom-call | flops 1 | bytes 1 | tf_op jit(solution)/shard_map/pallas_call | solution.py:563
  58.3 0.1 collective-permute-start.14
  58.4 2.7 %collective-permute-start.15 = (bf16[2,256,1024]{2,1,0:T(8,128)(2,1)S(1)}, bf16[2,256,1024]{2,1,0:T(8,128)(2,1)S(1)}, u32[]{:S(2)}, u32[]{:S(2)}) collective-permute-start(bf16[2,256,1024]{2,1,0:T(8,128)(2,1)S(1)} %get-tuple-element.105), channel_id=1, source_target_pairs={{0,24},{1,97},{2,26},{3,99},{4,28},{5,101},{6,30},{7,103},{8,0},{9... | collective-permute-start | bytes 3145736 | tf_op jit(solution)/shard_map/ppermute | solution.py:47
  61.1 6.1 %shard_map.139 = (bf16[64,4096]{1,0:T(8,128)(2,1)S(1)}, bf16[64,4096]{1,0:T(8,128)(2,1)S(1)}, bf16[64,4096]{1,0:T(8,128)(2,1)S(1)}, f32[64,4096]{1,0:T(8,128)S(1)}) custom-call(s32[4]{0:T(128)S(1)} %pad_add_fusion.at_ref, bf16[1024,512]{1,0:T(8,128)(2,1)S(1)} %collective-permute-done.10.got_ref.left_ref.right_ref, ...), custom_call_target="tpu_custom_call" | custom-call | flops 1 | bytes 1 | tf_op jit(solution)/shard_map/pallas_call | solution.py:664
  67.2 2.5 %collective-permute-start.17 = (bf16[64,4096]{1,0:T(8,128)(2,1)S(1)}, bf16[64,4096]{1,0:T(8,128)(2,1)S(1)}, u32[]{:S(2)}, u32[]{:S(2)}) collective-permute-start(bf16[64,4096]{1,0:T(8,128)(2,1)S(1)} %get-tuple-element.110), channel_id=1, source_target_pairs={{0,2},{1,7},{2,4},{3,1},{4,6},{5,3},{6,0},{7,5},{8,10},{9,15},{10,... | collective-permute-start | bytes 1572872 | tf_op jit(solution)/shard_map/ppermute | solution.py:47
  69.7 0.0 copy-start.8
  69.7 0.0 copy-start.14
  69.8 2.4 %shard_map.140 = (bf16[2,256,1024]{2,1,0:T(8,128)(2,1)S(1)}, bf16[2,256,1024]{2,1,0:T(8,128)(2,1)S(1)}) custom-call(s32[4]{0:T(128)S(1)} %pad_add_fusion.at_ref, bf16[512,4096]{1,0:T(8,128)(2,1)S(1)} %copy-done, bf16[512,4096]{1,0:T(8,128)(2,1)S(1)} %copy-done, bf16[512,512]{1,0:T(8,128)(2,1)S(1)} %get-tuple-element.103.keep_ref, ...), custom_call_target="tpu_custom_call" | custom-call | flops 1 | bytes 1 | tf_op jit(solution)/shard_map/pallas_call | solution.py:534
  72.2 0.1 collective-permute-start.13
  72.3 2.7 %collective-permute-start.16 = (bf16[2,256,1024]{2,1,0:T(8,128)(2,1)S(1)}, bf16[2,256,1024]{2,1,0:T(8,128)(2,1)S(1)}, u32[]{:S(2)}, u32[]{:S(2)}) collective-permute-start(bf16[2,256,1024]{2,1,0:T(8,128)(2,1)S(1)} %get-tuple-element.115), channel_id=1, source_target_pairs={{0,24},{1,97},{2,26},{3,99},{4,28},{5,101},{6,30},{7,103},{8,0},{9... | collective-permute-start | bytes 3145736 | tf_op jit(solution)/shard_map/ppermute | solution.py:47
  74.9 3.2 %collective-permute-done.14.below_plain = bf16[2,256,1024]{2,1,0:T(8,128)(2,1)S(1)} collective-permute-done((bf16[2,256,1024]{2,1,0:T(8,128)(2,1)S(1)}, bf16[2,256,1024]{2,1,0:T(8,128)(2,1)S(1)}, u32[]{:S(2)}, u32[]{:S(2)}) %collective-permute-start.14) | collective-permute-done | bytes 1048608 | tf_op jit(solution)/shard_map/ppermute | solution.py:47
  78.2 1.2 %collective-permute-start.18 = (bf16[64,4096]{1,0:T(8,128)(2,1)S(1)}, bf16[64,4096]{1,0:T(8,128)(2,1)S(1)}, u32[]{:S(2)}, u32[]{:S(2)}) collective-permute-start(bf16[64,4096]{1,0:T(8,128)(2,1)S(1)} %get-tuple-element.133), channel_id=1, source_target_pairs={{0,6},{1,3},{2,0},{3,5},{4,2},{5,7},{6,4},{7,1},{8,14},{9,11},{10,... | collective-permute-start | bytes 1572872 | tf_op jit(solution)/shard_map/ppermute | solution.py:47
  79.4 2.4 %collective-permute-start.19 = (bf16[64,4096]{1,0:T(8,128)(2,1)S(1)}, bf16[64,4096]{1,0:T(8,128)(2,1)S(1)}, u32[]{:S(2)}, u32[]{:S(2)}) collective-permute-start(bf16[64,4096]{1,0:T(8,128)(2,1)S(1)} %get-tuple-element.134), channel_id=1, source_target_pairs={{0,4},{1,5},{2,6},{3,7},{4,0},{5,1},{6,2},{7,3},{8,12},{9,13},{10,... | collective-permute-start | bytes 1572872 | tf_op jit(solution)/shard_map/ppermute | solution.py:47
  81.8 5.2 %shard_map.141 = (f32[512,128]{1,0:T(8,128)}, f32[512,128]{1,0:T(8,128)}) custom-call(f32[4,128,16]{2,1,0:T(8,128)S(1)} %copy-done.3, f32[4,16,128]{2,1,0:T(8,128)S(1)} %copy-done.11, f32[512,16]{1,0:T(8,128)S(1)} %copy-done.4, bf16[512,128]{1,0:T(8,128)(2,1)S(1)} %bitcast.17, bf16[512,128]{1,0:T(8,128)(2,1)S(1)} %bitcast.20, ...), custom_call_target="tpu_custom_call" | custom-call | flops 49999998976 | bytes 1 | tf_op jit(solution)/shard_map/pallas_call | solution.py:445
  87.0 2.4 %collective-permute-done.13.below_add = bf16[2,256,1024]{2,1,0:T(8,128)(2,1)S(1)} collective-permute-done((bf16[2,256,1024]{2,1,0:T(8,128)(2,1)S(1)}, bf16[2,256,1024]{2,1,0:T(8,128)(2,1)S(1)}, u32[]{:S(2)}, u32[]{:S(2)}) %collective-permute-start.13) | collective-permute-done | bytes 1048608 | tf_op jit(solution)/shard_map/ppermute | solution.py:47
  89.4 1.0 shard_map.142
  90.4 1.3 %collective-permute-start.20 = (bf16[256,512]{1,0:T(8,128)(2,1)S(1)}, bf16[256,512]{1,0:T(8,128)(2,1)S(1)}, u32[]{:S(2)}, u32[]{:S(2)}) collective-permute-start(bf16[256,512]{1,0:T(8,128)(2,1)S(1)} %get-tuple-element.124), channel_id=1, source_target_pairs={{0,64},{1,17},{2,66},{3,19},{4,68},{5,21},{6,70},{7,23},{8,72},{9,... | collective-permute-start | bytes 786440 | tf_op jit(solution)/shard_map/ppermute | solution.py:47
  91.7 1.4 %collective-permute-start.21 = (bf16[256,512]{1,0:T(8,128)(2,1)S(1)}, bf16[256,512]{1,0:T(8,128)(2,1)S(1)}, u32[]{:S(2)}, u32[]{:S(2)}) collective-permute-start(bf16[256,512]{1,0:T(8,128)(2,1)S(1)} %get-tuple-element.125), channel_id=1, source_target_pairs={{0,32},{1,9},{2,34},{3,11},{4,36},{5,13},{6,38},{7,15},{8,40},{9,1... | collective-permute-start | bytes 786440 | tf_op jit(solution)/shard_map/ppermute | solution.py:47
  93.1 1.2 %collective-permute-start.22 = (bf16[256,512]{1,0:T(8,128)(2,1)S(1)}, bf16[256,512]{1,0:T(8,128)(2,1)S(1)}, u32[]{:S(2)}, u32[]{:S(2)}) collective-permute-start(bf16[256,512]{1,0:T(8,128)(2,1)S(1)} %get-tuple-element.126), channel_id=1, source_target_pairs={{0,96},{1,25},{2,98},{3,27},{4,100},{5,29},{6,102},{7,31},{8,104},... | collective-permute-start | bytes 786440 | tf_op jit(solution)/shard_map/ppermute | solution.py:47
  94.3 6.0 %collective-permute-start.23 = (bf16[256,512]{1,0:T(8,128)(2,1)S(1)}, bf16[256,512]{1,0:T(8,128)(2,1)S(1)}, u32[]{:S(2)}, u32[]{:S(2)}) collective-permute-start(bf16[256,512]{1,0:T(8,128)(2,1)S(1)} %get-tuple-element.128), channel_id=1, source_target_pairs={{0,65},{1,16},{2,67},{3,18},{4,69},{5,20},{6,71},{7,22},{8,73},{9,... | collective-permute-start | bytes 786440 | tf_op jit(solution)/shard_map/ppermute | solution.py:47
  100.4 1.7 %collective-permute-start.25 = (bf16[256,512]{1,0:T(8,128)(2,1)S(1)}, bf16[256,512]{1,0:T(8,128)(2,1)S(1)}, u32[]{:S(2)}, u32[]{:S(2)}) collective-permute-start(bf16[256,512]{1,0:T(8,128)(2,1)S(1)} %get-tuple-element.130), channel_id=1, source_target_pairs={{0,97},{1,24},{2,99},{3,26},{4,101},{5,28},{6,103},{7,30},{8,105},... | collective-permute-start | bytes 786440 | tf_op jit(solution)/shard_map/ppermute | solution.py:47
  102.1 0.8 collective-permute-start.26
  103.0 1.1 shard_map.143
  104.1 0.4 collective-permute-done.23.refs_4_
  104.5 3.2 %collective-permute-done.24.refs_5_ = bf16[256,512]{1,0:T(8,128)(2,1)S(1)} collective-permute-done((bf16[256,512]{1,0:T(8,128)(2,1)S(1)}, bf16[256,512]{1,0:T(8,128)(2,1)S(1)}, u32[]{:S(2)}, u32[]{:S(2)}) %collective-permute-start.24) | collective-permute-done | bytes 262176 | tf_op jit(solution)/shard_map/ppermute | solution.py:47
  107.7 0.3 collective-permute-done.25.refs_6_
  108.0 1.6 %shard_map.144 = bf16[256,1024]{1,0:T(8,128)(2,1)} custom-call(s32[4]{0:T(128)S(1)} %pad_add_fusion.at_ref, bf16[256,512]{1,0:T(8,128)(2,1)S(1)} %collective-permute-done.20.refs_0_, bf16[256,512]{1,0:T(8,128)(2,1)S(1)} %collective-permute-done.21.refs_1_, bf16[256,512]{1,0:T(8,128)(2,1)S(1)} %collective-permute-done.22.refs_2_, ...), custom_call_target="tpu_custom_call" | custom-call | flops 1 | bytes 1 | tf_op jit(solution)/shard_map/pallas_call | solution.py:623
  (37 shorter events, 0.1 us)
Async XLA Ops:
  0.6 30.9 %collective-permute-start.6 = (bf16[4096,1024]{1,0:T(8,128)(2,1)}, bf16[4096,1024]{1,0:T(8,128)(2,1)}, u32[]{:S(2)}, u32[]{:S(2)}) collective-permute-start(bf16[4096,1024]{1,0:T(8,128)(2,1)} %w_ref.5), channel_id=1, source_target_pairs={{0,1},{1,0},{2,3},{3,2},{4,5},{5,4},{6,7},{7,6},{8,9},{9,8},{10,11... | collective-permute-start | bytes 25165832 | tf_op jit(solution)/shard_map/ppermute | solution.py:47
  6.5 10.8 %collective-permute-start = (bf16[272,256]{1,0:T(8,128)(2,1)}, bf16[272,256]{1,0:T(8,128)(2,1)S(1)}, u32[]{:S(2)}, u32[]{:S(2)}) collective-permute-start(bf16[272,256]{1,0:T(8,128)(2,1)} %get-tuple-element.71), channel_id=1, source_target_pairs={{0,8},{1,9},{2,10},{3,11},{4,12},{5,13},{6,14},{7,15},{8,16},{9,17... | collective-permute-start | bytes 417800 | tf_op jit(solution)/shard_map/ppermute | solution.py:47
  7.9 9.6 %collective-permute-start.1 = (bf16[272,256]{1,0:T(8,128)(2,1)}, bf16[272,256]{1,0:T(8,128)(2,1)S(1)}, u32[]{:S(2)}, u32[]{:S(2)}) collective-permute-start(bf16[272,256]{1,0:T(8,128)(2,1)} %get-tuple-element.72), channel_id=1, source_target_pairs={{0,16},{1,17},{2,18},{3,19},{4,20},{5,21},{6,22},{7,23},{8,24},{9,... | collective-permute-start | bytes 417800 | tf_op jit(solution)/shard_map/ppermute | solution.py:47
  10.5 7.0 %collective-permute-start.2 = (bf16[272,256]{1,0:T(8,128)(2,1)}, bf16[272,256]{1,0:T(8,128)(2,1)S(1)}, u32[]{:S(2)}, u32[]{:S(2)}) collective-permute-start(bf16[272,256]{1,0:T(8,128)(2,1)} %get-tuple-element.73), channel_id=1, source_target_pairs={{0,24},{1,25},{2,26},{3,27},{4,28},{5,29},{6,30},{7,31},{8,0},{9,1... | collective-permute-start | bytes 417800 | tf_op jit(solution)/shard_map/ppermute | solution.py:47
  11.5 6.0 %copy-start.6 = (bf16[272,256]{1,0:T(8,128)(2,1)S(1)}, bf16[272,256]{1,0:T(8,128)(2,1)}, u32[]{:S(2)}) copy-start(bf16[272,256]{1,0:T(8,128)(2,1)} %get-tuple-element.79.a0) | copy-start | bytes 417796
  18.2 18.2 %copy-start.2 = (bf16[512,1024]{1,0:T(8,128)(2,1)S(1)}, bf16[512,1024]{1,0:T(8,128)(2,1)}, u32[]{:S(2)}) copy-start(bf16[512,1024]{1,0:T(8,128)(2,1)} %grad_ref.4) | copy-start | bytes 3145732
  18.2 18.2 %copy-start.3 = (f32[4,128,16]{2,1,0:T(8,128)S(1)}, f32[4,128,16]{2,1,0:T(8,128)}, u32[]{:S(2)}) copy-start(f32[4,128,16]{2,1,0:T(8,128)} %get-tuple-element.93.rel_ref) | copy-start | bytes 98308
  18.2 18.2 %copy-start.4 = (f32[512,16]{1,0:T(8,128)S(1)}, f32[512,16]{1,0:T(8,128)}, u32[]{:S(2)}) copy-start(f32[512,16]{1,0:T(8,128)} %get-tuple-element.94.step_ref) | copy-start | bytes 98308
  18.2 18.2 %copy-start.9 = (bf16[512,1,128]{2,0,1:T(8,128)(2,1)S(1)}, bf16[512,1,128]{2,0,1:T(8,128)(2,1)}, u32[]{:S(2)}) copy-start(bf16[512,1,128]{2,0,1:T(8,128)(2,1)} %param.16) | copy-start | bytes 393220
  18.3 18.2 %copy-start.10 = (bf16[512,1,128]{2,0,1:T(8,128)(2,1)S(1)}, bf16[512,1,128]{2,0,1:T(8,128)(2,1)}, u32[]{:S(2)}) copy-start(bf16[512,1,128]{2,0,1:T(8,128)(2,1)} %param.15) | copy-start | bytes 393220
  18.3 18.2 %copy-start.11 = (f32[4,16,128]{2,1,0:T(8,128)S(1)}, f32[4,16,128]{2,1,0:T(8,128)}, u32[]{:S(2)}) copy-start(f32[4,16,128]{2,1,0:T(8,128)} %get-tuple-element.95.relt_ref) | copy-start | bytes 98308
  18.3 18.2 %copy-start.12 = (f32[16]{0:T(128)S(1)}, f32[16]{0:T(128)}, u32[]{:S(2)}) copy-start(f32[16]{0:T(128)} %skip_ref.1) | copy-start | bytes 196
  18.3 10.2 %collective-permute-start.5 = (bf16[272,256]{1,0:T(8,128)(2,1)S(1)}, bf16[272,256]{1,0:T(8,128)(2,1)S(1)}, u32[]{:S(2)}, u32[]{:S(2)}) collective-permute-start(bf16[272,256]{1,0:T(8,128)(2,1)S(1)} %shard_map.131.b0), channel_id=1, source_target_pairs={{0,96},{1,97},{2,98},{3,99},{4,100},{5,101},{6,102},{7,103},{8,104... | collective-permute-start | bytes 417800 | tf_op jit(solution)/shard_map/ppermute | solution.py:47
  22.1 6.4 %collective-permute-start.4 = (bf16[272,256]{1,0:T(8,128)(2,1)S(1)}, bf16[272,256]{1,0:T(8,128)(2,1)S(1)}, u32[]{:S(2)}, u32[]{:S(2)}) collective-permute-start(bf16[272,256]{1,0:T(8,128)(2,1)S(1)} %shard_map.131.b0), channel_id=1, source_target_pairs={{0,64},{1,65},{2,66},{3,67},{4,68},{5,69},{6,70},{7,71},{8,72},{9,... | collective-permute-start | bytes 417800 | tf_op jit(solution)/shard_map/ppermute | solution.py:47
  22.1 9.4 %collective-permute-start.3 = (bf16[272,256]{1,0:T(8,128)(2,1)S(1)}, bf16[272,256]{1,0:T(8,128)(2,1)S(1)}, u32[]{:S(2)}, u32[]{:S(2)}) collective-permute-start(bf16[272,256]{1,0:T(8,128)(2,1)S(1)} %shard_map.131.b0), channel_id=1, source_target_pairs={{0,32},{1,33},{2,34},{3,35},{4,36},{5,37},{6,38},{7,39},{8,40},{9,... | collective-permute-start | bytes 417800 | tf_op jit(solution)/shard_map/ppermute | solution.py:47
  28.5 11.0 %copy-start.5 = (bf16[3,128,1024]{2,1,0:T(8,128)(2,1)S(1)}, bf16[3,128,1024]{2,1,0:T(8,128)(2,1)}, u32[]{:S(2)}) copy-start(bf16[3,128,1024]{2,1,0:T(8,128)(2,1)} %get-tuple-element.92.state_ref) | copy-start | bytes 2359300
  32.3 6.6 %collective-permute-start.7 = (bf16[128,256]{1,0:T(8,128)(2,1)S(1)}, bf16[128,256]{1,0:T(8,128)(2,1)S(1)}, u32[]{:S(2)}, u32[]{:S(2)}) collective-permute-start(bf16[128,256]{1,0:T(8,128)(2,1)S(1)} %get-tuple-element.89), channel_id=1, source_target_pairs={{0,8},{1,9},{2,10},{3,11},{4,12},{5,13},{6,14},{7,15},{8,16},{9,17... | collective-permute-start | bytes 196616 | tf_op jit(solution)/shard_map/ppermute | solution.py:47
  32.8 6.1 %collective-permute-start.8 = (bf16[128,256]{1,0:T(8,128)(2,1)S(1)}, bf16[128,256]{1,0:T(8,128)(2,1)S(1)}, u32[]{:S(2)}, u32[]{:S(2)}) collective-permute-start(bf16[128,256]{1,0:T(8,128)(2,1)S(1)} %get-tuple-element.90), channel_id=1, source_target_pairs={{0,16},{1,17},{2,18},{3,19},{4,20},{5,21},{6,22},{7,23},{8,24},{9,... | collective-permute-start | bytes 196616 | tf_op jit(solution)/shard_map/ppermute | solution.py:47
  35.6 3.9 %collective-permute-start.9 = (bf16[128,256]{1,0:T(8,128)(2,1)S(1)}, bf16[128,256]{1,0:T(8,128)(2,1)S(1)}, u32[]{:S(2)}, u32[]{:S(2)}) collective-permute-start(bf16[128,256]{1,0:T(8,128)(2,1)S(1)} %get-tuple-element.91), channel_id=1, source_target_pairs={{0,24},{1,25},{2,26},{3,27},{4,28},{5,29},{6,30},{7,31},{8,0},{9,1... | collective-permute-start | bytes 196616 | tf_op jit(solution)/shard_map/ppermute | solution.py:47
  41.4 7.9 %collective-permute-start.10 = (bf16[1024,512]{1,0:T(8,128)(2,1)S(1)}, bf16[1024,512]{1,0:T(8,128)(2,1)S(1)}, u32[]{:S(2)}, u32[]{:S(2)}) collective-permute-start(bf16[1024,512]{1,0:T(8,128)(2,1)S(1)} %get-tuple-element.97), channel_id=1, source_target_pairs={{0,1},{1,0},{2,3},{3,2},{4,5},{5,4},{6,7},{7,6},{8,9},{9,8},{10,11... | collective-permute-start | bytes 3145736 | tf_op jit(solution)/shard_map/ppermute | solution.py:47
  43.2 3.4 %copy-start.1 = (bf16[4096,1024]{1,0:T(8,128)(2,1)S(1)}, bf16[4096,1024]{1,0:T(8,128)(2,1)}, u32[]{:S(2)}) copy-start(bf16[4096,1024]{1,0:T(8,128)(2,1)} %w_ref.5) | copy-start | bytes 25165828
  46.6 2.7 %copy-start = (bf16[512,4096]{1,0:T(8,128)(2,1)S(1)}, bf16[512,4096]{1,0:T(8,128)(2,1)}, u32[]{:S(2)}) copy-start(bf16[512,4096]{1,0:T(8,128)(2,1)} %down_ref.5) | copy-start | bytes 12582916
  51.7 18.0 %collective-permute-start.11 = (bf16[2,256,1024]{2,1,0:T(8,128)(2,1)S(1)}, bf16[2,256,1024]{2,1,0:T(8,128)(2,1)S(1)}, u32[]{:S(2)}, u32[]{:S(2)}) collective-permute-start(bf16[2,256,1024]{2,1,0:T(8,128)(2,1)S(1)} %get-tuple-element.101), channel_id=1, source_target_pairs={{0,8},{1,33},{2,10},{3,35},{4,12},{5,37},{6,14},{7,39},{8,16},{9,4... | collective-permute-start | bytes 3145736 | tf_op jit(solution)/shard_map/ppermute | solution.py:47
  51.8 17.9 %collective-permute-start.12 = (bf16[2,256,1024]{2,1,0:T(8,128)(2,1)S(1)}, bf16[2,256,1024]{2,1,0:T(8,128)(2,1)S(1)}, u32[]{:S(2)}, u32[]{:S(2)}) collective-permute-start(bf16[2,256,1024]{2,1,0:T(8,128)(2,1)S(1)} %get-tuple-element.102), channel_id=1, source_target_pairs={{0,24},{1,97},{2,26},{3,99},{4,28},{5,101},{6,30},{7,103},{8,0},{9... | collective-permute-start | bytes 3145736 | tf_op jit(solution)/shard_map/ppermute | solution.py:47
  58.3 19.8 %collective-permute-start.14 = (bf16[2,256,1024]{2,1,0:T(8,128)(2,1)S(1)}, bf16[2,256,1024]{2,1,0:T(8,128)(2,1)S(1)}, u32[]{:S(2)}, u32[]{:S(2)}) collective-permute-start(bf16[2,256,1024]{2,1,0:T(8,128)(2,1)S(1)} %get-tuple-element.104), channel_id=1, source_target_pairs={{0,8},{1,33},{2,10},{3,35},{4,12},{5,37},{6,14},{7,39},{8,16},{9,4... | collective-permute-start | bytes 3145736 | tf_op jit(solution)/shard_map/ppermute | solution.py:47
  58.4 19.8 %collective-permute-start.15 = (bf16[2,256,1024]{2,1,0:T(8,128)(2,1)S(1)}, bf16[2,256,1024]{2,1,0:T(8,128)(2,1)S(1)}, u32[]{:S(2)}, u32[]{:S(2)}) collective-permute-start(bf16[2,256,1024]{2,1,0:T(8,128)(2,1)S(1)} %get-tuple-element.105), channel_id=1, source_target_pairs={{0,24},{1,97},{2,26},{3,99},{4,28},{5,101},{6,30},{7,103},{8,0},{9... | collective-permute-start | bytes 3145736 | tf_op jit(solution)/shard_map/ppermute | solution.py:47
  67.2 19.9 %collective-permute-start.17 = (bf16[64,4096]{1,0:T(8,128)(2,1)S(1)}, bf16[64,4096]{1,0:T(8,128)(2,1)S(1)}, u32[]{:S(2)}, u32[]{:S(2)}) collective-permute-start(bf16[64,4096]{1,0:T(8,128)(2,1)S(1)} %get-tuple-element.110), channel_id=1, source_target_pairs={{0,2},{1,7},{2,4},{3,1},{4,6},{5,3},{6,0},{7,5},{8,10},{9,15},{10,... | collective-permute-start | bytes 1572872 | tf_op jit(solution)/shard_map/ppermute | solution.py:47
  69.7 12.1 %copy-start.7 = (bf16[512,512]{1,0:T(8,128)(2,1)S(1)}, bf16[512,512]{1,0:T(8,128)(2,1)}, u32[]{:S(2)}) copy-start(bf16[512,512]{1,0:T(8,128)(2,1)} %shard_map.130.first_ref) | copy-start | bytes 1572868
  69.7 12.1 %copy-start.8 = (bf16[512,512]{1,0:T(8,128)(2,1)S(1)}, bf16[512,512]{1,0:T(8,128)(2,1)}, u32[]{:S(2)}) copy-start(bf16[512,512]{1,0:T(8,128)(2,1)} %shard_map.132.second_ref) | copy-start | bytes 1572868
  69.7 12.1 %copy-start.13 = (bf16[512,1024]{1,0:T(8,128)(2,1)S(1)}, bf16[512,1024]{1,0:T(8,128)(2,1)}, u32[]{:S(2)}) copy-start(bf16[512,1024]{1,0:T(8,128)(2,1)} %get-tuple-element.116.scaled_ref) | copy-start | bytes 3145732
  69.7 12.1 %copy-start.14 = (f32[1,16,64,128]{3,2,1,0:T(8,128)S(1)}, f32[1,16,64,128]{3,2,1,0:T(8,128)}, u32[]{:S(2)}) copy-start(f32[1,16,64,128]{3,2,1,0:T(8,128)} %param.18) | copy-start | bytes 1572868
  72.2 17.2 %collective-permute-start.13 = (bf16[2,256,1024]{2,1,0:T(8,128)(2,1)S(1)}, bf16[2,256,1024]{2,1,0:T(8,128)(2,1)S(1)}, u32[]{:S(2)}, u32[]{:S(2)}) collective-permute-start(bf16[2,256,1024]{2,1,0:T(8,128)(2,1)S(1)} %get-tuple-element.114), channel_id=1, source_target_pairs={{0,8},{1,33},{2,10},{3,35},{4,12},{5,37},{6,14},{7,39},{8,16},{9,4... | collective-permute-start | bytes 3145736 | tf_op jit(solution)/shard_map/ppermute | solution.py:47
  72.3 17.1 %collective-permute-start.16 = (bf16[2,256,1024]{2,1,0:T(8,128)(2,1)S(1)}, bf16[2,256,1024]{2,1,0:T(8,128)(2,1)S(1)}, u32[]{:S(2)}, u32[]{:S(2)}) collective-permute-start(bf16[2,256,1024]{2,1,0:T(8,128)(2,1)S(1)} %get-tuple-element.115), channel_id=1, source_target_pairs={{0,24},{1,97},{2,26},{3,99},{4,28},{5,101},{6,30},{7,103},{8,0},{9... | collective-permute-start | bytes 3145736 | tf_op jit(solution)/shard_map/ppermute | solution.py:47
  78.2 16.2 %collective-permute-start.18 = (bf16[64,4096]{1,0:T(8,128)(2,1)S(1)}, bf16[64,4096]{1,0:T(8,128)(2,1)S(1)}, u32[]{:S(2)}, u32[]{:S(2)}) collective-permute-start(bf16[64,4096]{1,0:T(8,128)(2,1)S(1)} %get-tuple-element.133), channel_id=1, source_target_pairs={{0,6},{1,3},{2,0},{3,5},{4,2},{5,7},{6,4},{7,1},{8,14},{9,11},{10,... | collective-permute-start | bytes 1572872 | tf_op jit(solution)/shard_map/ppermute | solution.py:47
  79.4 21.0 %collective-permute-start.19 = (bf16[64,4096]{1,0:T(8,128)(2,1)S(1)}, bf16[64,4096]{1,0:T(8,128)(2,1)S(1)}, u32[]{:S(2)}, u32[]{:S(2)}) collective-permute-start(bf16[64,4096]{1,0:T(8,128)(2,1)S(1)} %get-tuple-element.134), channel_id=1, source_target_pairs={{0,4},{1,5},{2,6},{3,7},{4,0},{5,1},{6,2},{7,3},{8,12},{9,13},{10,... | collective-permute-start | bytes 1572872 | tf_op jit(solution)/shard_map/ppermute | solution.py:47
  90.4 10.0 %collective-permute-start.20 = (bf16[256,512]{1,0:T(8,128)(2,1)S(1)}, bf16[256,512]{1,0:T(8,128)(2,1)S(1)}, u32[]{:S(2)}, u32[]{:S(2)}) collective-permute-start(bf16[256,512]{1,0:T(8,128)(2,1)S(1)} %get-tuple-element.124), channel_id=1, source_target_pairs={{0,64},{1,17},{2,66},{3,19},{4,68},{5,21},{6,70},{7,23},{8,72},{9,... | collective-permute-start | bytes 786440 | tf_op jit(solution)/shard_map/ppermute | solution.py:47
  91.7 10.5 %collective-permute-start.21 = (bf16[256,512]{1,0:T(8,128)(2,1)S(1)}, bf16[256,512]{1,0:T(8,128)(2,1)S(1)}, u32[]{:S(2)}, u32[]{:S(2)}) collective-permute-start(bf16[256,512]{1,0:T(8,128)(2,1)S(1)} %get-tuple-element.125), channel_id=1, source_target_pairs={{0,32},{1,9},{2,34},{3,11},{4,36},{5,13},{6,38},{7,15},{8,40},{9,1... | collective-permute-start | bytes 786440 | tf_op jit(solution)/shard_map/ppermute | solution.py:47
  93.1 10.9 %collective-permute-start.22 = (bf16[256,512]{1,0:T(8,128)(2,1)S(1)}, bf16[256,512]{1,0:T(8,128)(2,1)S(1)}, u32[]{:S(2)}, u32[]{:S(2)}) collective-permute-start(bf16[256,512]{1,0:T(8,128)(2,1)S(1)} %get-tuple-element.126), channel_id=1, source_target_pairs={{0,96},{1,25},{2,98},{3,27},{4,100},{5,29},{6,102},{7,31},{8,104},... | collective-permute-start | bytes 786440 | tf_op jit(solution)/shard_map/ppermute | solution.py:47
  94.3 10.1 %collective-permute-start.23 = (bf16[256,512]{1,0:T(8,128)(2,1)S(1)}, bf16[256,512]{1,0:T(8,128)(2,1)S(1)}, u32[]{:S(2)}, u32[]{:S(2)}) collective-permute-start(bf16[256,512]{1,0:T(8,128)(2,1)S(1)} %get-tuple-element.128), channel_id=1, source_target_pairs={{0,65},{1,16},{2,67},{3,18},{4,69},{5,20},{6,71},{7,22},{8,73},{9,... | collective-permute-start | bytes 786440 | tf_op jit(solution)/shard_map/ppermute | solution.py:47
  100.4 7.3 %collective-permute-start.24 = (bf16[256,512]{1,0:T(8,128)(2,1)S(1)}, bf16[256,512]{1,0:T(8,128)(2,1)S(1)}, u32[]{:S(2)}, u32[]{:S(2)}) collective-permute-start(bf16[256,512]{1,0:T(8,128)(2,1)S(1)} %get-tuple-element.129), channel_id=1, source_target_pairs={{0,33},{1,8},{2,35},{3,10},{4,37},{5,12},{6,39},{7,14},{8,41},{9,1... | collective-permute-start | bytes 786440 | tf_op jit(solution)/shard_map/ppermute | solution.py:47
  100.4 7.6 %collective-permute-start.25 = (bf16[256,512]{1,0:T(8,128)(2,1)S(1)}, bf16[256,512]{1,0:T(8,128)(2,1)S(1)}, u32[]{:S(2)}, u32[]{:S(2)}) collective-permute-start(bf16[256,512]{1,0:T(8,128)(2,1)S(1)} %get-tuple-element.130), channel_id=1, source_target_pairs={{0,97},{1,24},{2,99},{3,26},{4,101},{5,28},{6,103},{7,30},{8,105},... | collective-permute-start | bytes 786440 | tf_op jit(solution)/shard_map/ppermute | solution.py:47
  102.1 5.9 %collective-permute-start.26 = (bf16[256,512]{1,0:T(8,128)(2,1)S(1)}, bf16[256,512]{1,0:T(8,128)(2,1)S(1)}, u32[]{:S(2)}, u32[]{:S(2)}) collective-permute-start(bf16[256,512]{1,0:T(8,128)(2,1)S(1)} %get-tuple-element.131), channel_id=1, source_target_pairs={{0,1},{1,0},{2,3},{3,2},{4,5},{5,4},{6,7},{7,6},{8,9},{9,8},{10,11... | collective-permute-start | bytes 786440 | tf_op jit(solution)/shard_map/ppermute | solution.py:47

commit v6 on v5

--- a/solution.py
+++ b/solution.py
@@ -321,7 +321,7 @@
         ],
         out_specs=pl.BlockSpec((rows, WIDE), by_two),
         compiler_params=params(ROOMY_LIMIT),
-        cost_estimate=COST,
+        cost_estimate=pl.CostEstimate(flops=4000000000, bytes_accessed=1, transcendentals=0),
     )(skip_gain, rel, relt, step_size, reads, writes, out_grad)
 
 
@@ -746,22 +746,22 @@
     *plain, own = plain_product(at, layer_input, after(keep, *far), got)
     plain_in = first_hop(plain[0], 1, 0), first_hop(plain[1], -1, 0)
     sums = input_rest(at, after(got, *plain), other_weight, part)
-    near_terms = x_hop(sums[1], 1), x_hop(after(sums[2], plain_in), -1)
+    early_term = x_hop(sums[0], 2)
     added = ring_product(at, ADDED, layer_input, keep, got, after(far_in, *sums))
     added_in = first_hop(added[0], 1, 0), first_hop(added[1], -1, 0)
-    far_term = x_hop(after(sums[0], plain_in), 2)
+    late_terms = [x_hop(after(sums[k], plain_in), 3 - 2 * k) for k in (1, 2)]
     write_grad, read_grad = vectors(
         rel, relt, steps, reads, writes, out_grad, scaled, inputs_a, inputs_b, after(full, *added),
         start_state.reshape(WIDE, 128),
     )
     arrived = added_in[0], plain_in[0], plain_in[1], added_in[1]
-    totals = own_total(own, after(arrived, write_grad, near_terms[0]))
+    totals = own_total(own, after(arrived, write_grad, early_term))
     same, cross = list(totals[:4]), list(totals[4:])
     for g in range(3):
         same[g] = second_hop(same[g], ORDER[g], 0)
         cross[g] = second_hop(cross[g], ORDER[g], 1)
     cross[3] = second_hop(cross[3], 0, 1)
-    input_grad = input_final(after(sums[3], *totals), *near_terms, far_term)
+    input_grad = input_final(after(sums[3], *totals), early_term, *late_terms)
     scale = (length * lax.axis_size("ctx")) ** (-0.5)
     weight_grad = weight_final(at, scale, same + cross)
     return (input_grad, weight_grad, write_grad[:, None], read_grad[:, None])

time: 111 us -> 105 us (0.946); the launches traced: 110 us -> 105 us
  local copies, waits for them, and re-layouts: 3.45 us -> 0.08 us
  starting transfers between devices: 44.1 us -> 42.2 us
    unnamed x30 -> x32, local copies, waits for them, and re-layouts: 3.45 us -> 0.08 us
    ppermute x27, starting transfers between devices: 44.1 us -> 42.2 us  [routed(): return lax.ppermute(block, ('ctx', 'smp'), route)]
  transfers between devices with their start and end apart: 27 -> 27, of which waited for: 8 -> 8; matrix products, arithmetic and copies ran while one was open for 0% -> 0% of each run, Pallas kernels for 37% -> 39%
where the time goes in v6:
time: 105 us
  Pallas kernels  47.8 us (46%)
  starting transfers between devices  42.2 us (40%)
  waiting for transfers between devices  14.2 us (14%)
    ppermute x27, starting transfers between devices, routed(): return lax.ppermute(block, ('ctx', 'smp'), route)  42.2 us
    ppermute x27, waiting for transfers between devices, routed(): return lax.ppermute(block, ('ctx', 'smp'), route)  14.2 us
    pallas_call x2, Pallas kernels, project(): pl.pallas_call(project_kernel, grid=(2,), out_shape=jax.ShapeDtypeStruct(...  11.4 us
    pallas_call x1, Pallas kernels, input_rest(): pl.pallas_call(rest_kernel, grid_spec=pltpu.PrefetchScalarGridSpec(num_sc...  6.08 us
    pallas_call x1, Pallas kernels, vectors(): pl.pallas_call(vector_kernel, grid=(CHUNKS // 2,), out_shape=[jax.ShapeDt...  5.18 us
    pallas_call x2, Pallas kernels, ring_product(): pl.pallas_call(ring_kernel, grid_spec=pltpu.PrefetchScalarGridSpec(num_sc...  4.84 us
    pallas_call x1, Pallas kernels, pre(): pl.pallas_call(pre_kernel, grid=(1,), out_shape=[jax.ShapeDtypeStruct((CH...  4.32 us
    pallas_call x1, Pallas kernels, plain_product(): pl.pallas_call(plain_kernel, grid_spec=pltpu.PrefetchScalarGridSpec(num_s...  3.87 us
  transfers between devices with their start and end apart: 27, of which 8 were waited for; matrix products, arithmetic and copies ran while one was open for 0% of the time, Pallas kernels for 39%

profile of v6, /device:TPU:1, one launch (start us, length us, event | category | flops | bytes accessed | tf_op | source)
XLA Modules:
  0.0 105.3 jit_solution(3576267302315173014)
XLA Ops:
  0.6 1.5 %collective-permute-start.6 = (bf16[4096,1024]{1,0:T(8,128)(2,1)}, bf16[4096,1024]{1,0:T(8,128)(2,1)}, u32[]{:S(2)}, u32[]{:S(2)}) collective-permute-start(bf16[4096,1024]{1,0:T(8,128)(2,1)} %w_ref.5), channel_id=1, source_target_pairs={{0,1},{1,0},{2,3},{3,2},{4,5},{5,4},{6,7},{7,6},{8,9},{9,8},{10,11... | collective-permute-start | bytes 25165832 | tf_op jit(solution)/shard_map/ppermute | solution.py:47
  2.1 4.3 %shard_map.129 = (f32[4,128,16]{2,1,0:T(8,128)}, f32[4,16,128]{2,1,0:T(8,128)}, f32[512,16]{1,0:T(8,128)}, bf16[512,1024]{1,0:T(8,128)(2,1)}, bf16[3,128,1024]{2...) custom-call(f32[16]{0:T(128)} %dlog_ref.1, ...), custom_call_target="tpu_custom_call" | custom-call | flops 1 | bytes 1 | tf_op jit(solution)/shard_map/pallas_call | solution.py:181
  6.5 1.4 %collective-permute-start = (bf16[272,256]{1,0:T(8,128)(2,1)}, bf16[272,256]{1,0:T(8,128)(2,1)S(1)}, u32[]{:S(2)}, u32[]{:S(2)}) collective-permute-start(bf16[272,256]{1,0:T(8,128)(2,1)} %get-tuple-element.71), channel_id=1, source_target_pairs={{0,8},{1,9},{2,10},{3,11},{4,12},{5,13},{6,14},{7,15},{8,16},{9,17... | collective-permute-start | bytes 417800 | tf_op jit(solution)/shard_map/ppermute | solution.py:47
  7.8 2.6 %collective-permute-start.1 = (bf16[272,256]{1,0:T(8,128)(2,1)}, bf16[272,256]{1,0:T(8,128)(2,1)S(1)}, u32[]{:S(2)}, u32[]{:S(2)}) collective-permute-start(bf16[272,256]{1,0:T(8,128)(2,1)} %get-tuple-element.72), channel_id=1, source_target_pairs={{0,16},{1,17},{2,18},{3,19},{4,20},{5,21},{6,22},{7,23},{8,24},{9,... | collective-permute-start | bytes 417800 | tf_op jit(solution)/shard_map/ppermute | solution.py:47
  10.5 1.1 %collective-permute-start.2 = (bf16[272,256]{1,0:T(8,128)(2,1)}, bf16[272,256]{1,0:T(8,128)(2,1)S(1)}, u32[]{:S(2)}, u32[]{:S(2)}) collective-permute-start(bf16[272,256]{1,0:T(8,128)(2,1)} %get-tuple-element.73), channel_id=1, source_target_pairs={{0,24},{1,25},{2,26},{3,27},{4,28},{5,29},{6,30},{7,31},{8,0},{9,1... | collective-permute-start | bytes 417800 | tf_op jit(solution)/shard_map/ppermute | solution.py:47
  11.5 5.7 %shard_map.130.first_ref = bf16[512,512]{1,0:T(8,128)(2,1)} custom-call(bf16[512,4096]{1,0:T(8,128)(2,1)} %down_ref.5, bf16[4096,1024]{1,0:T(8,128)(2,1)} %w_ref.5), custom_call_target="tpu_custom_call" | custom-call | flops 1 | bytes 1 | tf_op jit(solution)/shard_map/pallas_call | solution.py:485
  17.2 0.1 pad_add_fusion.at_ref
  17.3 0.2 collective-permute-done.1.a2
  17.5 0.7 shard_map.131.b0
  18.2 0.0 copy-start.1
  18.2 0.0 copy-start.6
  18.2 0.0 copy-start.7
  18.2 0.0 copy-start.8
  18.2 0.0 copy-start.9
  18.3 0.0 copy-start.13
  18.3 3.8 %collective-permute-start.5 = (bf16[272,256]{1,0:T(8,128)(2,1)S(1)}, bf16[272,256]{1,0:T(8,128)(2,1)S(1)}, u32[]{:S(2)}, u32[]{:S(2)}) collective-permute-start(bf16[272,256]{1,0:T(8,128)(2,1)S(1)} %shard_map.131.b0), channel_id=1, source_target_pairs={{0,96},{1,97},{2,98},{3,99},{4,100},{5,101},{6,102},{7,103},{8,104... | collective-permute-start | bytes 417800 | tf_op jit(solution)/shard_map/ppermute | solution.py:47
  22.1 0.0 collective-permute-start.4
  22.1 0.7 collective-permute-start.3
  22.8 5.7 %shard_map.132.second_ref = bf16[512,512]{1,0:T(8,128)(2,1)} custom-call(bf16[512,4096]{1,0:T(8,128)(2,1)} %down_ref.5, bf16[4096,1024]{1,0:T(8,128)(2,1)} %w_ref.5), custom_call_target="tpu_custom_call" | custom-call | flops 1 | bytes 1 | tf_op jit(solution)/shard_map/pallas_call | solution.py:485
  28.5 3.1 %collective-permute-done.3.b1 = bf16[272,256]{1,0:T(8,128)(2,1)S(1)} collective-permute-done((bf16[272,256]{1,0:T(8,128)(2,1)S(1)}, bf16[272,256]{1,0:T(8,128)(2,1)S(1)}, u32[]{:S(2)}, u32[]{:S(2)}) %collective-permute-start.3) | collective-permute-done | bytes 139296 | tf_op jit(solution)/shard_map/ppermute | solution.py:47
  31.5 0.8 shard_map.133
  32.3 0.6 collective-permute-start.7
  32.9 2.7 %collective-permute-start.8 = (bf16[128,256]{1,0:T(8,128)(2,1)S(1)}, bf16[128,256]{1,0:T(8,128)(2,1)S(1)}, u32[]{:S(2)}, u32[]{:S(2)}) collective-permute-start(bf16[128,256]{1,0:T(8,128)(2,1)S(1)} %get-tuple-element.90), channel_id=1, source_target_pairs={{0,16},{1,17},{2,18},{3,19},{4,20},{5,21},{6,22},{7,23},{8,24},{9,... | collective-permute-start | bytes 196616 | tf_op jit(solution)/shard_map/ppermute | solution.py:47
  35.6 0.8 collective-permute-start.9
  36.5 0.0 slice-start.1
  36.5 2.4 %shard_map.134.base_ref = bf16[512,1024]{1,0:T(8,128)(2,1)S(1)} custom-call(f32[16]{0:T(128)S(1)} %copy-done.13, f32[4,128,16]{2,1,0:T(8,128)S(1)} %copy-done.6, f32[4,16,128]{2,1,0:T(8,128)S(1)} %copy-done.12, f32[512,16]{1,0:T(8,128)S(1)} %copy-done.7, bf16[512,128]{1,0:T(8,128)(2,1)S(1)} %bitcast.18, bf16[512,128]{1,0:T(8,128)(2,1)S(1)} %bitcast.20, ...), custom_call_target="tpu_custom_call" | custom-call | flops 4000000000 | bytes 1 | tf_op jit(solution)/shard_map/pallas_call | solution.py:309
  38.9 0.0 collective-permute-done.7.q1
  39.0 0.5 collective-permute-done.9.q3
  39.5 1.9 %shard_map.135 = (bf16[512,512]{1,0:T(8,128)(2,1)S(1)}, bf16[1024,512]{1,0:T(8,128)(2,1)S(1)}, bf16[256,1024]{1,0:T(8,128)(2,1)S(1)}, bf16[4,128,1024]{2,1,0:T(8,128)(2,1)S(1)}) custom-call(s32[4]{0:T(128)S(1)} %pad_add_fusion.at_ref, bf16[128,256]{1,0:T(8,128)(2,1)S(1)} %get-tuple-element.88.q0, bf16[128,256]{1,0:T(8,128)(2,1)S(1)} %collective-permute-done.7.q1, ...), custom_call_target="tpu_custom_call" | custom-call | flops 1 | bytes 1 | tf_op jit(solution)/shard_map/pallas_call | solution.py:370
  41.4 1.8 %collective-permute-start.10 = (bf16[1024,512]{1,0:T(8,128)(2,1)S(1)}, bf16[1024,512]{1,0:T(8,128)(2,1)S(1)}, u32[]{:S(2)}, u32[]{:S(2)}) collective-permute-start(bf16[1024,512]{1,0:T(8,128)(2,1)S(1)} %get-tuple-element.97), channel_id=1, source_target_pairs={{0,1},{1,0},{2,3},{3,2},{4,5},{5,4},{6,7},{7,6},{8,9},{9,8},{10,11... | collective-permute-start | bytes 3145736 | tf_op jit(solution)/shard_map/ppermute | solution.py:47
  43.3 2.7 %shard_map.136.part_ref = bf16[256,4096]{1,0:T(8,128)(2,1)S(1)} custom-call(bf16[256,1024]{1,0:T(8,128)(2,1)S(1)} %get-tuple-element.99.x_ref, bf16[4096,1024]{1,0:T(8,128)(2,1)S(1)} %bitcast.16), custom_call_target="tpu_custom_call" | custom-call | flops 1 | bytes 1 | tf_op jit(solution)/shard_map/pallas_call | solution.py:640
  46.0 2.4 %shard_map.137 = (bf16[2,256,1024]{2,1,0:T(8,128)(2,1)S(1)}, bf16[2,256,1024]{2,1,0:T(8,128)(2,1)S(1)}) custom-call(s32[4]{0:T(128)S(1)} %pad_add_fusion.at_ref, bf16[512,4096]{1,0:T(8,128)(2,1)S(1)} %copy-done, bf16[512,4096]{1,0:T(8,128)(2,1)S(1)} %copy-done, bf16[512,512]{1,0:T(8,128)(2,1)S(1)} %get-tuple-element.103.keep_ref, ...), custom_call_target="tpu_custom_call" | custom-call | flops 1 | bytes 1 | tf_op jit(solution)/shard_map/pallas_call | solution.py:534
  48.4 0.1 collective-permute-start.11
  48.5 2.7 %collective-permute-start.12 = (bf16[2,256,1024]{2,1,0:T(8,128)(2,1)S(1)}, bf16[2,256,1024]{2,1,0:T(8,128)(2,1)S(1)}, u32[]{:S(2)}, u32[]{:S(2)}) collective-permute-start(bf16[2,256,1024]{2,1,0:T(8,128)(2,1)S(1)} %get-tuple-element.102), channel_id=1, source_target_pairs={{0,24},{1,97},{2,26},{3,99},{4,28},{5,101},{6,30},{7,103},{8,0},{9... | collective-permute-start | bytes 3145736 | tf_op jit(solution)/shard_map/ppermute | solution.py:47
  51.2 3.9 %shard_map.138 = (bf16[2,256,1024]{2,1,0:T(8,128)(2,1)S(1)}, bf16[2,256,1024]{2,1,0:T(8,128)(2,1)S(1)}, bf16[4,256,1024]{2,1,0:T(8,128)(2,1)S(1)}) custom-call(s32[4]{0:T(128)S(1)} %pad_add_fusion.at_ref, bf16[512,4096]{1,0:T(8,128)(2,1)S(1)} %copy-done, bf16[512,4096]{1,0:T(8,128)(2,1)S(1)} %copy-done, bf16[512,4096]{1,0:T(8,128)(2,1)S(1)} %copy-done, ...), custom_call_target="tpu_custom_call" | custom-call | flops 1 | bytes 1 | tf_op jit(solution)/shard_map/pallas_call | solution.py:563
  55.0 0.1 collective-permute-start.14
  55.1 2.7 %collective-permute-start.15 = (bf16[2,256,1024]{2,1,0:T(8,128)(2,1)S(1)}, bf16[2,256,1024]{2,1,0:T(8,128)(2,1)S(1)}, u32[]{:S(2)}, u32[]{:S(2)}) collective-permute-start(bf16[2,256,1024]{2,1,0:T(8,128)(2,1)S(1)} %get-tuple-element.105), channel_id=1, source_target_pairs={{0,24},{1,97},{2,26},{3,99},{4,28},{5,101},{6,30},{7,103},{8,0},{9... | collective-permute-start | bytes 3145736 | tf_op jit(solution)/shard_map/ppermute | solution.py:47
  57.8 6.1 %shard_map.139 = (bf16[64,4096]{1,0:T(8,128)(2,1)S(1)}, bf16[64,4096]{1,0:T(8,128)(2,1)S(1)}, bf16[64,4096]{1,0:T(8,128)(2,1)S(1)}, f32[64,4096]{1,0:T(8,128)S(1)}) custom-call(s32[4]{0:T(128)S(1)} %pad_add_fusion.at_ref, bf16[1024,512]{1,0:T(8,128)(2,1)S(1)} %collective-permute-done.10.got_ref.left_ref.right_ref, ...), custom_call_target="tpu_custom_call" | custom-call | flops 1 | bytes 1 | tf_op jit(solution)/shard_map/pallas_call | solution.py:664
  63.9 2.8 %collective-permute-start.17 = (bf16[64,4096]{1,0:T(8,128)(2,1)S(1)}, bf16[64,4096]{1,0:T(8,128)(2,1)S(1)}, u32[]{:S(2)}, u32[]{:S(2)}) collective-permute-start(bf16[64,4096]{1,0:T(8,128)(2,1)S(1)} %get-tuple-element.109), channel_id=1, source_target_pairs={{0,4},{1,5},{2,6},{3,7},{4,0},{5,1},{6,2},{7,3},{8,12},{9,13},{10,... | collective-permute-start | bytes 1572872 | tf_op jit(solution)/shard_map/ppermute | solution.py:47
  66.7 0.0 collective-permute-done.11.refs_0_
  66.7 0.0 copy-start.5
  66.7 0.0 copy-start.11
  66.8 2.4 %shard_map.140 = (bf16[2,256,1024]{2,1,0:T(8,128)(2,1)S(1)}, bf16[2,256,1024]{2,1,0:T(8,128)(2,1)S(1)}) custom-call(s32[4]{0:T(128)S(1)} %pad_add_fusion.at_ref, bf16[512,4096]{1,0:T(8,128)(2,1)S(1)} %copy-done, bf16[512,4096]{1,0:T(8,128)(2,1)S(1)} %copy-done, bf16[512,512]{1,0:T(8,128)(2,1)S(1)} %get-tuple-element.103.keep_ref, ...), custom_call_target="tpu_custom_call" | custom-call | flops 1 | bytes 1 | tf_op jit(solution)/shard_map/pallas_call | solution.py:534
  69.2 0.1 collective-permute-start.13
  69.3 2.7 %collective-permute-start.16 = (bf16[2,256,1024]{2,1,0:T(8,128)(2,1)S(1)}, bf16[2,256,1024]{2,1,0:T(8,128)(2,1)S(1)}, u32[]{:S(2)}, u32[]{:S(2)}) collective-permute-start(bf16[2,256,1024]{2,1,0:T(8,128)(2,1)S(1)} %get-tuple-element.115), channel_id=1, source_target_pairs={{0,24},{1,97},{2,26},{3,99},{4,28},{5,101},{6,30},{7,103},{8,0},{9... | collective-permute-start | bytes 3145736 | tf_op jit(solution)/shard_map/ppermute | solution.py:47
  71.9 2.9 %collective-permute-done.14.below_plain = bf16[2,256,1024]{2,1,0:T(8,128)(2,1)S(1)} collective-permute-done((bf16[2,256,1024]{2,1,0:T(8,128)(2,1)S(1)}, bf16[2,256,1024]{2,1,0:T(8,128)(2,1)S(1)}, u32[]{:S(2)}, u32[]{:S(2)}) %collective-permute-start.14) | collective-permute-done | bytes 1048608 | tf_op jit(solution)/shard_map/ppermute | solution.py:47
  74.9 0.0 collective-permute-done.15.above_plain
  74.9 2.5 %collective-permute-start.18 = (bf16[64,4096]{1,0:T(8,128)(2,1)S(1)}, bf16[64,4096]{1,0:T(8,128)(2,1)S(1)}, u32[]{:S(2)}, u32[]{:S(2)}) collective-permute-start(bf16[64,4096]{1,0:T(8,128)(2,1)S(1)} %get-tuple-element.133), channel_id=1, source_target_pairs={{0,2},{1,7},{2,4},{3,1},{4,6},{5,3},{6,0},{7,5},{8,10},{9,15},{10,... | collective-permute-start | bytes 1572872 | tf_op jit(solution)/shard_map/ppermute | solution.py:47
  77.4 0.0 collective-permute-start.19
  77.4 5.2 %shard_map.141 = (f32[512,128]{1,0:T(8,128)}, f32[512,128]{1,0:T(8,128)}) custom-call(f32[4,128,16]{2,1,0:T(8,128)S(1)} %copy-done.6, f32[4,16,128]{2,1,0:T(8,128)S(1)} %copy-done.12, f32[512,16]{1,0:T(8,128)S(1)} %copy-done.7, bf16[512,128]{1,0:T(8,128)(2,1)S(1)} %bitcast.19, bf16[512,128]{1,0:T(8,128)(2,1)S(1)} %bitcast.22, ...), custom_call_target="tpu_custom_call" | custom-call | flops 49999998976 | bytes 1 | tf_op jit(solution)/shard_map/pallas_call | solution.py:445
  82.6 3.5 %collective-permute-done.13.below_add = bf16[2,256,1024]{2,1,0:T(8,128)(2,1)S(1)} collective-permute-done((bf16[2,256,1024]{2,1,0:T(8,128)(2,1)S(1)}, bf16[2,256,1024]{2,1,0:T(8,128)(2,1)S(1)}, u32[]{:S(2)}, u32[]{:S(2)}) %collective-permute-start.13) | collective-permute-done | bytes 1048608 | tf_op jit(solution)/shard_map/ppermute | solution.py:47
  86.1 0.9 shard_map.142
  87.1 1.3 %collective-permute-start.20 = (bf16[256,512]{1,0:T(8,128)(2,1)S(1)}, bf16[256,512]{1,0:T(8,128)(2,1)S(1)}, u32[]{:S(2)}, u32[]{:S(2)}) collective-permute-start(bf16[256,512]{1,0:T(8,128)(2,1)S(1)} %get-tuple-element.124), channel_id=1, source_target_pairs={{0,64},{1,17},{2,66},{3,19},{4,68},{5,21},{6,70},{7,23},{8,72},{9,... | collective-permute-start | bytes 786440 | tf_op jit(solution)/shard_map/ppermute | solution.py:47
  88.4 1.4 %collective-permute-start.21 = (bf16[256,512]{1,0:T(8,128)(2,1)S(1)}, bf16[256,512]{1,0:T(8,128)(2,1)S(1)}, u32[]{:S(2)}, u32[]{:S(2)}) collective-permute-start(bf16[256,512]{1,0:T(8,128)(2,1)S(1)} %get-tuple-element.125), channel_id=1, source_target_pairs={{0,32},{1,9},{2,34},{3,11},{4,36},{5,13},{6,38},{7,15},{8,40},{9,1... | collective-permute-start | bytes 786440 | tf_op jit(solution)/shard_map/ppermute | solution.py:47
  89.8 1.3 %collective-permute-start.22 = (bf16[256,512]{1,0:T(8,128)(2,1)S(1)}, bf16[256,512]{1,0:T(8,128)(2,1)S(1)}, u32[]{:S(2)}, u32[]{:S(2)}) collective-permute-start(bf16[256,512]{1,0:T(8,128)(2,1)S(1)} %get-tuple-element.126), channel_id=1, source_target_pairs={{0,96},{1,25},{2,98},{3,27},{4,100},{5,29},{6,102},{7,31},{8,104},... | collective-permute-start | bytes 786440 | tf_op jit(solution)/shard_map/ppermute | solution.py:47
  91.0 0.0 collective-permute-done.18.second
  91.0 3.0 %collective-permute-start.23 = (bf16[256,512]{1,0:T(8,128)(2,1)S(1)}, bf16[256,512]{1,0:T(8,128)(2,1)S(1)}, u32[]{:S(2)}, u32[]{:S(2)}) collective-permute-start(bf16[256,512]{1,0:T(8,128)(2,1)S(1)} %get-tuple-element.128), channel_id=1, source_target_pairs={{0,65},{1,16},{2,67},{3,18},{4,69},{5,20},{6,71},{7,22},{8,73},{9,... | collective-permute-start | bytes 786440 | tf_op jit(solution)/shard_map/ppermute | solution.py:47
  94.1 0.2 collective-permute-done.20.refs_0_
  94.2 4.7 %collective-permute-start.25 = (bf16[256,512]{1,0:T(8,128)(2,1)S(1)}, bf16[256,512]{1,0:T(8,128)(2,1)S(1)}, u32[]{:S(2)}, u32[]{:S(2)}) collective-permute-start(bf16[256,512]{1,0:T(8,128)(2,1)S(1)} %get-tuple-element.130), channel_id=1, source_target_pairs={{0,97},{1,24},{2,99},{3,26},{4,101},{5,28},{6,103},{7,30},{8,105},... | collective-permute-start | bytes 786440 | tf_op jit(solution)/shard_map/ppermute | solution.py:47
  98.9 0.0 collective-permute-start.26
  98.9 1.1 %shard_map.143 = bf16[64,4096]{1,0:T(8,128)(2,1)} custom-call(f32[64,4096]{1,0:T(8,128)S(1)} %get-tuple-element.132.own, bf16[64,4096]{1,0:T(8,128)(2,1)S(1)} %collective-permute-done.17.first, bf16[64,4096]{1,0:T(8,128)(2,1)S(1)} %collective-permute-done.18.second, bf16[64,4096]{1,0:T(8,128)(2,1)S(1)} %collective-permute-done.19.third), custom_call_target="tpu_custom_call" | custom-call | flops 1 | bytes 1 | tf_op jit(solution)/shard_map/pallas_call | solution.py:691
  99.9 1.1 %collective-permute-done.23.refs_4_ = bf16[256,512]{1,0:T(8,128)(2,1)S(1)} collective-permute-done((bf16[256,512]{1,0:T(8,128)(2,1)S(1)}, bf16[256,512]{1,0:T(8,128)(2,1)S(1)}, u32[]{:S(2)}, u32[]{:S(2)}) %collective-permute-start.23) | collective-permute-done | bytes 262176 | tf_op jit(solution)/shard_map/ppermute | solution.py:47
  101.0 2.7 %collective-permute-done.24.refs_5_ = bf16[256,512]{1,0:T(8,128)(2,1)S(1)} collective-permute-done((bf16[256,512]{1,0:T(8,128)(2,1)S(1)}, bf16[256,512]{1,0:T(8,128)(2,1)S(1)}, u32[]{:S(2)}, u32[]{:S(2)}) %collective-permute-start.24) | collective-permute-done | bytes 262176 | tf_op jit(solution)/shard_map/ppermute | solution.py:47
  103.7 1.6 %shard_map.144 = bf16[256,1024]{1,0:T(8,128)(2,1)} custom-call(s32[4]{0:T(128)S(1)} %pad_add_fusion.at_ref, bf16[256,512]{1,0:T(8,128)(2,1)S(1)} %collective-permute-done.20.refs_0_, bf16[256,512]{1,0:T(8,128)(2,1)S(1)} %collective-permute-done.21.refs_1_, bf16[256,512]{1,0:T(8,128)(2,1)S(1)} %collective-permute-done.22.refs_2_, ...), custom_call_target="tpu_custom_call" | custom-call | flops 1 | bytes 1 | tf_op jit(solution)/shard_map/pallas_call | solution.py:623
  (40 shorter events, 0.1 us)
Async XLA Ops:
  0.6 30.9 %collective-permute-start.6 = (bf16[4096,1024]{1,0:T(8,128)(2,1)}, bf16[4096,1024]{1,0:T(8,128)(2,1)}, u32[]{:S(2)}, u32[]{:S(2)}) collective-permute-start(bf16[4096,1024]{1,0:T(8,128)(2,1)} %w_ref.5), channel_id=1, source_target_pairs={{0,1},{1,0},{2,3},{3,2},{4,5},{5,4},{6,7},{7,6},{8,9},{9,8},{10,11... | collective-permute-start | bytes 25165832 | tf_op jit(solution)/shard_map/ppermute | solution.py:47
  6.5 10.8 %collective-permute-start = (bf16[272,256]{1,0:T(8,128)(2,1)}, bf16[272,256]{1,0:T(8,128)(2,1)S(1)}, u32[]{:S(2)}, u32[]{:S(2)}) collective-permute-start(bf16[272,256]{1,0:T(8,128)(2,1)} %get-tuple-element.71), channel_id=1, source_target_pairs={{0,8},{1,9},{2,10},{3,11},{4,12},{5,13},{6,14},{7,15},{8,16},{9,17... | collective-permute-start | bytes 417800 | tf_op jit(solution)/shard_map/ppermute | solution.py:47
  7.8 9.6 %collective-permute-start.1 = (bf16[272,256]{1,0:T(8,128)(2,1)}, bf16[272,256]{1,0:T(8,128)(2,1)S(1)}, u32[]{:S(2)}, u32[]{:S(2)}) collective-permute-start(bf16[272,256]{1,0:T(8,128)(2,1)} %get-tuple-element.72), channel_id=1, source_target_pairs={{0,16},{1,17},{2,18},{3,19},{4,20},{5,21},{6,22},{7,23},{8,24},{9,... | collective-permute-start | bytes 417800 | tf_op jit(solution)/shard_map/ppermute | solution.py:47
  10.5 7.0 %collective-permute-start.2 = (bf16[272,256]{1,0:T(8,128)(2,1)}, bf16[272,256]{1,0:T(8,128)(2,1)S(1)}, u32[]{:S(2)}, u32[]{:S(2)}) collective-permute-start(bf16[272,256]{1,0:T(8,128)(2,1)} %get-tuple-element.73), channel_id=1, source_target_pairs={{0,24},{1,25},{2,26},{3,27},{4,28},{5,29},{6,30},{7,31},{8,0},{9,1... | collective-permute-start | bytes 417800 | tf_op jit(solution)/shard_map/ppermute | solution.py:47
  11.5 6.0 %copy-start.3 = (bf16[272,256]{1,0:T(8,128)(2,1)S(1)}, bf16[272,256]{1,0:T(8,128)(2,1)}, u32[]{:S(2)}) copy-start(bf16[272,256]{1,0:T(8,128)(2,1)} %get-tuple-element.79.a0) | copy-start | bytes 417796
  18.2 18.2 %copy-start.1 = (bf16[512,1024]{1,0:T(8,128)(2,1)S(1)}, bf16[512,1024]{1,0:T(8,128)(2,1)}, u32[]{:S(2)}) copy-start(bf16[512,1024]{1,0:T(8,128)(2,1)} %grad_ref.4) | copy-start | bytes 3145732
  18.2 18.2 %copy-start.6 = (f32[4,128,16]{2,1,0:T(8,128)S(1)}, f32[4,128,16]{2,1,0:T(8,128)}, u32[]{:S(2)}) copy-start(f32[4,128,16]{2,1,0:T(8,128)} %get-tuple-element.93.rel_ref) | copy-start | bytes 98308
  18.2 18.2 %copy-start.7 = (f32[512,16]{1,0:T(8,128)S(1)}, f32[512,16]{1,0:T(8,128)}, u32[]{:S(2)}) copy-start(f32[512,16]{1,0:T(8,128)} %get-tuple-element.94.step_ref) | copy-start | bytes 98308
  18.2 18.2 %copy-start.8 = (bf16[512,1,128]{2,0,1:T(8,128)(2,1)S(1)}, bf16[512,1,128]{2,0,1:T(8,128)(2,1)}, u32[]{:S(2)}) copy-start(bf16[512,1,128]{2,0,1:T(8,128)(2,1)} %param.16) | copy-start | bytes 393220
  18.2 18.2 %copy-start.9 = (bf16[512,1,128]{2,0,1:T(8,128)(2,1)S(1)}, bf16[512,1,128]{2,0,1:T(8,128)(2,1)}, u32[]{:S(2)}) copy-start(bf16[512,1,128]{2,0,1:T(8,128)(2,1)} %param.15) | copy-start | bytes 393220
  18.2 18.2 %copy-start.12 = (f32[4,16,128]{2,1,0:T(8,128)S(1)}, f32[4,16,128]{2,1,0:T(8,128)}, u32[]{:S(2)}) copy-start(f32[4,16,128]{2,1,0:T(8,128)} %get-tuple-element.95.relt_ref) | copy-start | bytes 98308
  18.3 18.2 %copy-start.13 = (f32[16]{0:T(128)S(1)}, f32[16]{0:T(128)}, u32[]{:S(2)}) copy-start(f32[16]{0:T(128)} %skip_ref.1) | copy-start | bytes 196
  18.3 10.2 %collective-permute-start.5 = (bf16[272,256]{1,0:T(8,128)(2,1)S(1)}, bf16[272,256]{1,0:T(8,128)(2,1)S(1)}, u32[]{:S(2)}, u32[]{:S(2)}) collective-permute-start(bf16[272,256]{1,0:T(8,128)(2,1)S(1)} %shard_map.131.b0), channel_id=1, source_target_pairs={{0,96},{1,97},{2,98},{3,99},{4,100},{5,101},{6,102},{7,103},{8,104... | collective-permute-start | bytes 417800 | tf_op jit(solution)/shard_map/ppermute | solution.py:47
  22.1 6.4 %collective-permute-start.4 = (bf16[272,256]{1,0:T(8,128)(2,1)S(1)}, bf16[272,256]{1,0:T(8,128)(2,1)S(1)}, u32[]{:S(2)}, u32[]{:S(2)}) collective-permute-start(bf16[272,256]{1,0:T(8,128)(2,1)S(1)} %shard_map.131.b0), channel_id=1, source_target_pairs={{0,64},{1,65},{2,66},{3,67},{4,68},{5,69},{6,70},{7,71},{8,72},{9,... | collective-permute-start | bytes 417800 | tf_op jit(solution)/shard_map/ppermute | solution.py:47
  22.1 9.4 %collective-permute-start.3 = (bf16[272,256]{1,0:T(8,128)(2,1)S(1)}, bf16[272,256]{1,0:T(8,128)(2,1)S(1)}, u32[]{:S(2)}, u32[]{:S(2)}) collective-permute-start(bf16[272,256]{1,0:T(8,128)(2,1)S(1)} %shard_map.131.b0), channel_id=1, source_target_pairs={{0,32},{1,33},{2,34},{3,35},{4,36},{5,37},{6,38},{7,39},{8,40},{9,... | collective-permute-start | bytes 417800 | tf_op jit(solution)/shard_map/ppermute | solution.py:47
  32.3 6.6 %collective-permute-start.7 = (bf16[128,256]{1,0:T(8,128)(2,1)S(1)}, bf16[128,256]{1,0:T(8,128)(2,1)S(1)}, u32[]{:S(2)}, u32[]{:S(2)}) collective-permute-start(bf16[128,256]{1,0:T(8,128)(2,1)S(1)} %get-tuple-element.89), channel_id=1, source_target_pairs={{0,8},{1,9},{2,10},{3,11},{4,12},{5,13},{6,14},{7,15},{8,16},{9,17... | collective-permute-start | bytes 196616 | tf_op jit(solution)/shard_map/ppermute | solution.py:47
  32.9 6.1 %collective-permute-start.8 = (bf16[128,256]{1,0:T(8,128)(2,1)S(1)}, bf16[128,256]{1,0:T(8,128)(2,1)S(1)}, u32[]{:S(2)}, u32[]{:S(2)}) collective-permute-start(bf16[128,256]{1,0:T(8,128)(2,1)S(1)} %get-tuple-element.90), channel_id=1, source_target_pairs={{0,16},{1,17},{2,18},{3,19},{4,20},{5,21},{6,22},{7,23},{8,24},{9,... | collective-permute-start | bytes 196616 | tf_op jit(solution)/shard_map/ppermute | solution.py:47
  35.6 3.9 %collective-permute-start.9 = (bf16[128,256]{1,0:T(8,128)(2,1)S(1)}, bf16[128,256]{1,0:T(8,128)(2,1)S(1)}, u32[]{:S(2)}, u32[]{:S(2)}) collective-permute-start(bf16[128,256]{1,0:T(8,128)(2,1)S(1)} %get-tuple-element.91), channel_id=1, source_target_pairs={{0,24},{1,25},{2,26},{3,27},{4,28},{5,29},{6,30},{7,31},{8,0},{9,1... | collective-permute-start | bytes 196616 | tf_op jit(solution)/shard_map/ppermute | solution.py:47
  36.4 6.8 %slice-start = ((s8[8388608]{0:T(1024)(128)(4,1)}), s8[4194304]{0:T(1024)(128)(4,1)S(1)}, s32[]{:S(2)}) async-start(s8[8388608]{0:T(1024)(128)(4,1)} %bitcast.15), calls=%async_computation | async-start | bytes 8388608
  36.5 3.0 %copy-start.2 = (bf16[3,128,1024]{2,1,0:T(8,128)(2,1)S(1)}, bf16[3,128,1024]{2,1,0:T(8,128)(2,1)}, u32[]{:S(2)}) copy-start(bf16[3,128,1024]{2,1,0:T(8,128)(2,1)} %get-tuple-element.92.state_ref) | copy-start | bytes 2359300
  36.5 6.8 %slice-start.1 = ((s8[8388608]{0:T(1024)(128)(4,1)}), s8[4194304]{0:T(1024)(128)(4,1)S(1)}, s32[]{:S(2)}) async-start(s8[8388608]{0:T(1024)(128)(4,1)} %bitcast.15), calls=%async_computation.1 | async-start | bytes 8388608
  41.4 4.6 %collective-permute-start.10 = (bf16[1024,512]{1,0:T(8,128)(2,1)S(1)}, bf16[1024,512]{1,0:T(8,128)(2,1)S(1)}, u32[]{:S(2)}, u32[]{:S(2)}) collective-permute-start(bf16[1024,512]{1,0:T(8,128)(2,1)S(1)} %get-tuple-element.97), channel_id=1, source_target_pairs={{0,1},{1,0},{2,3},{3,2},{4,5},{5,4},{6,7},{7,6},{8,9},{9,8},{10,11... | collective-permute-start | bytes 3145736 | tf_op jit(solution)/shard_map/ppermute | solution.py:47
  43.3 2.8 %copy-start = (bf16[512,4096]{1,0:T(8,128)(2,1)S(1)}, bf16[512,4096]{1,0:T(8,128)(2,1)}, u32[]{:S(2)}) copy-start(bf16[512,4096]{1,0:T(8,128)(2,1)} %down_ref.5) | copy-start | bytes 12582916
  48.4 18.3 %collective-permute-start.11 = (bf16[2,256,1024]{2,1,0:T(8,128)(2,1)S(1)}, bf16[2,256,1024]{2,1,0:T(8,128)(2,1)S(1)}, u32[]{:S(2)}, u32[]{:S(2)}) collective-permute-start(bf16[2,256,1024]{2,1,0:T(8,128)(2,1)S(1)} %get-tuple-element.101), channel_id=1, source_target_pairs={{0,8},{1,33},{2,10},{3,35},{4,12},{5,37},{6,14},{7,39},{8,16},{9,4... | collective-permute-start | bytes 3145736 | tf_op jit(solution)/shard_map/ppermute | solution.py:47
  48.5 18.2 %collective-permute-start.12 = (bf16[2,256,1024]{2,1,0:T(8,128)(2,1)S(1)}, bf16[2,256,1024]{2,1,0:T(8,128)(2,1)S(1)}, u32[]{:S(2)}, u32[]{:S(2)}) collective-permute-start(bf16[2,256,1024]{2,1,0:T(8,128)(2,1)S(1)} %get-tuple-element.102), channel_id=1, source_target_pairs={{0,24},{1,97},{2,26},{3,99},{4,28},{5,101},{6,30},{7,103},{8,0},{9... | collective-permute-start | bytes 3145736 | tf_op jit(solution)/shard_map/ppermute | solution.py:47
  55.0 19.8 %collective-permute-start.14 = (bf16[2,256,1024]{2,1,0:T(8,128)(2,1)S(1)}, bf16[2,256,1024]{2,1,0:T(8,128)(2,1)S(1)}, u32[]{:S(2)}, u32[]{:S(2)}) collective-permute-start(bf16[2,256,1024]{2,1,0:T(8,128)(2,1)S(1)} %get-tuple-element.104), channel_id=1, source_target_pairs={{0,8},{1,33},{2,10},{3,35},{4,12},{5,37},{6,14},{7,39},{8,16},{9,4... | collective-permute-start | bytes 3145736 | tf_op jit(solution)/shard_map/ppermute | solution.py:47
  55.1 19.8 %collective-permute-start.15 = (bf16[2,256,1024]{2,1,0:T(8,128)(2,1)S(1)}, bf16[2,256,1024]{2,1,0:T(8,128)(2,1)S(1)}, u32[]{:S(2)}, u32[]{:S(2)}) collective-permute-start(bf16[2,256,1024]{2,1,0:T(8,128)(2,1)S(1)} %get-tuple-element.105), channel_id=1, source_target_pairs={{0,24},{1,97},{2,26},{3,99},{4,28},{5,101},{6,30},{7,103},{8,0},{9... | collective-permute-start | bytes 3145736 | tf_op jit(solution)/shard_map/ppermute | solution.py:47
  63.9 18.7 %collective-permute-start.17 = (bf16[64,4096]{1,0:T(8,128)(2,1)S(1)}, bf16[64,4096]{1,0:T(8,128)(2,1)S(1)}, u32[]{:S(2)}, u32[]{:S(2)}) collective-permute-start(bf16[64,4096]{1,0:T(8,128)(2,1)S(1)} %get-tuple-element.109), channel_id=1, source_target_pairs={{0,4},{1,5},{2,6},{3,7},{4,0},{5,1},{6,2},{7,3},{8,12},{9,13},{10,... | collective-permute-start | bytes 1572872 | tf_op jit(solution)/shard_map/ppermute | solution.py:47
  66.7 10.7 %copy-start.4 = (bf16[512,512]{1,0:T(8,128)(2,1)S(1)}, bf16[512,512]{1,0:T(8,128)(2,1)}, u32[]{:S(2)}) copy-start(bf16[512,512]{1,0:T(8,128)(2,1)} %shard_map.130.first_ref) | copy-start | bytes 1572868
  66.7 10.7 %copy-start.5 = (bf16[512,512]{1,0:T(8,128)(2,1)S(1)}, bf16[512,512]{1,0:T(8,128)(2,1)}, u32[]{:S(2)}) copy-start(bf16[512,512]{1,0:T(8,128)(2,1)} %shard_map.132.second_ref) | copy-start | bytes 1572868
  66.7 10.6 %copy-start.10 = (bf16[512,1024]{1,0:T(8,128)(2,1)S(1)}, bf16[512,1024]{1,0:T(8,128)(2,1)}, u32[]{:S(2)}) copy-start(bf16[512,1024]{1,0:T(8,128)(2,1)} %get-tuple-element.116.scaled_ref) | copy-start | bytes 3145732
  66.7 10.6 %copy-start.11 = (f32[1,16,64,128]{3,2,1,0:T(8,128)S(1)}, f32[1,16,64,128]{3,2,1,0:T(8,128)}, u32[]{:S(2)}) copy-start(f32[1,16,64,128]{3,2,1,0:T(8,128)} %param.18) | copy-start | bytes 1572868
  69.2 16.9 %collective-permute-start.13 = (bf16[2,256,1024]{2,1,0:T(8,128)(2,1)S(1)}, bf16[2,256,1024]{2,1,0:T(8,128)(2,1)S(1)}, u32[]{:S(2)}, u32[]{:S(2)}) collective-permute-start(bf16[2,256,1024]{2,1,0:T(8,128)(2,1)S(1)} %get-tuple-element.114), channel_id=1, source_target_pairs={{0,8},{1,33},{2,10},{3,35},{4,12},{5,37},{6,14},{7,39},{8,16},{9,4... | collective-permute-start | bytes 3145736 | tf_op jit(solution)/shard_map/ppermute | solution.py:47
  69.3 16.8 %collective-permute-start.16 = (bf16[2,256,1024]{2,1,0:T(8,128)(2,1)S(1)}, bf16[2,256,1024]{2,1,0:T(8,128)(2,1)S(1)}, u32[]{:S(2)}, u32[]{:S(2)}) collective-permute-start(bf16[2,256,1024]{2,1,0:T(8,128)(2,1)S(1)} %get-tuple-element.115), channel_id=1, source_target_pairs={{0,24},{1,97},{2,26},{3,99},{4,28},{5,101},{6,30},{7,103},{8,0},{9... | collective-permute-start | bytes 3145736 | tf_op jit(solution)/shard_map/ppermute | solution.py:47
  74.9 16.2 %collective-permute-start.18 = (bf16[64,4096]{1,0:T(8,128)(2,1)S(1)}, bf16[64,4096]{1,0:T(8,128)(2,1)S(1)}, u32[]{:S(2)}, u32[]{:S(2)}) collective-permute-start(bf16[64,4096]{1,0:T(8,128)(2,1)S(1)} %get-tuple-element.133), channel_id=1, source_target_pairs={{0,2},{1,7},{2,4},{3,1},{4,6},{5,3},{6,0},{7,5},{8,10},{9,15},{10,... | collective-permute-start | bytes 1572872 | tf_op jit(solution)/shard_map/ppermute | solution.py:47
  77.4 16.7 %collective-permute-start.19 = (bf16[64,4096]{1,0:T(8,128)(2,1)S(1)}, bf16[64,4096]{1,0:T(8,128)(2,1)S(1)}, u32[]{:S(2)}, u32[]{:S(2)}) collective-permute-start(bf16[64,4096]{1,0:T(8,128)(2,1)S(1)} %get-tuple-element.134), channel_id=1, source_target_pairs={{0,6},{1,3},{2,0},{3,5},{4,2},{5,7},{6,4},{7,1},{8,14},{9,11},{10,... | collective-permute-start | bytes 1572872 | tf_op jit(solution)/shard_map/ppermute | solution.py:47
  87.1 7.1 %collective-permute-start.20 = (bf16[256,512]{1,0:T(8,128)(2,1)S(1)}, bf16[256,512]{1,0:T(8,128)(2,1)S(1)}, u32[]{:S(2)}, u32[]{:S(2)}) collective-permute-start(bf16[256,512]{1,0:T(8,128)(2,1)S(1)} %get-tuple-element.124), channel_id=1, source_target_pairs={{0,64},{1,17},{2,66},{3,19},{4,68},{5,21},{6,70},{7,23},{8,72},{9,... | collective-permute-start | bytes 786440 | tf_op jit(solution)/shard_map/ppermute | solution.py:47
  88.4 10.5 %collective-permute-start.21 = (bf16[256,512]{1,0:T(8,128)(2,1)S(1)}, bf16[256,512]{1,0:T(8,128)(2,1)S(1)}, u32[]{:S(2)}, u32[]{:S(2)}) collective-permute-start(bf16[256,512]{1,0:T(8,128)(2,1)S(1)} %get-tuple-element.125), channel_id=1, source_target_pairs={{0,32},{1,9},{2,34},{3,11},{4,36},{5,13},{6,38},{7,15},{8,40},{9,1... | collective-permute-start | bytes 786440 | tf_op jit(solution)/shard_map/ppermute | solution.py:47
  89.8 10.1 %collective-permute-start.22 = (bf16[256,512]{1,0:T(8,128)(2,1)S(1)}, bf16[256,512]{1,0:T(8,128)(2,1)S(1)}, u32[]{:S(2)}, u32[]{:S(2)}) collective-permute-start(bf16[256,512]{1,0:T(8,128)(2,1)S(1)} %get-tuple-element.126), channel_id=1, source_target_pairs={{0,96},{1,25},{2,98},{3,27},{4,100},{5,29},{6,102},{7,31},{8,104},... | collective-permute-start | bytes 786440 | tf_op jit(solution)/shard_map/ppermute | solution.py:47
  91.0 9.9 %collective-permute-start.23 = (bf16[256,512]{1,0:T(8,128)(2,1)S(1)}, bf16[256,512]{1,0:T(8,128)(2,1)S(1)}, u32[]{:S(2)}, u32[]{:S(2)}) collective-permute-start(bf16[256,512]{1,0:T(8,128)(2,1)S(1)} %get-tuple-element.128), channel_id=1, source_target_pairs={{0,65},{1,16},{2,67},{3,18},{4,69},{5,20},{6,71},{7,22},{8,73},{9,... | collective-permute-start | bytes 786440 | tf_op jit(solution)/shard_map/ppermute | solution.py:47
  94.1 9.6 %collective-permute-start.24 = (bf16[256,512]{1,0:T(8,128)(2,1)S(1)}, bf16[256,512]{1,0:T(8,128)(2,1)S(1)}, u32[]{:S(2)}, u32[]{:S(2)}) collective-permute-start(bf16[256,512]{1,0:T(8,128)(2,1)S(1)} %get-tuple-element.129), channel_id=1, source_target_pairs={{0,33},{1,8},{2,35},{3,10},{4,37},{5,12},{6,39},{7,14},{8,41},{9,1... | collective-permute-start | bytes 786440 | tf_op jit(solution)/shard_map/ppermute | solution.py:47
  94.2 9.5 %collective-permute-start.25 = (bf16[256,512]{1,0:T(8,128)(2,1)S(1)}, bf16[256,512]{1,0:T(8,128)(2,1)S(1)}, u32[]{:S(2)}, u32[]{:S(2)}) collective-permute-start(bf16[256,512]{1,0:T(8,128)(2,1)S(1)} %get-tuple-element.130), channel_id=1, source_target_pairs={{0,97},{1,24},{2,99},{3,26},{4,101},{5,28},{6,103},{7,30},{8,105},... | collective-permute-start | bytes 786440 | tf_op jit(solution)/shard_map/ppermute | solution.py:47
  98.9 4.8 %collective-permute-start.26 = (bf16[256,512]{1,0:T(8,128)(2,1)S(1)}, bf16[256,512]{1,0:T(8,128)(2,1)S(1)}, u32[]{:S(2)}, u32[]{:S(2)}) collective-permute-start(bf16[256,512]{1,0:T(8,128)(2,1)S(1)} %get-tuple-element.131), channel_id=1, source_target_pairs={{0,1},{1,0},{2,3},{3,2},{4,5},{5,4},{6,7},{7,6},{8,9},{9,8},{10,11... | collective-permute-start | bytes 786440 | tf_op jit(solution)/shard_map/ppermute | solution.py:47

commit v7 on v6

--- a/solution.py
+++ b/solution.py
@@ -130,7 +130,7 @@
 
 def pre_kernel(
     dlog_ref, stept_ref, grad_ref, read_ref, fork_ref,
-    rel_ref, relt_ref, step_ref, scaled_ref, state_ref, m0, m1, m2, m3, message,
+    rel_ref, relt_ref, step_ref, state_ref, m0, m1, m2, m3, message, scaled_ref,
 ):
     y = lax.rem(lax.axis_index("ctx"), SIDE)
     row = lax.broadcasted_iota(jnp.int32, (CHUNK, CHUNK), 0)
@@ -185,7 +185,6 @@
             jax.ShapeDtypeStruct((CHUNKS, CHUNK, HEADS), F32),
             jax.ShapeDtypeStruct((CHUNKS, HEADS, CHUNK), F32),
             jax.ShapeDtypeStruct((length, HEADS), F32),
-            jax.ShapeDtypeStruct((length, WIDE), BF16),
             jax.ShapeDtypeStruct((CHUNKS - 1, 128, WIDE), BF16),
         ]
         + [sent] * 4,
@@ -200,11 +199,10 @@
             full_block(CHUNKS, CHUNK, HEADS),
             full_block(CHUNKS, HEADS, CHUNK),
             full_block(length, HEADS),
-            full_block(length, WIDE),
             full_block(CHUNKS - 1, 128, WIDE),
         ]
         + [full_block(256 + TAIL, QUARTER)] * 4,
-        scratch_shapes=[pltpu.VMEM((256 + TAIL, WIDE), BF16)],
+        scratch_shapes=[pltpu.VMEM((256 + TAIL, WIDE), BF16), pltpu.VMEM((length, WIDE), BF16)],
         compiler_params=params(64 * MIB),
         cost_estimate=COST,
     )(decay_log, stept, out_grad, reads, fork_grad)
@@ -282,7 +280,9 @@
     )(at, *first, *second)
 
 
-def diag_kernel(skip_ref, rel_ref, relt_ref, step_ref, read_ref, write_ref, grad_ref, out_ref):
+def diag_kernel(
+    skip_ref, rel_ref, relt_ref, step_ref, read_ref, write_ref, grad_ref, out_ref, scaled_ref
+):
     matrix = spread_matrix()
     row = lax.broadcasted_iota(jnp.int32, (CHUNK, CHUNK), 0)
     col = lax.broadcasted_iota(jnp.int32, (CHUNK, CHUNK), 1)
@@ -291,6 +291,7 @@
         scores = jnp.where(col >= row, dot_nt(write_ref[here], read_ref[here]), 0.0)
         rel, relt = rel_ref[c], relt_ref[c]
         steps = spread(step_ref[here], matrix)
+        scaled_ref[here] = (spread(jnp.exp(rel), matrix) * grad_ref[here].astype(F32)).astype(BF16)
         for pair in range(HEADS // 2):
             at = slice(pair * 128, pair * 128 + 128)
             grads = grad_ref[here, at]
@@ -309,7 +310,7 @@
     return pl.pallas_call(
         diag_kernel,
         grid=(CHUNKS // 2,),
-        out_shape=jax.ShapeDtypeStruct((CHUNKS * CHUNK, WIDE), BF16),
+        out_shape=[jax.ShapeDtypeStruct((CHUNKS * CHUNK, WIDE), BF16)] * 2,
         in_specs=[
             whole(pltpu.SMEM),
             pl.BlockSpec((2, CHUNK, HEADS), lambda c: (c, 0, 0)),
@@ -319,7 +320,7 @@
             pl.BlockSpec((rows, 128), by_two),
             pl.BlockSpec((rows, WIDE), by_two),
         ],
-        out_specs=pl.BlockSpec((rows, WIDE), by_two),
+        out_specs=[pl.BlockSpec((rows, WIDE), by_two)] * 2,
         compiler_params=params(ROOMY_LIMIT),
         cost_estimate=pl.CostEstimate(flops=4000000000, bytes_accessed=1, transcendentals=0),
     )(skip_gain, rel, relt, step_size, reads, writes, out_grad)
@@ -722,7 +723,7 @@
     x, core = column // 2, column % 2
     writes = write_vec[:, 0]
     reads = read_vec[:, 0]
-    rel, relt, steps, scaled, states, *messages = pre(
+    rel, relt, steps, states, *messages = pre(
         decay_log, step_size.T, out_grad, reads, fork_grad.reshape(2, WIDE, 128)
     )
     at = jnp.stack(after([z, y, x, core], *messages))
@@ -736,7 +737,7 @@
     second = after([message, above, far, below], inputs_b, other_weight)
     sent = carry_over(at, first, second)
     far, above, below = (hop(sent[d], 0, d) for d in (2, 1, 3))
-    base = diag(skip_gain, rel, relt, steps, reads, writes, after(out_grad, sent[0]))
+    base, scaled = diag(skip_gain, rel, relt, steps, reads, writes, after(out_grad, sent[0]))
     quarters = [sent[0], above, far, below]
     keep, give, x_mine, full = x_final(at, quarters, states, rel, steps, writes, base)
     got = first_hop(give, 0, 1)

time: 105 us -> 105 us (level)
  no operation moved by 1% of the time
where the time goes in v7:
time: 105 us
  Pallas kernels  48.3 us (46%)
  starting transfers between devices  42.3 us (40%)
  waiting for transfers between devices  13.7 us (13%)
    ppermute x27, starting transfers between devices, routed(): return lax.ppermute(block, ('ctx', 'smp'), route)  42.3 us
    ppermute x27, waiting for transfers between devices, routed(): return lax.ppermute(block, ('ctx', 'smp'), route)  13.7 us
    pallas_call x2, Pallas kernels, project(): pl.pallas_call(project_kernel, grid=(2,), out_shape=jax.ShapeDtypeStruct(...  11.4 us
    pallas_call x1, Pallas kernels, input_rest(): pl.pallas_call(rest_kernel, grid_spec=pltpu.PrefetchScalarGridSpec(num_sc...  6.08 us
    pallas_call x1, Pallas kernels, vectors(): pl.pallas_call(vector_kernel, grid=(CHUNKS // 2,), out_shape=[jax.ShapeDt...  5.18 us
    pallas_call x2, Pallas kernels, ring_product(): pl.pallas_call(ring_kernel, grid_spec=pltpu.PrefetchScalarGridSpec(num_sc...  4.84 us
    pallas_call x1, Pallas kernels, pre(): pl.pallas_call(pre_kernel, grid=(1,), out_shape=[jax.ShapeDtypeStruct((CH...  4.36 us
    pallas_call x1, Pallas kernels, plain_product(): pl.pallas_call(plain_kernel, grid_spec=pltpu.PrefetchScalarGridSpec(num_s...  3.87 us
  transfers between devices with their start and end apart: 27, of which 8 were waited for; matrix products, arithmetic and copies ran while one was open for 0% of the time, Pallas kernels for 39%

profile of v7, /device:TPU:1, one launch (start us, length us, event | category | flops | bytes accessed | tf_op | source)
XLA Modules:
  0.0 105.3 jit_solution(9863366135428858344)
XLA Ops:
  0.6 1.5 %collective-permute-start.6 = (bf16[4096,1024]{1,0:T(8,128)(2,1)}, bf16[4096,1024]{1,0:T(8,128)(2,1)}, u32[]{:S(2)}, u32[]{:S(2)}) collective-permute-start(bf16[4096,1024]{1,0:T(8,128)(2,1)} %w_ref.5), channel_id=1, source_target_pairs={{0,1},{1,0},{2,3},{3,2},{4,5},{5,4},{6,7},{7,6},{8,9},{9,8},{10,11... | collective-permute-start | bytes 25165832 | tf_op jit(solution)/shard_map/ppermute | solution.py:47
  2.1 4.4 %shard_map.129 = (f32[4,128,16]{2,1,0:T(8,128)}, f32[4,16,128]{2,1,0:T(8,128)}, f32[512,16]{1,0:T(8,128)}, bf16[3,128,1024]{2,1,0:T(8,128)(2,1)}, bf16[272,256]{...) custom-call(f32[16]{0:T(128)} %dlog_ref.1, f32[16,512]{1,0:T(8,128)} %bitcast.25, ...), custom_call_target="tpu_custom_call" | custom-call | flops 1 | bytes 1 | tf_op jit(solution)/shard_map/pallas_call | solution.py:181
  6.5 1.4 %collective-permute-start = (bf16[272,256]{1,0:T(8,128)(2,1)}, bf16[272,256]{1,0:T(8,128)(2,1)S(1)}, u32[]{:S(2)}, u32[]{:S(2)}) collective-permute-start(bf16[272,256]{1,0:T(8,128)(2,1)} %get-tuple-element.72), channel_id=1, source_target_pairs={{0,8},{1,9},{2,10},{3,11},{4,12},{5,13},{6,14},{7,15},{8,16},{9,17... | collective-permute-start | bytes 417800 | tf_op jit(solution)/shard_map/ppermute | solution.py:47
  7.9 2.6 %collective-permute-start.1 = (bf16[272,256]{1,0:T(8,128)(2,1)}, bf16[272,256]{1,0:T(8,128)(2,1)S(1)}, u32[]{:S(2)}, u32[]{:S(2)}) collective-permute-start(bf16[272,256]{1,0:T(8,128)(2,1)} %get-tuple-element.73), channel_id=1, source_target_pairs={{0,16},{1,17},{2,18},{3,19},{4,20},{5,21},{6,22},{7,23},{8,24},{9,... | collective-permute-start | bytes 417800 | tf_op jit(solution)/shard_map/ppermute | solution.py:47
  10.5 1.1 %collective-permute-start.2 = (bf16[272,256]{1,0:T(8,128)(2,1)}, bf16[272,256]{1,0:T(8,128)(2,1)S(1)}, u32[]{:S(2)}, u32[]{:S(2)}) collective-permute-start(bf16[272,256]{1,0:T(8,128)(2,1)} %get-tuple-element.74), channel_id=1, source_target_pairs={{0,24},{1,25},{2,26},{3,27},{4,28},{5,29},{6,30},{7,31},{8,0},{9,1... | collective-permute-start | bytes 417800 | tf_op jit(solution)/shard_map/ppermute | solution.py:47
  11.6 5.7 %shard_map.130.first_ref = bf16[512,512]{1,0:T(8,128)(2,1)} custom-call(bf16[512,4096]{1,0:T(8,128)(2,1)} %down_ref.5, bf16[4096,1024]{1,0:T(8,128)(2,1)} %w_ref.5), custom_call_target="tpu_custom_call" | custom-call | flops 1 | bytes 1 | tf_op jit(solution)/shard_map/pallas_call | solution.py:486
  17.3 0.1 pad_add_fusion.at_ref
  17.3 0.2 collective-permute-done.1.a2
  17.5 0.0 collective-permute-done.2.a3
  17.5 0.7 shard_map.131.b0
  18.2 0.0 copy-start.1
  18.2 0.0 copy-start.6
  18.3 0.0 copy-start.7
  18.3 0.0 copy-start.8
  18.3 0.0 copy-start.9
  18.3 0.0 copy-start.12
  18.3 3.8 %collective-permute-start.5 = (bf16[272,256]{1,0:T(8,128)(2,1)S(1)}, bf16[272,256]{1,0:T(8,128)(2,1)S(1)}, u32[]{:S(2)}, u32[]{:S(2)}) collective-permute-start(bf16[272,256]{1,0:T(8,128)(2,1)S(1)} %shard_map.131.b0), channel_id=1, source_target_pairs={{0,96},{1,97},{2,98},{3,99},{4,100},{5,101},{6,102},{7,103},{8,104... | collective-permute-start | bytes 417800 | tf_op jit(solution)/shard_map/ppermute | solution.py:47
  22.1 0.0 collective-permute-start.4
  22.1 0.7 collective-permute-start.3
  22.9 5.7 %shard_map.132.second_ref = bf16[512,512]{1,0:T(8,128)(2,1)} custom-call(bf16[512,4096]{1,0:T(8,128)(2,1)} %down_ref.5, bf16[4096,1024]{1,0:T(8,128)(2,1)} %w_ref.5), custom_call_target="tpu_custom_call" | custom-call | flops 1 | bytes 1 | tf_op jit(solution)/shard_map/pallas_call | solution.py:486
  28.5 3.0 %collective-permute-done.3.b1 = bf16[272,256]{1,0:T(8,128)(2,1)S(1)} collective-permute-done((bf16[272,256]{1,0:T(8,128)(2,1)S(1)}, bf16[272,256]{1,0:T(8,128)(2,1)S(1)}, u32[]{:S(2)}, u32[]{:S(2)}) %collective-permute-start.3) | collective-permute-done | bytes 139296 | tf_op jit(solution)/shard_map/ppermute | solution.py:47
  31.6 0.8 shard_map.133
  32.3 0.5 collective-permute-start.7
  32.9 2.7 %collective-permute-start.8 = (bf16[128,256]{1,0:T(8,128)(2,1)S(1)}, bf16[128,256]{1,0:T(8,128)(2,1)S(1)}, u32[]{:S(2)}, u32[]{:S(2)}) collective-permute-start(bf16[128,256]{1,0:T(8,128)(2,1)S(1)} %get-tuple-element.91), channel_id=1, source_target_pairs={{0,16},{1,17},{2,18},{3,19},{4,20},{5,21},{6,22},{7,23},{8,24},{9,... | collective-permute-start | bytes 196616 | tf_op jit(solution)/shard_map/ppermute | solution.py:47
  35.6 0.9 collective-permute-start.9
  36.5 2.8 %shard_map.134 = (bf16[512,1024]{1,0:T(8,128)(2,1)S(1)}, bf16[512,1024]{1,0:T(8,128)(2,1)S(1)}) custom-call(f32[16]{0:T(128)S(1)} %copy-done.12, f32[4,128,16]{2,1,0:T(8,128)S(1)} %copy-done.6, f32[4,16,128]{2,1,0:T(8,128)S(1)} %copy-done.11, f32[512,16]{1,0:T(8,128)S(1)} %copy-done.7, bf16[512,128]{1,0:T(8,128)(2,1)S(1)} %bitcast.18, ...), custom_call_target="tpu_custom_call" | custom-call | flops 4000000000 | bytes 1 | tf_op jit(solution)/shard_map/pallas_call | solution.py:310
  39.4 0.0 collective-permute-done.7.q1
  39.4 0.1 collective-permute-done.9.q3
  39.5 1.9 %shard_map.135 = (bf16[512,512]{1,0:T(8,128)(2,1)S(1)}, bf16[1024,512]{1,0:T(8,128)(2,1)S(1)}, bf16[256,1024]{1,0:T(8,128)(2,1)S(1)}, bf16[4,128,1024]{2,1,0:T(8,128)(2,1)S(1)}) custom-call(s32[4]{0:T(128)S(1)} %pad_add_fusion.at_ref, bf16[128,256]{1,0:T(8,128)(2,1)S(1)} %get-tuple-element.89.q0, bf16[128,256]{1,0:T(8,128)(2,1)S(1)} %collective-permute-done.7.q1, ...), custom_call_target="tpu_custom_call" | custom-call | flops 1 | bytes 1 | tf_op jit(solution)/shard_map/pallas_call | solution.py:371
  41.4 1.8 %collective-permute-start.10 = (bf16[1024,512]{1,0:T(8,128)(2,1)S(1)}, bf16[1024,512]{1,0:T(8,128)(2,1)S(1)}, u32[]{:S(2)}, u32[]{:S(2)}) collective-permute-start(bf16[1024,512]{1,0:T(8,128)(2,1)S(1)} %get-tuple-element.99), channel_id=1, source_target_pairs={{0,1},{1,0},{2,3},{3,2},{4,5},{5,4},{6,7},{7,6},{8,9},{9,8},{10,11... | collective-permute-start | bytes 3145736 | tf_op jit(solution)/shard_map/ppermute | solution.py:47
  43.3 2.7 %shard_map.136.part_ref = bf16[256,4096]{1,0:T(8,128)(2,1)S(1)} custom-call(bf16[256,1024]{1,0:T(8,128)(2,1)S(1)} %get-tuple-element.101.x_ref, bf16[4096,1024]{1,0:T(8,128)(2,1)S(1)} %bitcast.16), custom_call_target="tpu_custom_call" | custom-call | flops 1 | bytes 1 | tf_op jit(solution)/shard_map/pallas_call | solution.py:641
  46.0 0.0 collective-permute-done.10.got_ref.left_ref.right_ref
  46.0 2.4 %shard_map.137 = (bf16[2,256,1024]{2,1,0:T(8,128)(2,1)S(1)}, bf16[2,256,1024]{2,1,0:T(8,128)(2,1)S(1)}) custom-call(s32[4]{0:T(128)S(1)} %pad_add_fusion.at_ref, bf16[512,4096]{1,0:T(8,128)(2,1)S(1)} %copy-done, bf16[512,4096]{1,0:T(8,128)(2,1)S(1)} %copy-done, bf16[512,512]{1,0:T(8,128)(2,1)S(1)} %get-tuple-element.105.keep_ref, ...), custom_call_target="tpu_custom_call" | custom-call | flops 1 | bytes 1 | tf_op jit(solution)/shard_map/pallas_call | solution.py:535
  48.4 0.1 collective-permute-start.11
  48.5 2.7 %collective-permute-start.12 = (bf16[2,256,1024]{2,1,0:T(8,128)(2,1)S(1)}, bf16[2,256,1024]{2,1,0:T(8,128)(2,1)S(1)}, u32[]{:S(2)}, u32[]{:S(2)}) collective-permute-start(bf16[2,256,1024]{2,1,0:T(8,128)(2,1)S(1)} %get-tuple-element.104), channel_id=1, source_target_pairs={{0,24},{1,97},{2,26},{3,99},{4,28},{5,101},{6,30},{7,103},{8,0},{9... | collective-permute-start | bytes 3145736 | tf_op jit(solution)/shard_map/ppermute | solution.py:47
  51.2 3.9 %shard_map.138 = (bf16[2,256,1024]{2,1,0:T(8,128)(2,1)S(1)}, bf16[2,256,1024]{2,1,0:T(8,128)(2,1)S(1)}, bf16[4,256,1024]{2,1,0:T(8,128)(2,1)S(1)}) custom-call(s32[4]{0:T(128)S(1)} %pad_add_fusion.at_ref, bf16[512,4096]{1,0:T(8,128)(2,1)S(1)} %copy-done, bf16[512,4096]{1,0:T(8,128)(2,1)S(1)} %copy-done, bf16[512,4096]{1,0:T(8,128)(2,1)S(1)} %copy-done, ...), custom_call_target="tpu_custom_call" | custom-call | flops 1 | bytes 1 | tf_op jit(solution)/shard_map/pallas_call | solution.py:564
  55.1 0.1 collective-permute-start.14
  55.1 2.7 %collective-permute-start.15 = (bf16[2,256,1024]{2,1,0:T(8,128)(2,1)S(1)}, bf16[2,256,1024]{2,1,0:T(8,128)(2,1)S(1)}, u32[]{:S(2)}, u32[]{:S(2)}) collective-permute-start(bf16[2,256,1024]{2,1,0:T(8,128)(2,1)S(1)} %get-tuple-element.107), channel_id=1, source_target_pairs={{0,24},{1,97},{2,26},{3,99},{4,28},{5,101},{6,30},{7,103},{8,0},{9... | collective-permute-start | bytes 3145736 | tf_op jit(solution)/shard_map/ppermute | solution.py:47
  57.8 6.1 %shard_map.139 = (bf16[64,4096]{1,0:T(8,128)(2,1)S(1)}, bf16[64,4096]{1,0:T(8,128)(2,1)S(1)}, bf16[64,4096]{1,0:T(8,128)(2,1)S(1)}, f32[64,4096]{1,0:T(8,128)S(1)}) custom-call(s32[4]{0:T(128)S(1)} %pad_add_fusion.at_ref, bf16[1024,512]{1,0:T(8,128)(2,1)S(1)} %collective-permute-done.10.got_ref.left_ref.right_ref, ...), custom_call_target="tpu_custom_call" | custom-call | flops 1 | bytes 1 | tf_op jit(solution)/shard_map/pallas_call | solution.py:665
  63.9 2.8 %collective-permute-start.17 = (bf16[64,4096]{1,0:T(8,128)(2,1)S(1)}, bf16[64,4096]{1,0:T(8,128)(2,1)S(1)}, u32[]{:S(2)}, u32[]{:S(2)}) collective-permute-start(bf16[64,4096]{1,0:T(8,128)(2,1)S(1)} %get-tuple-element.111), channel_id=1, source_target_pairs={{0,4},{1,5},{2,6},{3,7},{4,0},{5,1},{6,2},{7,3},{8,12},{9,13},{10,... | collective-permute-start | bytes 1572872 | tf_op jit(solution)/shard_map/ppermute | solution.py:47
  66.7 0.0 collective-permute-done.11.refs_0_
  66.7 0.0 collective-permute-done.12.refs_1_
  66.7 0.0 copy-start.5
  66.8 0.0 copy-start.10
  66.8 2.4 %shard_map.140 = (bf16[2,256,1024]{2,1,0:T(8,128)(2,1)S(1)}, bf16[2,256,1024]{2,1,0:T(8,128)(2,1)S(1)}) custom-call(s32[4]{0:T(128)S(1)} %pad_add_fusion.at_ref, bf16[512,4096]{1,0:T(8,128)(2,1)S(1)} %copy-done, bf16[512,4096]{1,0:T(8,128)(2,1)S(1)} %copy-done, bf16[512,512]{1,0:T(8,128)(2,1)S(1)} %get-tuple-element.105.keep_ref, ...), custom_call_target="tpu_custom_call" | custom-call | flops 1 | bytes 1 | tf_op jit(solution)/shard_map/pallas_call | solution.py:535
  69.2 0.1 collective-permute-start.13
  69.3 2.7 %collective-permute-start.16 = (bf16[2,256,1024]{2,1,0:T(8,128)(2,1)S(1)}, bf16[2,256,1024]{2,1,0:T(8,128)(2,1)S(1)}, u32[]{:S(2)}, u32[]{:S(2)}) collective-permute-start(bf16[2,256,1024]{2,1,0:T(8,128)(2,1)S(1)} %get-tuple-element.117), channel_id=1, source_target_pairs={{0,24},{1,97},{2,26},{3,99},{4,28},{5,101},{6,30},{7,103},{8,0},{9... | collective-permute-start | bytes 3145736 | tf_op jit(solution)/shard_map/ppermute | solution.py:47
  72.0 2.9 %collective-permute-done.14.below_plain = bf16[2,256,1024]{2,1,0:T(8,128)(2,1)S(1)} collective-permute-done((bf16[2,256,1024]{2,1,0:T(8,128)(2,1)S(1)}, bf16[2,256,1024]{2,1,0:T(8,128)(2,1)S(1)}, u32[]{:S(2)}, u32[]{:S(2)}) %collective-permute-start.14) | collective-permute-done | bytes 1048608 | tf_op jit(solution)/shard_map/ppermute | solution.py:47
  74.9 0.0 collective-permute-done.15.above_plain
  74.9 2.5 %collective-permute-start.18 = (bf16[64,4096]{1,0:T(8,128)(2,1)S(1)}, bf16[64,4096]{1,0:T(8,128)(2,1)S(1)}, u32[]{:S(2)}, u32[]{:S(2)}) collective-permute-start(bf16[64,4096]{1,0:T(8,128)(2,1)S(1)} %get-tuple-element.135), channel_id=1, source_target_pairs={{0,2},{1,7},{2,4},{3,1},{4,6},{5,3},{6,0},{7,5},{8,10},{9,15},{10,... | collective-permute-start | bytes 1572872 | tf_op jit(solution)/shard_map/ppermute | solution.py:47
  77.4 5.2 %shard_map.141 = (f32[512,128]{1,0:T(8,128)}, f32[512,128]{1,0:T(8,128)}) custom-call(f32[4,128,16]{2,1,0:T(8,128)S(1)} %copy-done.6, f32[4,16,128]{2,1,0:T(8,128)S(1)} %copy-done.11, f32[512,16]{1,0:T(8,128)S(1)} %copy-done.7, bf16[512,128]{1,0:T(8,128)(2,1)S(1)} %bitcast.19, bf16[512,128]{1,0:T(8,128)(2,1)S(1)} %bitcast.22, ...), custom_call_target="tpu_custom_call" | custom-call | flops 49999998976 | bytes 1 | tf_op jit(solution)/shard_map/pallas_call | solution.py:446
  82.6 0.0 collective-permute-done.17.first
  82.6 3.5 %collective-permute-done.13.below_add = bf16[2,256,1024]{2,1,0:T(8,128)(2,1)S(1)} collective-permute-done((bf16[2,256,1024]{2,1,0:T(8,128)(2,1)S(1)}, bf16[2,256,1024]{2,1,0:T(8,128)(2,1)S(1)}, u32[]{:S(2)}, u32[]{:S(2)}) %collective-permute-start.13) | collective-permute-done | bytes 1048608 | tf_op jit(solution)/shard_map/ppermute | solution.py:47
  86.1 0.9 shard_map.142
  87.1 1.3 %collective-permute-start.20 = (bf16[256,512]{1,0:T(8,128)(2,1)S(1)}, bf16[256,512]{1,0:T(8,128)(2,1)S(1)}, u32[]{:S(2)}, u32[]{:S(2)}) collective-permute-start(bf16[256,512]{1,0:T(8,128)(2,1)S(1)} %get-tuple-element.126), channel_id=1, source_target_pairs={{0,64},{1,17},{2,66},{3,19},{4,68},{5,21},{6,70},{7,23},{8,72},{9,... | collective-permute-start | bytes 786440 | tf_op jit(solution)/shard_map/ppermute | solution.py:47
  88.4 1.4 %collective-permute-start.21 = (bf16[256,512]{1,0:T(8,128)(2,1)S(1)}, bf16[256,512]{1,0:T(8,128)(2,1)S(1)}, u32[]{:S(2)}, u32[]{:S(2)}) collective-permute-start(bf16[256,512]{1,0:T(8,128)(2,1)S(1)} %get-tuple-element.127), channel_id=1, source_target_pairs={{0,32},{1,9},{2,34},{3,11},{4,36},{5,13},{6,38},{7,15},{8,40},{9,1... | collective-permute-start | bytes 786440 | tf_op jit(solution)/shard_map/ppermute | solution.py:47
  89.8 1.3 %collective-permute-start.22 = (bf16[256,512]{1,0:T(8,128)(2,1)S(1)}, bf16[256,512]{1,0:T(8,128)(2,1)S(1)}, u32[]{:S(2)}, u32[]{:S(2)}) collective-permute-start(bf16[256,512]{1,0:T(8,128)(2,1)S(1)} %get-tuple-element.128), channel_id=1, source_target_pairs={{0,96},{1,25},{2,98},{3,27},{4,100},{5,29},{6,102},{7,31},{8,104},... | collective-permute-start | bytes 786440 | tf_op jit(solution)/shard_map/ppermute | solution.py:47
  91.1 3.0 %collective-permute-start.23 = (bf16[256,512]{1,0:T(8,128)(2,1)S(1)}, bf16[256,512]{1,0:T(8,128)(2,1)S(1)}, u32[]{:S(2)}, u32[]{:S(2)}) collective-permute-start(bf16[256,512]{1,0:T(8,128)(2,1)S(1)} %get-tuple-element.130), channel_id=1, source_target_pairs={{0,65},{1,16},{2,67},{3,18},{4,69},{5,20},{6,71},{7,22},{8,73},{9,... | collective-permute-start | bytes 786440 | tf_op jit(solution)/shard_map/ppermute | solution.py:47
  94.1 0.1 collective-permute-done.20.refs_0_
  94.2 4.7 %collective-permute-start.25 = (bf16[256,512]{1,0:T(8,128)(2,1)S(1)}, bf16[256,512]{1,0:T(8,128)(2,1)S(1)}, u32[]{:S(2)}, u32[]{:S(2)}) collective-permute-start(bf16[256,512]{1,0:T(8,128)(2,1)S(1)} %get-tuple-element.132), channel_id=1, source_target_pairs={{0,97},{1,24},{2,99},{3,26},{4,101},{5,28},{6,103},{7,30},{8,105},... | collective-permute-start | bytes 786440 | tf_op jit(solution)/shard_map/ppermute | solution.py:47
  98.9 1.1 %shard_map.143 = bf16[64,4096]{1,0:T(8,128)(2,1)} custom-call(f32[64,4096]{1,0:T(8,128)S(1)} %get-tuple-element.134.own, bf16[64,4096]{1,0:T(8,128)(2,1)S(1)} %collective-permute-done.17.first, bf16[64,4096]{1,0:T(8,128)(2,1)S(1)} %collective-permute-done.18.second, bf16[64,4096]{1,0:T(8,128)(2,1)S(1)} %collective-permute-done.19.third), custom_call_target="tpu_custom_call" | custom-call | flops 1 | bytes 1 | tf_op jit(solution)/shard_map/pallas_call | solution.py:692
  99.9 1.1 %collective-permute-done.23.refs_4_ = bf16[256,512]{1,0:T(8,128)(2,1)S(1)} collective-permute-done((bf16[256,512]{1,0:T(8,128)(2,1)S(1)}, bf16[256,512]{1,0:T(8,128)(2,1)S(1)}, u32[]{:S(2)}, u32[]{:S(2)}) %collective-permute-start.23) | collective-permute-done | bytes 262176 | tf_op jit(solution)/shard_map/ppermute | solution.py:47
  101.0 2.7 %collective-permute-done.24.refs_5_ = bf16[256,512]{1,0:T(8,128)(2,1)S(1)} collective-permute-done((bf16[256,512]{1,0:T(8,128)(2,1)S(1)}, bf16[256,512]{1,0:T(8,128)(2,1)S(1)}, u32[]{:S(2)}, u32[]{:S(2)}) %collective-permute-start.24) | collective-permute-done | bytes 262176 | tf_op jit(solution)/shard_map/ppermute | solution.py:47
  103.7 1.6 %shard_map.144 = bf16[256,1024]{1,0:T(8,128)(2,1)} custom-call(s32[4]{0:T(128)S(1)} %pad_add_fusion.at_ref, bf16[256,512]{1,0:T(8,128)(2,1)S(1)} %collective-permute-done.20.refs_0_, bf16[256,512]{1,0:T(8,128)(2,1)S(1)} %collective-permute-done.21.refs_1_, bf16[256,512]{1,0:T(8,128)(2,1)S(1)} %collective-permute-done.22.refs_2_, ...), custom_call_target="tpu_custom_call" | custom-call | flops 1 | bytes 1 | tf_op jit(solution)/shard_map/pallas_call | solution.py:624
  (38 shorter events, 0.1 us)
Async XLA Ops:
  0.6 30.9 %collective-permute-start.6 = (bf16[4096,1024]{1,0:T(8,128)(2,1)}, bf16[4096,1024]{1,0:T(8,128)(2,1)}, u32[]{:S(2)}, u32[]{:S(2)}) collective-permute-start(bf16[4096,1024]{1,0:T(8,128)(2,1)} %w_ref.5), channel_id=1, source_target_pairs={{0,1},{1,0},{2,3},{3,2},{4,5},{5,4},{6,7},{7,6},{8,9},{9,8},{10,11... | collective-permute-start | bytes 25165832 | tf_op jit(solution)/shard_map/ppermute | solution.py:47
  6.5 10.8 %collective-permute-start = (bf16[272,256]{1,0:T(8,128)(2,1)}, bf16[272,256]{1,0:T(8,128)(2,1)S(1)}, u32[]{:S(2)}, u32[]{:S(2)}) collective-permute-start(bf16[272,256]{1,0:T(8,128)(2,1)} %get-tuple-element.72), channel_id=1, source_target_pairs={{0,8},{1,9},{2,10},{3,11},{4,12},{5,13},{6,14},{7,15},{8,16},{9,17... | collective-permute-start | bytes 417800 | tf_op jit(solution)/shard_map/ppermute | solution.py:47
  7.9 9.6 %collective-permute-start.1 = (bf16[272,256]{1,0:T(8,128)(2,1)}, bf16[272,256]{1,0:T(8,128)(2,1)S(1)}, u32[]{:S(2)}, u32[]{:S(2)}) collective-permute-start(bf16[272,256]{1,0:T(8,128)(2,1)} %get-tuple-element.73), channel_id=1, source_target_pairs={{0,16},{1,17},{2,18},{3,19},{4,20},{5,21},{6,22},{7,23},{8,24},{9,... | collective-permute-start | bytes 417800 | tf_op jit(solution)/shard_map/ppermute | solution.py:47
  10.5 7.0 %collective-permute-start.2 = (bf16[272,256]{1,0:T(8,128)(2,1)}, bf16[272,256]{1,0:T(8,128)(2,1)S(1)}, u32[]{:S(2)}, u32[]{:S(2)}) collective-permute-start(bf16[272,256]{1,0:T(8,128)(2,1)} %get-tuple-element.74), channel_id=1, source_target_pairs={{0,24},{1,25},{2,26},{3,27},{4,28},{5,29},{6,30},{7,31},{8,0},{9,1... | collective-permute-start | bytes 417800 | tf_op jit(solution)/shard_map/ppermute | solution.py:47
  11.6 6.0 %copy-start.3 = (bf16[272,256]{1,0:T(8,128)(2,1)S(1)}, bf16[272,256]{1,0:T(8,128)(2,1)}, u32[]{:S(2)}) copy-start(bf16[272,256]{1,0:T(8,128)(2,1)} %get-tuple-element.80.a0) | copy-start | bytes 417796
  18.2 18.2 %copy-start.1 = (bf16[512,1024]{1,0:T(8,128)(2,1)S(1)}, bf16[512,1024]{1,0:T(8,128)(2,1)}, u32[]{:S(2)}) copy-start(bf16[512,1024]{1,0:T(8,128)(2,1)} %grad_ref.4) | copy-start | bytes 3145732
  18.2 18.2 %copy-start.6 = (f32[4,128,16]{2,1,0:T(8,128)S(1)}, f32[4,128,16]{2,1,0:T(8,128)}, u32[]{:S(2)}) copy-start(f32[4,128,16]{2,1,0:T(8,128)} %get-tuple-element.94.rel_ref) | copy-start | bytes 98308
  18.3 18.2 %copy-start.7 = (f32[512,16]{1,0:T(8,128)S(1)}, f32[512,16]{1,0:T(8,128)}, u32[]{:S(2)}) copy-start(f32[512,16]{1,0:T(8,128)} %get-tuple-element.95.step_ref) | copy-start | bytes 98308
  18.3 18.2 %copy-start.8 = (bf16[512,1,128]{2,0,1:T(8,128)(2,1)S(1)}, bf16[512,1,128]{2,0,1:T(8,128)(2,1)}, u32[]{:S(2)}) copy-start(bf16[512,1,128]{2,0,1:T(8,128)(2,1)} %param.16) | copy-start | bytes 393220
  18.3 18.2 %copy-start.9 = (bf16[512,1,128]{2,0,1:T(8,128)(2,1)S(1)}, bf16[512,1,128]{2,0,1:T(8,128)(2,1)}, u32[]{:S(2)}) copy-start(bf16[512,1,128]{2,0,1:T(8,128)(2,1)} %param.15) | copy-start | bytes 393220
  18.3 18.2 %copy-start.11 = (f32[4,16,128]{2,1,0:T(8,128)S(1)}, f32[4,16,128]{2,1,0:T(8,128)}, u32[]{:S(2)}) copy-start(f32[4,16,128]{2,1,0:T(8,128)} %get-tuple-element.96.relt_ref) | copy-start | bytes 98308
  18.3 18.2 %copy-start.12 = (f32[16]{0:T(128)S(1)}, f32[16]{0:T(128)}, u32[]{:S(2)}) copy-start(f32[16]{0:T(128)} %skip_ref.1) | copy-start | bytes 196
  18.3 10.2 %collective-permute-start.5 = (bf16[272,256]{1,0:T(8,128)(2,1)S(1)}, bf16[272,256]{1,0:T(8,128)(2,1)S(1)}, u32[]{:S(2)}, u32[]{:S(2)}) collective-permute-start(bf16[272,256]{1,0:T(8,128)(2,1)S(1)} %shard_map.131.b0), channel_id=1, source_target_pairs={{0,96},{1,97},{2,98},{3,99},{4,100},{5,101},{6,102},{7,103},{8,104... | collective-permute-start | bytes 417800 | tf_op jit(solution)/shard_map/ppermute | solution.py:47
  22.1 6.4 %collective-permute-start.4 = (bf16[272,256]{1,0:T(8,128)(2,1)S(1)}, bf16[272,256]{1,0:T(8,128)(2,1)S(1)}, u32[]{:S(2)}, u32[]{:S(2)}) collective-permute-start(bf16[272,256]{1,0:T(8,128)(2,1)S(1)} %shard_map.131.b0), channel_id=1, source_target_pairs={{0,64},{1,65},{2,66},{3,67},{4,68},{5,69},{6,70},{7,71},{8,72},{9,... | collective-permute-start | bytes 417800 | tf_op jit(solution)/shard_map/ppermute | solution.py:47
  22.1 9.4 %collective-permute-start.3 = (bf16[272,256]{1,0:T(8,128)(2,1)S(1)}, bf16[272,256]{1,0:T(8,128)(2,1)S(1)}, u32[]{:S(2)}, u32[]{:S(2)}) collective-permute-start(bf16[272,256]{1,0:T(8,128)(2,1)S(1)} %shard_map.131.b0), channel_id=1, source_target_pairs={{0,32},{1,33},{2,34},{3,35},{4,36},{5,37},{6,38},{7,39},{8,40},{9,... | collective-permute-start | bytes 417800 | tf_op jit(solution)/shard_map/ppermute | solution.py:47
  32.3 7.0 %collective-permute-start.7 = (bf16[128,256]{1,0:T(8,128)(2,1)S(1)}, bf16[128,256]{1,0:T(8,128)(2,1)S(1)}, u32[]{:S(2)}, u32[]{:S(2)}) collective-permute-start(bf16[128,256]{1,0:T(8,128)(2,1)S(1)} %get-tuple-element.90), channel_id=1, source_target_pairs={{0,8},{1,9},{2,10},{3,11},{4,12},{5,13},{6,14},{7,15},{8,16},{9,17... | collective-permute-start | bytes 196616 | tf_op jit(solution)/shard_map/ppermute | solution.py:47
  32.9 6.5 %collective-permute-start.8 = (bf16[128,256]{1,0:T(8,128)(2,1)S(1)}, bf16[128,256]{1,0:T(8,128)(2,1)S(1)}, u32[]{:S(2)}, u32[]{:S(2)}) collective-permute-start(bf16[128,256]{1,0:T(8,128)(2,1)S(1)} %get-tuple-element.91), channel_id=1, source_target_pairs={{0,16},{1,17},{2,18},{3,19},{4,20},{5,21},{6,22},{7,23},{8,24},{9,... | collective-permute-start | bytes 196616 | tf_op jit(solution)/shard_map/ppermute | solution.py:47
  35.6 3.9 %collective-permute-start.9 = (bf16[128,256]{1,0:T(8,128)(2,1)S(1)}, bf16[128,256]{1,0:T(8,128)(2,1)S(1)}, u32[]{:S(2)}, u32[]{:S(2)}) collective-permute-start(bf16[128,256]{1,0:T(8,128)(2,1)S(1)} %get-tuple-element.92), channel_id=1, source_target_pairs={{0,24},{1,25},{2,26},{3,27},{4,28},{5,29},{6,30},{7,31},{8,0},{9,1... | collective-permute-start | bytes 196616 | tf_op jit(solution)/shard_map/ppermute | solution.py:47
  36.4 6.8 %slice-start = ((s8[8388608]{0:T(1024)(128)(4,1)}), s8[4194304]{0:T(1024)(128)(4,1)S(1)}, s32[]{:S(2)}) async-start(s8[8388608]{0:T(1024)(128)(4,1)} %bitcast.15), calls=%async_computation | async-start | bytes 8388608
  36.5 3.0 %copy-start.2 = (bf16[3,128,1024]{2,1,0:T(8,128)(2,1)S(1)}, bf16[3,128,1024]{2,1,0:T(8,128)(2,1)}, u32[]{:S(2)}) copy-start(bf16[3,128,1024]{2,1,0:T(8,128)(2,1)} %get-tuple-element.93.state_ref) | copy-start | bytes 2359300
  36.5 6.8 %slice-start.1 = ((s8[8388608]{0:T(1024)(128)(4,1)}), s8[4194304]{0:T(1024)(128)(4,1)S(1)}, s32[]{:S(2)}) async-start(s8[8388608]{0:T(1024)(128)(4,1)} %bitcast.15), calls=%async_computation.1 | async-start | bytes 8388608
  41.4 4.6 %collective-permute-start.10 = (bf16[1024,512]{1,0:T(8,128)(2,1)S(1)}, bf16[1024,512]{1,0:T(8,128)(2,1)S(1)}, u32[]{:S(2)}, u32[]{:S(2)}) collective-permute-start(bf16[1024,512]{1,0:T(8,128)(2,1)S(1)} %get-tuple-element.99), channel_id=1, source_target_pairs={{0,1},{1,0},{2,3},{3,2},{4,5},{5,4},{6,7},{7,6},{8,9},{9,8},{10,11... | collective-permute-start | bytes 3145736 | tf_op jit(solution)/shard_map/ppermute | solution.py:47
  43.3 2.8 %copy-start = (bf16[512,4096]{1,0:T(8,128)(2,1)S(1)}, bf16[512,4096]{1,0:T(8,128)(2,1)}, u32[]{:S(2)}) copy-start(bf16[512,4096]{1,0:T(8,128)(2,1)} %down_ref.5) | copy-start | bytes 12582916
  48.4 18.3 %collective-permute-start.11 = (bf16[2,256,1024]{2,1,0:T(8,128)(2,1)S(1)}, bf16[2,256,1024]{2,1,0:T(8,128)(2,1)S(1)}, u32[]{:S(2)}, u32[]{:S(2)}) collective-permute-start(bf16[2,256,1024]{2,1,0:T(8,128)(2,1)S(1)} %get-tuple-element.103), channel_id=1, source_target_pairs={{0,8},{1,33},{2,10},{3,35},{4,12},{5,37},{6,14},{7,39},{8,16},{9,4... | collective-permute-start | bytes 3145736 | tf_op jit(solution)/shard_map/ppermute | solution.py:47
  48.5 18.2 %collective-permute-start.12 = (bf16[2,256,1024]{2,1,0:T(8,128)(2,1)S(1)}, bf16[2,256,1024]{2,1,0:T(8,128)(2,1)S(1)}, u32[]{:S(2)}, u32[]{:S(2)}) collective-permute-start(bf16[2,256,1024]{2,1,0:T(8,128)(2,1)S(1)} %get-tuple-element.104), channel_id=1, source_target_pairs={{0,24},{1,97},{2,26},{3,99},{4,28},{5,101},{6,30},{7,103},{8,0},{9... | collective-permute-start | bytes 3145736 | tf_op jit(solution)/shard_map/ppermute | solution.py:47
  55.1 19.8 %collective-permute-start.14 = (bf16[2,256,1024]{2,1,0:T(8,128)(2,1)S(1)}, bf16[2,256,1024]{2,1,0:T(8,128)(2,1)S(1)}, u32[]{:S(2)}, u32[]{:S(2)}) collective-permute-start(bf16[2,256,1024]{2,1,0:T(8,128)(2,1)S(1)} %get-tuple-element.106), channel_id=1, source_target_pairs={{0,8},{1,33},{2,10},{3,35},{4,12},{5,37},{6,14},{7,39},{8,16},{9,4... | collective-permute-start | bytes 3145736 | tf_op jit(solution)/shard_map/ppermute | solution.py:47
  55.1 19.8 %collective-permute-start.15 = (bf16[2,256,1024]{2,1,0:T(8,128)(2,1)S(1)}, bf16[2,256,1024]{2,1,0:T(8,128)(2,1)S(1)}, u32[]{:S(2)}, u32[]{:S(2)}) collective-permute-start(bf16[2,256,1024]{2,1,0:T(8,128)(2,1)S(1)} %get-tuple-element.107), channel_id=1, source_target_pairs={{0,24},{1,97},{2,26},{3,99},{4,28},{5,101},{6,30},{7,103},{8,0},{9... | collective-permute-start | bytes 3145736 | tf_op jit(solution)/shard_map/ppermute | solution.py:47
  63.9 18.7 %collective-permute-start.17 = (bf16[64,4096]{1,0:T(8,128)(2,1)S(1)}, bf16[64,4096]{1,0:T(8,128)(2,1)S(1)}, u32[]{:S(2)}, u32[]{:S(2)}) collective-permute-start(bf16[64,4096]{1,0:T(8,128)(2,1)S(1)} %get-tuple-element.111), channel_id=1, source_target_pairs={{0,4},{1,5},{2,6},{3,7},{4,0},{5,1},{6,2},{7,3},{8,12},{9,13},{10,... | collective-permute-start | bytes 1572872 | tf_op jit(solution)/shard_map/ppermute | solution.py:47
  66.7 10.6 %copy-start.4 = (bf16[512,512]{1,0:T(8,128)(2,1)S(1)}, bf16[512,512]{1,0:T(8,128)(2,1)}, u32[]{:S(2)}) copy-start(bf16[512,512]{1,0:T(8,128)(2,1)} %shard_map.130.first_ref) | copy-start | bytes 1572868
  66.7 10.6 %copy-start.5 = (bf16[512,512]{1,0:T(8,128)(2,1)S(1)}, bf16[512,512]{1,0:T(8,128)(2,1)}, u32[]{:S(2)}) copy-start(bf16[512,512]{1,0:T(8,128)(2,1)} %shard_map.132.second_ref) | copy-start | bytes 1572868
  66.8 10.6 %copy-start.10 = (f32[1,16,64,128]{3,2,1,0:T(8,128)S(1)}, f32[1,16,64,128]{3,2,1,0:T(8,128)}, u32[]{:S(2)}) copy-start(f32[1,16,64,128]{3,2,1,0:T(8,128)} %param.18) | copy-start | bytes 1572868
  69.2 16.9 %collective-permute-start.13 = (bf16[2,256,1024]{2,1,0:T(8,128)(2,1)S(1)}, bf16[2,256,1024]{2,1,0:T(8,128)(2,1)S(1)}, u32[]{:S(2)}, u32[]{:S(2)}) collective-permute-start(bf16[2,256,1024]{2,1,0:T(8,128)(2,1)S(1)} %get-tuple-element.116), channel_id=1, source_target_pairs={{0,8},{1,33},{2,10},{3,35},{4,12},{5,37},{6,14},{7,39},{8,16},{9,4... | collective-permute-start | bytes 3145736 | tf_op jit(solution)/shard_map/ppermute | solution.py:47
  69.3 16.8 %collective-permute-start.16 = (bf16[2,256,1024]{2,1,0:T(8,128)(2,1)S(1)}, bf16[2,256,1024]{2,1,0:T(8,128)(2,1)S(1)}, u32[]{:S(2)}, u32[]{:S(2)}) collective-permute-start(bf16[2,256,1024]{2,1,0:T(8,128)(2,1)S(1)} %get-tuple-element.117), channel_id=1, source_target_pairs={{0,24},{1,97},{2,26},{3,99},{4,28},{5,101},{6,30},{7,103},{8,0},{9... | collective-permute-start | bytes 3145736 | tf_op jit(solution)/shard_map/ppermute | solution.py:47
  74.9 16.2 %collective-permute-start.18 = (bf16[64,4096]{1,0:T(8,128)(2,1)S(1)}, bf16[64,4096]{1,0:T(8,128)(2,1)S(1)}, u32[]{:S(2)}, u32[]{:S(2)}) collective-permute-start(bf16[64,4096]{1,0:T(8,128)(2,1)S(1)} %get-tuple-element.135), channel_id=1, source_target_pairs={{0,2},{1,7},{2,4},{3,1},{4,6},{5,3},{6,0},{7,5},{8,10},{9,15},{10,... | collective-permute-start | bytes 1572872 | tf_op jit(solution)/shard_map/ppermute | solution.py:47
  77.4 16.7 %collective-permute-start.19 = (bf16[64,4096]{1,0:T(8,128)(2,1)S(1)}, bf16[64,4096]{1,0:T(8,128)(2,1)S(1)}, u32[]{:S(2)}, u32[]{:S(2)}) collective-permute-start(bf16[64,4096]{1,0:T(8,128)(2,1)S(1)} %get-tuple-element.136), channel_id=1, source_target_pairs={{0,6},{1,3},{2,0},{3,5},{4,2},{5,7},{6,4},{7,1},{8,14},{9,11},{10,... | collective-permute-start | bytes 1572872 | tf_op jit(solution)/shard_map/ppermute | solution.py:47
  87.1 7.1 %collective-permute-start.20 = (bf16[256,512]{1,0:T(8,128)(2,1)S(1)}, bf16[256,512]{1,0:T(8,128)(2,1)S(1)}, u32[]{:S(2)}, u32[]{:S(2)}) collective-permute-start(bf16[256,512]{1,0:T(8,128)(2,1)S(1)} %get-tuple-element.126), channel_id=1, source_target_pairs={{0,64},{1,17},{2,66},{3,19},{4,68},{5,21},{6,70},{7,23},{8,72},{9,... | collective-permute-start | bytes 786440 | tf_op jit(solution)/shard_map/ppermute | solution.py:47
  88.4 10.5 %collective-permute-start.21 = (bf16[256,512]{1,0:T(8,128)(2,1)S(1)}, bf16[256,512]{1,0:T(8,128)(2,1)S(1)}, u32[]{:S(2)}, u32[]{:S(2)}) collective-permute-start(bf16[256,512]{1,0:T(8,128)(2,1)S(1)} %get-tuple-element.127), channel_id=1, source_target_pairs={{0,32},{1,9},{2,34},{3,11},{4,36},{5,13},{6,38},{7,15},{8,40},{9,1... | collective-permute-start | bytes 786440 | tf_op jit(solution)/shard_map/ppermute | solution.py:47
  89.8 10.1 %collective-permute-start.22 = (bf16[256,512]{1,0:T(8,128)(2,1)S(1)}, bf16[256,512]{1,0:T(8,128)(2,1)S(1)}, u32[]{:S(2)}, u32[]{:S(2)}) collective-permute-start(bf16[256,512]{1,0:T(8,128)(2,1)S(1)} %get-tuple-element.128), channel_id=1, source_target_pairs={{0,96},{1,25},{2,98},{3,27},{4,100},{5,29},{6,102},{7,31},{8,104},... | collective-permute-start | bytes 786440 | tf_op jit(solution)/shard_map/ppermute | solution.py:47
  91.1 9.9 %collective-permute-start.23 = (bf16[256,512]{1,0:T(8,128)(2,1)S(1)}, bf16[256,512]{1,0:T(8,128)(2,1)S(1)}, u32[]{:S(2)}, u32[]{:S(2)}) collective-permute-start(bf16[256,512]{1,0:T(8,128)(2,1)S(1)} %get-tuple-element.130), channel_id=1, source_target_pairs={{0,65},{1,16},{2,67},{3,18},{4,69},{5,20},{6,71},{7,22},{8,73},{9,... | collective-permute-start | bytes 786440 | tf_op jit(solution)/shard_map/ppermute | solution.py:47
  94.1 9.6 %collective-permute-start.24 = (bf16[256,512]{1,0:T(8,128)(2,1)S(1)}, bf16[256,512]{1,0:T(8,128)(2,1)S(1)}, u32[]{:S(2)}, u32[]{:S(2)}) collective-permute-start(bf16[256,512]{1,0:T(8,128)(2,1)S(1)} %get-tuple-element.131), channel_id=1, source_target_pairs={{0,33},{1,8},{2,35},{3,10},{4,37},{5,12},{6,39},{7,14},{8,41},{9,1... | collective-permute-start | bytes 786440 | tf_op jit(solution)/shard_map/ppermute | solution.py:47
  94.2 9.5 %collective-permute-start.25 = (bf16[256,512]{1,0:T(8,128)(2,1)S(1)}, bf16[256,512]{1,0:T(8,128)(2,1)S(1)}, u32[]{:S(2)}, u32[]{:S(2)}) collective-permute-start(bf16[256,512]{1,0:T(8,128)(2,1)S(1)} %get-tuple-element.132), channel_id=1, source_target_pairs={{0,97},{1,24},{2,99},{3,26},{4,101},{5,28},{6,103},{7,30},{8,105},... | collective-permute-start | bytes 786440 | tf_op jit(solution)/shard_map/ppermute | solution.py:47
  98.9 4.8 %collective-permute-start.26 = (bf16[256,512]{1,0:T(8,128)(2,1)S(1)}, bf16[256,512]{1,0:T(8,128)(2,1)S(1)}, u32[]{:S(2)}, u32[]{:S(2)}) collective-permute-start(bf16[256,512]{1,0:T(8,128)(2,1)S(1)} %get-tuple-element.133), channel_id=1, source_target_pairs={{0,1},{1,0},{2,3},{3,2},{4,5},{5,4},{6,7},{7,6},{8,9},{9,8},{10,11... | collective-permute-start | bytes 786440 | tf_op jit(solution)/shard_map/ppermute | solution.py:47
